TPU v7x, 32 devices: a whole 2x2x4 slice. The times are simulated.
32 devices in a mesh: dp: 16 (over z, x, core), tensor: 2 (over y).
Axes of the slice: x: 2, y: 2, z: 4, core: 2. Of those that a mesh axis runs over, the one named last changes fastest.
Arguments:
- hidden_in: bfloat16 [64, 512, 768], P(('dp', 'tensor')), may hold values from -6 to 6
- lengths: int32 [64], P('dp'), may hold values from 32 to 512, as said below
- queries: bfloat16 [64, 768], P(('dp', 'tensor')), may hold values from -6 to 6
- positives: int32 [64], P(('dp', 'tensor')), may hold values from 0 to 63, each once
- gain_attn: float32 [768], replicated, may hold values from 0.5 to 1.5
- w_query: bfloat16 [768, 768], P(None, 'tensor'), may hold values from -0.0546875 to 0.0546875
- w_key: bfloat16 [768, 768], P(None, 'tensor'), may hold values from -0.21875 to 0.21875
- w_value: bfloat16 [768, 768], P(None, 'tensor'), may hold values from -0.21875 to 0.21875
- w_out: bfloat16 [768, 768], P('tensor'), may hold values from -1.25 to 1.25
- rel_table: float32 [32, 12], P(None, 'tensor'), may hold values from -6 to 6
- gain_ffn: float32 [768], replicated, may hold values from 0.5 to 1.5
- w_inner: bfloat16 [768, 3072], P(None, 'tensor'), may hold values from -0.21875 to 0.21875
- w_outer: bfloat16 [3072, 768], P('tensor'), may hold values from -0.109375 to 0.109375
- w_proj: bfloat16 [768, 768], replicated, may hold values from -0.21875 to 0.21875
Outputs:
- layer_out: bfloat16 [64, 512, 768], P(('dp', 'tensor'))
- query_loss: float32 [64], P(('dp', 'tensor'))
- input_grad: float32 [64, 512, 768], P(('dp', 'tensor'))
- gain_attn_grad: float32 [768], replicated
- query_w_grad: float32 [768, 768], P(None, 'tensor')
- key_w_grad: float32 [768, 768], P(None, 'tensor')
- value_w_grad: float32 [768, 768], P(None, 'tensor')
- out_w_grad: float32 [768, 768], P('tensor')
- table_grad: float32 [32, 12], P(None, 'tensor')
- gain_ffn_grad: float32 [768], replicated
- inner_w_grad: float32 [768, 3072], P(None, 'tensor')
- outer_w_grad: float32 [3072, 768], P('tensor')
- proj_w_grad: float32 [768, 768], replicated
Inputs may be any that keep to these rules, and one draw needn't show every extreme that they name: `lengths`: among the 4 passages of each index of dp one has exactly 512 tokens. `positives`: each passage is the positive of exactly one query.
All inputs are finite; a program needn't handle non-finite values.
Results may differ from a plain program's by a relative error of at most 0.028.
Values may be sent and summed in bfloat16 or wider, within the bound.
No kernel may reach another device: no remote copies, remote signals or barrier semaphores. Data moves between devices by JAX's collectives and lax.ppermute only.
A program may use at most 192 MiB of HBM per device.

v0:
```python
import functools

import numpy as np

import jax
import jax.numpy as jnp
from jax import lax
from jax.experimental import pallas as pl
from jax.experimental.pallas import tpu as pltpu
from jax.sharding import PartitionSpec as P

LARGE_STEPS = (12, 16, 23, 32, 46, 64, 91)
SHARPNESS = 0.02
LOSS_SCALE = 256.0
EPS = 1e-06
NEG = -1e30
BF = jnp.bfloat16
F32 = jnp.float32
TILE = 128
BUCKETS = 32
GELU_A = 0.7978845608028654
GELU_B = 0.044715
MIB = 1024 * 1024

NN = (((1,), (0,)), ((), ()))
NT = (((1,), (1,)), ((), ()))
TN = (((0,), (0,)), ((), ()))


def mm(a, b, dims=NN):
    return lax.dot_general(a, b, dims, preferred_element_type=F32)


def bucket_of(r):
    a = np.abs(r)
    far = 8 + sum((a >= t).astype(np.int32) for t in LARGE_STEPS)
    return np.where(r > 0, 16, 0) + np.where(a < 8, a, far)


def diag_onehot(buckets, back):
    lane = np.arange(2 * TILE)
    at = lane - TILE + 1 if back else TILE - 1 - lane
    idx = np.concatenate([bucket_of(TILE * d + at) for d in (-1, 0, 1)])
    hot = (idx[:, None] == np.arange(buckets)[None, :]).astype(np.float32)
    hot[2 * TILE - 1 :: 2 * TILE] = 0.0
    return hot


def params(**kw):
    return pltpu.CompilerParams(vmem_limit_bytes=60 * MIB, **kw)


def cost(us):
    return pl.CostEstimate(flops=0, bytes_accessed=int(us * 3.6e6), transcendentals=0)

ANY = pl.BlockSpec(memory_space=pl.ANY)
SMEM_SPEC = pl.BlockSpec(memory_space=pltpu.SMEM)


def const_spec(shape):
    zeros = (0,) * len(shape)
    return pl.BlockSpec(tuple(shape), lambda b: zeros, pipeline_mode=pl.Buffered(1))


def out_const(shape):
    zeros = (0,) * len(shape)
    return pl.BlockSpec(tuple(shape), lambda b: zeros)


def row_spec(shape):
    tail = (0,) * (len(shape) - 1)
    return pl.BlockSpec((1,) + tuple(shape[1:]), lambda b: (b,) + tail)


def sds(shape, dtype):
    return jax.ShapeDtypeStruct(tuple(shape), dtype)


def split3(t):
    hi = t.astype(BF)
    rest = t - hi.astype(F32)
    mid = rest.astype(BF)
    return hi, mid, (rest - mid.astype(F32)).astype(BF)


def run_copies(copies):
    for c in copies:
        c.start()
    for c in copies:
        c.wait()


def pack_kernel(at_ref, tab_ref, wq, wk, wv, wo, wi, wu, s0, s1, s2, s3, sem):
    at = at_ref[0]
    width = wq.shape[1]
    rows = s2.shape[0]

    def part(w, dst, i, spot, count):
        src = w.at[pl.ds(pl.multiple_of(spot * count, count), count)]
        return pltpu.make_async_copy(src, dst, sem.at[i])

    spread = [(w, s0.at[pl.ds(0, rows), width * i : width * (i + 1)]) for i, w in enumerate((wq, wk, wv))]
    copies = [part(w, dst, i, at, rows) for i, (w, dst) in enumerate(spread + [(wi, s2)])]
    copies += [part(w, dst, 4 + i, at // 2, dst.shape[0]) for i, (w, dst) in enumerate(((wo, s1), (wu, s3)))]
    for c in copies:
        c.start()
    s0[rows:, :] = jnp.zeros((16, s0.shape[1]), BF)
    heads, buckets = tab_ref.shape
    for k, t in enumerate(split3(tab_ref[...])):
        s0[rows : rows + heads, TILE * k : TILE * k + buckets] = t
    for c in copies:
        c.wait()


def pack_weights(at, table, wq, wk, wv, wo, wi, wu):
    d, half = wi.shape
    width = wq.shape[1]
    vm = pl.BlockSpec(memory_space=pltpu.VMEM)
    return pl.pallas_call(
        pack_kernel,
        in_specs=[SMEM_SPEC, vm] + [ANY] * 6,
        out_specs=[vm] * 4,
        out_shape=[
            sds((d // 4 + 16, 3 * width), BF),
            sds((width // 2, d), BF),
            sds((d // 4, half), BF),
            sds((half // 2, d), BF),
        ],
        scratch_shapes=[pltpu.SemaphoreType.DMA((6,))],
        compiler_params=params(),
        cost_estimate=cost(3),
        name="pack_weights",
    )(at, table, wq, wk, wv, wo, wi, wu)


def join_copies(at, packs, dst, sem):
    core, xb = at // 2, at % 2
    spots = [at, 2 * core + 1 - xb, 2 * (1 - core) + xb, 2 * (1 - core) + 1 - xb]
    if len(packs) == 2:
        spots = [core, 1 - core]
    rows = dst.shape[0] // len(packs)
    out = []
    for i, (p, s) in enumerate(zip(packs, spots)):
        to = dst.at[pl.ds(pl.multiple_of(s * rows, rows), rows)]
        out.append(pltpu.make_async_copy(p.at[pl.ds(0, rows)], to, sem.at[i]))
    return out


EXTRA = 16


def key_extras(length, rows):
    row = lax.broadcasted_iota(jnp.int32, (rows, TILE), 0)
    lane = lax.broadcasted_iota(jnp.int32, (rows, TILE), 1) & 63
    blk = (lane - 1) & 3
    hot = (lane >= 1) & (lane < 13) & (blk == row // TILE)
    one = ((lane == 0) & (row >= length)) | hot | ((lane >= 13) & (lane < EXTRA))
    return jnp.where(one, 1.0, 0.0)


def far_rows(tf_ref, h, seq):
    row = lax.broadcasted_iota(jnp.int32, (EXTRA, seq), 0)
    diff = ((row - 1) & 3) - lax.broadcasted_iota(jnp.int32, (EXTRA, seq), 1) // TILE
    out = jnp.where(row == 0, NEG, 0.0)
    last, mid = BUCKETS - 1, BUCKETS // 2 - 1
    for k in range(3):
        mine = (row >= 1 + 4 * k) & (row < 5 + 4 * k)
        out = out + jnp.where(mine & (diff >= 2), tf_ref[k, h : h + 1, last : last + 1], 0.0)
        out = out + jnp.where(mine & (diff <= -2), tf_ref[k, h : h + 1, mid : mid + 1], 0.0)
    return out


def stack_rows(e, main, extra):
    pad = jnp.zeros((64 - extra.shape[0], extra.shape[1]), BF)
    return jnp.concatenate([main, extra, pad] if e == 0 else [extra, pad, main], axis=0)


def near_bias(s, nb_ref, h, ib):
    rows = []
    for bj in range(s.shape[0] // TILE):
        parts = []
        for t in range(2):
            piece = s[TILE * bj : TILE * (bj + 1), TILE * t : TILE * (t + 1)]
            d = bj - (2 * ib + t)
            parts.append(piece + nb_ref[3 * h + d + 1] if abs(d) <= 1 else piece)
        rows.append(jnp.concatenate(parts, axis=1))
    return rows


def set_bias(parts, hot_ref, tf_ref, nb_ref):
    for k in range(3):
        tf_ref[k] = parts[k].astype(F32)
    hot = hot_ref[...]
    bv = mm(parts[0], hot) + mm(parts[1], hot) + mm(parts[2], hot)
    for t in range(nb_ref.shape[0]):
        h, k = t // 3, t % 3
        v = jnp.broadcast_to(bv[h : h + 1, 2 * TILE * k : 2 * TILE * (k + 1)], (TILE, 2 * TILE))
        nb_ref[t] = pltpu.roll(v, TILE + 1, 1, stride=1, stride_axis=0)[:, :TILE]


def attn_rows(an, length, ws, outs, nb_ref, tf_ref, s_ref, p_ref):
    q_ref, qt_ref, k_ref, v_ref, ctx_ref, ctxt_ref, lse_ref = outs
    seq = an.shape[0]
    width = q_ref.shape[2]
    for ref, w in zip((q_ref, k_ref, v_ref), ws):
        ref[0] = mm(an, w[...]).astype(BF)
    kx = key_extras(length, seq)
    lane = lax.broadcasted_iota(jnp.int32, (seq, TILE), 1)
    blocks = [(h, ib) for h in range(width // 64) for ib in range(seq // 256)]
    keys, queries, values, tops, sums, rows = {}, {}, {}, {}, {}, {}

    def prepare(h):
        pair, e = h // 2, h % 2
        cols = slice(TILE * pair, TILE * (pair + 1))
        if e == 0:
            qt_ref[0, cols, :] = jnp.transpose(q_ref[0, :, cols])
            values[pair] = jnp.transpose(v_ref[0, :, cols])
        mine = lane < 64 if e == 0 else lane >= 64
        keys[h] = jnp.where(mine, k_ref[0, :, cols].astype(F32), kx).astype(BF)
        qt = qt_ref[0, 64 * h : 64 * (h + 1), :]
        queries[h] = stack_rows(e, qt, far_rows(tf_ref, h, seq).astype(BF))

    def score(t):
        h, ib = blocks[t]
        if ib == 0:
            prepare(h)
        s = mm(keys[h], queries[h][:, 256 * ib : 256 * (ib + 1)])
        top = None
        for bj, piece in enumerate(near_bias(s, nb_ref, h, ib)):
            s_ref[t % 2, TILE * bj : TILE * (bj + 1), :] = piece
            m = jnp.max(piece.reshape(TILE // 8, 8, 256), axis=0)
            top = m if top is None else jnp.maximum(top, m)
        tops[t] = jnp.max(top, axis=0, keepdims=True)

    def soft(t):
        h, ib = blocks[t]
        total = None
        for bj in range(seq // TILE):
            at = slice(TILE * bj, TILE * (bj + 1))
            p = jnp.exp(s_ref[t % 2, at, :] - tops[t])
            one = jnp.sum(p.reshape(TILE // 8, 8, 256), axis=0)
            total = one if total is None else total + one
            p_ref[h % 2, at, 256 * ib : 256 * (ib + 1)] = p.astype(BF)
        sums[t] = jnp.sum(total, axis=0, keepdims=True)
        lse_ref[0, h : h + 1, 256 * ib : 256 * (ib + 1)] = tops[t] + jnp.log(sums[t])

    def combine(h):
        per = seq // 256
        total = jnp.concatenate([sums[per * h + i] for i in range(per)], axis=1)
        vt = values[h // 2][64 * (h % 2) : 64 * (h % 2 + 1), :]
        rows[h] = mm(vt, p_ref[h % 2]) * (1.0 / total)
        if h % 2 == 1:
            pair = h // 2
            cols = slice(TILE * pair, TILE * (pair + 1))
            ct = jnp.concatenate([rows[h - 1], rows[h]], axis=0).astype(BF)
            ctxt_ref[0, cols, :] = ct
            ctx_ref[0, :, cols] = jnp.transpose(ct)

    score(0)
    for t, (h, ib) in enumerate(blocks):
        if t + 1 < len(blocks):
            score(t + 1)
        soft(t)
        if ib == seq // 256 - 1:
            combine(h)


def attn_own_kernel(lens, x_ref, gain_ref, wq, wk, wv, tab_ref, hot_ref, an_ref, ant_ref, *refs):
    outs, (nb_ref, tf_ref, s_ref, p_ref) = refs[:7], refs[7:]
    b = pl.program_id(0)

    @pl.when(b == 0)
    def _():
        heads, buckets = tab_ref.shape
        wide = jnp.concatenate([tab_ref[...], jnp.zeros((heads, TILE - buckets), F32)], axis=1)
        wide = jnp.concatenate([wide, jnp.zeros((16 - heads, TILE), F32)], axis=0)
        set_bias(split3(wide), hot_ref, tf_ref, nb_ref)

    x = x_ref[0].astype(F32)
    inv = lax.rsqrt(jnp.mean(x * x, axis=-1, keepdims=True) + EPS)
    an = (x * inv * gain_ref[...]).astype(BF)
    an_ref[0] = an
    ant_ref[...] = jnp.transpose(an)
    attn_rows(an, lens[b], (wq, wk, wv), outs, nb_ref, tf_ref, s_ref, p_ref)


def attn_other_kernel(lens, at_ref, an_ref, hot_ref, x_ref, ca_ref, wo_ref, gain_ref, p0, p1, p2, p3, o0, o1, *refs):
    outs, (nb_ref, tf_ref, res_ref, fin_ref, fint_ref, rsum_ref) = refs[:7], refs[7:13]
    (s_ref, p_ref, w_ref, tab_ref, wb_ref, sem, sem1) = refs[13:]
    b = pl.program_id(0)
    late = join_copies(at_ref[0], (o0, o1), wb_ref, sem1)

    @pl.when(b == 0)
    def _():
        rows = w_ref.shape[0] // 4
        copies = join_copies(at_ref[0], (p0, p1, p2, p3), w_ref, sem)
        copies.append(pltpu.make_async_copy(p0.at[pl.ds(rows, 16)], tab_ref, sem.at[4]))
        for c in copies + late:
            c.start()
        for c in copies:
            c.wait()
        parts = [tab_ref[:, TILE * k : TILE * (k + 1)] for k in range(3)]
        set_bias(parts, hot_ref, tf_ref, nb_ref)

    width = outs[0].shape[2]
    ws = [w_ref.at[:, width * k : width * (k + 1)] for k in range(3)]
    attn_rows(an_ref[0], lens[b], ws, outs, nb_ref, tf_ref, s_ref, p_ref)

    @pl.when(b == 0)
    def _():
        for c in late:
            c.wait()

    res = x_ref[0].astype(F32) + mm(ca_ref[0], wo_ref[...]) + mm(outs[4][0], wb_ref[...])
    res_ref[0] = res
    inv = lax.rsqrt(jnp.mean(res * res, axis=-1, keepdims=True) + EPS)
    fin = (res * inv * gain_ref[...]).astype(BF)
    fin_ref[0] = fin
    fint_ref[...] = jnp.transpose(fin)
    vcol = (lax.broadcasted_iota(jnp.int32, (res.shape[0], TILE), 0) < lens[b]).astype(F32)[:, :1]
    rsum_ref[0] = jnp.sum(res * vcol, axis=0, keepdims=True)


def attn_outs(n, seq, width):
    heads = width // 64
    tok, turned = sds((n, seq, width), BF), sds((n, width, seq), BF)
    rows = [tok, turned, tok, tok, tok, turned, sds((n, 8, seq), F32)]
    flat = [sds((3 * heads, TILE, TILE), F32), sds((3, 16, TILE), F32)]
    scratch = [pltpu.VMEM((2, seq, 256), F32), pltpu.VMEM((2, seq, seq), BF)]
    return rows + flat, [row_spec(o.shape) for o in rows] + [out_const(o.shape) for o in flat], scratch


def attn_own(lens, x, gain, wq, wk, wv, table, hot):
    n, seq, d = x.shape
    outs, specs, scratch = attn_outs(n, seq, wq.shape[1])
    return pl.pallas_call(
        attn_own_kernel,
        grid=(n,),
        in_specs=[SMEM_SPEC, row_spec(x.shape), const_spec((1, d))]
        + [const_spec(wq.shape)] * 3
        + [const_spec(table.shape), const_spec(hot.shape)],
        out_specs=[row_spec(x.shape), pl.BlockSpec((d, seq), lambda b: (0, b))] + specs,
        out_shape=[sds((n, seq, d), BF), sds((d, n * seq), BF)] + outs,
        scratch_shapes=scratch,
        compiler_params=params(),
        cost_estimate=cost(12),
        name="attn_own",
    )(lens, x, gain.reshape(1, d), wq, wk, wv, table, hot)


def attn_other(lens, at, an, hot, x, ctx_a, wo, gain, packs, packs_o):
    n, seq, d = an.shape
    width = wo.shape[0]
    outs, specs, scratch = attn_outs(n, seq, width)
    more = [sds((n, seq, d), F32), sds((n, seq, d), BF), sds((d, n * seq), BF), sds((n, 1, d), F32)]
    more_specs = [row_spec(o.shape) for o in more]
    more_specs[2] = pl.BlockSpec((d, seq), lambda b: (0, b))
    return pl.pallas_call(
        attn_other_kernel,
        grid=(n,),
        in_specs=[SMEM_SPEC, SMEM_SPEC, row_spec(an.shape), const_spec(hot.shape), row_spec(x.shape)]
        + [row_spec(ctx_a.shape), const_spec(wo.shape), const_spec((1, d))]
        + [ANY] * 6,
        out_specs=specs + more_specs,
        out_shape=outs + more,
        scratch_shapes=scratch
        + [
            pltpu.VMEM((d, 3 * width), BF),
            pltpu.VMEM((16, 3 * width), BF),
            pltpu.VMEM(wo.shape, BF),
            pltpu.SemaphoreType.DMA((5,)),
            pltpu.SemaphoreType.DMA((2,)),
        ],
        compiler_params=params(),
        cost_estimate=cost(15),
        name="attn_other",
    )(lens, at, an, hot, x, ctx_a, wo, gain.reshape(1, d), *packs, *packs_o)


def attn_bwd_kernel(lens, at_ref, *refs):
    (q_ref, qt_ref, k_ref, v_ref, dc_ref, dct_ref, ct_ref, lse_ref, nb_ref, tf_ref, hot_ref, ant_hbm, go_hbm) = refs[:13]
    (dq_ref, dk_ref, dv_ref, send_ref, keep_ref, table_ref) = refs[13:19]
    (t_ref, fsum_ref, p_ref, ds_ref, all_ref, ant_ref, go_ref, sem) = refs[19:]
    b = pl.program_id(0)
    seq, width = q_ref.shape[1], q_ref.shape[2]
    heads = width // 64
    nblk = seq // TILE

    late = [pltpu.make_async_copy(ant_hbm, ant_ref, sem.at[0]), pltpu.make_async_copy(go_hbm, go_ref, sem.at[1])]

    @pl.when(b == 0)
    def _():
        for c in late:
            c.start()
        t_ref[...] = jnp.zeros_like(t_ref)
        fsum_ref[...] = jnp.zeros_like(fsum_ref)
        table_ref[...] = jnp.zeros_like(table_ref)

    kx = key_extras(lens[b], seq)
    lane = lax.broadcasted_iota(jnp.int32, (seq, TILE), 1)
    vx = jnp.where((lane & 63) < 3, 1.0, 0.0)
    keys, values, queries, grads, turned = {}, {}, {}, {}, {}

    def prepare(h):
        pair, e = h // 2, h % 2
        cols = slice(TILE * pair, TILE * (pair + 1))
        mine = lane < 64 if e == 0 else lane >= 64
        if e == 0:
            turned[pair] = jnp.transpose(k_ref[0, :, cols])
        keys[h] = jnp.where(mine, k_ref[0, :, cols].astype(F32), kx).astype(BF)
        values[h] = jnp.where(mine, v_ref[0, :, cols].astype(F32), vx).astype(BF)
        at = slice(64 * h, 64 * (h + 1))
        lse = split3(-lse_ref[0, h : h + 1, :])
        extra = far_rows(tf_ref, h, seq)
        row = lax.broadcasted_iota(jnp.int32, (EXTRA, seq), 0)
        for k in range(3):
            extra = jnp.where(row == 13 + k, lse[k].astype(F32), extra)
        queries[h] = stack_rows(e, qt_ref[0, at, :], extra.astype(BF))
        along = jnp.sum(dct_ref[0, at, :].astype(F32) * ct_ref[0, at, :].astype(F32), axis=0, keepdims=True)
        extra = jnp.zeros((EXTRA, seq), F32)
        for k, part in enumerate(split3(-along)):
            extra = jnp.where(row == k, part.astype(F32), extra)
        grads[h] = stack_rows(e, dct_ref[0, at, :], extra.astype(BF))

    def block(h, ib):
        pair, e = h // 2, h % 2
        at = slice(256 * ib, 256 * (ib + 1))
        to = slice(seq * e + 256 * ib, seq * e + 256 * (ib + 1))
        s = mm(keys[h], queries[h][:, at])
        dp = mm(values[h], grads[h][:, at])
        near, far = {}, {}
        for bj, piece in enumerate(near_bias(s, nb_ref, h, ib)):
            rows = slice(TILE * bj, TILE * (bj + 1))
            p = jnp.exp(piece)
            ds = p * dp[rows, :]
            p_ref[pair % 2, rows, to] = p.astype(BF)
            ds_ref[pair % 2, rows, to] = ds.astype(BF)
            for t in range(2):
                d = bj - (2 * ib + t)
                one = ds[:, TILE * t : TILE * (t + 1)]
                if abs(d) <= 1:
                    near[d] = near[d] + one if d in near else one
                else:
                    one = jnp.sum(one.reshape(TILE // 8, 8, TILE), axis=0)
                    side = 1 if d > 0 else 0
                    far[side] = far[side] + one if side in far else one
        for d, one in near.items():
            t_ref[3 * h + d + 1] += one
        for side, one in far.items():
            fsum_ref[2 * h + side] += one

    def finish(pair, part):
        slot = pair % 2
        cols = slice(TILE * pair, TILE * (pair + 1))
        rows = pl.ds(pl.multiple_of(b * seq, seq), seq)
        if part < 2:
            src, other, out_ref = ((p_ref, dc_ref, dv_ref), (ds_ref, q_ref, dk_ref))[part]
            rhs = other[0, :, cols]
            one = jnp.where(lane < 64, mm(src[slot, :, :seq], rhs), mm(src[slot, :, seq:], rhs)).astype(BF)
            out_ref[0, :, cols] = one
            base = width * (2 - part)
            all_ref[rows, base + TILE * pair : base + TILE * (pair + 1)] = one
        if part == 2:
            kt = turned[pair]
            dqt = [mm(kt[64 * e : 64 * (e + 1), :], ds_ref[slot, :, seq * e : seq * (e + 1)]) for e in range(2)]
            one = jnp.transpose(jnp.concatenate(dqt, axis=0).astype(BF))
            dq_ref[0, :, cols] = one
            all_ref[rows, TILE * pair : TILE * (pair + 1)] = one

    for pair in range(heads // 2):
        step = 0
        for e in range(2):
            prepare(2 * pair + e)
            for ib in range(seq // 256):
                block(2 * pair + e, ib)
                if pair > 0 and step < 3:
                    finish(pair - 1, step)
                step += 1
    for part in range(3):
        finish(heads // 2 - 1, part)

    @pl.when(b == pl.num_programs(0) - 1)
    def _():
        for c in late:
            c.wait()
        rows = ant_ref.shape[0] // 2
        core = at_ref[0] // 2
        for ref, half in ((send_ref, 1 - core), (keep_ref, core)):
            at = pl.ds(pl.multiple_of(half * rows, rows), rows)
            ref[:, : 3 * width] = mm(ant_ref[at, :], all_ref[...]).astype(BF)
            ref[:, 3 * width :] = go_ref[at, :].astype(BF)
        turn = lax.broadcasted_iota(jnp.int32, (TILE, TILE), 0) + lax.broadcasted_iota(jnp.int32, (TILE, TILE), 1)
        turn = jnp.where(turn == TILE - 1, 1.0, 0.0).astype(BF)
        tiles = t_ref.shape[0]
        parts = split3(t_ref[...].reshape(tiles * TILE, TILE))
        back = mm(parts[0], turn) + mm(parts[1], turn) + mm(parts[2], turn)
        diag = []
        for t in range(tiles):
            x = jnp.concatenate([back[TILE * t : TILE * (t + 1)], jnp.zeros((TILE, TILE), F32)], axis=1)
            x = pltpu.roll(x, 0, 1, stride=1, stride_axis=0)
            diag.append(jnp.sum(x, axis=0, keepdims=True))
        rows = [jnp.concatenate(diag[3 * h : 3 * h + 3], axis=1) for h in range(heads)]
        rows.append(jnp.zeros((16 - heads, rows[0].shape[1]), F32))
        near = [mm(part, hot_ref[...]) for part in split3(jnp.concatenate(rows, axis=0))]
        lane = lax.broadcasted_iota(jnp.int32, (1, TILE), 1)
        for h in range(heads):
            one = near[0][h : h + 1] + near[1][h : h + 1] + near[2][h : h + 1]
            for side, bucket in ((0, BUCKETS // 2 - 1), (1, BUCKETS - 1)):
                far = jnp.sum(jnp.sum(fsum_ref[2 * h + side], axis=0, keepdims=True), axis=1, keepdims=True)
                one = one + jnp.where(lane == bucket, far, 0.0)
            table_ref[h : h + 1, :] = one


def attn_bwd(lens, at, q, qt, k, v, dctx, dctxt, ctxt, lse, nb, tf, hot, ant, go):
    n, seq, width = q.shape
    d = ant.shape[0]
    heads = width // 64
    tok = sds((n, seq, width), BF)
    flat = [
        sds((d // 2, 4 * width), BF),
        sds((d // 2, 4 * width), BF),
        sds((8, TILE), F32),
    ]
    ins = [q, qt, k, v, dctx, dctxt, ctxt, lse]
    return pl.pallas_call(
        attn_bwd_kernel,
        grid=(n,),
        in_specs=[SMEM_SPEC, SMEM_SPEC]
        + [row_spec(x.shape) for x in ins]
        + [const_spec(nb.shape), const_spec(tf.shape), const_spec(hot.shape), ANY, ANY],
        out_specs=[row_spec(q.shape)] * 3 + [out_const(o.shape) for o in flat],
        out_shape=[tok, tok, tok] + flat,
        scratch_shapes=[
            pltpu.VMEM((3 * heads, TILE, TILE), F32),
            pltpu.VMEM((2 * heads, 8, TILE), F32),
            pltpu.VMEM((2, seq, 2 * seq), BF),
            pltpu.VMEM((2, seq, 2 * seq), BF),
            pltpu.VMEM((n * seq, 3 * width), BF),
            pltpu.VMEM(ant.shape, BF),
            pltpu.VMEM(go.shape, F32),
            pltpu.SemaphoreType.DMA((2,)),
        ],
        compiler_params=params(),
        cost_estimate=cost(20),
        name="attn_bwd",
    )(lens, at, *ins, nb, tf, hot, ant, go)


def gelu_parts(v):
    v2 = v * v
    th = jnp.tanh(v * (GELU_A + (GELU_A * GELU_B) * v2))
    hh = 0.5 + 0.5 * th
    slope = hh + (v * (0.5 - 0.5 * th * th)) * (GELU_A + (3.0 * GELU_A * GELU_B) * v2)
    return v * hh, slope


def ffn_fwd_kernel(lens, at_ref, fin_ref, rs_ref, wi_ref, wu_ref, p0, p1, p2, p3, *refs):
    (act_ref, gp_ref, actb_ref, gpb_ref, asum_ref, rsum_ref) = refs[:6]
    (wib_ref, wu_buf, v_ref, sem1, sem2) = refs[6:]
    b = pl.program_id(0)
    late = join_copies(at_ref[0], (p0, p1, p2, p3), wib_ref, sem1) + [pltpu.make_async_copy(wu_ref, wu_buf, sem2)]

    @pl.when(b == 0)
    def _():
        for c in late:
            c.start()

    fin = fin_ref[0]
    seq = fin.shape[0]
    half = wi_ref.shape[1]
    chunk = v_ref.shape[2]
    length = lens[b]
    vrow = (lax.broadcasted_iota(jnp.int32, (8, seq), 1) < length).astype(F32).astype(BF)
    vcol = (lax.broadcasted_iota(jnp.int32, (seq, TILE), 0) < length).astype(F32)[:, :1]
    spot = lambda c: slice(c * chunk, (c + 1) * chunk)
    parts = [(w, a, g, c) for w, a, g in ((wi_ref, act_ref, gp_ref), (wib_ref, actb_ref, gpb_ref)) for c in range(half // chunk)]

    def project(t):
        w, _, _, c = parts[t]
        v_ref[t % 2] = mm(fin, w[:, spot(c)])

    project(0)
    for t, (_, a_ref, g_ref, c) in enumerate(parts):
        if t + 1 == half // chunk:

            @pl.when(b == 0)
            def _():
                for copy in late:
                    copy.wait()

        if t + 1 < len(parts):
            project(t + 1)
        for r in range(seq // TILE):
            rows = slice(TILE * r, TILE * (r + 1))
            act, slope = gelu_parts(v_ref[t % 2, rows, :])
            a_ref[0, rows, spot(c)] = act.astype(BF)
            g_ref[0, rows, spot(c)] = (slope * vcol[rows]).astype(BF)
        asum_ref[0, :, spot(t)] = mm(vrow, a_ref[0, :, spot(c)])[:1]
    own = asum_ref[0, :, :half]
    hi = own.astype(BF)
    lo = (own - hi.astype(F32)).astype(BF)
    two_rows = jnp.concatenate([hi.astype(F32), lo.astype(F32), jnp.zeros((14, half), F32)], axis=0).astype(BF)
    branch = mm(two_rows, wu_buf[...])
    rsum_ref[0] = rs_ref[0] + branch[0:1] + branch[1:2]


def ffn_fwd(lens, at, fin, rsum, wi, wu, packs):
    n, seq, d = fin.shape
    half = wi.shape[1]
    wide = sds((n, seq, half), BF)
    outs = [wide, wide, wide, wide, sds((n, 1, 2 * half), F32), sds((n, 1, d), F32)]
    return pl.pallas_call(
        ffn_fwd_kernel,
        grid=(n,),
        in_specs=[SMEM_SPEC, SMEM_SPEC, row_spec(fin.shape), row_spec(rsum.shape), const_spec(wi.shape)] + [ANY] * 5,
        out_specs=[row_spec(o.shape) for o in outs],
        out_shape=outs,
        scratch_shapes=[
            pltpu.VMEM(wi.shape, BF),
            pltpu.VMEM(wu.shape, BF),
            pltpu.VMEM((2, seq, 512), F32),
            pltpu.SemaphoreType.DMA((4,)),
            pltpu.SemaphoreType.DMA,
        ],
        compiler_params=params(),
        cost_estimate=cost(16),
        name="ffn_fwd",
    )(lens, at, fin, rsum, wi, wu, *packs)


def pool_kernel(lens, at_ref, asum_ref, rs_ref, p0, p1, out_ref, wb_ref, sem):
    run_copies(join_copies(at_ref[0], (p0, p1), wb_ref, sem))
    n = asum_ref.shape[0]
    half = wb_ref.shape[0]
    rows = [asum_ref[i, :, half:] for i in range(n)]
    hi = [r.astype(BF) for r in rows]
    lo = [(r - h.astype(F32)).astype(BF) for r, h in zip(rows, hi)]
    pad = jnp.zeros((16 - 2 * n, half), F32)
    br = mm(jnp.concatenate([t.astype(F32) for t in hi + lo] + [pad], axis=0).astype(BF), wb_ref[...])
    for i in range(n):
        total = rs_ref[i] + br[i : i + 1] + br[n + i : n + i + 1]
        out_ref[i : i + 1, :] = total / lens[i].astype(F32)


def pool(lens, at, asum, rsum, packs):
    n, _, d = rsum.shape
    half = asum.shape[2] // 2
    vm = pl.BlockSpec(memory_space=pltpu.VMEM)
    return pl.pallas_call(
        pool_kernel,
        in_specs=[SMEM_SPEC, SMEM_SPEC, vm, vm] + [ANY] * 2,
        out_specs=vm,
        out_shape=sds((8, d), F32),
        scratch_shapes=[pltpu.VMEM((half, d), BF), pltpu.SemaphoreType.DMA((4,))],
        compiler_params=params(),
        cost_estimate=cost(4),
        name="pool",
    )(lens, at, asum, rsum, *packs)


def loss_kernel(me_ref, at_ref, lens, pool_ref, q_ref, wp_ref, fint_hbm, gp_hbm, fn0, fn1, wi_hbm, wu_hbm, p0, p1, *refs):
    (loss_ref, row_ref, g_ref, drow_ref, demb_ref, send_ref, keep_ref) = refs[:7]
    (wu_ref, wb_ref, fint_ref, gp_ref, fnb_ref, wi_ref, ft_ref, gn_ref, v_ref, d_ref, dn_ref, sem, sem2) = refs[7:]
    copies = join_copies(at_ref[0], (p0, p1), wb_ref, sem)
    moves = [(wu_hbm, wu_ref), (wi_hbm, wi_ref), (gp_hbm, gp_ref), (fint_hbm, fint_ref)]
    moves += [(f, fnb_ref.at[pl.ds(i, 1)]) for i, f in enumerate((fn0, fn1))]
    loads = [pltpu.make_async_copy(a, b, sem2.at[i]) for i, (a, b) in enumerate(moves)]
    for c in [loads[0]] + copies + loads[1:]:
        c.start()
    d = wp_ref.shape[0]
    count = pool_ref.shape[0]
    pooled = pool_ref[...]
    qs = q_ref[:, :d]
    ints = q_ref[:, d : d + TILE].astype(F32)
    pos = (ints[:, 0:1] * 256.0 + ints[:, 1:2]).astype(jnp.int32)
    length = ints[:, 2:3] * 256.0 + ints[:, 3:4]
    wp = wp_ref[...]
    emb = mm(pooled, wp)
    inv = lax.rsqrt(jnp.sum(emb * emb, axis=-1, keepdims=True) + EPS)
    unit = (emb * inv).astype(BF)
    logits = mm(qs, unit, NT) / SHARPNESS
    top = jnp.max(logits, axis=-1, keepdims=True)
    total = top + jnp.log(jnp.sum(jnp.exp(logits - top), axis=-1, keepdims=True))
    hit = lax.broadcasted_iota(jnp.int32, (count, count), 1) == pos
    loss = total - jnp.sum(jnp.where(hit, logits, 0.0), axis=1, keepdims=True)
    d_logits = (LOSS_SCALE * (jnp.exp(logits - total) - jnp.where(hit, 1.0, 0.0))).astype(BF)
    d_unit = mm(d_logits, qs, TN) / SHARPNESS
    along = jnp.sum(emb * d_unit, axis=-1, keepdims=True)
    d_emb = (inv * d_unit - inv * inv * inv * along * emb).astype(BF)
    demb_ref[...] = d_emb
    rows = mm(d_emb, wp, NT) / length
    drow_ref[...] = rows.astype(BF)
    index = lax.broadcasted_iota(jnp.int32, (count, 1), 0)
    pick = lambda t, i: jnp.sum(jnp.where(index == i, t, 0.0), axis=0, keepdims=True)
    n, seq, half = gp_ref.shape
    own = [pick(rows, me_ref[i]) for i in range(n)]
    near = [pick(rows, me_ref[n + i]) for i in range(n)]
    lost = jnp.broadcast_to(loss, (count, TILE))
    pad = jnp.zeros((8 - n, d), F32)
    row_ref[...] = jnp.concatenate(own + [pad], axis=0)
    loss_ref[...] = jnp.concatenate([pick(lost, me_ref[i]) for i in range(n)] + [pad[:, :TILE]], axis=0)
    four = jnp.concatenate(own + near + [jnp.zeros((16 - 2 * n, d), F32)], axis=0).astype(BF)
    loads[0].wait()
    ga = mm(four, wu_ref[...], NT)
    gn_ref[...] = ga[:8]
    for c in copies:
        c.wait()
    g_ref[:, :half] = ga[:8]
    g_ref[:, half:] = mm(four, wb_ref[...], NT)[:8]
    for c in loads[1:]:
        c.wait()

    for i in range(n):
        ft_ref[:, seq * i : seq * (i + 1)] = jnp.transpose(fnb_ref[i])
    chunk = v_ref.shape[3]
    steps = half // chunk
    spot = lambda c: slice(c * chunk, (c + 1) * chunk)

    def project(c):
        for i in range(n):
            v_ref[c % 2, i] = mm(fnb_ref[i], wi_ref[:, spot(c)])

    def scale(c):
        for i in range(n):
            at = slice(seq * i, seq * (i + 1))
            d_ref[c % 2, at, :] = (gp_ref[i, :, spot(c)].astype(F32) * gn_ref[i : i + 1, spot(c)]).astype(BF)
            for r in range(seq // TILE):
                part = slice(TILE * r, TILE * (r + 1))
                valid = lax.broadcasted_iota(jnp.int32, (TILE, TILE), 0) + TILE * r < lens[n + i]
                slope = gelu_parts(v_ref[c % 2, i, part, :])[1]
                one = slope * valid.astype(F32)[:, :1] * gn_ref[n + i : n + i + 1, spot(c)]
                dn_ref[c % 2, seq * i + TILE * r : seq * i + TILE * (r + 1), :] = one.astype(BF)

    rows2 = d // 2
    core = at_ref[0] // 2
    project(0)
    scale(0)
    for c in range(steps):
        if c + 1 < steps:
            project(c + 1)
        for ref, side in ((send_ref, 1 - core), (keep_ref, core)):
            at = pl.ds(pl.multiple_of(side * rows2, rows2), rows2)
            one = mm(fint_ref[at, :], d_ref[c % 2]) + mm(ft_ref[at, :], dn_ref[c % 2])
            ref[:, spot(c)] = one.astype(BF)
        if c + 1 < steps:
            scale(c + 1)


def loss_all(me, at, lens4, pooled, queries, wp, fint, gp, fin_nb, wi, wu, packs):
    half, d = wu.shape
    n, seq, _ = gp.shape
    count = pooled.shape[0]
    chunk = 512
    vm = pl.BlockSpec(memory_space=pltpu.VMEM)
    return pl.pallas_call(
        loss_kernel,
        in_specs=[SMEM_SPEC] * 3 + [vm] * 3 + [ANY] * 8,
        out_specs=[vm] * 7,
        out_shape=[
            sds((8, TILE), F32),
            sds((8, d), F32),
            sds((8, 2 * half), F32),
            sds((count, d), BF),
            sds((count, d), BF),
            sds((d // 2, half), BF),
            sds((d // 2, half), BF),
        ],
        scratch_shapes=[
            pltpu.VMEM(wu.shape, BF),
            pltpu.VMEM(wu.shape, BF),
            pltpu.VMEM(fint.shape, BF),
            pltpu.VMEM(gp.shape, BF),
            pltpu.VMEM((n, seq, d), BF),
            pltpu.VMEM(wi.shape, BF),
            pltpu.VMEM(fint.shape, BF),
            pltpu.VMEM((8, half), F32),
            pltpu.VMEM((2, n, seq, chunk), F32),
            pltpu.VMEM((2, n * seq, chunk), BF),
            pltpu.VMEM((2, n * seq, chunk), BF),
            pltpu.SemaphoreType.DMA((4,)),
            pltpu.SemaphoreType.DMA((6,)),
        ],
        compiler_params=params(),
        cost_estimate=cost(17),
        name="loss_inner",
    )(me, at, lens4, pooled, queries, wp, fint, gp, *fin_nb, wi, wu, *packs)


def ffn_bwd_kernel(lens, at_ref, res_ref, gpa_ref, gpb_ref, g_ref, row_ref, gain_ref, wi_ref, wo_ref, cta_ref, ctb_ref, *refs):
    packs0, packs1 = refs[:2], refs[2:6]
    (dres_ref, dca_ref, dta_ref, dcb_ref, dtb_ref, goa_ref, gob_ref) = refs[6:13]
    (wib_ref, wob_ref, cta_buf, ctb_buf, d_ref, da_ref, sem0, sem1, sem2) = refs[13:]
    b = pl.program_id(0)
    n = pl.num_programs(0)
    res = res_ref[0]
    seq, d = res.shape
    half = wi_ref.shape[1]
    chunk = d_ref.shape[2]
    copies0 = join_copies(at_ref[0], packs0, wob_ref, sem0)
    copies1 = join_copies(at_ref[0], packs1, wib_ref, sem1)
    late = [pltpu.make_async_copy(cta_ref, cta_buf, sem2.at[0]), pltpu.make_async_copy(ctb_ref, ctb_buf, sem2.at[1])]

    @pl.when(b == 0)
    def _():
        for c in copies1 + copies0 + late:
            c.start()
        for c in copies1 + copies0:
            c.wait()

    parts = [(gp, w, c) for gp, w in ((gpa_ref, wi_ref), (gpb_ref, wib_ref)) for c in range(half // chunk)]

    def scale(t):
        gp, _, c = parts[t]
        base = half if gp is gpb_ref else 0
        g = g_ref[pl.ds(b, 1), base + c * chunk : base + (c + 1) * chunk]
        d_ref[t % 2] = (gp[0, :, c * chunk : (c + 1) * chunk].astype(F32) * g).astype(BF)

    d_two = None
    scale(0)
    for t, (_, w, c) in enumerate(parts):
        if t + 1 < len(parts):
            scale(t + 1)
        one = mm(d_ref[t % 2], w[:, c * chunk : (c + 1) * chunk], NT)
        d_two = one if d_two is None else d_two + one
    inv = lax.rsqrt(jnp.mean(res * res, axis=-1, keepdims=True) + EPS)
    dr = d_two * res
    gain = gain_ref[...]
    along = jnp.sum(dr * gain, axis=-1, keepdims=True)
    valid = lax.broadcasted_iota(jnp.int32, (seq, TILE), 0) < lens[b]
    vcol = valid.astype(F32)[:, :1]
    d_res = vcol * row_ref[pl.ds(b, 1), :] + d_two * gain * inv - res * (inv * inv * inv * along / d)
    dres_ref[0] = d_res
    d_attn = d_res.astype(BF)
    da_ref[pl.ds(pl.multiple_of(b * seq, seq), seq), :] = d_attn
    for w, o_ref, t_ref in ((wo_ref, dca_ref, dta_ref), (wob_ref, dcb_ref, dtb_ref)):
        turned = mm(w[...], d_attn, NT).astype(BF)
        t_ref[0] = turned
        o_ref[0] = jnp.transpose(turned)

    @pl.when(b == n - 1)
    def _():
        for c in late:
            c.wait()
        rows = cta_buf.shape[1]
        for ct_ref, o_ref in ((cta_buf, goa_ref), (ctb_buf, gob_ref)):
            total = None
            for i in range(cta_buf.shape[0]):
                one = mm(ct_ref[i], da_ref[seq * i : seq * (i + 1), :])
                total = one if total is None else total + one
            o_ref[:rows, :] = total[:, :rows]
            o_ref[rows:, :] = total[:, rows:]


def ffn_bwd(lens, at, res, gpa, gpb, g, row, gain, wi, wo, cta, ctb, packs0, packs1):
    n, seq, d = res.shape
    width = wo.shape[0]
    outs = [sds((n, seq, d), F32)] + [sds((n, seq, width), BF), sds((n, width, seq), BF)] * 2
    flat = [sds((d, width), F32), sds((d, width), F32)]
    return pl.pallas_call(
        ffn_bwd_kernel,
        grid=(n,),
        in_specs=[SMEM_SPEC, SMEM_SPEC, row_spec(res.shape), row_spec(gpa.shape), row_spec(gpb.shape)]
        + [const_spec(g.shape), const_spec(row.shape), const_spec((1, d)), const_spec(wi.shape), const_spec(wo.shape)]
        + [ANY] * 8,
        out_specs=[row_spec(o.shape) for o in outs] + [out_const(o.shape) for o in flat],
        out_shape=outs + flat,
        scratch_shapes=[
            pltpu.VMEM(wi.shape, BF),
            pltpu.VMEM(wo.shape, BF),
            pltpu.VMEM(cta.shape, BF),
            pltpu.VMEM(ctb.shape, BF),
            pltpu.VMEM((2, seq, 512), BF),
            pltpu.VMEM((n * seq, d), BF),
            pltpu.SemaphoreType.DMA((4,)),
            pltpu.SemaphoreType.DMA((4,)),
            pltpu.SemaphoreType.DMA((2,)),
        ],
        compiler_params=params(),
        cost_estimate=cost(15),
        name="ffn_bwd",
    )(lens, at, res, gpa, gpb, g, row, gain.reshape(1, d), wi, wo, cta, ctb, *packs0, *packs1)


def input_kernel(at_ref, x_ref, dres_ref, gain_ref, qa, ka, va, qb, kb, vb, wq, wk, wv, p0, p1, p2, p3, out_ref, w_ref, sem):
    @pl.when(pl.program_id(0) == 0)
    def _():
        run_copies(join_copies(at_ref[0], (p0, p1, p2, p3), w_ref, sem))

    width = wq.shape[1]
    d_one = mm(qa[0], wq[...], NT) + mm(ka[0], wk[...], NT) + mm(va[0], wv[...], NT)
    for i, t in enumerate((qb, kb, vb)):
        d_one = d_one + mm(t[0], w_ref[:, width * i : width * (i + 1)], NT)
    x = x_ref[0].astype(F32)
    inv = lax.rsqrt(jnp.mean(x * x, axis=-1, keepdims=True) + EPS)
    dx = d_one * x
    gain = gain_ref[...]
    along = jnp.sum(dx * gain, axis=-1, keepdims=True)
    out_ref[0] = dres_ref[0] + d_one * gain * inv - x * (inv * inv * inv * along / x.shape[1])


def input_part(at, x, dres, gain, toks, wq, wk, wv, packs):
    n, seq, d = x.shape
    width = wq.shape[1]
    return pl.pallas_call(
        input_kernel,
        grid=(n,),
        in_specs=[SMEM_SPEC, row_spec(x.shape), row_spec(dres.shape), const_spec((1, d))]
        + [row_spec(toks[0].shape)] * 6
        + [const_spec(wq.shape)] * 3
        + [ANY] * 4,
        out_specs=row_spec(x.shape),
        out_shape=sds(x.shape, F32),
        scratch_shapes=[pltpu.VMEM((d, 3 * width), BF), pltpu.SemaphoreType.DMA((4,))],
        compiler_params=params(),
        cost_estimate=cost(12),
        name="input_part",
    )(at, x, dres, gain.reshape(1, d), *toks, wq, wk, wv, *packs)


def layer_kernel(at_ref, res_ref, aa_ref, ab_ref, w_ref, p0, p1, out_ref, wb_ref, sem):
    @pl.when(pl.program_id(0) == 0)
    def _():
        run_copies(join_copies(at_ref[0], (p0, p1), wb_ref, sem))

    out_ref[0] = (res_ref[0] + mm(aa_ref[0], w_ref[...]) + mm(ab_ref[0], wb_ref[...])).astype(BF)


def layer_part(at, res, act_a, act_b, wu, packs):
    n, seq, d = res.shape
    return pl.pallas_call(
        layer_kernel,
        grid=(n,),
        in_specs=[SMEM_SPEC, row_spec(res.shape), row_spec(act_a.shape), row_spec(act_b.shape), const_spec(wu.shape)]
        + [ANY] * 2,
        out_specs=row_spec(res.shape),
        out_shape=sds(res.shape, BF),
        scratch_shapes=[pltpu.VMEM(wu.shape, BF), pltpu.SemaphoreType.DMA((4,))],
        compiler_params=params(),
        cost_estimate=cost(12),
        name="layer_part",
    )(at, res, act_a, act_b, wu, *packs)


def gain_row(prod):
    ones = jnp.ones((16, prod.shape[1]), BF)
    return sum(mm(ones, part, NT)[:1] for part in split3(prod))


def inner_done_kernel(at_ref, own_ref, near_ref, w_ref, out_ref, gain_ref):
    rows = own_ref.shape[0]
    core = at_ref[0] // 2
    halves = [own_ref[...].astype(F32), near_ref[...].astype(F32)]
    for half in range(2):
        one = jnp.where(core == half, halves[0], halves[1])
        at = slice(rows * half, rows * (half + 1))
        out_ref[at, :] = one
        gain_ref[:, at] = jnp.broadcast_to(gain_row(one * w_ref[at, :].astype(F32)), (8, rows))


def inner_done(at, own, near, w):
    d, half = w.shape
    chunk = 512
    cols = lambda r: pl.BlockSpec((r, chunk), lambda c: (0, c))
    return pl.pallas_call(
        inner_done_kernel,
        grid=(half // chunk,),
        in_specs=[SMEM_SPEC, cols(d // 2), cols(d // 2), cols(d)],
        out_specs=[cols(d), pl.BlockSpec((8, d), lambda c: (c, 0))],
        out_shape=[sds((d, half), F32), sds((8 * (half // chunk), d), F32)],
        compiler_params=params(),
        cost_estimate=cost(5),
        name="inner_done",
    )(at, own, near, w)


def attn_done_kernel(at_ref, own_ref, near_ref, wq, wk, wv, q_ref, k_ref, v_ref, o_ref, gain_ref):
    rows = own_ref.shape[0]
    width = wq.shape[1]
    core = at_ref[0] // 2
    for half in range(2):
        at = slice(rows * half, rows * (half + 1))
        total = None
        for i, (w, out) in enumerate(((wq, q_ref), (wk, k_ref), (wv, v_ref), (None, o_ref))):
            cols = slice(width * i, width * (i + 1))
            one = jnp.where(core == half, own_ref[:, cols].astype(F32), near_ref[:, cols].astype(F32))
            if w is None:
                out[:, at] = one
            else:
                out[at, :] = one
                prod = one * w[at, :].astype(F32)
                total = prod if total is None else total + prod
        gain_ref[:, at] = jnp.broadcast_to(gain_row(total), (8, rows))


def attn_done(at, own, near, wq, wk, wv):
    d, width = wq.shape
    vm = pl.BlockSpec(memory_space=pltpu.VMEM)
    grad = sds((d, width), F32)
    return pl.pallas_call(
        attn_done_kernel,
        in_specs=[SMEM_SPEC] + [vm] * 5,
        out_specs=[vm] * 5,
        out_shape=[grad, grad, grad, sds((width, d), F32), sds((8, d), F32)],
        compiler_params=params(),
        cost_estimate=cost(5),
        name="attn_done",
    )(at, own, near, wq, wk, wv)


def after(*xs):
    return lax.optimization_barrier(xs)


def swap(x, axis, bit, size):
    return lax.ppermute(x, axis, [(i, i ^ bit) for i in range(size)])


class Place:
    def __init__(self, chips, tensor):
        self.chips, self.tensor = chips, tensor
        self.chip = lax.axis_index("chip")
        self.core = lax.axis_index("core")
        self.ti = lax.axis_index("tensor")

    def across(self, x):
        return swap(x, "tensor", 1, self.tensor)

    def core_swap(self, x):
        return swap(x, "core", 1, 2)

    def share(self, x):
        return lax.all_to_all(x, ("chip", "core", "tensor"), 0, 0, tiled=True)

    def side(self, mine):
        return swap(mine, "chip", 1, self.chips)

    def spread(self, mine, side):
        return [mine, side, self.core_swap(mine), self.core_swap(side)]

    def exchange(self, x):
        rows, width = x.shape
        return lax.all_to_all(x.reshape(self.chips, rows // self.chips, width), "chip", 0, 0, tiled=True)

    def add(self, got):
        return jnp.sum(got.astype(F32), axis=0).astype(BF)

    def gather(self, x):
        got = lax.all_to_all(jnp.broadcast_to(x[None], (self.chips,) + x.shape), "chip", 0, 0, tiled=True)
        return got.reshape(-1, x.shape[1])

    def total(self, x):
        x = x + self.core_swap(x)
        for i in range(self.chips.bit_length() - 1):
            x = x + swap(x, "chip", 1 << i, self.chips)
        return x


def body(
    mesh_shape,
    hidden_in,
    lengths,
    queries,
    positives,
    gain_attn,
    w_query,
    w_key,
    w_value,
    w_out,
    rel_table,
    gain_ffn,
    w_inner,
    w_outer,
    w_proj,
):
    pc = Place(mesh_shape["chip"], mesh_shape["tensor"])
    n, seq, d = hidden_in.shape
    half = w_inner.shape[1]
    width = w_query.shape[1]
    buckets = rel_table.shape[0]
    lens = lax.dynamic_slice_in_dim(lengths, pc.ti * n, n, 0)
    near_lens = lax.dynamic_slice_in_dim(lengths, (1 - pc.ti) * n, n, 0)
    lens4 = jnp.concatenate([lens, near_lens])
    at = (2 * pc.core + (pc.chip & 1)).reshape(1)
    devices = pc.chips * 2 * pc.tensor
    hot_t = jnp.asarray(np.pad(diag_onehot(buckets, False).T, ((0, TILE - buckets), (0, 0))), BF)
    hot_back = jnp.asarray(np.pad(diag_onehot(buckets, True), ((0, 0), (0, TILE - buckets))), BF)

    turned = rel_table.T
    packs = pack_weights(at, turned, w_query, w_key, w_value, w_out, w_inner, w_outer)
    y_attn, y_out, y_inner, y_outer = [pc.across(p) for p in packs]

    qf = queries.astype(F32)
    q_unit = (qf * lax.rsqrt(jnp.sum(qf * qf, axis=-1, keepdims=True) + EPS)).astype(BF)
    ints = jnp.stack([positives // 256, positives % 256, lens // 256, lens % 256], axis=1)
    ints = jnp.pad(ints.astype(BF), ((0, 0), (0, TILE - 4)))
    q_all = jnp.concatenate([q_unit, ints], axis=1)

    an, ant, q_a, qt_a, k_a, v_a, ctx_a, ctxt_a, lse_a, nb_a, tf_a = attn_own(
        lens, hidden_in, gain_attn, w_query, w_key, w_value, turned, hot_t
    )
    y_attn, an, q_all = after(y_attn, an, q_all)
    x_attn = pc.side(y_attn)
    q_all = pc.share(jnp.broadcast_to(q_all[None], (devices,) + q_all.shape))
    x_attn, y_out, q_all = after(x_attn, y_out, q_all)
    p_attn = pc.spread(y_attn, x_attn)
    p_out = [y_out, pc.core_swap(y_out)]
    y_inner, an = after(y_inner, an)
    x_inner = pc.side(y_inner)
    q_b, qt_b, k_b, v_b, ctx_b, ctxt_b, lse_b, nb_b, tf_b, res, fin, fint, rsum = attn_other(
        lens, at, an, hot_t, hidden_in, ctx_a, w_out, gain_ffn, p_attn, p_out
    )
    y_inner, x_inner, fin = after(y_inner, x_inner, fin)
    p_inner = pc.spread(y_inner, x_inner)
    fin_nb = [pc.across(fin[i : i + 1]) for i in range(n)]
    act_a, gp_a, act_b, gp_b, asum, rsum = ffn_fwd(lens, at, fin, rsum, w_inner, w_outer, p_inner)
    y_outer, asum, fin_nb[0] = after(y_outer, asum, fin_nb[0])
    p_outer = [y_outer, pc.core_swap(y_outer)]
    pooled = pool(lens, at, asum, rsum, p_outer)[:n].astype(BF)

    sums_a, sums_b = asum[:, 0, :half].astype(BF), asum[:, 0, half:].astype(BF)
    sums = jnp.where(pc.ti > 0, jnp.stack([sums_b, sums_a]), jnp.stack([sums_a, sums_b]))
    msg = jnp.concatenate([jnp.broadcast_to(pooled[None], (2,) + pooled.shape), sums], axis=2)
    msg = jnp.broadcast_to(msg[None], (2 * pc.chips,) + msg.shape).reshape((devices,) + msg.shape[1:])
    got = pc.share(msg).reshape(devices * n, -1)
    pooled = got[:, :d]
    base = (2 * pc.chip + pc.core) * pc.tensor * n
    me = jnp.stack([base + pc.ti * n, base + pc.ti * n + 1, base + (1 - pc.ti) * n, base + (1 - pc.ti) * n + 1])
    loss8, row8, g8, d_rows, d_emb, gi_send, gi_keep = loss_all(
        me, at, lens4, pooled, q_all.reshape(devices * n, -1), w_proj, fint, gp_a, fin_nb, w_inner, w_outer, p_outer
    )
    query_loss = loss8[:n, 0]

    inner_half, gp_a = after(gi_keep + pc.core_swap(gi_send), gp_a)
    inner_parts = pc.exchange(inner_half)
    d_res, dctx_a, dctxt_a, dctx_b, dctxt_b, go_a, go_b = ffn_bwd(
        lens, at, res, gp_a, gp_b, g8, row8, gain_ffn, w_inner, w_out, ctxt_a, ctxt_b, p_out, p_inner
    )
    dq_b, dk_b, dv_b, send_b, keep_b, table_b = attn_bwd(
        lens, at, q_b, qt_b, k_b, v_b, dctx_b, dctxt_b, ctxt_b, lse_b, nb_b, tf_b, hot_back, ant, go_b
    )
    half_b, dctx_a = after(keep_b + pc.core_swap(send_b), dctx_a)
    far_part = pc.across(half_b)
    inner_part, dctx_a = after(pc.add(inner_parts), dctx_a)
    dq_a, dk_a, dv_a, send_a, keep_a, table_a = attn_bwd(
        lens, at, q_a, qt_a, k_a, v_a, dctx_a, dctxt_a, ctxt_a, lse_a, nb_a, tf_a, hot_back, ant, go_a
    )
    inner_all, far_part, send_a = after(pc.gather(inner_part), far_part, send_a)
    parts = pc.exchange(keep_a + far_part + pc.core_swap(send_a))
    toks = (dq_a, dk_a, dv_a, dq_b, dk_b, dv_b)
    input_grad = input_part(at, hidden_in, d_res, gain_attn, toks, w_query, w_key, w_value, p_attn)

    table_sum = pc.total(table_a + pc.across(table_b))

    layer = layer_part(at, res, act_a, act_b, w_outer, p_outer)
    parts, input_grad, layer, inner_all = after(parts, input_grad, layer, inner_all)
    attn_all = pc.gather(pc.add(parts))
    inner_sum, gain_ffn_part = inner_done(at, inner_all, pc.core_swap(inner_all), w_inner)
    gain_ffn_part = jnp.sum(gain_ffn_part[::8], axis=0)
    gain_ffn_grad = (gain_ffn_part + pc.across(gain_ffn_part)) / gain_ffn
    proj_grad = mm(pooled, d_emb, TN)
    outer_grad = mm(got[:, d:], d_rows, TN)
    attn_all, proj_grad, outer_grad, gain_ffn_grad, inner_sum, table_sum = after(
        attn_all, proj_grad, outer_grad, gain_ffn_grad, inner_sum, table_sum
    )
    q_grad, k_grad, v_grad, out_grad, gain_attn_part = attn_done(
        at, attn_all, pc.core_swap(attn_all), w_query, w_key, w_value
    )
    gain_attn_part = gain_attn_part[0]
    gain_attn_grad = (gain_attn_part + pc.across(gain_attn_part)) / gain_attn
    return (
        layer,
        query_loss,
        input_grad,
        gain_attn_grad,
        q_grad,
        k_grad,
        v_grad,
        out_grad,
        table_sum[: rel_table.shape[1], :buckets].T,
        gain_ffn_grad,
        inner_sum,
        outer_grad,
        proj_grad,
    )


def solution(mesh):
    dp, tensor = mesh.shape["dp"], mesh.shape["tensor"]
    fine = jax.sharding.Mesh(mesh.devices.reshape(dp // 2, 2, tensor), ("chip", "core", "tensor"))
    rows = ("chip", "core")
    both = rows + ("tensor",)
    return jax.shard_map(
        functools.partial(body, dict(fine.shape)),
        mesh=fine,
        in_specs=(
            P(both, None, None),
            P(rows),
            P(both, None),
            P(both),
            P(),
            P(None, "tensor"),
            P(None, "tensor"),
            P(None, "tensor"),
            P("tensor", None),
            P(None, "tensor"),
            P(),
            P(None, "tensor"),
            P("tensor", None),
            P(),
        ),
        out_specs=(
            P(both, None, None),
            P(both),
            P(both, None, None),
            P(),
            P(None, "tensor"),
            P(None, "tensor"),
            P(None, "tensor"),
            P("tensor", None),
            P(None, "tensor"),
            P(),
            P(None, "tensor"),
            P("tensor", None),
            P(),
        ),
        check_vma=False,
    )
```

profile of v0, /device:TPU:0, one launch (start us, length us, event | category | flops | bytes accessed | tf_op | source)
XLA Modules:
  0.0 309.2 jit_solution(1353269660250619120)
XLA Ops:
  0.7 4.0 %pack_weights.1 = (bf16[208,1152]{1,0:T(8,128)(2,1)}, bf16[192,768]{1,0:T(8,128)(2,1)}, bf16[192,1536]{1,0:T(8,128)(2,1)}, bf16[768,768]{1,0:T(8,128)(2,1)}) custom-call(s32[1]{0:T(128)} %bitcast.at_ref, f32[6,32]{1,0:T(8,128)} %bitcast.35, bf16[768,384]{1,0:T(8,128)(2,1)} %wq.7, bf16[768,384]{1,0:T(8,128)(2,1)} %wk.7, bf16[768,384]{1,0:T(8,128)(2,1)} %wv.7, ...), custom_call_target="tpu_custom_call" | custom-call | bytes 10800000 | tf_op jit(solution)/shard_map/pack_weights/pallas_call | solution.py:119
  4.7 3.0 collective-permute-start.2
  8.9 12.6 %attn_own.1 = (bf16[2,512,768]{2,1,0:T(8,128)(2,1)}, bf16[768,1024]{1,0:T(8,128)(2,1)}, bf16[2,512,384]{2,1,0:T(8,128)(2,1)}, bf16[2,384,512]{2,1,0:T(8,128)(2,1...) custom-call(s32[2]{0:T(128)} %copy-done.18, ...), custom_call_target="tpu_custom_call" | custom-call | bytes 43200000 | tf_op jit(solution)/shard_map/attn_own/pallas_call | solution.py:336
  25.7 4.5 %all-to-all-start = ((bf16[32,2,896]{2,1,0:T(2,128)(2,1)}), bf16[32,2,896]{2,1,0:T(2,128)(2,1)S(1)}, u32[]{:S(2)}, u32[]{:S(2)}) async-start(bf16[32,2,896]{2,1,0:T(2,128)(2,1)} %broadcast_in_dim.10), calls=%async_computation | async-start | bytes 229376 | tf_op jit(solution)/shard_map/all_to_all | solution.py:1032
  34.4 4.7 %collective-permute-done.5.o0.refs_0_ = bf16[192,768]{1,0:T(8,128)(2,1)} collective-permute-done((bf16[192,768]{1,0:T(8,128)(2,1)S(1)}, bf16[192,768]{1,0:T(8,128)(2,1)}, u32[]{:S(2)}, u32[]{:S(2)}) %collective-permute-start.5) | collective-permute-done | bytes 294944 | tf_op jit(solution)/shard_map/ppermute | solution.py:1015
  43.5 18.1 %attn_other.1 = (bf16[2,512,384]{2,1,0:T(8,128)(2,1)}, bf16[2,384,512]{2,1,0:T(8,128)(2,1)}, bf16[2,512,384]{2,1,0:T(8,128)(2,1)}, bf16[2,512,384]{2,1,0:T(8,128...) custom-call(s32[2]{0:T(128)} %copy-done.18, ...), custom_call_target="tpu_custom_call" | custom-call | bytes 54000000 | tf_op jit(solution)/shard_map/attn_other/pallas_call | solution.py:358
  61.6 2.8 fusion.11
  69.5 15.8 %ffn_fwd.1 = (bf16[2,512,1536]{2,1,0:T(8,128)(2,1)}, bf16[2,512,1536]{2,1,0:T(8,128)(2,1)}, bf16[2,512,1536]{2,1,0:T(8,128)(2,1)}, bf16[2,512,1536]{2,1,0:T(8,12...) custom-call(s32[2]{0:T(128)} %copy-done.18, s32[1]{0:T(128)} %bitcast.at_ref, ...), custom_call_target="tpu_custom_call" | custom-call | bytes 57600000 | tf_op jit(solution)/shard_map/ffn_fwd/pallas_call | solution.py:612
  89.3 3.5 %pool.1 = f32[8,768]{1,0:T(8,128)} custom-call(s32[2]{0:T(128)} %copy-done.18, s32[1]{0:T(128)} %bitcast.at_ref, f32[2,1,3072]{2,1,0:T(1,128)} %get-tuple-element.135.asum_ref, f32[2,1,768]{2,1,0:T(1,128)} %get-tuple-element.136.rs_ref, bf16[768,768]{1,0:T(8,128)(2,1)} %copy-done, bf16[768,768]{1,0:T(8,128)(2,1)} %copy-done.1), custom_call_target="tpu_custom_call" | custom-call | bytes 14400000 | tf_op jit(solution)/shard_map/pool/pallas_call | solution.py:649
  94.5 5.5 %all-to-all-start.1 = ((bf16[32,2,2304]{2,1,0:T(2,128)(2,1)}), bf16[32,2,2304]{2,1,0:T(2,128)(2,1)S(1)}, u32[]{:S(2)}, u32[]{:S(2)}) async-start(bf16[32,2,2304]{2,1,0:T(2,128)(2,1)} %bitcast.10), calls=%async_computation.1 | async-start | bytes 589824 | tf_op jit(solution)/shard_map/all_to_all | solution.py:1032
  101.3 9.8 %all-to-all-done.1 = bf16[32,2,2304]{2,1,0:T(2,128)(2,1)S(1)} async-done(((bf16[32,2,2304]{2,1,0:T(2,128)(2,1)}), bf16[32,2,2304]{2,1,0:T(2,128)(2,1)S(1)}, u32[]{:S(2)}, u32[]{:S(2)}) %all-to-all-start.1) | async-done | bytes 294944 | tf_op jit(solution)/shard_map/all_to_all | solution.py:1032
  111.9 16.5 %loss_inner.1 = (f32[8,128]{1,0:T(8,128)}, f32[8,768]{1,0:T(8,128)}, f32[8,3072]{1,0:T(8,128)}, bf16[64,768]{1,0:T(8,128)(2,1)}, bf16[64,768]{1,0:T(8,128)(2,1)}...) custom-call(s32[4]{0:T(128)} %get-tuple-element.221.me_ref, s32[1]{0:T(128)} %bitcast.at_ref, ...), custom_call_target="tpu_custom_call" | custom-call | bytes 61200000 | tf_op jit(solution)/shard_map/loss_inner/pallas_call | solution.py:755
  128.7 2.8 collective-permute-done.14
  134.1 3.8 %all-to-all-start.2 = ((bf16[8,48,1536]{2,1,0:T(8,128)(2,1)}), bf16[8,48,1536]{2,1,0:T(8,128)(2,1)S(1)}, u32[]{:S(2)}, u32[]{:S(2)}) async-start(bf16[8,48,1536]{2,1,0:T(8,128)(2,1)} %bitcast.11), calls=%async_computation.2 | async-start | bytes 2359296 | tf_op jit(solution)/shard_map/all_to_all | solution.py:1042
  137.9 19.8 %ffn_bwd.1 = (f32[2,512,768]{2,1,0:T(8,128)}, bf16[2,512,384]{2,1,0:T(8,128)(2,1)}, bf16[2,384,512]{2,1,0:T(8,128)(2,1)}, bf16[2,512,384]{2,1,0:T(8,128)(2,1)}, ...) custom-call(s32[2]{0:T(128)} %copy-done.18, s32[1]{0:T(128)} %bitcast.at_ref, ...), custom_call_target="tpu_custom_call" | custom-call | bytes 54000000 | tf_op jit(solution)/shard_map/ffn_bwd/pallas_call | solution.py:859
  157.8 16.5 %attn_bwd.2 = (bf16[2,512,384]{2,1,0:T(8,128)(2,1)}, bf16[2,512,384]{2,1,0:T(8,128)(2,1)}, bf16[2,512,384]{2,1,0:T(8,128)(2,1)}, bf16[384,1536]{1,0:T(8,128)(2,1...) custom-call(s32[2]{0:T(128)} %copy-done.18, s32[1]{0:T(128)} %bitcast.at_ref, ...), custom_call_target="tpu_custom_call" | custom-call | bytes 72000000 | tf_op jit(solution)/shard_map/attn_bwd/pallas_call | solution.py:525
  174.6 2.8 collective-permute-done.15
  180.3 6.0 %all-to-all-start.3 = ((bf16[8,48,1536]{2,1,0:T(8,128)(2,1)}), bf16[8,48,1536]{2,1,0:T(8,128)(2,1)S(1)}, u32[]{:S(2)}, u32[]{:S(2)}) async-start(bf16[8,48,1536]{2,1,0:T(8,128)(2,1)} %broadcast_in_dim.13), calls=%async_computation.3 | async-start | bytes 2359296 | tf_op jit(solution)/shard_map/all_to_all | solution.py:1048
  187.2 16.1 %attn_bwd.3 = (bf16[2,512,384]{2,1,0:T(8,128)(2,1)}, bf16[2,512,384]{2,1,0:T(8,128)(2,1)}, bf16[2,512,384]{2,1,0:T(8,128)(2,1)}, bf16[384,1536]{1,0:T(8,128)(2,1...) custom-call(s32[2]{0:T(128)} %copy-done.18, s32[1]{0:T(128)} %bitcast.at_ref, ...), custom_call_target="tpu_custom_call" | custom-call | bytes 72000000 | tf_op jit(solution)/shard_map/attn_bwd/pallas_call | solution.py:525
  203.3 10.8 %collective-permute-done.16 = bf16[384,1536]{1,0:T(8,128)(2,1)} collective-permute-done((bf16[384,1536]{1,0:T(8,128)(2,1)S(1)}, bf16[384,1536]{1,0:T(8,128)(2,1)}, u32[]{:S(2)}, u32[]{:S(2)}) %collective-permute-start.16) | collective-permute-done | bytes 1179680 | tf_op jit(solution)/shard_map/ppermute | solution.py:1015
  215.2 3.1 collective-permute-done.17
  221.0 4.7 %all-to-all-start.4 = ((bf16[8,48,1536]{2,1,0:T(8,128)(2,1)}), bf16[8,48,1536]{2,1,0:T(8,128)(2,1)S(1)}, u32[]{:S(2)}, u32[]{:S(2)}) async-start(bf16[8,48,1536]{2,1,0:T(8,128)(2,1)} %bitcast.13), calls=%async_computation.4 | async-start | bytes 2359296 | tf_op jit(solution)/shard_map/all_to_all | solution.py:1042
  225.7 11.6 %layer_part.1 = bf16[2,512,768]{2,1,0:T(8,128)(2,1)} custom-call(s32[1]{0:T(128)} %bitcast.at_ref, f32[2,512,768]{2,1,0:T(8,128)} %get-tuple-element.149.res_ref, bf16[2,512,1536]{2,1,0:T(8,128)(2,1)} %get-tuple-element.186.aa_ref, bf16[2,512,1536]{2,1,0:T(8,128)(2,1)} %get-tuple-element.187.ab_ref, bf16[1536,768]{1,0:T(8,128)(2,1)} %w_ref.2, ...), custom_call_target="tpu_custom_call" | custom-call | bytes 43200000 | tf_op jit(solution)/shard_map/layer_part/pallas_call | solution.py:930
  237.3 12.2 %input_part.1 = f32[2,512,768]{2,1,0:T(8,128)} custom-call(s32[1]{0:T(128)} %bitcast.at_ref, bf16[2,512,768]{2,1,0:T(8,128)(2,1)} %x_ref.5, f32[2,512,768]{2,1,0:T(8,128)} %get-tuple-element.179.dres_ref, f32[1,768]{1,0:T(1,128)} %reshape.92.gain_ref, bf16[2,512,384]{2,1,0:T(8,128)(2,1)} %get-tuple-element.180.qa, ...), custom_call_target="tpu_custom_call" | custom-call | bytes 43200000 | tf_op jit(solution)/shard_map/input_part/pallas_call | solution.py:904
  249.5 5.1 %all-to-all-done.4 = bf16[8,48,1536]{2,1,0:T(8,128)(2,1)S(1)} async-done(((bf16[8,48,1536]{2,1,0:T(8,128)(2,1)}), bf16[8,48,1536]{2,1,0:T(8,128)(2,1)S(1)}, u32[]{:S(2)}, u32[]{:S(2)}) %all-to-all-start.4) | async-done | bytes 1179680 | tf_op jit(solution)/shard_map/all_to_all | solution.py:1042
  255.9 4.0 %all-to-all-start.5 = ((bf16[8,48,1536]{2,1,0:T(8,128)(2,1)}), bf16[8,48,1536]{2,1,0:T(8,128)(2,1)S(1)}, u32[]{:S(2)}, u32[]{:S(2)}) async-start(bf16[8,48,1536]{2,1,0:T(8,128)(2,1)} %broadcast_in_dim.14), calls=%async_computation.5 | async-start | bytes 2359296 | tf_op jit(solution)/shard_map/all_to_all | solution.py:1048
  268.5 3.0 collective-permute-start.23
  271.6 3.0 fusion
  274.6 5.3 %collective-permute-done.23 = f32[8,128]{1,0:T(8,128)S(1)} collective-permute-done((f32[8,128]{1,0:T(8,128)S(1)}, f32[8,128]{1,0:T(8,128)S(1)}, u32[]{:S(2)}, u32[]{:S(2)}) %collective-permute-start.23) | collective-permute-done | bytes 4128 | tf_op jit(solution)/shard_map/ppermute | solution.py:1015
  279.9 4.0 %collective-permute-start.24 = (f32[8,128]{1,0:T(8,128)S(1)}, f32[8,128]{1,0:T(8,128)S(1)}, u32[]{:S(2)}, u32[]{:S(2)}) collective-permute-start(f32[8,128]{1,0:T(8,128)S(1)} %add.100), channel_id=1, source_target_pairs={{0,16},{4,20},{8,24},{12,28},{16,0},{20,4},{24,8},{28,12},{1,17},{... | collective-permute-start | bytes 12296 | tf_op jit(solution)/shard_map/ppermute | solution.py:1015
  283.9 6.0 %inner_done.1 = (f32[768,1536]{1,0:T(8,128)}, f32[24,768]{1,0:T(8,128)}) custom-call(s32[1]{0:T(128)} %bitcast.at_ref, bf16[384,1536]{1,0:T(8,128)(2,1)} %bitcast.30, bf16[384,1536]{1,0:T(8,128)(2,1)} %collective-permute-done.18.near_ref, bf16[768,1536]{1,0:T(8,128)(2,1)} %w_ref.3), custom_call_target="tpu_custom_call" | custom-call | bytes 18000000 | tf_op jit(solution)/shard_map/inner_done/pallas_call | solution.py:964
  298.9 5.1 %attn_done.1 = (f32[768,384]{1,0:T(8,128)}, f32[768,384]{1,0:T(8,128)}, f32[768,384]{1,0:T(8,128)}, f32[384,768]{1,0:T(8,128)}, f32[8,768]{1,0:T(8,128)}) custom-call(s32[1]{0:T(128)} %bitcast.at_ref, bf16[384,1536]{1,0:T(8,128)(2,1)} %bitcast.32, bf16[384,1536]{1,0:T(8,128)(2,1)} %copy-done.11, bf16[768,384]{1,0:T(8,128)(2,1)} %wq.7, bf16[768,384]{1,0:T(8,128)(2,1)} %wk.7, ...), custom_call_target="tpu_custom_call" | custom-call | bytes 18000000 | tf_op jit(solution)/shard_map/attn_done/pallas_call | solution.py:999
  (149 shorter events, 61.6 us)
Async XLA Ops:
  4.7 16.8 %collective-permute-start.2 = (bf16[208,1152]{1,0:T(8,128)(2,1)}, bf16[208,1152]{1,0:T(8,128)(2,1)S(1)}, u32[]{:S(2)}, u32[]{:S(2)}) collective-permute-start(bf16[208,1152]{1,0:T(8,128)(2,1)} %get-tuple-element.118), channel_id=1, source_target_pairs={{0,1},{1,0},{2,3},{3,2},{4,5},{5,4},{6,7},{7,6},{8,9},{9,8},{10,11... | collective-permute-start | bytes 1437704 | tf_op jit(solution)/shard_map/ppermute | solution.py:1015
  7.7 24.6 %collective-permute-start.1 = (bf16[192,1536]{1,0:T(8,128)(2,1)}, bf16[192,1536]{1,0:T(8,128)(2,1)S(1)}, u32[]{:S(2)}, u32[]{:S(2)}) collective-permute-start(bf16[192,1536]{1,0:T(8,128)(2,1)} %get-tuple-element.117), channel_id=1, source_target_pairs={{0,1},{1,0},{2,3},{3,2},{4,5},{5,4},{6,7},{7,6},{8,9},{9,8},{10,11... | collective-permute-start | bytes 1769480 | tf_op jit(solution)/shard_map/ppermute | solution.py:1015
  21.5 17.7 %collective-permute-start.4 = (bf16[208,1152]{1,0:T(8,128)(2,1)S(1)}, bf16[208,1152]{1,0:T(8,128)(2,1)S(1)}, u32[]{:S(2)}, u32[]{:S(2)}) collective-permute-start(bf16[208,1152]{1,0:T(8,128)(2,1)S(1)} %collective-permute-done.2.p0), channel_id=1, source_target_pairs={{0,4},{4,0},{8,12},{12,8},{16,20},{20,16},{24,28},{28,24},{1,5},{5... | collective-permute-start | bytes 1437704 | tf_op jit(solution)/shard_map/ppermute | solution.py:1015
  23.5 15.7 %collective-permute-start.5 = (bf16[192,768]{1,0:T(8,128)(2,1)S(1)}, bf16[192,768]{1,0:T(8,128)(2,1)}, u32[]{:S(2)}, u32[]{:S(2)}) collective-permute-start(bf16[192,768]{1,0:T(8,128)(2,1)S(1)} %copy-done.26), channel_id=1, source_target_pairs={{0,1},{1,0},{2,3},{3,2},{4,5},{5,4},{6,7},{7,6},{8,9},{9,8},{10,11... | collective-permute-start | bytes 884744 | tf_op jit(solution)/shard_map/ppermute | solution.py:1015
  25.7 13.4 %all-to-all-start = ((bf16[32,2,896]{2,1,0:T(2,128)(2,1)}), bf16[32,2,896]{2,1,0:T(2,128)(2,1)S(1)}, u32[]{:S(2)}, u32[]{:S(2)}) async-start(bf16[32,2,896]{2,1,0:T(2,128)(2,1)} %broadcast_in_dim.10), calls=%async_computation | async-start | bytes 229376 | tf_op jit(solution)/shard_map/all_to_all | solution.py:1032
  32.4 29.3 %collective-permute-start.3 = (bf16[192,1536]{1,0:T(8,128)(2,1)S(1)}, bf16[192,1536]{1,0:T(8,128)(2,1)S(1)}, u32[]{:S(2)}, u32[]{:S(2)}) collective-permute-start(bf16[192,1536]{1,0:T(8,128)(2,1)S(1)} %collective-permute-done.1.p0.refs_2_), channel_id=1, source_target_pairs={{0,4},{4,0},{8,12},{12,8},{16,20},{20,16},{24,28},{28,24},{1,5},{5... | collective-permute-start | bytes 1769480 | tf_op jit(solution)/shard_map/ppermute | solution.py:1015
  34.4 7.6 %collective-permute-start.6 = (bf16[208,1152]{1,0:T(8,128)(2,1)S(1)}, bf16[208,1152]{1,0:T(8,128)(2,1)}, u32[]{:S(2)}, u32[]{:S(2)}) collective-permute-start(bf16[208,1152]{1,0:T(8,128)(2,1)S(1)} %collective-permute-done.2.p0), channel_id=1, source_target_pairs={{0,2},{2,0},{1,3},{3,1},{4,6},{6,4},{5,7},{7,5},{8,10},{10,8},{9,1... | collective-permute-start | bytes 1437704 | tf_op jit(solution)/shard_map/ppermute | solution.py:1015
  39.1 2.9 collective-permute-start.7
  39.3 2.7 collective-permute-start.8
  39.7 45.6 %collective-permute-start = (bf16[768,768]{1,0:T(8,128)(2,1)}, bf16[768,768]{1,0:T(8,128)(2,1)S(1)}, u32[]{:S(2)}, u32[]{:S(2)}) collective-permute-start(bf16[768,768]{1,0:T(8,128)(2,1)} %get-tuple-element.116), channel_id=1, source_target_pairs={{0,1},{1,0},{2,3},{3,2},{4,5},{5,4},{6,7},{7,6},{8,9},{9,8},{10,11... | collective-permute-start | bytes 3538952 | tf_op jit(solution)/shard_map/ppermute | solution.py:1015
  64.5 20.9 %collective-permute-start.11 = (bf16[1,512,768]{2,1,0:T(8,128)(2,1)}, bf16[1,512,768]{2,1,0:T(8,128)(2,1)}, u32[]{:S(2)}, u32[]{:S(2)}) collective-permute-start(bf16[1,512,768]{2,1,0:T(8,128)(2,1)} %get-tuple-element.214), channel_id=1, source_target_pairs={{0,1},{1,0},{2,3},{3,2},{4,5},{5,4},{6,7},{7,6},{8,9},{9,8},{10,11... | collective-permute-start | bytes 2359304 | tf_op jit(solution)/shard_map/ppermute | solution.py:1015
  65.8 2.0 collective-permute-start.9
  65.9 2.8 collective-permute-start.10
  85.4 2.9 collective-permute-start.12
  85.6 26.4 %collective-permute-start.13 = (bf16[1,512,768]{2,1,0:T(8,128)(2,1)S(1)}, bf16[1,512,768]{2,1,0:T(8,128)(2,1)}, u32[]{:S(2)}, u32[]{:S(2)}) collective-permute-start(bf16[1,512,768]{2,1,0:T(8,128)(2,1)S(1)} %copy-done.13), channel_id=1, source_target_pairs={{0,1},{1,0},{2,3},{3,2},{4,5},{5,4},{6,7},{7,6},{8,9},{9,8},{10,11... | collective-permute-start | bytes 2359304 | tf_op jit(solution)/shard_map/ppermute | solution.py:1015
  94.5 16.7 %all-to-all-start.1 = ((bf16[32,2,2304]{2,1,0:T(2,128)(2,1)}), bf16[32,2,2304]{2,1,0:T(2,128)(2,1)S(1)}, u32[]{:S(2)}, u32[]{:S(2)}) async-start(bf16[32,2,2304]{2,1,0:T(2,128)(2,1)} %bitcast.10), calls=%async_computation.1 | async-start | bytes 589824 | tf_op jit(solution)/shard_map/all_to_all | solution.py:1032
  128.4 3.1 %collective-permute-start.14 = (bf16[384,1536]{1,0:T(8,128)(2,1)}, bf16[384,1536]{1,0:T(8,128)(2,1)S(1)}, u32[]{:S(2)}, u32[]{:S(2)}) collective-permute-start(bf16[384,1536]{1,0:T(8,128)(2,1)} %get-tuple-element.143), channel_id=1, source_target_pairs={{0,2},{2,0},{1,3},{3,1},{4,6},{6,4},{5,7},{7,5},{8,10},{10,8},{9,1... | collective-permute-start | bytes 3538952 | tf_op jit(solution)/shard_map/ppermute | solution.py:1015
  134.1 44.8 %all-to-all-start.2 = ((bf16[8,48,1536]{2,1,0:T(8,128)(2,1)}), bf16[8,48,1536]{2,1,0:T(8,128)(2,1)S(1)}, u32[]{:S(2)}, u32[]{:S(2)}) async-start(bf16[8,48,1536]{2,1,0:T(8,128)(2,1)} %bitcast.11), calls=%async_computation.2 | async-start | bytes 2359296 | tf_op jit(solution)/shard_map/all_to_all | solution.py:1042
  174.3 3.1 %collective-permute-start.15 = (bf16[384,1536]{1,0:T(8,128)(2,1)}, bf16[384,1536]{1,0:T(8,128)(2,1)S(1)}, u32[]{:S(2)}, u32[]{:S(2)}) collective-permute-start(bf16[384,1536]{1,0:T(8,128)(2,1)} %get-tuple-element.164), channel_id=1, source_target_pairs={{0,2},{2,0},{1,3},{3,1},{4,6},{6,4},{5,7},{7,5},{8,10},{10,8},{9,1... | collective-permute-start | bytes 3538952 | tf_op jit(solution)/shard_map/ppermute | solution.py:1015
  180.3 34.8 %all-to-all-start.3 = ((bf16[8,48,1536]{2,1,0:T(8,128)(2,1)}), bf16[8,48,1536]{2,1,0:T(8,128)(2,1)S(1)}, u32[]{:S(2)}, u32[]{:S(2)}) async-start(bf16[8,48,1536]{2,1,0:T(8,128)(2,1)} %broadcast_in_dim.13), calls=%async_computation.3 | async-start | bytes 2359296 | tf_op jit(solution)/shard_map/all_to_all | solution.py:1048
  186.3 27.8 %collective-permute-start.16 = (bf16[384,1536]{1,0:T(8,128)(2,1)S(1)}, bf16[384,1536]{1,0:T(8,128)(2,1)}, u32[]{:S(2)}, u32[]{:S(2)}) collective-permute-start(bf16[384,1536]{1,0:T(8,128)(2,1)S(1)} %add.93), channel_id=1, source_target_pairs={{0,1},{1,0},{2,3},{3,2},{4,5},{5,4},{6,7},{7,6},{8,9},{9,8},{10,11... | collective-permute-start | bytes 3538952 | tf_op jit(solution)/shard_map/ppermute | solution.py:1015
  215.2 3.1 collective-permute-start.17
  221.0 33.6 %all-to-all-start.4 = ((bf16[8,48,1536]{2,1,0:T(8,128)(2,1)}), bf16[8,48,1536]{2,1,0:T(8,128)(2,1)S(1)}, u32[]{:S(2)}, u32[]{:S(2)}) async-start(bf16[8,48,1536]{2,1,0:T(8,128)(2,1)} %bitcast.13), calls=%async_computation.4 | async-start | bytes 2359296 | tf_op jit(solution)/shard_map/all_to_all | solution.py:1042
  255.9 39.2 %all-to-all-start.5 = ((bf16[8,48,1536]{2,1,0:T(8,128)(2,1)}), bf16[8,48,1536]{2,1,0:T(8,128)(2,1)S(1)}, u32[]{:S(2)}, u32[]{:S(2)}) async-start(bf16[8,48,1536]{2,1,0:T(8,128)(2,1)} %broadcast_in_dim.14), calls=%async_computation.5 | async-start | bytes 2359296 | tf_op jit(solution)/shard_map/all_to_all | solution.py:1048
  259.9 24.0 %collective-permute-start.18 = (bf16[384,1536]{1,0:T(8,128)(2,1)S(1)}, bf16[384,1536]{1,0:T(8,128)(2,1)}, u32[]{:S(2)}, u32[]{:S(2)}) collective-permute-start(bf16[384,1536]{1,0:T(8,128)(2,1)S(1)} %bitcast.29), channel_id=1, source_target_pairs={{0,2},{2,0},{1,3},{3,1},{4,6},{6,4},{5,7},{7,5},{8,10},{10,8},{9,1... | collective-permute-start | bytes 3538952 | tf_op jit(solution)/shard_map/ppermute | solution.py:1015
  260.0 3.7 %collective-permute-start.20 = (f32[8,128]{1,0:T(8,128)S(1)}, f32[8,128]{1,0:T(8,128)S(1)}, u32[]{:S(2)}, u32[]{:S(2)}) collective-permute-start(f32[8,128]{1,0:T(8,128)S(1)} %copy-done.27), channel_id=1, source_target_pairs={{0,1},{1,0},{2,3},{3,2},{4,5},{5,4},{6,7},{7,6},{8,9},{9,8},{10,11... | collective-permute-start | bytes 12296 | tf_op jit(solution)/shard_map/ppermute | solution.py:1015
  264.8 3.7 %collective-permute-start.22 = (f32[8,128]{1,0:T(8,128)S(1)}, f32[8,128]{1,0:T(8,128)S(1)}, u32[]{:S(2)}, u32[]{:S(2)}) collective-permute-start(f32[8,128]{1,0:T(8,128)S(1)} %add.98), channel_id=1, source_target_pairs={{0,4},{4,0},{8,12},{12,8},{16,20},{20,16},{24,28},{28,24},{1,5},{5... | collective-permute-start | bytes 12296 | tf_op jit(solution)/shard_map/ppermute | solution.py:1015
  268.5 11.4 %collective-permute-start.23 = (f32[8,128]{1,0:T(8,128)S(1)}, f32[8,128]{1,0:T(8,128)S(1)}, u32[]{:S(2)}, u32[]{:S(2)}) collective-permute-start(f32[8,128]{1,0:T(8,128)S(1)} %add.99), channel_id=1, source_target_pairs={{0,8},{4,12},{8,0},{12,4},{16,24},{20,28},{24,16},{28,20},{1,9},{5... | collective-permute-start | bytes 12296 | tf_op jit(solution)/shard_map/ppermute | solution.py:1015
  279.9 13.8 %collective-permute-start.24 = (f32[8,128]{1,0:T(8,128)S(1)}, f32[8,128]{1,0:T(8,128)S(1)}, u32[]{:S(2)}, u32[]{:S(2)}) collective-permute-start(f32[8,128]{1,0:T(8,128)S(1)} %add.100), channel_id=1, source_target_pairs={{0,16},{4,20},{8,24},{12,28},{16,0},{20,4},{24,8},{28,12},{1,17},{... | collective-permute-start | bytes 12296 | tf_op jit(solution)/shard_map/ppermute | solution.py:1015
  290.8 3.7 %collective-permute-start.19 = (f32[768]{0:T(1024)S(1)}, f32[768]{0:T(1024)S(1)}, u32[]{:S(2)}, u32[]{:S(2)}) collective-permute-start(f32[768]{0:T(1024)S(1)} %reduce_sum.45), channel_id=1, source_target_pairs={{0,1},{1,0},{2,3},{3,2},{4,5},{5,4},{6,7},{7,6},{8,9},{9,8},{10,11... | collective-permute-start | bytes 9224 | tf_op jit(solution)/shard_map/ppermute | solution.py:1015
  295.0 2.8 collective-permute-start.25
  304.8 3.7 %collective-permute-start.26 = (f32[768]{0:T(1024)S(1)}, f32[768]{0:T(1024)S(1)}, u32[]{:S(2)}, u32[]{:S(2)}) collective-permute-start(f32[768]{0:T(1024)S(1)} %slice_reduce_fusion), channel_id=1, source_target_pairs={{0,1},{1,0},{2,3},{3,2},{4,5},{5,4},{6,7},{7,6},{8,9},{9,8},{10,11... | collective-permute-start | bytes 9224 | tf_op jit(solution)/shard_map/ppermute | solution.py:1015
  (29 other events, 296.9 us)
where the time goes:
time: 315 us; the launch traced here: 309 us
  Pallas kernels  158 us (50%)
  waiting for transfers between devices  60.7 us (19%)
  starting transfers between devices  56.1 us (18%)
  local copies, waits for them, and re-layouts  18.2 us (6%)
  other arithmetic  10.3 us (3%)
  matrix products  4.89 us (2%)
    ppermute x27, waiting for transfers between devices, swap(): return lax.ppermute(x, axis, [(i, i ^ bit) for i in range(size)])  44.8 us
    pallas_call x2, Pallas kernels, attn_bwd(): pl.pallas_call(attn_bwd_kernel, grid=(n,), in_specs=[SMEM_SPEC, SMEM_SPEC...  32.5 us
    ppermute x27, starting transfers between devices, swap(): return lax.ppermute(x, axis, [(i, i ^ bit) for i in range(size)])  27.7 us
    pallas_call x1, Pallas kernels, ffn_bwd(): pl.pallas_call(ffn_bwd_kernel, grid=(n,), in_specs=[SMEM_SPEC, SMEM_SPEC,...  19.8 us
    pallas_call x1, Pallas kernels, attn_other(): pl.pallas_call(attn_other_kernel, grid=(n,), in_specs=[SMEM_SPEC, SMEM_SP...  18.1 us
    pallas_call x1, Pallas kernels, loss_all(): pl.pallas_call(loss_kernel, in_specs=[SMEM_SPEC] * 3 + [vm] * 3 + [ANY] *...  16.5 us
    pallas_call x1, Pallas kernels, ffn_fwd(): pl.pallas_call(ffn_fwd_kernel, grid=(n,), in_specs=[SMEM_SPEC, SMEM_SPEC,...  15.8 us
    pallas_call x1, Pallas kernels, attn_own(): pl.pallas_call(attn_own_kernel, grid=(n,), in_specs=[SMEM_SPEC, row_spec(...  12.6 us
  transfers between devices with their start and end apart: 33, of which 19 were waited for; matrix products, arithmetic and copies ran while one was open for 6% of the time, Pallas kernels for 43%

commit v1 on v0

--- a/solution.py
+++ b/solution.py
@@ -90,21 +90,34 @@
         c.wait()
 
 
-def pack_kernel(at_ref, tab_ref, wq, wk, wv, wo, wi, wu, s0, s1, s2, s3, sem):
+def out_pieces(width, d):
+    rows, tall = width // 4, width // 6
+    rest = rows - tall
+    out = [((0, tall, 0, d), (0, tall, 0, d))]
+    for i in range(2):
+        out.append(((tall, rest, i * width, width), (i * rest, rest, d, width)))
+    return out
+
+
+def pack_kernel(at_ref, tab_ref, wq, wk, wv, wo, wi, wu, s0, s1, s2, sem):
     at = at_ref[0]
-    width = wq.shape[1]
-    rows = s2.shape[0]
-
-    def part(w, dst, i, spot, count):
-        src = w.at[pl.ds(pl.multiple_of(spot * count, count), count)]
+    d, width = wq.shape
+    rows = d // 4
+
+    def part(w, dst, i):
+        count = w.shape[0] // 4
+        src = w.at[pl.ds(pl.multiple_of(at * count, count), count)]
         return pltpu.make_async_copy(src, dst, sem.at[i])
 
-    spread = [(w, s0.at[pl.ds(0, rows), width * i : width * (i + 1)]) for i, w in enumerate((wq, wk, wv))]
-    copies = [part(w, dst, i, at, rows) for i, (w, dst) in enumerate(spread + [(wi, s2)])]
-    copies += [part(w, dst, 4 + i, at // 2, dst.shape[0]) for i, (w, dst) in enumerate(((wo, s1), (wu, s3)))]
+    copies = [part(w, s0.at[pl.ds(0, rows), width * i : width * (i + 1)], i) for i, w in enumerate((wq, wk, wv))]
+    copies += [part(wi, s1, 3), part(wu, s2, 4)]
+    for i, (a, b) in enumerate(out_pieces(width, d)):
+        src = wo.at[pl.ds(pl.multiple_of(at * (width // 4) + a[0], 32), a[1]), a[2] : a[2] + a[3]]
+        dst = s0.at[pl.ds(rows + 16 + b[0], b[1]), b[2] : b[2] + b[3]]
+        copies.append(pltpu.make_async_copy(src, dst, sem.at[5 + i]))
     for c in copies:
         c.start()
-    s0[rows:, :] = jnp.zeros((16, s0.shape[1]), BF)
+    s0[rows : rows + 16, :] = jnp.zeros((16, s0.shape[1]), BF)
     heads, buckets = tab_ref.shape
     for k, t in enumerate(split3(tab_ref[...])):
         s0[rows : rows + heads, TILE * k : TILE * k + buckets] = t
@@ -119,28 +132,40 @@
     return pl.pallas_call(
         pack_kernel,
         in_specs=[SMEM_SPEC, vm] + [ANY] * 6,
-        out_specs=[vm] * 4,
+        out_specs=[vm] * 3,
         out_shape=[
-            sds((d // 4 + 16, 3 * width), BF),
-            sds((width // 2, d), BF),
+            sds((d // 4 + 16 + width // 6, 3 * width), BF),
             sds((d // 4, half), BF),
-            sds((half // 2, d), BF),
+            sds((half // 4, d), BF),
         ],
-        scratch_shapes=[pltpu.SemaphoreType.DMA((6,))],
+        scratch_shapes=[pltpu.SemaphoreType.DMA((8,))],
         compiler_params=params(),
         cost_estimate=cost(3),
         name="pack_weights",
     )(at, table, wq, wk, wv, wo, wi, wu)
 
 
+def quarter_spots(at):
+    core, xb = at // 2, at % 2
+    return [at, 2 * core + 1 - xb, 2 * (1 - core) + xb, 2 * (1 - core) + 1 - xb]
+
+
+def out_copies(at, packs, dst, sem):
+    width, d = dst.shape
+    base = d // 4 + 16
+    out = []
+    for i, (p, s) in enumerate(zip(packs, quarter_spots(at))):
+        for j, (a, b) in enumerate(out_pieces(width, d)):
+            src = p.at[pl.ds(base + b[0], b[1]), b[2] : b[2] + b[3]]
+            to = dst.at[pl.ds(pl.multiple_of(s * (width // 4) + a[0], 32), a[1]), a[2] : a[2] + a[3]]
+            out.append(pltpu.make_async_copy(src, to, sem.at[3 * i + j]))
+    return out
+
+
 def join_copies(at, packs, dst, sem):
-    core, xb = at // 2, at % 2
-    spots = [at, 2 * core + 1 - xb, 2 * (1 - core) + xb, 2 * (1 - core) + 1 - xb]
-    if len(packs) == 2:
-        spots = [core, 1 - core]
-    rows = dst.shape[0] // len(packs)
+    rows = dst.shape[0] // 4
     out = []
-    for i, (p, s) in enumerate(zip(packs, spots)):
+    for i, (p, s) in enumerate(zip(packs, quarter_spots(at))):
         to = dst.at[pl.ds(pl.multiple_of(s * rows, rows), rows)]
         out.append(pltpu.make_async_copy(p.at[pl.ds(0, rows)], to, sem.at[i]))
     return out
@@ -220,29 +245,31 @@
         qt = qt_ref[0, 64 * h : 64 * (h + 1), :]
         queries[h] = stack_rows(e, qt, far_rows(tf_ref, h, seq).astype(BF))
 
-    def score(t):
+    def start(t):
         h, ib = blocks[t]
         if ib == 0:
             prepare(h)
         s = mm(keys[h], queries[h][:, 256 * ib : 256 * (ib + 1)])
-        top = None
-        for bj, piece in enumerate(near_bias(s, nb_ref, h, ib)):
-            s_ref[t % 2, TILE * bj : TILE * (bj + 1), :] = piece
-            m = jnp.max(piece.reshape(TILE // 8, 8, 256), axis=0)
-            top = m if top is None else jnp.maximum(top, m)
-        tops[t] = jnp.max(top, axis=0, keepdims=True)
-
-    def soft(t):
+        return near_bias(s, nb_ref, h, ib)
+
+    def score(t, bj, pieces):
+        piece = pieces[bj]
+        s_ref[t % 2, TILE * bj : TILE * (bj + 1), :] = piece
+        m = jnp.max(piece.reshape(TILE // 8, 8, 256), axis=0)
+        tops[t] = m if bj == 0 else jnp.maximum(tops[t], m)
+        if bj == seq // TILE - 1:
+            tops[t] = jnp.max(tops[t], axis=0, keepdims=True)
+
+    def soft(t, bj):
         h, ib = blocks[t]
-        total = None
-        for bj in range(seq // TILE):
-            at = slice(TILE * bj, TILE * (bj + 1))
-            p = jnp.exp(s_ref[t % 2, at, :] - tops[t])
-            one = jnp.sum(p.reshape(TILE // 8, 8, 256), axis=0)
-            total = one if total is None else total + one
-            p_ref[h % 2, at, 256 * ib : 256 * (ib + 1)] = p.astype(BF)
-        sums[t] = jnp.sum(total, axis=0, keepdims=True)
-        lse_ref[0, h : h + 1, 256 * ib : 256 * (ib + 1)] = tops[t] + jnp.log(sums[t])
+        at = slice(TILE * bj, TILE * (bj + 1))
+        p = jnp.exp(s_ref[t % 2, at, :] - tops[t])
+        one = jnp.sum(p.reshape(TILE // 8, 8, 256), axis=0)
+        sums[t] = one if bj == 0 else sums[t] + one
+        p_ref[h % 2, at, 256 * ib : 256 * (ib + 1)] = p.astype(BF)
+        if bj == seq // TILE - 1:
+            sums[t] = jnp.sum(sums[t], axis=0, keepdims=True)
+            lse_ref[0, h : h + 1, 256 * ib : 256 * (ib + 1)] = tops[t] + jnp.log(sums[t])
 
     def combine(h):
         per = seq // 256
@@ -256,13 +283,16 @@
             ctxt_ref[0, cols, :] = ct
             ctx_ref[0, :, cols] = jnp.transpose(ct)
 
-    score(0)
-    for t, (h, ib) in enumerate(blocks):
-        if t + 1 < len(blocks):
-            score(t + 1)
-        soft(t)
-        if ib == seq // 256 - 1:
-            combine(h)
+    for t in range(len(blocks) + 1):
+        if t < len(blocks):
+            pieces = start(t)
+            for bj in range(seq // TILE):
+                score(t, bj, pieces)
+        if t > 0:
+            for bj in range(seq // TILE):
+                soft(t - 1, bj)
+            if blocks[t - 1][1] == seq // 256 - 1:
+                combine(blocks[t - 1][0])
 
 
 def attn_own_kernel(lens, x_ref, gain_ref, wq, wk, wv, tab_ref, hot_ref, an_ref, ant_ref, *refs):
@@ -284,11 +314,12 @@
     attn_rows(an, lens[b], (wq, wk, wv), outs, nb_ref, tf_ref, s_ref, p_ref)
 
 
-def attn_other_kernel(lens, at_ref, an_ref, hot_ref, x_ref, ca_ref, wo_ref, gain_ref, p0, p1, p2, p3, o0, o1, *refs):
-    outs, (nb_ref, tf_ref, res_ref, fin_ref, fint_ref, rsum_ref) = refs[:7], refs[7:13]
-    (s_ref, p_ref, w_ref, tab_ref, wb_ref, sem, sem1) = refs[13:]
+def attn_other_kernel(lens, at_ref, an_ref, hot_ref, x_ref, ca_ref, wo_ref, gain_ref, p0, p1, p2, p3, *refs):
+    outs, (nb_ref, tf_ref, res_ref, fin_ref, fint_ref, rsum_ref, f0_ref, f1_ref) = list(refs[:6]), refs[6:14]
+    (s_ref, p_ref, w_ref, tab_ref, wb_ref, c_ref, sem, sem1) = refs[14:]
+    outs.insert(4, c_ref)
     b = pl.program_id(0)
-    late = join_copies(at_ref[0], (o0, o1), wb_ref, sem1)
+    late = out_copies(at_ref[0], (p0, p1, p2, p3), wb_ref, sem1)
 
     @pl.when(b == 0)
     def _():
@@ -316,8 +347,14 @@
     inv = lax.rsqrt(jnp.mean(res * res, axis=-1, keepdims=True) + EPS)
     fin = (res * inv * gain_ref[...]).astype(BF)
     fin_ref[0] = fin
-    fint_ref[...] = jnp.transpose(fin)
+    for i, f_ref in enumerate((f0_ref, f1_ref)):
+
+        @pl.when(b == i)
+        def _():
+            f_ref[0] = fin
+
     vcol = (lax.broadcasted_iota(jnp.int32, (res.shape[0], TILE), 0) < lens[b]).astype(F32)[:, :1]
+    fint_ref[...] = jnp.transpose((fin.astype(F32) * vcol).astype(BF))
     rsum_ref[0] = jnp.sum(res * vcol, axis=0, keepdims=True)
 
 
@@ -348,19 +385,22 @@
     )(lens, x, gain.reshape(1, d), wq, wk, wv, table, hot)
 
 
-def attn_other(lens, at, an, hot, x, ctx_a, wo, gain, packs, packs_o):
+def attn_other(lens, at, an, hot, x, ctx_a, wo, gain, packs):
     n, seq, d = an.shape
     width = wo.shape[0]
     outs, specs, scratch = attn_outs(n, seq, width)
+    del outs[4], specs[4]
     more = [sds((n, seq, d), F32), sds((n, seq, d), BF), sds((d, n * seq), BF), sds((n, 1, d), F32)]
     more_specs = [row_spec(o.shape) for o in more]
     more_specs[2] = pl.BlockSpec((d, seq), lambda b: (0, b))
+    more += [sds((1, seq, d), BF)] * n
+    more_specs += [out_const((1, seq, d))] * n
     return pl.pallas_call(
         attn_other_kernel,
         grid=(n,),
         in_specs=[SMEM_SPEC, SMEM_SPEC, row_spec(an.shape), const_spec(hot.shape), row_spec(x.shape)]
         + [row_spec(ctx_a.shape), const_spec(wo.shape), const_spec((1, d))]
-        + [ANY] * 6,
+        + [ANY] * 4,
         out_specs=specs + more_specs,
         out_shape=outs + more,
         scratch_shapes=scratch
@@ -368,35 +408,35 @@
             pltpu.VMEM((d, 3 * width), BF),
             pltpu.VMEM((16, 3 * width), BF),
             pltpu.VMEM(wo.shape, BF),
+            pltpu.VMEM((1, seq, width), BF),
             pltpu.SemaphoreType.DMA((5,)),
-            pltpu.SemaphoreType.DMA((2,)),
+            pltpu.SemaphoreType.DMA((12,)),
         ],
         compiler_params=params(),
         cost_estimate=cost(15),
         name="attn_other",
-    )(lens, at, an, hot, x, ctx_a, wo, gain.reshape(1, d), *packs, *packs_o)
-
-
-def attn_bwd_kernel(lens, at_ref, *refs):
-    (q_ref, qt_ref, k_ref, v_ref, dc_ref, dct_ref, ct_ref, lse_ref, nb_ref, tf_ref, hot_ref, ant_hbm, go_hbm) = refs[:13]
-    (dq_ref, dk_ref, dv_ref, send_ref, keep_ref, table_ref) = refs[13:19]
-    (t_ref, fsum_ref, p_ref, ds_ref, all_ref, ant_ref, go_ref, sem) = refs[19:]
-    b = pl.program_id(0)
+    )(lens, at, an, hot, x, ctx_a, wo, gain.reshape(1, d), *packs)
+
+
+def attn_back(b, n, length, core, w, d_attn, ins, outs, scratch, late):
+    (q_ref, qt_ref, k_ref, v_ref, ct_ref, lse_ref, nb_ref, tf_ref, ant_ref, hot_ref) = ins
+    (dq_ref, dk_ref, dv_ref, send_ref, keep_ref, table_ref) = outs
+    (dc_ref, dct_ref, t_ref, fsum_ref, p_ref, ds_ref, all_ref, da_ref, go_ref) = scratch
     seq, width = q_ref.shape[1], q_ref.shape[2]
     heads = width // 64
     nblk = seq // TILE
-
-    late = [pltpu.make_async_copy(ant_hbm, ant_ref, sem.at[0]), pltpu.make_async_copy(go_hbm, go_ref, sem.at[1])]
+    here = pl.ds(pl.multiple_of(b * seq, seq), seq)
 
     @pl.when(b == 0)
     def _():
-        for c in late:
-            c.start()
         t_ref[...] = jnp.zeros_like(t_ref)
         fsum_ref[...] = jnp.zeros_like(fsum_ref)
         table_ref[...] = jnp.zeros_like(table_ref)
 
-    kx = key_extras(lens[b], seq)
+    da_ref[here, :] = d_attn
+    dct_ref[...] = mm(w, d_attn, NT).astype(BF)
+    dc_ref[...] = jnp.transpose(dct_ref[...])
+    kx = key_extras(length, seq)
     lane = lax.broadcasted_iota(jnp.int32, (seq, TILE), 1)
     vx = jnp.where((lane & 63) < 3, 1.0, 0.0)
     keys, values, queries, grads, turned = {}, {}, {}, {}, {}
@@ -406,21 +446,21 @@
         cols = slice(TILE * pair, TILE * (pair + 1))
         mine = lane < 64 if e == 0 else lane >= 64
         if e == 0:
-            turned[pair] = jnp.transpose(k_ref[0, :, cols])
-        keys[h] = jnp.where(mine, k_ref[0, :, cols].astype(F32), kx).astype(BF)
-        values[h] = jnp.where(mine, v_ref[0, :, cols].astype(F32), vx).astype(BF)
+            turned[pair] = jnp.transpose(k_ref[b, :, cols])
+        keys[h] = jnp.where(mine, k_ref[b, :, cols].astype(F32), kx).astype(BF)
+        values[h] = jnp.where(mine, v_ref[b, :, cols].astype(F32), vx).astype(BF)
         at = slice(64 * h, 64 * (h + 1))
-        lse = split3(-lse_ref[0, h : h + 1, :])
+        lse = split3(-lse_ref[b, h : h + 1, :])
         extra = far_rows(tf_ref, h, seq)
         row = lax.broadcasted_iota(jnp.int32, (EXTRA, seq), 0)
         for k in range(3):
             extra = jnp.where(row == 13 + k, lse[k].astype(F32), extra)
-        queries[h] = stack_rows(e, qt_ref[0, at, :], extra.astype(BF))
-        along = jnp.sum(dct_ref[0, at, :].astype(F32) * ct_ref[0, at, :].astype(F32), axis=0, keepdims=True)
+        queries[h] = stack_rows(e, qt_ref[b, at, :], extra.astype(BF))
+        along = jnp.sum(dct_ref[at, :].astype(F32) * ct_ref[b, at, :].astype(F32), axis=0, keepdims=True)
         extra = jnp.zeros((EXTRA, seq), F32)
         for k, part in enumerate(split3(-along)):
             extra = jnp.where(row == k, part.astype(F32), extra)
-        grads[h] = stack_rows(e, dct_ref[0, at, :], extra.astype(BF))
+        grads[h] = stack_rows(e, dct_ref[at, :], extra.astype(BF))
 
     def block(h, ib):
         pair, e = h // 2, h % 2
@@ -452,20 +492,18 @@
     def finish(pair, part):
         slot = pair % 2
         cols = slice(TILE * pair, TILE * (pair + 1))
-        rows = pl.ds(pl.multiple_of(b * seq, seq), seq)
         if part < 2:
-            src, other, out_ref = ((p_ref, dc_ref, dv_ref), (ds_ref, q_ref, dk_ref))[part]
-            rhs = other[0, :, cols]
+            src, rhs, out_ref = ((p_ref, dc_ref[:, cols], dv_ref), (ds_ref, q_ref[b, :, cols], dk_ref))[part]
             one = jnp.where(lane < 64, mm(src[slot, :, :seq], rhs), mm(src[slot, :, seq:], rhs)).astype(BF)
             out_ref[0, :, cols] = one
             base = width * (2 - part)
-            all_ref[rows, base + TILE * pair : base + TILE * (pair + 1)] = one
+            all_ref[here, base + TILE * pair : base + TILE * (pair + 1)] = one
         if part == 2:
             kt = turned[pair]
             dqt = [mm(kt[64 * e : 64 * (e + 1), :], ds_ref[slot, :, seq * e : seq * (e + 1)]) for e in range(2)]
             one = jnp.transpose(jnp.concatenate(dqt, axis=0).astype(BF))
             dq_ref[0, :, cols] = one
-            all_ref[rows, TILE * pair : TILE * (pair + 1)] = one
+            all_ref[here, TILE * pair : TILE * (pair + 1)] = one
 
     for pair in range(heads // 2):
         step = 0
@@ -479,16 +517,21 @@
     for part in range(3):
         finish(heads // 2 - 1, part)
 
-    @pl.when(b == pl.num_programs(0) - 1)
+    @pl.when(b == n - 1)
     def _():
         for c in late:
             c.wait()
         rows = ant_ref.shape[0] // 2
-        core = at_ref[0] // 2
+        out = None
+        for i in range(n):
+            one = mm(ct_ref[i], da_ref[seq * i : seq * (i + 1), :])
+            out = one if out is None else out + one
+        go_ref[:width, :] = out[:, :width].astype(BF)
+        go_ref[width:, :] = out[:, width:].astype(BF)
         for ref, half in ((send_ref, 1 - core), (keep_ref, core)):
             at = pl.ds(pl.multiple_of(half * rows, rows), rows)
             ref[:, : 3 * width] = mm(ant_ref[at, :], all_ref[...]).astype(BF)
-            ref[:, 3 * width :] = go_ref[at, :].astype(BF)
+            ref[:, 3 * width :] = go_ref[at, :]
         turn = lax.broadcasted_iota(jnp.int32, (TILE, TILE), 0) + lax.broadcasted_iota(jnp.int32, (TILE, TILE), 1)
         turn = jnp.where(turn == TILE - 1, 1.0, 0.0).astype(BF)
         tiles = t_ref.shape[0]
@@ -499,59 +542,85 @@
             x = jnp.concatenate([back[TILE * t : TILE * (t + 1)], jnp.zeros((TILE, TILE), F32)], axis=1)
             x = pltpu.roll(x, 0, 1, stride=1, stride_axis=0)
             diag.append(jnp.sum(x, axis=0, keepdims=True))
-        rows = [jnp.concatenate(diag[3 * h : 3 * h + 3], axis=1) for h in range(heads)]
-        rows.append(jnp.zeros((16 - heads, rows[0].shape[1]), F32))
-        near = [mm(part, hot_ref[...]) for part in split3(jnp.concatenate(rows, axis=0))]
-        lane = lax.broadcasted_iota(jnp.int32, (1, TILE), 1)
+        lines = [jnp.concatenate(diag[3 * h : 3 * h + 3], axis=1) for h in range(heads)]
+        lines.append(jnp.zeros((16 - heads, lines[0].shape[1]), F32))
+        near = [mm(part, hot_ref[...]) for part in split3(jnp.concatenate(lines, axis=0))]
+        spot = lax.broadcasted_iota(jnp.int32, (1, TILE), 1)
         for h in range(heads):
             one = near[0][h : h + 1] + near[1][h : h + 1] + near[2][h : h + 1]
             for side, bucket in ((0, BUCKETS // 2 - 1), (1, BUCKETS - 1)):
                 far = jnp.sum(jnp.sum(fsum_ref[2 * h + side], axis=0, keepdims=True), axis=1, keepdims=True)
-                one = one + jnp.where(lane == bucket, far, 0.0)
+                one = one + jnp.where(spot == bucket, far, 0.0)
             table_ref[h : h + 1, :] = one
 
 
-def attn_bwd(lens, at, q, qt, k, v, dctx, dctxt, ctxt, lse, nb, tf, hot, ant, go):
-    n, seq, width = q.shape
-    d = ant.shape[0]
+def back_outs(n, seq, width, d):
+    tok = sds((n, seq, width), BF)
+    half = sds((d // 2, 4 * width), BF)
+    outs = [tok, tok, tok, half, half, sds((8, TILE), F32)]
+    return outs, [row_spec(tok.shape)] * 3 + [out_const(o.shape) for o in outs[3:]]
+
+
+def back_scratch(n, seq, width, d):
     heads = width // 64
-    tok = sds((n, seq, width), BF)
-    flat = [
-        sds((d // 2, 4 * width), BF),
-        sds((d // 2, 4 * width), BF),
-        sds((8, TILE), F32),
+    return [
+        pltpu.VMEM((seq, width), BF),
+        pltpu.VMEM((width, seq), BF),
+        pltpu.VMEM((3 * heads, TILE, TILE), F32),
+        pltpu.VMEM((2 * heads, 8, TILE), F32),
+        pltpu.VMEM((2, seq, 2 * seq), BF),
+        pltpu.VMEM((2, seq, 2 * seq), BF),
+        pltpu.VMEM((n * seq, 3 * width), BF),
+        pltpu.VMEM((n * seq, d), BF),
+        pltpu.VMEM((d, width), BF),
     ]
-    ins = [q, qt, k, v, dctx, dctxt, ctxt, lse]
+
+
+def attn_bwd_kernel(lens, at_ref, da_blk, wo_ref, hot_ref, lse_ref, tf_ref, *refs):
+    hbm, outs, scratch = refs[:7], refs[7:13], refs[13:22]
+    bufs, sem = refs[22:29], refs[29]
+    b = pl.program_id(0)
+    n = da_blk.shape[0] * lse_ref.shape[0]
+    copies = [pltpu.make_async_copy(x, y, sem.at[i]) for i, (x, y) in enumerate(zip(hbm, bufs))]
+
+    @pl.when(b == 0)
+    def _():
+        for c in copies:
+            c.start()
+        for c in copies[:-1]:
+            c.wait()
+
+    q, qt, k, v, ct, nb, ant = bufs
+    ins = (q, qt, k, v, ct, lse_ref, nb, tf_ref, ant, hot_ref)
+    attn_back(b, n, lens[b], at_ref[0] // 2, wo_ref[...], da_blk[0], ins, outs, scratch, copies[-1:])
+
+
+def attn_bwd(lens, at, d_attn, wo, hot, lse, tf, *arrays):
+    n, seq, d = d_attn.shape
+    width = wo.shape[0]
+    outs, specs = back_outs(n, seq, width, d)
     return pl.pallas_call(
         attn_bwd_kernel,
         grid=(n,),
-        in_specs=[SMEM_SPEC, SMEM_SPEC]
-        + [row_spec(x.shape) for x in ins]
-        + [const_spec(nb.shape), const_spec(tf.shape), const_spec(hot.shape), ANY, ANY],
-        out_specs=[row_spec(q.shape)] * 3 + [out_const(o.shape) for o in flat],
-        out_shape=[tok, tok, tok] + flat,
-        scratch_shapes=[
-            pltpu.VMEM((3 * heads, TILE, TILE), F32),
-            pltpu.VMEM((2 * heads, 8, TILE), F32),
-            pltpu.VMEM((2, seq, 2 * seq), BF),
-            pltpu.VMEM((2, seq, 2 * seq), BF),
-            pltpu.VMEM((n * seq, 3 * width), BF),
-            pltpu.VMEM(ant.shape, BF),
-            pltpu.VMEM(go.shape, F32),
-            pltpu.SemaphoreType.DMA((2,)),
-        ],
+        in_specs=[SMEM_SPEC, SMEM_SPEC, row_spec(d_attn.shape)]
+        + [const_spec(x.shape) for x in (wo, hot, lse, tf)]
+        + [ANY] * 7,
+        out_specs=specs,
+        out_shape=outs,
+        scratch_shapes=back_scratch(n, seq, width, d)
+        + [pltpu.VMEM(x.shape, x.dtype) for x in arrays]
+        + [pltpu.SemaphoreType.DMA((7,))],
         compiler_params=params(),
-        cost_estimate=cost(20),
+        cost_estimate=cost(16),
         name="attn_bwd",
-    )(lens, at, *ins, nb, tf, hot, ant, go)
+    )(lens, at, d_attn, wo, hot, lse, tf, *arrays)
 
 
 def gelu_parts(v):
     v2 = v * v
-    th = jnp.tanh(v * (GELU_A + (GELU_A * GELU_B) * v2))
-    hh = 0.5 + 0.5 * th
-    slope = hh + (v * (0.5 - 0.5 * th * th)) * (GELU_A + (3.0 * GELU_A * GELU_B) * v2)
-    return v * hh, slope
+    half = 0.5 + 0.5 * jnp.tanh(v * (GELU_A + (GELU_A * GELU_B) * v2))
+    act = v * half
+    return act, half + (act - act * half) * (2.0 * GELU_A + (6.0 * GELU_A * GELU_B) * v2)
 
 
 def ffn_fwd_kernel(lens, at_ref, fin_ref, rs_ref, wi_ref, wu_ref, p0, p1, p2, p3, *refs):
@@ -571,7 +640,6 @@
     chunk = v_ref.shape[2]
     length = lens[b]
     vrow = (lax.broadcasted_iota(jnp.int32, (8, seq), 1) < length).astype(F32).astype(BF)
-    vcol = (lax.broadcasted_iota(jnp.int32, (seq, TILE), 0) < length).astype(F32)[:, :1]
     spot = lambda c: slice(c * chunk, (c + 1) * chunk)
     parts = [(w, a, g, c) for w, a, g in ((wi_ref, act_ref, gp_ref), (wib_ref, actb_ref, gpb_ref)) for c in range(half // chunk)]
 
@@ -594,7 +662,7 @@
             rows = slice(TILE * r, TILE * (r + 1))
             act, slope = gelu_parts(v_ref[t % 2, rows, :])
             a_ref[0, rows, spot(c)] = act.astype(BF)
-            g_ref[0, rows, spot(c)] = (slope * vcol[rows]).astype(BF)
+            g_ref[0, rows, spot(c)] = slope.astype(BF)
         asum_ref[0, :, spot(t)] = mm(vrow, a_ref[0, :, spot(c)])[:1]
     own = asum_ref[0, :, :half]
     hi = own.astype(BF)
@@ -628,8 +696,8 @@
     )(lens, at, fin, rsum, wi, wu, *packs)
 
 
-def pool_kernel(lens, at_ref, asum_ref, rs_ref, p0, p1, out_ref, wb_ref, sem):
-    run_copies(join_copies(at_ref[0], (p0, p1), wb_ref, sem))
+def pool_kernel(lens, at_ref, asum_ref, rs_ref, p0, p1, p2, p3, out_ref, wb_ref, sem):
+    run_copies(join_copies(at_ref[0], (p0, p1, p2, p3), wb_ref, sem))
     n = asum_ref.shape[0]
     half = wb_ref.shape[0]
     rows = [asum_ref[i, :, half:] for i in range(n)]
@@ -648,7 +716,7 @@
     vm = pl.BlockSpec(memory_space=pltpu.VMEM)
     return pl.pallas_call(
         pool_kernel,
-        in_specs=[SMEM_SPEC, SMEM_SPEC, vm, vm] + [ANY] * 2,
+        in_specs=[SMEM_SPEC, SMEM_SPEC, vm, vm] + [ANY] * 4,
         out_specs=vm,
         out_shape=sds((8, d), F32),
         scratch_shapes=[pltpu.VMEM((half, d), BF), pltpu.SemaphoreType.DMA((4,))],
@@ -658,11 +726,12 @@
     )(lens, at, asum, rsum, *packs)
 
 
-def loss_kernel(me_ref, at_ref, lens, pool_ref, q_ref, wp_ref, fint_hbm, gp_hbm, fn0, fn1, wi_hbm, wu_hbm, p0, p1, *refs):
+def loss_kernel(me_ref, at_ref, lens, pool_ref, q_ref, wp_ref, fint_hbm, gp_hbm, fn0, fn1, wi_hbm, wu_hbm, p0, p1, p2, p3, *refs):
     (loss_ref, row_ref, g_ref, drow_ref, demb_ref, send_ref, keep_ref) = refs[:7]
-    (wu_ref, wb_ref, fint_ref, gp_ref, fnb_ref, wi_ref, ft_ref, gn_ref, v_ref, d_ref, dn_ref, sem, sem2) = refs[7:]
-    copies = join_copies(at_ref[0], (p0, p1), wb_ref, sem)
-    moves = [(wu_hbm, wu_ref), (wi_hbm, wi_ref), (gp_hbm, gp_ref), (fint_hbm, fint_ref)]
+    (wu_ref, wb_ref, gp_ref, fnb_ref, wi_ref, ft_ref, gn_ref, v_ref, d_ref, sum_ref, sem, sem2) = refs[7:]
+    copies = join_copies(at_ref[0], (p0, p1, p2, p3), wb_ref, sem)
+    moves = [(wu_hbm, wu_ref), (wi_hbm, wi_ref), (gp_hbm, gp_ref)]
+    moves.append((fint_hbm, ft_ref.at[:, pl.ds(0, fint_hbm.shape[1])]))
     moves += [(f, fnb_ref.at[pl.ds(i, 1)]) for i, f in enumerate((fn0, fn1))]
     loads = [pltpu.make_async_copy(a, b, sem2.at[i]) for i, (a, b) in enumerate(moves)]
     for c in [loads[0]] + copies + loads[1:]:
@@ -710,8 +779,11 @@
     for c in loads[1:]:
         c.wait()
 
+    tokens = n * seq
     for i in range(n):
-        ft_ref[:, seq * i : seq * (i + 1)] = jnp.transpose(fnb_ref[i])
+        valid = lax.broadcasted_iota(jnp.int32, (seq, TILE), 0) < lens[n + i]
+        fin = (fnb_ref[i].astype(F32) * valid.astype(F32)[:, :1]).astype(BF)
+        ft_ref[:, tokens + seq * i : tokens + seq * (i + 1)] = jnp.transpose(fin)
     chunk = v_ref.shape[3]
     steps = half // chunk
     spot = lambda c: slice(c * chunk, (c + 1) * chunk)
@@ -726,10 +798,10 @@
             d_ref[c % 2, at, :] = (gp_ref[i, :, spot(c)].astype(F32) * gn_ref[i : i + 1, spot(c)]).astype(BF)
             for r in range(seq // TILE):
                 part = slice(TILE * r, TILE * (r + 1))
-                valid = lax.broadcasted_iota(jnp.int32, (TILE, TILE), 0) + TILE * r < lens[n + i]
                 slope = gelu_parts(v_ref[c % 2, i, part, :])[1]
-                one = slope * valid.astype(F32)[:, :1] * gn_ref[n + i : n + i + 1, spot(c)]
-                dn_ref[c % 2, seq * i + TILE * r : seq * i + TILE * (r + 1), :] = one.astype(BF)
+                one = slope * gn_ref[n + i : n + i + 1, spot(c)]
+                base = tokens + seq * i + TILE * r
+                d_ref[c % 2, base : base + TILE, :] = one.astype(BF)
 
     rows2 = d // 2
     core = at_ref[0] // 2
@@ -738,10 +810,9 @@
     for c in range(steps):
         if c + 1 < steps:
             project(c + 1)
+        sum_ref[...] = mm(ft_ref[...], d_ref[c % 2]).astype(BF)
         for ref, side in ((send_ref, 1 - core), (keep_ref, core)):
-            at = pl.ds(pl.multiple_of(side * rows2, rows2), rows2)
-            one = mm(fint_ref[at, :], d_ref[c % 2]) + mm(ft_ref[at, :], dn_ref[c % 2])
-            ref[:, spot(c)] = one.astype(BF)
+            ref[:, spot(c)] = sum_ref[pl.ds(pl.multiple_of(side * rows2, rows2), rows2), :]
         if c + 1 < steps:
             scale(c + 1)
 
@@ -754,7 +825,7 @@
     vm = pl.BlockSpec(memory_space=pltpu.VMEM)
     return pl.pallas_call(
         loss_kernel,
-        in_specs=[SMEM_SPEC] * 3 + [vm] * 3 + [ANY] * 8,
+        in_specs=[SMEM_SPEC] * 3 + [vm] * 3 + [ANY] * 10,
         out_specs=[vm] * 7,
         out_shape=[
             sds((8, TILE), F32),
@@ -768,15 +839,14 @@
         scratch_shapes=[
             pltpu.VMEM(wu.shape, BF),
             pltpu.VMEM(wu.shape, BF),
-            pltpu.VMEM(fint.shape, BF),
             pltpu.VMEM(gp.shape, BF),
             pltpu.VMEM((n, seq, d), BF),
             pltpu.VMEM(wi.shape, BF),
-            pltpu.VMEM(fint.shape, BF),
+            pltpu.VMEM((d, 2 * n * seq), BF),
             pltpu.VMEM((8, half), F32),
             pltpu.VMEM((2, n, seq, chunk), F32),
-            pltpu.VMEM((2, n * seq, chunk), BF),
-            pltpu.VMEM((2, n * seq, chunk), BF),
+            pltpu.VMEM((2, 2 * n * seq, chunk), BF),
+            pltpu.VMEM((d, chunk), BF),
             pltpu.SemaphoreType.DMA((4,)),
             pltpu.SemaphoreType.DMA((6,)),
         ],
@@ -786,99 +856,96 @@
     )(me, at, lens4, pooled, queries, wp, fint, gp, *fin_nb, wi, wu, *packs)
 
 
-def ffn_bwd_kernel(lens, at_ref, res_ref, gpa_ref, gpb_ref, g_ref, row_ref, gain_ref, wi_ref, wo_ref, cta_ref, ctb_ref, *refs):
-    packs0, packs1 = refs[:2], refs[2:6]
-    (dres_ref, dca_ref, dta_ref, dcb_ref, dtb_ref, goa_ref, gob_ref) = refs[6:13]
-    (wib_ref, wob_ref, cta_buf, ctb_buf, d_ref, da_ref, sem0, sem1, sem2) = refs[13:]
+def mid_bwd_kernel(lens, at_ref, g_ref, row_ref, gain_ref, hot_ref, lse_ref, tf_ref, *refs):
+    hbm, packs0, packs1 = refs[:11], refs[11:15], refs[15:19]
+    (dres_ref, dattn_ref), outs, scratch = refs[19:21], refs[21:27], refs[27:36]
+    bufs, (wib_ref, wob_ref, d_ref, sem, sem0, sem1) = refs[36:47], refs[47:]
+    wi_ref, gpa_ref, gpb_ref, res_all, q, qt, k, v, ct, nb, ant = bufs
     b = pl.program_id(0)
-    n = pl.num_programs(0)
-    res = res_ref[0]
-    seq, d = res.shape
+    n = lse_ref.shape[0]
+    copies = [pltpu.make_async_copy(x, y, sem.at[i]) for i, (x, y) in enumerate(zip(hbm, bufs))]
+    copies0 = out_copies(at_ref[0], packs0, wob_ref, sem0)
+    copies1 = join_copies(at_ref[0], packs1, wib_ref, sem1)
+
+    def first(group):
+        @pl.when(b == 0)
+        def _():
+            for c in group:
+                c.wait()
+
+    @pl.when(b == 0)
+    def _():
+        for c in copies[:2] + copies1 + copies[2:4] + copies0 + copies[4:]:
+            c.start()
+
+    first(copies[:2])
+    _, seq, d = res_all.shape
     half = wi_ref.shape[1]
     chunk = d_ref.shape[2]
-    copies0 = join_copies(at_ref[0], packs0, wob_ref, sem0)
-    copies1 = join_copies(at_ref[0], packs1, wib_ref, sem1)
-    late = [pltpu.make_async_copy(cta_ref, cta_buf, sem2.at[0]), pltpu.make_async_copy(ctb_ref, ctb_buf, sem2.at[1])]
-
-    @pl.when(b == 0)
-    def _():
-        for c in copies1 + copies0 + late:
-            c.start()
-        for c in copies1 + copies0:
-            c.wait()
-
-    parts = [(gp, w, c) for gp, w in ((gpa_ref, wi_ref), (gpb_ref, wib_ref)) for c in range(half // chunk)]
+    steps = half // chunk
+    parts = [(gp, w, c) for gp, w in ((gpa_ref, wi_ref), (gpb_ref, wib_ref)) for c in range(steps)]
 
     def scale(t):
         gp, _, c = parts[t]
-        base = half if gp is gpb_ref else 0
-        g = g_ref[pl.ds(b, 1), base + c * chunk : base + (c + 1) * chunk]
-        d_ref[t % 2] = (gp[0, :, c * chunk : (c + 1) * chunk].astype(F32) * g).astype(BF)
+        g = g_ref[pl.ds(b, 1), t * chunk : (t + 1) * chunk]
+        d_ref[t % 2] = (gp[b, :, c * chunk : (c + 1) * chunk].astype(F32) * g).astype(BF)
 
     d_two = None
     scale(0)
     for t, (_, w, c) in enumerate(parts):
+        if t + 1 == steps:
+            first(copies[2:4] + copies1)
         if t + 1 < len(parts):
             scale(t + 1)
         one = mm(d_ref[t % 2], w[:, c * chunk : (c + 1) * chunk], NT)
         d_two = one if d_two is None else d_two + one
+    res = res_all[b]
     inv = lax.rsqrt(jnp.mean(res * res, axis=-1, keepdims=True) + EPS)
-    dr = d_two * res
-    gain = gain_ref[...]
-    along = jnp.sum(dr * gain, axis=-1, keepdims=True)
+    scaled = d_two * gain_ref[...]
+    along = jnp.sum(scaled * res, axis=-1, keepdims=True)
     valid = lax.broadcasted_iota(jnp.int32, (seq, TILE), 0) < lens[b]
     vcol = valid.astype(F32)[:, :1]
-    d_res = vcol * row_ref[pl.ds(b, 1), :] + d_two * gain * inv - res * (inv * inv * inv * along / d)
+    inv = inv * vcol
+    d_res = vcol * row_ref[pl.ds(b, 1), :] + scaled * inv - res * (inv * inv * inv * along / d)
     dres_ref[0] = d_res
     d_attn = d_res.astype(BF)
-    da_ref[pl.ds(pl.multiple_of(b * seq, seq), seq), :] = d_attn
-    for w, o_ref, t_ref in ((wo_ref, dca_ref, dta_ref), (wob_ref, dcb_ref, dtb_ref)):
-        turned = mm(w[...], d_attn, NT).astype(BF)
-        t_ref[0] = turned
-        o_ref[0] = jnp.transpose(turned)
-
-    @pl.when(b == n - 1)
-    def _():
-        for c in late:
-            c.wait()
-        rows = cta_buf.shape[1]
-        for ct_ref, o_ref in ((cta_buf, goa_ref), (ctb_buf, gob_ref)):
-            total = None
-            for i in range(cta_buf.shape[0]):
-                one = mm(ct_ref[i], da_ref[seq * i : seq * (i + 1), :])
-                total = one if total is None else total + one
-            o_ref[:rows, :] = total[:, :rows]
-            o_ref[rows:, :] = total[:, rows:]
-
-
-def ffn_bwd(lens, at, res, gpa, gpb, g, row, gain, wi, wo, cta, ctb, packs0, packs1):
+    dattn_ref[0] = d_attn
+    first(copies0 + copies[4:-1])
+    ins = (q, qt, k, v, ct, lse_ref, nb, tf_ref, ant, hot_ref)
+    attn_back(b, n, lens[b], at_ref[0] // 2, wob_ref[...], d_attn, ins, outs, scratch, copies[-1:])
+
+
+def mid_bwd(lens, at, g, row, gain, hot, lse, tf, arrays, packs0, packs1):
+    wi, _, _, res = arrays[:4]
     n, seq, d = res.shape
-    width = wo.shape[0]
-    outs = [sds((n, seq, d), F32)] + [sds((n, seq, width), BF), sds((n, width, seq), BF)] * 2
-    flat = [sds((d, width), F32), sds((d, width), F32)]
+    half = wi.shape[1]
+    width = packs0[0].shape[1] // 3
+    outs, specs = back_outs(n, seq, width, d)
+    more = [sds((n, seq, d), F32), sds((n, seq, d), BF)]
     return pl.pallas_call(
-        ffn_bwd_kernel,
+        mid_bwd_kernel,
         grid=(n,),
-        in_specs=[SMEM_SPEC, SMEM_SPEC, row_spec(res.shape), row_spec(gpa.shape), row_spec(gpb.shape)]
-        + [const_spec(g.shape), const_spec(row.shape), const_spec((1, d)), const_spec(wi.shape), const_spec(wo.shape)]
-        + [ANY] * 8,
-        out_specs=[row_spec(o.shape) for o in outs] + [out_const(o.shape) for o in flat],
-        out_shape=outs + flat,
-        scratch_shapes=[
-            pltpu.VMEM(wi.shape, BF),
-            pltpu.VMEM(wo.shape, BF),
-            pltpu.VMEM(cta.shape, BF),
-            pltpu.VMEM(ctb.shape, BF),
+        in_specs=[SMEM_SPEC, SMEM_SPEC]
+        + [const_spec(x.shape) for x in (g, row)]
+        + [const_spec((1, d))]
+        + [const_spec(x.shape) for x in (hot, lse, tf)]
+        + [ANY] * 19,
+        out_specs=[row_spec(o.shape) for o in more] + specs,
+        out_shape=more + outs,
+        scratch_shapes=back_scratch(n, seq, width, d)
+        + [pltpu.VMEM(x.shape, x.dtype) for x in arrays]
+        + [
+            pltpu.VMEM((d, half), BF),
+            pltpu.VMEM((width, d), BF),
             pltpu.VMEM((2, seq, 512), BF),
-            pltpu.VMEM((n * seq, d), BF),
+            pltpu.SemaphoreType.DMA((11,)),
+            pltpu.SemaphoreType.DMA((12,)),
             pltpu.SemaphoreType.DMA((4,)),
-            pltpu.SemaphoreType.DMA((4,)),
-            pltpu.SemaphoreType.DMA((2,)),
         ],
         compiler_params=params(),
-        cost_estimate=cost(15),
-        name="ffn_bwd",
-    )(lens, at, res, gpa, gpb, g, row, gain.reshape(1, d), wi, wo, cta, ctb, *packs0, *packs1)
+        cost_estimate=cost(32),
+        name="mid_bwd",
+    )(lens, at, g, row, gain.reshape(1, d), hot, lse, tf, *arrays, *packs0, *packs1)
 
 
 def input_kernel(at_ref, x_ref, dres_ref, gain_ref, qa, ka, va, qb, kb, vb, wq, wk, wv, p0, p1, p2, p3, out_ref, w_ref, sem):
@@ -917,10 +984,10 @@
     )(at, x, dres, gain.reshape(1, d), *toks, wq, wk, wv, *packs)
 
 
-def layer_kernel(at_ref, res_ref, aa_ref, ab_ref, w_ref, p0, p1, out_ref, wb_ref, sem):
+def layer_kernel(at_ref, res_ref, aa_ref, ab_ref, w_ref, p0, p1, p2, p3, out_ref, wb_ref, sem):
     @pl.when(pl.program_id(0) == 0)
     def _():
-        run_copies(join_copies(at_ref[0], (p0, p1), wb_ref, sem))
+        run_copies(join_copies(at_ref[0], (p0, p1, p2, p3), wb_ref, sem))
 
     out_ref[0] = (res_ref[0] + mm(aa_ref[0], w_ref[...]) + mm(ab_ref[0], wb_ref[...])).astype(BF)
 
@@ -931,7 +998,7 @@
         layer_kernel,
         grid=(n,),
         in_specs=[SMEM_SPEC, row_spec(res.shape), row_spec(act_a.shape), row_spec(act_b.shape), const_spec(wu.shape)]
-        + [ANY] * 2,
+        + [ANY] * 4,
         out_specs=row_spec(res.shape),
         out_shape=sds(res.shape, BF),
         scratch_shapes=[pltpu.VMEM(wu.shape, BF), pltpu.SemaphoreType.DMA((4,))],
@@ -973,38 +1040,39 @@
     )(at, own, near, w)
 
 
-def attn_done_kernel(at_ref, own_ref, near_ref, wq, wk, wv, q_ref, k_ref, v_ref, o_ref, gain_ref):
-    rows = own_ref.shape[0]
+def attn_done_kernel(half_ref, sum_ref, wq, wk, wv, *refs):
+    q_ref, k_ref, v_ref, o_ref, gain_ref = refs[-5:]
     width = wq.shape[1]
-    core = at_ref[0] // 2
-    for half in range(2):
-        at = slice(rows * half, rows * (half + 1))
-        total = None
-        for i, (w, out) in enumerate(((wq, q_ref), (wk, k_ref), (wv, v_ref), (None, o_ref))):
-            cols = slice(width * i, width * (i + 1))
-            one = jnp.where(core == half, own_ref[:, cols].astype(F32), near_ref[:, cols].astype(F32))
-            if w is None:
-                out[:, at] = one
-            else:
-                out[at, :] = one
-                prod = one * w[at, :].astype(F32)
-                total = prod if total is None else total + prod
-        gain_ref[:, at] = jnp.broadcast_to(gain_row(total), (8, rows))
-
-
-def attn_done(at, own, near, wq, wk, wv):
+    total = None
+    for i, (w, out) in enumerate(((wq, q_ref), (wk, k_ref), (wv, v_ref))):
+        one = sum_ref[:, width * i : width * (i + 1)].astype(F32)
+        out[...] = one
+        prod = one * w[...].astype(F32)
+        total = prod if total is None else total + prod
+    o_ref[...] = sum_ref[:, 3 * width :].astype(F32)
+    gain_ref[...] = jnp.broadcast_to(gain_row(total), gain_ref.shape)
+
+
+def attn_done(half, sums, wq, wk, wv, into=()):
     d, width = wq.shape
-    vm = pl.BlockSpec(memory_space=pltpu.VMEM)
+    rows = d // 2
     grad = sds((d, width), F32)
+    block = pl.BlockSpec((rows, width), lambda b, half: (half[0], 0))
+    across = pl.BlockSpec((width, rows), lambda b, half: (0, half[0]))
     return pl.pallas_call(
         attn_done_kernel,
-        in_specs=[SMEM_SPEC] + [vm] * 5,
-        out_specs=[vm] * 5,
-        out_shape=[grad, grad, grad, sds((width, d), F32), sds((8, d), F32)],
+        grid_spec=pltpu.PrefetchScalarGridSpec(
+            num_scalar_prefetch=1,
+            grid=(1,),
+            in_specs=[pl.BlockSpec(sums.shape, lambda b, half: (0, 0))] + [block] * 3 + [ANY] * len(into),
+            out_specs=[block] * 3 + [across, pl.BlockSpec((8, rows), lambda b, half: (0, 0))],
+        ),
+        out_shape=[grad, grad, grad, sds((width, d), F32), sds((8, rows), F32)],
+        input_output_aliases={5 + i: i for i in range(len(into))},
         compiler_params=params(),
-        cost_estimate=cost(5),
+        cost_estimate=cost(3),
         name="attn_done",
-    )(at, own, near, wq, wk, wv)
+    )(half, sums, wq, wk, wv, *into)
 
 
 def after(*xs):
@@ -1049,7 +1117,6 @@
         return got.reshape(-1, x.shape[1])
 
     def total(self, x):
-        x = x + self.core_swap(x)
         for i in range(self.chips.bit_length() - 1):
             x = x + swap(x, "chip", 1 << i, self.chips)
         return x
@@ -1087,7 +1154,7 @@
 
     turned = rel_table.T
     packs = pack_weights(at, turned, w_query, w_key, w_value, w_out, w_inner, w_outer)
-    y_attn, y_out, y_inner, y_outer = [pc.across(p) for p in packs]
+    y_attn = pc.across(packs[0])
 
     qf = queries.astype(F32)
     q_unit = (qf * lax.rsqrt(jnp.sum(qf * qf, axis=-1, keepdims=True) + EPS)).astype(BF)
@@ -1098,23 +1165,24 @@
     an, ant, q_a, qt_a, k_a, v_a, ctx_a, ctxt_a, lse_a, nb_a, tf_a = attn_own(
         lens, hidden_in, gain_attn, w_query, w_key, w_value, turned, hot_t
     )
-    y_attn, an, q_all = after(y_attn, an, q_all)
+    y_attn, an, q_all, *packs = after(y_attn, an, q_all, *packs[1:])
+    y_inner, y_outer = [pc.across(p) for p in packs]
     x_attn = pc.side(y_attn)
     q_all = pc.share(jnp.broadcast_to(q_all[None], (devices,) + q_all.shape))
-    x_attn, y_out, q_all = after(x_attn, y_out, q_all)
+    x_attn, q_all = after(x_attn, q_all)
     p_attn = pc.spread(y_attn, x_attn)
-    p_out = [y_out, pc.core_swap(y_out)]
     y_inner, an = after(y_inner, an)
     x_inner = pc.side(y_inner)
-    q_b, qt_b, k_b, v_b, ctx_b, ctxt_b, lse_b, nb_b, tf_b, res, fin, fint, rsum = attn_other(
-        lens, at, an, hot_t, hidden_in, ctx_a, w_out, gain_ffn, p_attn, p_out
+    q_b, qt_b, k_b, v_b, ctxt_b, lse_b, nb_b, tf_b, res, fin, fint, rsum, *fins = attn_other(
+        lens, at, an, hot_t, hidden_in, ctx_a, w_out, gain_ffn, p_attn
     )
-    y_inner, x_inner, fin = after(y_inner, x_inner, fin)
+    y_inner, x_inner, y_outer, fin, *fins = after(y_inner, x_inner, y_outer, fin, *fins)
+    x_outer = pc.side(y_outer)
     p_inner = pc.spread(y_inner, x_inner)
-    fin_nb = [pc.across(fin[i : i + 1]) for i in range(n)]
+    fin_nb = [pc.across(f) for f in fins]
     act_a, gp_a, act_b, gp_b, asum, rsum = ffn_fwd(lens, at, fin, rsum, w_inner, w_outer, p_inner)
-    y_outer, asum, fin_nb[0] = after(y_outer, asum, fin_nb[0])
-    p_outer = [y_outer, pc.core_swap(y_outer)]
+    y_outer, x_outer, asum, fin_nb[0] = after(y_outer, x_outer, asum, fin_nb[0])
+    p_outer = pc.spread(y_outer, x_outer)
     pooled = pool(lens, at, asum, rsum, p_outer)[:n].astype(BF)
 
     sums_a, sums_b = asum[:, 0, :half].astype(BF), asum[:, 0, half:].astype(BF)
@@ -1132,41 +1200,47 @@
 
     inner_half, gp_a = after(gi_keep + pc.core_swap(gi_send), gp_a)
     inner_parts = pc.exchange(inner_half)
-    d_res, dctx_a, dctxt_a, dctx_b, dctxt_b, go_a, go_b = ffn_bwd(
-        lens, at, res, gp_a, gp_b, g8, row8, gain_ffn, w_inner, w_out, ctxt_a, ctxt_b, p_out, p_inner
+    arrays = [w_inner, gp_a, gp_b, res, q_b, qt_b, k_b, v_b, ctxt_b, nb_b, ant]
+    d_res, d_attn, dq_b, dk_b, dv_b, send_b, keep_b, table_b = mid_bwd(
+        lens, at, g8, row8, gain_ffn, hot_back, lse_b, tf_b, arrays, p_attn, p_inner
     )
-    dq_b, dk_b, dv_b, send_b, keep_b, table_b = attn_bwd(
-        lens, at, q_b, qt_b, k_b, v_b, dctx_b, dctxt_b, ctxt_b, lse_b, nb_b, tf_b, hot_back, ant, go_b
+    half_b, d_attn = after(keep_b + pc.core_swap(send_b), d_attn)
+    far_part = pc.across(half_b)
+    inner_part, d_attn = after(pc.add(inner_parts), d_attn)
+    dq_a, dk_a, dv_a, send_a, keep_a, table_a = attn_bwd(
+        lens, at, d_attn, w_out, hot_back, lse_a, tf_a, q_a, qt_a, k_a, v_a, ctxt_a, nb_a, ant
     )
-    half_b, dctx_a = after(keep_b + pc.core_swap(send_b), dctx_a)
-    far_part = pc.across(half_b)
-    inner_part, dctx_a = after(pc.add(inner_parts), dctx_a)
-    dq_a, dk_a, dv_a, send_a, keep_a, table_a = attn_bwd(
-        lens, at, q_a, qt_a, k_a, v_a, dctx_a, dctxt_a, ctxt_a, lse_a, nb_a, tf_a, hot_back, ant, go_a
+    proj_grad = mm(pooled, d_emb, TN)
+    outer_grad = mm(got[:, d:], d_rows, TN)
+    inner_all, far_part, far_table, send_a, proj_grad, outer_grad = after(
+        pc.gather(inner_part), far_part, pc.across(table_b), send_a, proj_grad, outer_grad
     )
-    inner_all, far_part, send_a = after(pc.gather(inner_part), far_part, send_a)
-    parts = pc.exchange(keep_a + far_part + pc.core_swap(send_a))
+    table = table_a + far_table
+    near_a, near_table = after(pc.core_swap(send_a), pc.core_swap(table))
+    parts = pc.exchange(keep_a + far_part + near_a)
     toks = (dq_a, dk_a, dv_a, dq_b, dk_b, dv_b)
     input_grad = input_part(at, hidden_in, d_res, gain_attn, toks, w_query, w_key, w_value, p_attn)
 
-    table_sum = pc.total(table_a + pc.across(table_b))
-
+    inner_sum, gain_ffn_part = inner_done(at, inner_all, pc.core_swap(inner_all), w_inner)
     layer = layer_part(at, res, act_a, act_b, w_outer, p_outer)
-    parts, input_grad, layer, inner_all = after(parts, input_grad, layer, inner_all)
+    parts, input_grad, layer = after(parts, input_grad, layer)
     attn_all = pc.gather(pc.add(parts))
-    inner_sum, gain_ffn_part = inner_done(at, inner_all, pc.core_swap(inner_all), w_inner)
+    table_sum = pc.total(table + near_table)
     gain_ffn_part = jnp.sum(gain_ffn_part[::8], axis=0)
     gain_ffn_grad = (gain_ffn_part + pc.across(gain_ffn_part)) / gain_ffn
-    proj_grad = mm(pooled, d_emb, TN)
-    outer_grad = mm(got[:, d:], d_rows, TN)
-    attn_all, proj_grad, outer_grad, gain_ffn_grad, inner_sum, table_sum = after(
-        attn_all, proj_grad, outer_grad, gain_ffn_grad, inner_sum, table_sum
-    )
-    q_grad, k_grad, v_grad, out_grad, gain_attn_part = attn_done(
-        at, attn_all, pc.core_swap(attn_all), w_query, w_key, w_value
-    )
-    gain_attn_part = gain_attn_part[0]
-    gain_attn_grad = (gain_attn_part + pc.across(gain_attn_part)) / gain_attn
+    attn_all, gain_ffn_grad, table_sum, inner_sum = after(attn_all, gain_ffn_grad, table_sum, inner_sum)
+    half = pc.core.reshape(1)
+    near = pc.core_swap(attn_all)
+    *grads, gain_own = attn_done(half, attn_all, w_query, w_key, w_value)
+    near, *grads = after(near, *grads)
+    gain_own = gain_own[0] + pc.across(gain_own[0])
+    *grads, _ = attn_done(1 - half, near, w_query, w_key, w_value, grads)
+    gain_own, *grads = after(gain_own, *grads)
+    q_grad, k_grad, v_grad, out_grad = grads
+    gain_near = pc.core_swap(gain_own)
+    gain_attn_grad = jnp.where(
+        pc.core > 0, jnp.concatenate([gain_near, gain_own]), jnp.concatenate([gain_own, gain_near])
+    ) / gain_attn
     return (
         layer,
         query_loss,

time: 315 us -> 303 us (0.962)
  waiting for transfers between devices: 60.7 us -> 49.5 us
    ppermute x27 -> x28, waiting for transfers between devices: 44.8 us -> 25.4 us  [swap(): return lax.ppermute(x, axis, [(i, i ^ bit) for i in range(size)])]
    pallas_call x2 -> x3, Pallas kernels: 24.9 us -> 38.4 us  [the longest x1 32.2 us: mid_bwd(): pl.pallas_call(mid_bwd_kernel, grid=(n,), in_specs=[SMEM_SPEC, SMEM_SPEC]...]
    pallas_call x2 -> x1, Pallas kernels: 32.5 us -> 19.1 us  [attn_bwd(): pl.pallas_call(attn_bwd_kernel, grid=(n,), in_specs=[SMEM_SPEC, SMEM_SPEC...]
    all_to_all x2, waiting for transfers between devices: 9.84 us -> 18.3 us  [share(): return lax.all_to_all(x, ('chip', 'core', 'tensor'), 0, 0, tiled=True)]
    ppermute x27 -> x28, starting transfers between devices: 27.7 us -> 27.8 us  [swap(): return lax.ppermute(x, axis, [(i, i ^ bit) for i in range(size)])]
  transfers between devices with their start and end apart: 33 -> 34, of which waited for: 19 -> 18; matrix products, arithmetic and copies ran while one was open for 6% -> 6% of each run, Pallas kernels for 43% -> 45%
where the time goes in v1:
time: 303 us; the launch traced here: 297 us
  Pallas kernels  158 us (52%)
  starting transfers between devices  56.2 us (19%)
  waiting for transfers between devices  49.5 us (16%)
  local copies, waits for them, and re-layouts  16.6 us (5%)
  other arithmetic  11.1 us (4%)
  matrix products  4.9 us (2%)
    pallas_call x1, Pallas kernels, mid_bwd(): pl.pallas_call(mid_bwd_kernel, grid=(n,), in_specs=[SMEM_SPEC, SMEM_SPEC]...  32.2 us
    ppermute x28, starting transfers between devices, swap(): return lax.ppermute(x, axis, [(i, i ^ bit) for i in range(size)])  27.8 us
    ppermute x28, waiting for transfers between devices, swap(): return lax.ppermute(x, axis, [(i, i ^ bit) for i in range(size)])  25.4 us
    pallas_call x1, Pallas kernels, attn_other(): pl.pallas_call(attn_other_kernel, grid=(n,), in_specs=[SMEM_SPEC, SMEM_SP...  19.5 us
    pallas_call x1, Pallas kernels, attn_bwd(): pl.pallas_call(attn_bwd_kernel, grid=(n,), in_specs=[SMEM_SPEC, SMEM_SPEC...  19.1 us
    all_to_all x2, waiting for transfers between devices, share(): return lax.all_to_all(x, ('chip', 'core', 'tensor'), 0, 0, tiled=True)  18.3 us
    pallas_call x1, Pallas kernels, loss_all(): pl.pallas_call(loss_kernel, in_specs=[SMEM_SPEC] * 3 + [vm] * 3 + [ANY] *...  16.6 us
    pallas_call x1, Pallas kernels, ffn_fwd(): pl.pallas_call(ffn_fwd_kernel, grid=(n,), in_specs=[SMEM_SPEC, SMEM_SPEC,...  15 us
  transfers between devices with their start and end apart: 34, of which 18 were waited for; matrix products, arithmetic and copies ran while one was open for 6% of the time, Pallas kernels for 45%

profile of v1, /device:TPU:0, one launch (start us, length us, event | category | flops | bytes accessed | tf_op | source)
XLA Modules:
  0.0 297.4 jit_solution(3771085180903572706)
XLA Ops:
  0.7 3.5 %pack_weights.1 = (bf16[272,1152]{1,0:T(8,128)(2,1)}, bf16[192,1536]{1,0:T(8,128)(2,1)}, bf16[384,768]{1,0:T(8,128)(2,1)}) custom-call(s32[1]{0:T(128)} %bitcast.at_ref, f32[6,32]{1,0:T(8,128)} %bitcast.36, bf16[768,384]{1,0:T(8,128)(2,1)} %wq.9, bf16[768,384]{1,0:T(8,128)(2,1)} %wk.9, bf16[768,384]{1,0:T(8,128)(2,1)} %wv.9, bf16[384,768]{1,0:T(8,128)(2,1)} %wo_ref.3, ...), custom_call_target="tpu_custom_call" | custom-call | bytes 10800000 | tf_op jit(solution)/shard_map/pack_weights/pallas_call | solution.py:132
  4.2 3.0 %collective-permute-start = (bf16[272,1152]{1,0:T(8,128)(2,1)}, bf16[272,1152]{1,0:T(8,128)(2,1)S(1)}, u32[]{:S(2)}, u32[]{:S(2)}) collective-permute-start(bf16[272,1152]{1,0:T(8,128)(2,1)} %get-tuple-element.129), channel_id=1, source_target_pairs={{0,1},{1,0},{2,3},{3,2},{4,5},{5,4},{6,7},{7,6},{8,9},{9,8},{10,11... | collective-permute-start | bytes 1880072 | tf_op jit(solution)/shard_map/ppermute | solution.py:1083
  8.0 12.6 %attn_own.1 = (bf16[2,512,768]{2,1,0:T(8,128)(2,1)}, bf16[768,1024]{1,0:T(8,128)(2,1)}, bf16[2,512,384]{2,1,0:T(8,128)(2,1)}, bf16[2,384,512]{2,1,0:T(8,128)(2,1...) custom-call(s32[2]{0:T(128)} %copy-done.17, ...), custom_call_target="tpu_custom_call" | custom-call | bytes 43200000 | tf_op jit(solution)/shard_map/attn_own/pallas_call | solution.py:373
  25.5 4.5 %all-to-all-start = ((bf16[32,2,896]{2,1,0:T(2,128)(2,1)}), bf16[32,2,896]{2,1,0:T(2,128)(2,1)S(1)}, u32[]{:S(2)}, u32[]{:S(2)}) async-start(bf16[32,2,896]{2,1,0:T(2,128)(2,1)} %broadcast_in_dim.10), calls=%async_computation | async-start | bytes 229376 | tf_op jit(solution)/shard_map/all_to_all | solution.py:1100
  30.4 8.4 %all-to-all-done = bf16[32,2,896]{2,1,0:T(2,128)(2,1)S(1)} async-done(((bf16[32,2,896]{2,1,0:T(2,128)(2,1)}), bf16[32,2,896]{2,1,0:T(2,128)(2,1)S(1)}, u32[]{:S(2)}, u32[]{:S(2)}) %all-to-all-start) | async-done | bytes 114720 | tf_op jit(solution)/shard_map/all_to_all | solution.py:1100
  42.6 19.5 %attn_other.1 = (bf16[2,512,384]{2,1,0:T(8,128)(2,1)}, bf16[2,384,512]{2,1,0:T(8,128)(2,1)}, bf16[2,512,384]{2,1,0:T(8,128)(2,1)}, bf16[2,512,384]{2,1,0:T(8,128...) custom-call(s32[2]{0:T(128)} %copy-done.17, ...), custom_call_target="tpu_custom_call" | custom-call | bytes 54000000 | tf_op jit(solution)/shard_map/attn_other/pallas_call | solution.py:398
  67.6 15.0 %ffn_fwd.1 = (bf16[2,512,1536]{2,1,0:T(8,128)(2,1)}, bf16[2,512,1536]{2,1,0:T(8,128)(2,1)}, bf16[2,512,1536]{2,1,0:T(8,128)(2,1)}, bf16[2,512,1536]{2,1,0:T(8,12...) custom-call(s32[2]{0:T(128)} %copy-done.17, s32[1]{0:T(128)} %bitcast.at_ref, ...), custom_call_target="tpu_custom_call" | custom-call | bytes 57600000 | tf_op jit(solution)/shard_map/ffn_fwd/pallas_call | solution.py:680
  87.4 3.4 %pool.1 = f32[8,768]{1,0:T(8,128)} custom-call(s32[2]{0:T(128)} %copy-done.17, s32[1]{0:T(128)} %bitcast.at_ref, f32[2,1,3072]{2,1,0:T(1,128)} %get-tuple-element.152.asum_ref, f32[2,1,768]{2,1,0:T(1,128)} %get-tuple-element.153.rs_ref, bf16[384,768]{1,0:T(8,128)(2,1)} %copy-done.4, bf16[384,768]{1,0:T(8,128)(2,1)} %copy-done.5, bf16[384,768]{1,0:T(8,128)(2,1)} %copy-done.6, ...), custom_call_target="tpu_custom_call" | custom-call | bytes 14400000 | tf_op jit(solution)/shard_map/pool/pallas_call | solution.py:717
  92.4 4.9 %all-to-all-start.1 = ((bf16[32,2,2304]{2,1,0:T(2,128)(2,1)}), bf16[32,2,2304]{2,1,0:T(2,128)(2,1)S(1)}, u32[]{:S(2)}, u32[]{:S(2)}) async-start(bf16[32,2,2304]{2,1,0:T(2,128)(2,1)} %bitcast.10), calls=%async_computation.1 | async-start | bytes 589824 | tf_op jit(solution)/shard_map/all_to_all | solution.py:1100
  98.7 9.8 %all-to-all-done.1 = bf16[32,2,2304]{2,1,0:T(2,128)(2,1)S(1)} async-done(((bf16[32,2,2304]{2,1,0:T(2,128)(2,1)}), bf16[32,2,2304]{2,1,0:T(2,128)(2,1)S(1)}, u32[]{:S(2)}, u32[]{:S(2)}) %all-to-all-start.1) | async-done | bytes 294944 | tf_op jit(solution)/shard_map/all_to_all | solution.py:1100
  109.3 16.6 %loss_inner.1 = (f32[8,128]{1,0:T(8,128)}, f32[8,768]{1,0:T(8,128)}, f32[8,3072]{1,0:T(8,128)}, bf16[64,768]{1,0:T(8,128)(2,1)}, bf16[64,768]{1,0:T(8,128)(2,1)}...) custom-call(s32[4]{0:T(128)} %get-tuple-element.253.me_ref, s32[1]{0:T(128)} %bitcast.at_ref, ...), custom_call_target="tpu_custom_call" | custom-call | bytes 61200000 | tf_op jit(solution)/shard_map/loss_inner/pallas_call | solution.py:826
  126.2 2.8 collective-permute-done.14
  129.0 2.6 add.92
  131.6 3.8 %all-to-all-start.2 = ((bf16[8,48,1536]{2,1,0:T(8,128)(2,1)}), bf16[8,48,1536]{2,1,0:T(8,128)(2,1)S(1)}, u32[]{:S(2)}, u32[]{:S(2)}) async-start(bf16[8,48,1536]{2,1,0:T(8,128)(2,1)} %bitcast.11), calls=%async_computation.2 | async-start | bytes 2359296 | tf_op jit(solution)/shard_map/all_to_all | solution.py:1110
  135.4 32.2 %mid_bwd.1 = (f32[2,512,768]{2,1,0:T(8,128)}, bf16[2,512,768]{2,1,0:T(8,128)(2,1)}, bf16[2,512,384]{2,1,0:T(8,128)(2,1)}, bf16[2,512,384]{2,1,0:T(8,128)(2,1)}, ...) custom-call(s32[2]{0:T(128)} %copy-done.17, ...), custom_call_target="tpu_custom_call" | custom-call | bytes 115200000 | tf_op jit(solution)/shard_map/mid_bwd/pallas_call | solution.py:925
  167.8 2.8 collective-permute-done.15
  173.5 6.5 %all-to-all-start.3 = ((bf16[8,48,1536]{2,1,0:T(8,128)(2,1)}), bf16[8,48,1536]{2,1,0:T(8,128)(2,1)S(1)}, u32[]{:S(2)}, u32[]{:S(2)}) async-start(bf16[8,48,1536]{2,1,0:T(8,128)(2,1)} %broadcast_in_dim.13), calls=%async_computation.3 | async-start | bytes 2359296 | tf_op jit(solution)/shard_map/all_to_all | solution.py:1116
  181.1 3.0 %fusion = f32[1536,768]{1,0:T(8,128)} fusion(bf16[64,768]{1,0:T(8,128)(2,1)S(1)} %copy-done.16, bf16[64,2304]{1,0:T(8,128)(2,1)S(1)} %reshape.98), kind=kOutput, calls=%fused_computation.1 | convolution fusion | flops 150994944 | bytes 5013504 | tf_op jit(solution)/shard_map/dot_general | solution.py:31
  187.1 19.1 %attn_bwd.1 = (bf16[2,512,384]{2,1,0:T(8,128)(2,1)}, bf16[2,512,384]{2,1,0:T(8,128)(2,1)}, bf16[2,512,384]{2,1,0:T(8,128)(2,1)}, bf16[384,1536]{1,0:T(8,128)(2,1...) custom-call(s32[2]{0:T(128)} %copy-done.17, s32[1]{0:T(128)} %bitcast.at_ref, ...), custom_call_target="tpu_custom_call" | custom-call | bytes 57600000 | tf_op jit(solution)/shard_map/attn_bwd/pallas_call | solution.py:602
  211.9 2.9 add_add_fusion
  214.9 5.1 %all-to-all-start.4 = ((bf16[8,48,1536]{2,1,0:T(8,128)(2,1)}), bf16[8,48,1536]{2,1,0:T(8,128)(2,1)S(1)}, u32[]{:S(2)}, u32[]{:S(2)}) async-start(bf16[8,48,1536]{2,1,0:T(8,128)(2,1)} %bitcast.13), calls=%async_computation.4 | async-start | bytes 2359296 | tf_op jit(solution)/shard_map/all_to_all | solution.py:1110
  220.0 11.6 %layer_part.1 = bf16[2,512,768]{2,1,0:T(8,128)(2,1)} custom-call(s32[1]{0:T(128)} %bitcast.at_ref, f32[2,512,768]{2,1,0:T(8,128)} %get-tuple-element.170.refs_3_.res_ref, bf16[2,512,1536]{2,1,0:T(8,128)(2,1)} %get-tuple-element.210.aa_ref, bf16[2,512,1536]{2,1,0:T(8,128)(2,1)} %get-tuple-element.211.ab_ref, bf16[1536,768]{1,0:T(8,128)(2,1)} %w_ref.2, ...), custom_call_target="tpu_custom_call" | custom-call | bytes 43200000 | tf_op jit(solution)/shard_map/layer_part/pallas_call | solution.py:997
  231.6 12.2 %input_part.1 = f32[2,512,768]{2,1,0:T(8,128)} custom-call(s32[1]{0:T(128)} %bitcast.at_ref, bf16[2,512,768]{2,1,0:T(8,128)(2,1)} %x_ref.5, f32[2,512,768]{2,1,0:T(8,128)} %get-tuple-element.203.dres_ref, f32[1,768]{1,0:T(1,128)} %reshape.95.gain_ref, bf16[2,512,384]{2,1,0:T(8,128)(2,1)} %get-tuple-element.204.qa, ...), custom_call_target="tpu_custom_call" | custom-call | bytes 43200000 | tf_op jit(solution)/shard_map/input_part/pallas_call | solution.py:971
  243.8 5.0 %all-to-all-done.4 = bf16[8,48,1536]{2,1,0:T(8,128)(2,1)S(1)} async-done(((bf16[8,48,1536]{2,1,0:T(8,128)(2,1)}), bf16[8,48,1536]{2,1,0:T(8,128)(2,1)S(1)}, u32[]{:S(2)}, u32[]{:S(2)}) %all-to-all-start.4) | async-done | bytes 1179680 | tf_op jit(solution)/shard_map/all_to_all | solution.py:1110
  250.1 3.6 %all-to-all-start.5 = ((bf16[8,48,1536]{2,1,0:T(8,128)(2,1)}), bf16[8,48,1536]{2,1,0:T(8,128)(2,1)S(1)}, u32[]{:S(2)}, u32[]{:S(2)}) async-start(bf16[8,48,1536]{2,1,0:T(8,128)(2,1)} %broadcast_in_dim.14), calls=%async_computation.5 | async-start | bytes 2359296 | tf_op jit(solution)/shard_map/all_to_all | solution.py:1116
  255.9 5.9 %collective-permute-done.22 = f32[8,128]{1,0:T(8,128)S(1)} collective-permute-done((f32[8,128]{1,0:T(8,128)S(1)}, f32[8,128]{1,0:T(8,128)S(1)}, u32[]{:S(2)}, u32[]{:S(2)}) %collective-permute-start.22) | collective-permute-done | bytes 4128 | tf_op jit(solution)/shard_map/ppermute | solution.py:1083
  261.8 3.7 %collective-permute-start.23 = (f32[8,128]{1,0:T(8,128)S(1)}, f32[8,128]{1,0:T(8,128)S(1)}, u32[]{:S(2)}, u32[]{:S(2)}) collective-permute-start(f32[8,128]{1,0:T(8,128)S(1)} %add.99), channel_id=1, source_target_pairs={{0,8},{4,12},{8,0},{12,4},{16,24},{20,28},{24,16},{28,20},{1,9},{5... | collective-permute-start | bytes 12296 | tf_op jit(solution)/shard_map/ppermute | solution.py:1083
  266.5 6.0 %inner_done.1 = (f32[768,1536]{1,0:T(8,128)}, f32[24,768]{1,0:T(8,128)}) custom-call(s32[1]{0:T(128)} %bitcast.at_ref, bf16[384,1536]{1,0:T(8,128)(2,1)} %bitcast.31, bf16[384,1536]{1,0:T(8,128)(2,1)} %copy-done.12, bf16[768,1536]{1,0:T(8,128)(2,1)} %w_ref.3), custom_call_target="tpu_custom_call" | custom-call | bytes 18000000 | tf_op jit(solution)/shard_map/inner_done/pallas_call | solution.py:1031
  274.4 3.4 %collective-permute-start.24 = (f32[8,128]{1,0:T(8,128)S(1)}, f32[8,128]{1,0:T(8,128)S(1)}, u32[]{:S(2)}, u32[]{:S(2)}) collective-permute-start(f32[8,128]{1,0:T(8,128)S(1)} %add.100), channel_id=1, source_target_pairs={{0,16},{4,20},{8,24},{12,28},{16,0},{20,4},{24,8},{28,12},{1,17},{... | collective-permute-start | bytes 12296 | tf_op jit(solution)/shard_map/ppermute | solution.py:1083
  278.4 4.3 %collective-permute-done.24 = f32[8,128]{1,0:T(8,128)S(1)} collective-permute-done((f32[8,128]{1,0:T(8,128)S(1)}, f32[8,128]{1,0:T(8,128)S(1)}, u32[]{:S(2)}, u32[]{:S(2)}) %collective-permute-start.24) | collective-permute-done | bytes 4128 | tf_op jit(solution)/shard_map/ppermute | solution.py:1083
  283.8 3.1 %attn_done.2 = (f32[768,384]{1,0:T(8,128)}, f32[768,384]{1,0:T(8,128)}, f32[768,384]{1,0:T(8,128)}, f32[384,768]{1,0:T(8,128)}, f32[8,384]{1,0:T(8,128)}) custom-call(s32[1]{0:T(128)} %bitcast.14.half_ref, bf16[384,1536]{1,0:T(8,128)(2,1)} %bitcast.33, bf16[768,384]{1,0:T(8,128)(2,1)} %wq.9, bf16[768,384]{1,0:T(8,128)(2,1)} %wk.9, bf16[768,384]{1,0:T(8,128)(2,1)} %wv.9), custom_call_target="tpu_custom_call" | custom-call | bytes 10800000 | tf_op jit(solution)/shard_map/attn_done/pallas_call | solution.py:1062
  292.4 3.1 %attn_done.3 = (f32[768,384]{1,0:T(8,128)}, f32[768,384]{1,0:T(8,128)}, f32[768,384]{1,0:T(8,128)}, f32[384,768]{1,0:T(8,128)}, f32[8,384]{1,0:T(8,128)}) custom-call(s32[1]{0:T(128)S(6)} %sub.18.half_ref, bf16[384,1536]{1,0:T(8,128)(2,1)} %copy-done.13, ...), custom_call_target="tpu_custom_call", output_to_operand_aliasing={{0}: (5, {}), {1}: (6, {}), {2}: (7, {}), {3}: (8, {})} | custom-call | bytes 10800000 | tf_op jit(solution)/shard_map/attn_done/pallas_call | solution.py:1062
  (145 shorter events, 52.2 us)
Async XLA Ops:
  4.2 17.4 %collective-permute-start = (bf16[272,1152]{1,0:T(8,128)(2,1)}, bf16[272,1152]{1,0:T(8,128)(2,1)S(1)}, u32[]{:S(2)}, u32[]{:S(2)}) collective-permute-start(bf16[272,1152]{1,0:T(8,128)(2,1)} %get-tuple-element.129), channel_id=1, source_target_pairs={{0,1},{1,0},{2,3},{3,2},{4,5},{5,4},{6,7},{7,6},{8,9},{9,8},{10,11... | collective-permute-start | bytes 1880072 | tf_op jit(solution)/shard_map/ppermute | solution.py:1083
  21.5 17.3 %collective-permute-start.4 = (bf16[272,1152]{1,0:T(8,128)(2,1)S(1)}, bf16[272,1152]{1,0:T(8,128)(2,1)S(1)}, u32[]{:S(2)}, u32[]{:S(2)}) collective-permute-start(bf16[272,1152]{1,0:T(8,128)(2,1)S(1)} %collective-permute-done.p0.refs_11_), channel_id=1, source_target_pairs={{0,4},{4,0},{8,12},{12,8},{16,20},{20,16},{24,28},{28,24},{1,5},{5... | collective-permute-start | bytes 1880072 | tf_op jit(solution)/shard_map/ppermute | solution.py:1083
  23.2 17.1 %collective-permute-start.1 = (bf16[192,1536]{1,0:T(8,128)(2,1)}, bf16[192,1536]{1,0:T(8,128)(2,1)}, u32[]{:S(2)}, u32[]{:S(2)}) collective-permute-start(bf16[192,1536]{1,0:T(8,128)(2,1)} %get-tuple-element.133), channel_id=1, source_target_pairs={{0,1},{1,0},{2,3},{3,2},{4,5},{5,4},{6,7},{7,6},{8,9},{9,8},{10,11... | collective-permute-start | bytes 1769480 | tf_op jit(solution)/shard_map/ppermute | solution.py:1083
  25.5 13.4 %all-to-all-start = ((bf16[32,2,896]{2,1,0:T(2,128)(2,1)}), bf16[32,2,896]{2,1,0:T(2,128)(2,1)S(1)}, u32[]{:S(2)}, u32[]{:S(2)}) async-start(bf16[32,2,896]{2,1,0:T(2,128)(2,1)} %broadcast_in_dim.10), calls=%async_computation | async-start | bytes 229376 | tf_op jit(solution)/shard_map/all_to_all | solution.py:1100
  30.0 11.6 %collective-permute-start.5 = (bf16[272,1152]{1,0:T(8,128)(2,1)S(1)}, bf16[272,1152]{1,0:T(8,128)(2,1)S(1)}, u32[]{:S(2)}, u32[]{:S(2)}) collective-permute-start(bf16[272,1152]{1,0:T(8,128)(2,1)S(1)} %collective-permute-done.p0.refs_11_), channel_id=1, source_target_pairs={{0,2},{2,0},{1,3},{3,1},{4,6},{6,4},{5,7},{7,5},{8,10},{10,8},{9,1... | collective-permute-start | bytes 1880072 | tf_op jit(solution)/shard_map/ppermute | solution.py:1083
  38.8 2.8 collective-permute-start.6
  38.8 23.3 %collective-permute-start.3 = (bf16[384,768]{1,0:T(8,128)(2,1)}, bf16[384,768]{1,0:T(8,128)(2,1)S(1)}, u32[]{:S(2)}, u32[]{:S(2)}) collective-permute-start(bf16[384,768]{1,0:T(8,128)(2,1)} %get-tuple-element.136), channel_id=1, source_target_pairs={{0,1},{1,0},{2,3},{3,2},{4,5},{5,4},{6,7},{7,6},{8,9},{9,8},{10,11... | collective-permute-start | bytes 1769480 | tf_op jit(solution)/shard_map/ppermute | solution.py:1083
  40.3 21.8 %collective-permute-start.2 = (bf16[192,1536]{1,0:T(8,128)(2,1)}, bf16[192,1536]{1,0:T(8,128)(2,1)}, u32[]{:S(2)}, u32[]{:S(2)}) collective-permute-start(bf16[192,1536]{1,0:T(8,128)(2,1)} %collective-permute-done.1.p0.refs_15_), channel_id=1, source_target_pairs={{0,4},{4,0},{8,12},{12,8},{16,20},{20,16},{24,28},{28,24},{1,5},{5... | collective-permute-start | bytes 1769480 | tf_op jit(solution)/shard_map/ppermute | solution.py:1083
  62.1 20.7 %collective-permute-start.10 = (bf16[1,512,768]{2,1,0:T(8,128)(2,1)}, bf16[1,512,768]{2,1,0:T(8,128)(2,1)S(1)}, u32[]{:S(2)}, u32[]{:S(2)}) collective-permute-start(bf16[1,512,768]{2,1,0:T(8,128)(2,1)} %get-tuple-element.151), channel_id=1, source_target_pairs={{0,1},{1,0},{2,3},{3,2},{4,5},{5,4},{6,7},{7,6},{8,9},{9,8},{10,11... | collective-permute-start | bytes 2359304 | tf_op jit(solution)/shard_map/ppermute | solution.py:1083
  63.7 2.4 collective-permute-start.8
  63.7 3.1 %collective-permute-start.9 = (bf16[192,1536]{1,0:T(8,128)(2,1)}, bf16[192,1536]{1,0:T(8,128)(2,1)S(1)}, u32[]{:S(2)}, u32[]{:S(2)}) collective-permute-start(bf16[192,1536]{1,0:T(8,128)(2,1)} %collective-permute-done.2.p1.refs_16_), channel_id=1, source_target_pairs={{0,2},{2,0},{1,3},{3,1},{4,6},{6,4},{5,7},{7,5},{8,10},{10,8},{9,1... | collective-permute-start | bytes 1769480 | tf_op jit(solution)/shard_map/ppermute | solution.py:1083
  64.2 18.4 %collective-permute-start.7 = (bf16[384,768]{1,0:T(8,128)(2,1)S(1)}, bf16[384,768]{1,0:T(8,128)(2,1)S(1)}, u32[]{:S(2)}, u32[]{:S(2)}) collective-permute-start(bf16[384,768]{1,0:T(8,128)(2,1)S(1)} %collective-permute-done.3.p0), channel_id=1, source_target_pairs={{0,4},{4,0},{8,12},{12,8},{16,20},{20,16},{24,28},{28,24},{1,5},{5... | collective-permute-start | bytes 1769480 | tf_op jit(solution)/shard_map/ppermute | solution.py:1083
  64.7 44.6 %collective-permute-start.13 = (bf16[1,512,768]{2,1,0:T(8,128)(2,1)}, bf16[1,512,768]{2,1,0:T(8,128)(2,1)}, u32[]{:S(2)}, u32[]{:S(2)}) collective-permute-start(bf16[1,512,768]{2,1,0:T(8,128)(2,1)} %get-tuple-element.160), channel_id=1, source_target_pairs={{0,1},{1,0},{2,3},{3,2},{4,5},{5,4},{6,7},{7,6},{8,9},{9,8},{10,11... | collective-permute-start | bytes 2359304 | tf_op jit(solution)/shard_map/ppermute | solution.py:1083
  83.7 2.8 collective-permute-start.12
  92.4 16.1 %all-to-all-start.1 = ((bf16[32,2,2304]{2,1,0:T(2,128)(2,1)}), bf16[32,2,2304]{2,1,0:T(2,128)(2,1)S(1)}, u32[]{:S(2)}, u32[]{:S(2)}) async-start(bf16[32,2,2304]{2,1,0:T(2,128)(2,1)} %bitcast.10), calls=%async_computation.1 | async-start | bytes 589824 | tf_op jit(solution)/shard_map/all_to_all | solution.py:1100
  125.9 3.1 %collective-permute-start.14 = (bf16[384,1536]{1,0:T(8,128)(2,1)}, bf16[384,1536]{1,0:T(8,128)(2,1)S(1)}, u32[]{:S(2)}, u32[]{:S(2)}) collective-permute-start(bf16[384,1536]{1,0:T(8,128)(2,1)} %get-tuple-element.162), channel_id=1, source_target_pairs={{0,2},{2,0},{1,3},{3,1},{4,6},{6,4},{5,7},{7,5},{8,10},{10,8},{9,1... | collective-permute-start | bytes 3538952 | tf_op jit(solution)/shard_map/ppermute | solution.py:1083
  131.6 40.6 %all-to-all-start.2 = ((bf16[8,48,1536]{2,1,0:T(8,128)(2,1)}), bf16[8,48,1536]{2,1,0:T(8,128)(2,1)S(1)}, u32[]{:S(2)}, u32[]{:S(2)}) async-start(bf16[8,48,1536]{2,1,0:T(8,128)(2,1)} %bitcast.11), calls=%async_computation.2 | async-start | bytes 2359296 | tf_op jit(solution)/shard_map/all_to_all | solution.py:1110
  167.5 3.1 %collective-permute-start.15 = (bf16[384,1536]{1,0:T(8,128)(2,1)}, bf16[384,1536]{1,0:T(8,128)(2,1)S(1)}, u32[]{:S(2)}, u32[]{:S(2)}) collective-permute-start(bf16[384,1536]{1,0:T(8,128)(2,1)} %get-tuple-element.179), channel_id=1, source_target_pairs={{0,2},{2,0},{1,3},{3,1},{4,6},{6,4},{5,7},{7,5},{8,10},{10,8},{9,1... | collective-permute-start | bytes 3538952 | tf_op jit(solution)/shard_map/ppermute | solution.py:1083
  173.5 35.4 %all-to-all-start.3 = ((bf16[8,48,1536]{2,1,0:T(8,128)(2,1)}), bf16[8,48,1536]{2,1,0:T(8,128)(2,1)S(1)}, u32[]{:S(2)}, u32[]{:S(2)}) async-start(bf16[8,48,1536]{2,1,0:T(8,128)(2,1)} %broadcast_in_dim.13), calls=%async_computation.3 | async-start | bytes 2359296 | tf_op jit(solution)/shard_map/all_to_all | solution.py:1116
  180.1 27.9 %collective-permute-start.16 = (bf16[384,1536]{1,0:T(8,128)(2,1)S(1)}, bf16[384,1536]{1,0:T(8,128)(2,1)}, u32[]{:S(2)}, u32[]{:S(2)}) collective-permute-start(bf16[384,1536]{1,0:T(8,128)(2,1)S(1)} %add.93), channel_id=1, source_target_pairs={{0,1},{1,0},{2,3},{3,2},{4,5},{5,4},{6,7},{7,6},{8,9},{9,8},{10,11... | collective-permute-start | bytes 3538952 | tf_op jit(solution)/shard_map/ppermute | solution.py:1083
  184.1 23.9 %collective-permute-start.17 = (f32[8,128]{1,0:T(8,128)S(1)}, f32[8,128]{1,0:T(8,128)S(1)}, u32[]{:S(2)}, u32[]{:S(2)}) collective-permute-start(f32[8,128]{1,0:T(8,128)S(1)} %copy-done.24), channel_id=1, source_target_pairs={{0,1},{1,0},{2,3},{3,2},{4,5},{5,4},{6,7},{7,6},{8,9},{9,8},{10,11... | collective-permute-start | bytes 12296 | tf_op jit(solution)/shard_map/ppermute | solution.py:1083
  208.9 3.1 %collective-permute-start.18 = (bf16[384,1536]{1,0:T(8,128)(2,1)}, bf16[384,1536]{1,0:T(8,128)(2,1)S(1)}, u32[]{:S(2)}, u32[]{:S(2)}) collective-permute-start(bf16[384,1536]{1,0:T(8,128)(2,1)} %get-tuple-element.199), channel_id=1, source_target_pairs={{0,2},{2,0},{1,3},{3,1},{4,6},{6,4},{5,7},{7,5},{8,10},{10,8},{9,1... | collective-permute-start | bytes 3538952 | tf_op jit(solution)/shard_map/ppermute | solution.py:1083
  209.6 2.2 collective-permute-start.19
  214.9 33.9 %all-to-all-start.4 = ((bf16[8,48,1536]{2,1,0:T(8,128)(2,1)}), bf16[8,48,1536]{2,1,0:T(8,128)(2,1)S(1)}, u32[]{:S(2)}, u32[]{:S(2)}) async-start(bf16[8,48,1536]{2,1,0:T(8,128)(2,1)} %bitcast.13), calls=%async_computation.4 | async-start | bytes 2359296 | tf_op jit(solution)/shard_map/all_to_all | solution.py:1110
  250.1 32.6 %all-to-all-start.5 = ((bf16[8,48,1536]{2,1,0:T(8,128)(2,1)}), bf16[8,48,1536]{2,1,0:T(8,128)(2,1)S(1)}, u32[]{:S(2)}, u32[]{:S(2)}) async-start(bf16[8,48,1536]{2,1,0:T(8,128)(2,1)} %broadcast_in_dim.14), calls=%async_computation.5 | async-start | bytes 2359296 | tf_op jit(solution)/shard_map/all_to_all | solution.py:1116
  253.8 11.7 %collective-permute-start.20 = (bf16[384,1536]{1,0:T(8,128)(2,1)S(1)}, bf16[384,1536]{1,0:T(8,128)(2,1)S(1)}, u32[]{:S(2)}, u32[]{:S(2)}) collective-permute-start(bf16[384,1536]{1,0:T(8,128)(2,1)S(1)} %bitcast.30), channel_id=1, source_target_pairs={{0,2},{2,0},{1,3},{3,1},{4,6},{6,4},{5,7},{7,5},{8,10},{10,8},{9,1... | collective-permute-start | bytes 3538952 | tf_op jit(solution)/shard_map/ppermute | solution.py:1083
  253.9 7.9 %collective-permute-start.22 = (f32[8,128]{1,0:T(8,128)S(1)}, f32[8,128]{1,0:T(8,128)S(1)}, u32[]{:S(2)}, u32[]{:S(2)}) collective-permute-start(f32[8,128]{1,0:T(8,128)S(1)} %add.98), channel_id=1, source_target_pairs={{0,4},{4,0},{8,12},{12,8},{16,20},{20,16},{24,28},{28,24},{1,5},{5... | collective-permute-start | bytes 12296 | tf_op jit(solution)/shard_map/ppermute | solution.py:1083
  261.8 12.6 %collective-permute-start.23 = (f32[8,128]{1,0:T(8,128)S(1)}, f32[8,128]{1,0:T(8,128)S(1)}, u32[]{:S(2)}, u32[]{:S(2)}) collective-permute-start(f32[8,128]{1,0:T(8,128)S(1)} %add.99), channel_id=1, source_target_pairs={{0,8},{4,12},{8,0},{12,4},{16,24},{20,28},{24,16},{28,20},{1,9},{5... | collective-permute-start | bytes 12296 | tf_op jit(solution)/shard_map/ppermute | solution.py:1083
  273.4 4.4 %collective-permute-start.21 = (f32[768]{0:T(1024)S(1)}, f32[768]{0:T(1024)S(1)}, u32[]{:S(2)}, u32[]{:S(2)}) collective-permute-start(f32[768]{0:T(1024)S(1)} %reduce_sum.45), channel_id=1, source_target_pairs={{0,1},{1,0},{2,3},{3,2},{4,5},{5,4},{6,7},{7,6},{8,9},{9,8},{10,11... | collective-permute-start | bytes 9224 | tf_op jit(solution)/shard_map/ppermute | solution.py:1083
  274.4 8.3 %collective-permute-start.24 = (f32[8,128]{1,0:T(8,128)S(1)}, f32[8,128]{1,0:T(8,128)S(1)}, u32[]{:S(2)}, u32[]{:S(2)}) collective-permute-start(f32[8,128]{1,0:T(8,128)S(1)} %add.100), channel_id=1, source_target_pairs={{0,16},{4,20},{8,24},{12,28},{16,0},{20,4},{24,8},{28,12},{1,17},{... | collective-permute-start | bytes 12296 | tf_op jit(solution)/shard_map/ppermute | solution.py:1083
  282.7 8.6 %collective-permute-start.26 = (bf16[384,1536]{1,0:T(8,128)(2,1)S(1)}, bf16[384,1536]{1,0:T(8,128)(2,1)S(1)}, u32[]{:S(2)}, u32[]{:S(2)}) collective-permute-start(bf16[384,1536]{1,0:T(8,128)(2,1)S(1)} %bitcast.32), channel_id=1, source_target_pairs={{0,2},{2,0},{1,3},{3,1},{4,6},{6,4},{5,7},{7,5},{8,10},{10,8},{9,1... | collective-permute-start | bytes 3538952 | tf_op jit(solution)/shard_map/ppermute | solution.py:1083
  287.6 3.6 %collective-permute-start.25 = (f32[384]{0:T(512)S(1)}, f32[384]{0:T(512)S(1)}, u32[]{:S(2)}, u32[]{:S(2)}) collective-permute-start(f32[384]{0:T(512)S(1)} %slice_reduce_fusion), channel_id=1, source_target_pairs={{0,1},{1,0},{2,3},{3,2},{4,5},{5,4},{6,7},{7,6},{8,9},{9,8},{10,11... | collective-permute-start | bytes 4616 | tf_op jit(solution)/shard_map/ppermute | solution.py:1083
  (27 other events, 222.0 us)

commit v2 on v1

--- a/solution.py
+++ b/solution.py
@@ -46,8 +46,8 @@
     return hot
 
 
-def params(**kw):
-    return pltpu.CompilerParams(vmem_limit_bytes=60 * MIB, **kw)
+def params(mib=60):
+    return pltpu.CompilerParams(vmem_limit_bytes=mib * MIB)
 
 
 def cost(us):
@@ -223,23 +223,22 @@
         nb_ref[t] = pltpu.roll(v, TILE + 1, 1, stride=1, stride_axis=0)[:, :TILE]
 
 
-def attn_rows(an, length, ws, outs, nb_ref, tf_ref, s_ref, p_ref):
+def attn_rows(an, length, ws, outs, nb_ref, tf_ref, s_ref, p_ref, between=None):
     q_ref, qt_ref, k_ref, v_ref, ctx_ref, ctxt_ref, lse_ref = outs
     seq = an.shape[0]
     width = q_ref.shape[2]
-    for ref, w in zip((q_ref, k_ref, v_ref), ws):
+    for ref, w in zip((q_ref, k_ref), ws):
         ref[0] = mm(an, w[...]).astype(BF)
     kx = key_extras(length, seq)
     lane = lax.broadcasted_iota(jnp.int32, (seq, TILE), 1)
     blocks = [(h, ib) for h in range(width // 64) for ib in range(seq // 256)]
-    keys, queries, values, tops, sums, rows = {}, {}, {}, {}, {}, {}
+    keys, queries, values, tops, rows = {}, {}, {}, {}, {}
 
     def prepare(h):
         pair, e = h // 2, h % 2
         cols = slice(TILE * pair, TILE * (pair + 1))
         if e == 0:
             qt_ref[0, cols, :] = jnp.transpose(q_ref[0, :, cols])
-            values[pair] = jnp.transpose(v_ref[0, :, cols])
         mine = lane < 64 if e == 0 else lane >= 64
         keys[h] = jnp.where(mine, k_ref[0, :, cols].astype(F32), kx).astype(BF)
         qt = qt_ref[0, 64 * h : 64 * (h + 1), :]
@@ -263,19 +262,18 @@
     def soft(t, bj):
         h, ib = blocks[t]
         at = slice(TILE * bj, TILE * (bj + 1))
-        p = jnp.exp(s_ref[t % 2, at, :] - tops[t])
-        one = jnp.sum(p.reshape(TILE // 8, 8, 256), axis=0)
-        sums[t] = one if bj == 0 else sums[t] + one
-        p_ref[h % 2, at, 256 * ib : 256 * (ib + 1)] = p.astype(BF)
-        if bj == seq // TILE - 1:
-            sums[t] = jnp.sum(sums[t], axis=0, keepdims=True)
-            lse_ref[0, h : h + 1, 256 * ib : 256 * (ib + 1)] = tops[t] + jnp.log(sums[t])
+        p_ref[h % 2, at, 256 * ib : 256 * (ib + 1)] = jnp.exp(s_ref[t % 2, at, :] - tops[t]).astype(BF)
 
     def combine(h):
         per = seq // 256
-        total = jnp.concatenate([sums[per * h + i] for i in range(per)], axis=1)
+        top = jnp.concatenate([tops[per * h + i] for i in range(per)], axis=1)
+        if h % 2 == 0:
+            values[h // 2] = jnp.transpose(v_ref[0, :, TILE * (h // 2) : TILE * (h // 2 + 1)])
         vt = values[h // 2][64 * (h % 2) : 64 * (h % 2 + 1), :]
-        rows[h] = mm(vt, p_ref[h % 2]) * (1.0 / total)
+        got = mm(jnp.concatenate([vt, jnp.ones((16, seq), BF)], axis=0), p_ref[h % 2])
+        total = got[64:65]
+        lse_ref[0, h : h + 1, :] = top + jnp.log(total)
+        rows[h] = got[:64] * (1.0 / total)
         if h % 2 == 1:
             pair = h // 2
             cols = slice(TILE * pair, TILE * (pair + 1))
@@ -288,6 +286,10 @@
             pieces = start(t)
             for bj in range(seq // TILE):
                 score(t, bj, pieces)
+        if t == 0:
+            v_ref[0] = mm(an, ws[2][...]).astype(BF)
+        if t == 5 and between is not None:
+            between()
         if t > 0:
             for bj in range(seq // TILE):
                 soft(t - 1, bj)
@@ -314,35 +316,43 @@
     attn_rows(an, lens[b], (wq, wk, wv), outs, nb_ref, tf_ref, s_ref, p_ref)
 
 
-def attn_other_kernel(lens, at_ref, an_ref, hot_ref, x_ref, ca_ref, wo_ref, gain_ref, p0, p1, p2, p3, *refs):
+def attn_other_kernel(lens, at_ref, an_ref, hot_ref, gain_ref, x_hbm, ca_hbm, wo_hbm, p0, p1, p2, p3, *refs):
     outs, (nb_ref, tf_ref, res_ref, fin_ref, fint_ref, rsum_ref, f0_ref, f1_ref) = list(refs[:6]), refs[6:14]
-    (s_ref, p_ref, w_ref, tab_ref, wb_ref, c_ref, sem, sem1) = refs[14:]
+    (s_ref, p_ref, w_ref, tab_ref, wb_ref, c_ref, x_ref, ca_ref, wo_ref, sem, sem1, sem2) = refs[14:]
     outs.insert(4, c_ref)
     b = pl.program_id(0)
     late = out_copies(at_ref[0], (p0, p1, p2, p3), wb_ref, sem1)
+    moves = ((x_hbm, x_ref), (ca_hbm, ca_ref), (wo_hbm, wo_ref))
+    more = [pltpu.make_async_copy(x, y, sem2.at[i]) for i, (x, y) in enumerate(moves)]
 
     @pl.when(b == 0)
     def _():
         rows = w_ref.shape[0] // 4
         copies = join_copies(at_ref[0], (p0, p1, p2, p3), w_ref, sem)
         copies.append(pltpu.make_async_copy(p0.at[pl.ds(rows, 16)], tab_ref, sem.at[4]))
-        for c in copies + late:
+        for c in copies + more + late:
             c.start()
         for c in copies:
             c.wait()
         parts = [tab_ref[:, TILE * k : TILE * (k + 1)] for k in range(3)]
         set_bias(parts, hot_ref, tf_ref, nb_ref)
+        for c in more:
+            c.wait()
 
     width = outs[0].shape[2]
     ws = [w_ref.at[:, width * k : width * (k + 1)] for k in range(3)]
-    attn_rows(an_ref[0], lens[b], ws, outs, nb_ref, tf_ref, s_ref, p_ref)
+
+    def between():
+        res_ref[0] = x_ref[b].astype(F32) + mm(ca_ref[b], wo_ref[...])
+
+    attn_rows(an_ref[0], lens[b], ws, outs, nb_ref, tf_ref, s_ref, p_ref, between)
 
     @pl.when(b == 0)
     def _():
         for c in late:
             c.wait()
 
-    res = x_ref[0].astype(F32) + mm(ca_ref[0], wo_ref[...]) + mm(outs[4][0], wb_ref[...])
+    res = res_ref[0] + mm(outs[4][0], wb_ref[...])
     res_ref[0] = res
     inv = lax.rsqrt(jnp.mean(res * res, axis=-1, keepdims=True) + EPS)
     fin = (res * inv * gain_ref[...]).astype(BF)
@@ -398,9 +408,8 @@
     return pl.pallas_call(
         attn_other_kernel,
         grid=(n,),
-        in_specs=[SMEM_SPEC, SMEM_SPEC, row_spec(an.shape), const_spec(hot.shape), row_spec(x.shape)]
-        + [row_spec(ctx_a.shape), const_spec(wo.shape), const_spec((1, d))]
-        + [ANY] * 4,
+        in_specs=[SMEM_SPEC, SMEM_SPEC, row_spec(an.shape), const_spec(hot.shape), const_spec((1, d))]
+        + [ANY] * 7,
         out_specs=specs + more_specs,
         out_shape=outs + more,
         scratch_shapes=scratch
@@ -409,19 +418,23 @@
             pltpu.VMEM((16, 3 * width), BF),
             pltpu.VMEM(wo.shape, BF),
             pltpu.VMEM((1, seq, width), BF),
+            pltpu.VMEM(x.shape, BF),
+            pltpu.VMEM(ctx_a.shape, BF),
+            pltpu.VMEM(wo.shape, BF),
             pltpu.SemaphoreType.DMA((5,)),
             pltpu.SemaphoreType.DMA((12,)),
+            pltpu.SemaphoreType.DMA((3,)),
         ],
         compiler_params=params(),
         cost_estimate=cost(15),
         name="attn_other",
-    )(lens, at, an, hot, x, ctx_a, wo, gain.reshape(1, d), *packs)
+    )(lens, at, an, hot, gain.reshape(1, d), x, ctx_a, wo, *packs)
 
 
 def attn_back(b, n, length, core, w, d_attn, ins, outs, scratch, late):
     (q_ref, qt_ref, k_ref, v_ref, ct_ref, lse_ref, nb_ref, tf_ref, ant_ref, hot_ref) = ins
-    (dq_ref, dk_ref, dv_ref, send_ref, keep_ref, table_ref) = outs
-    (dc_ref, dct_ref, t_ref, fsum_ref, p_ref, ds_ref, all_ref, da_ref, go_ref) = scratch
+    (all_hbm, send_ref, keep_ref, table_ref) = outs
+    (dc_ref, dct_ref, t_ref, fsum_ref, p_ref, ds_ref, all_ref, da_ref, go_ref, out_sem) = scratch
     seq, width = q_ref.shape[1], q_ref.shape[2]
     heads = width // 64
     nblk = seq // TILE
@@ -433,7 +446,6 @@
         fsum_ref[...] = jnp.zeros_like(fsum_ref)
         table_ref[...] = jnp.zeros_like(table_ref)
 
-    da_ref[here, :] = d_attn
     dct_ref[...] = mm(w, d_attn, NT).astype(BF)
     dc_ref[...] = jnp.transpose(dct_ref[...])
     kx = key_extras(length, seq)
@@ -493,16 +505,14 @@
         slot = pair % 2
         cols = slice(TILE * pair, TILE * (pair + 1))
         if part < 2:
-            src, rhs, out_ref = ((p_ref, dc_ref[:, cols], dv_ref), (ds_ref, q_ref[b, :, cols], dk_ref))[part]
+            src, rhs = ((p_ref, dc_ref[:, cols]), (ds_ref, q_ref[b, :, cols]))[part]
             one = jnp.where(lane < 64, mm(src[slot, :, :seq], rhs), mm(src[slot, :, seq:], rhs)).astype(BF)
-            out_ref[0, :, cols] = one
             base = width * (2 - part)
             all_ref[here, base + TILE * pair : base + TILE * (pair + 1)] = one
         if part == 2:
             kt = turned[pair]
             dqt = [mm(kt[64 * e : 64 * (e + 1), :], ds_ref[slot, :, seq * e : seq * (e + 1)]) for e in range(2)]
             one = jnp.transpose(jnp.concatenate(dqt, axis=0).astype(BF))
-            dq_ref[0, :, cols] = one
             all_ref[here, TILE * pair : TILE * (pair + 1)] = one
 
     for pair in range(heads // 2):
@@ -516,6 +526,7 @@
                 step += 1
     for part in range(3):
         finish(heads // 2 - 1, part)
+    done = send_rows(b, n, all_ref, all_hbm, out_sem)
 
     @pl.when(b == n - 1)
     def _():
@@ -535,8 +546,8 @@
         turn = lax.broadcasted_iota(jnp.int32, (TILE, TILE), 0) + lax.broadcasted_iota(jnp.int32, (TILE, TILE), 1)
         turn = jnp.where(turn == TILE - 1, 1.0, 0.0).astype(BF)
         tiles = t_ref.shape[0]
-        parts = split3(t_ref[...].reshape(tiles * TILE, TILE))
-        back = mm(parts[0], turn) + mm(parts[1], turn) + mm(parts[2], turn)
+        hi, lo, _ = split3(t_ref[...].reshape(tiles * TILE, TILE))
+        back = mm(jnp.concatenate([hi, lo], axis=1), jnp.concatenate([turn, turn], axis=0))
         diag = []
         for t in range(tiles):
             x = jnp.concatenate([back[TILE * t : TILE * (t + 1)], jnp.zeros((TILE, TILE), F32)], axis=1)
@@ -552,13 +563,26 @@
                 far = jnp.sum(jnp.sum(fsum_ref[2 * h + side], axis=0, keepdims=True), axis=1, keepdims=True)
                 one = one + jnp.where(spot == bucket, far, 0.0)
             table_ref[h : h + 1, :] = one
+        for c in done:
+            c.wait()
+
+
+def send_rows(b, n, src, dst, sem):
+    rows = src.shape[0] // n
+    copies = [pltpu.make_async_copy(src.at[pl.ds(i * rows, rows)], dst.at[pl.ds(i * rows, rows)], sem.at[i]) for i in range(n)]
+    for i, c in enumerate(copies):
+
+        @pl.when(b == i)
+        def _():
+            c.start()
+
+    return copies
 
 
 def back_outs(n, seq, width, d):
-    tok = sds((n, seq, width), BF)
     half = sds((d // 2, 4 * width), BF)
-    outs = [tok, tok, tok, half, half, sds((8, TILE), F32)]
-    return outs, [row_spec(tok.shape)] * 3 + [out_const(o.shape) for o in outs[3:]]
+    outs = [sds((n * seq, 3 * width), BF), half, half, sds((8, TILE), F32)]
+    return outs, [ANY] + [out_const(o.shape) for o in outs[1:]]
 
 
 def back_scratch(n, seq, width, d):
@@ -573,12 +597,13 @@
         pltpu.VMEM((n * seq, 3 * width), BF),
         pltpu.VMEM((n * seq, d), BF),
         pltpu.VMEM((d, width), BF),
+        pltpu.SemaphoreType.DMA((n,)),
     ]
 
 
 def attn_bwd_kernel(lens, at_ref, da_blk, wo_ref, hot_ref, lse_ref, tf_ref, *refs):
-    hbm, outs, scratch = refs[:7], refs[7:13], refs[13:22]
-    bufs, sem = refs[22:29], refs[29]
+    hbm, outs, scratch = refs[:7], refs[7:11], refs[11:21]
+    bufs, sem = refs[21:28], refs[28]
     b = pl.program_id(0)
     n = da_blk.shape[0] * lse_ref.shape[0]
     copies = [pltpu.make_async_copy(x, y, sem.at[i]) for i, (x, y) in enumerate(zip(hbm, bufs))]
@@ -592,6 +617,8 @@
 
     q, qt, k, v, ct, nb, ant = bufs
     ins = (q, qt, k, v, ct, lse_ref, nb, tf_ref, ant, hot_ref)
+    seq = da_blk.shape[1]
+    scratch[7][pl.ds(pl.multiple_of(b * seq, seq), seq), :] = da_blk[0]
     attn_back(b, n, lens[b], at_ref[0] // 2, wo_ref[...], da_blk[0], ins, outs, scratch, copies[-1:])
 
 
@@ -631,8 +658,7 @@
 
     @pl.when(b == 0)
     def _():
-        for c in late:
-            c.start()
+        run_copies(late)
 
     fin = fin_ref[0]
     seq = fin.shape[0]
@@ -649,13 +675,6 @@
 
     project(0)
     for t, (_, a_ref, g_ref, c) in enumerate(parts):
-        if t + 1 == half // chunk:
-
-            @pl.when(b == 0)
-            def _():
-                for copy in late:
-                    copy.wait()
-
         if t + 1 < len(parts):
             project(t + 1)
         for r in range(seq // TILE):
@@ -720,7 +739,7 @@
         out_specs=vm,
         out_shape=sds((8, d), F32),
         scratch_shapes=[pltpu.VMEM((half, d), BF), pltpu.SemaphoreType.DMA((4,))],
-        compiler_params=params(),
+        compiler_params=params(16),
         cost_estimate=cost(4),
         name="pool",
     )(lens, at, asum, rsum, *packs)
@@ -858,8 +877,9 @@
 
 def mid_bwd_kernel(lens, at_ref, g_ref, row_ref, gain_ref, hot_ref, lse_ref, tf_ref, *refs):
     hbm, packs0, packs1 = refs[:11], refs[11:15], refs[15:19]
-    (dres_ref, dattn_ref), outs, scratch = refs[19:21], refs[21:27], refs[27:36]
-    bufs, (wib_ref, wob_ref, d_ref, sem, sem0, sem1) = refs[36:47], refs[47:]
+    (dres_hbm, dattn_hbm), outs, scratch = refs[19:21], refs[21:25], refs[25:35]
+    bufs, (wib_ref, wob_ref, d_ref, dres_ref, sem, sem0, sem1, sem2) = refs[35:46], refs[46:]
+    da_ref = scratch[7]
     wi_ref, gpa_ref, gpb_ref, res_all, q, qt, k, v, ct, nb, ant = bufs
     b = pl.program_id(0)
     n = lse_ref.shape[0]
@@ -907,12 +927,19 @@
     vcol = valid.astype(F32)[:, :1]
     inv = inv * vcol
     d_res = vcol * row_ref[pl.ds(b, 1), :] + scaled * inv - res * (inv * inv * inv * along / d)
-    dres_ref[0] = d_res
+    here = pl.ds(pl.multiple_of(b * seq, seq), seq)
+    dres_ref[here, :] = d_res
     d_attn = d_res.astype(BF)
-    dattn_ref[0] = d_attn
+    da_ref[here, :] = d_attn
+    done = send_rows(b, n, dres_ref, dres_hbm, sem2.at[0]) + send_rows(b, n, da_ref, dattn_hbm, sem2.at[1])
     first(copies0 + copies[4:-1])
     ins = (q, qt, k, v, ct, lse_ref, nb, tf_ref, ant, hot_ref)
     attn_back(b, n, lens[b], at_ref[0] // 2, wob_ref[...], d_attn, ins, outs, scratch, copies[-1:])
+
+    @pl.when(b == n - 1)
+    def _():
+        for c in done:
+            c.wait()
 
 
 def mid_bwd(lens, at, g, row, gain, hot, lse, tf, arrays, packs0, packs1):
@@ -921,7 +948,7 @@
     half = wi.shape[1]
     width = packs0[0].shape[1] // 3
     outs, specs = back_outs(n, seq, width, d)
-    more = [sds((n, seq, d), F32), sds((n, seq, d), BF)]
+    more = [sds((n * seq, d), F32), sds((n * seq, d), BF)]
     return pl.pallas_call(
         mid_bwd_kernel,
         grid=(n,),
@@ -930,7 +957,7 @@
         + [const_spec((1, d))]
         + [const_spec(x.shape) for x in (hot, lse, tf)]
         + [ANY] * 19,
-        out_specs=[row_spec(o.shape) for o in more] + specs,
+        out_specs=[ANY] * 2 + specs,
         out_shape=more + outs,
         scratch_shapes=back_scratch(n, seq, width, d)
         + [pltpu.VMEM(x.shape, x.dtype) for x in arrays]
@@ -938,9 +965,11 @@
             pltpu.VMEM((d, half), BF),
             pltpu.VMEM((width, d), BF),
             pltpu.VMEM((2, seq, 512), BF),
+            pltpu.VMEM((n * seq, d), F32),
             pltpu.SemaphoreType.DMA((11,)),
             pltpu.SemaphoreType.DMA((12,)),
             pltpu.SemaphoreType.DMA((4,)),
+            pltpu.SemaphoreType.DMA((2, n)),
         ],
         compiler_params=params(),
         cost_estimate=cost(32),
@@ -948,31 +977,30 @@
     )(lens, at, g, row, gain.reshape(1, d), hot, lse, tf, *arrays, *packs0, *packs1)
 
 
-def input_kernel(at_ref, x_ref, dres_ref, gain_ref, qa, ka, va, qb, kb, vb, wq, wk, wv, p0, p1, p2, p3, out_ref, w_ref, sem):
+def input_kernel(at_ref, x_ref, dres_ref, gain_ref, ta_ref, tb_ref, wq, wk, wv, p0, p1, p2, p3, out_ref, w_ref, sem):
     @pl.when(pl.program_id(0) == 0)
     def _():
         run_copies(join_copies(at_ref[0], (p0, p1, p2, p3), w_ref, sem))
 
     width = wq.shape[1]
-    d_one = mm(qa[0], wq[...], NT) + mm(ka[0], wk[...], NT) + mm(va[0], wv[...], NT)
-    for i, t in enumerate((qb, kb, vb)):
-        d_one = d_one + mm(t[0], w_ref[:, width * i : width * (i + 1)], NT)
+    d_one = mm(tb_ref[...], w_ref[...], NT)
+    for i, w in enumerate((wq, wk, wv)):
+        d_one = d_one + mm(ta_ref[:, width * i : width * (i + 1)], w[...], NT)
     x = x_ref[0].astype(F32)
     inv = lax.rsqrt(jnp.mean(x * x, axis=-1, keepdims=True) + EPS)
-    dx = d_one * x
-    gain = gain_ref[...]
-    along = jnp.sum(dx * gain, axis=-1, keepdims=True)
-    out_ref[0] = dres_ref[0] + d_one * gain * inv - x * (inv * inv * inv * along / x.shape[1])
-
-
-def input_part(at, x, dres, gain, toks, wq, wk, wv, packs):
+    scaled = d_one * gain_ref[...]
+    along = jnp.sum(scaled * x, axis=-1, keepdims=True)
+    out_ref[0] = dres_ref[...] + scaled * inv - x * (inv * inv * inv * along / x.shape[1])
+
+
+def input_part(at, x, dres, gain, tok_a, tok_b, wq, wk, wv, packs):
     n, seq, d = x.shape
     width = wq.shape[1]
+    rows = lambda cols: pl.BlockSpec((seq, cols), lambda b: (b, 0))
     return pl.pallas_call(
         input_kernel,
         grid=(n,),
-        in_specs=[SMEM_SPEC, row_spec(x.shape), row_spec(dres.shape), const_spec((1, d))]
-        + [row_spec(toks[0].shape)] * 6
+        in_specs=[SMEM_SPEC, row_spec(x.shape), rows(d), const_spec((1, d)), rows(3 * width), rows(3 * width)]
         + [const_spec(wq.shape)] * 3
         + [ANY] * 4,
         out_specs=row_spec(x.shape),
@@ -981,7 +1009,7 @@
         compiler_params=params(),
         cost_estimate=cost(12),
         name="input_part",
-    )(at, x, dres, gain.reshape(1, d), *toks, wq, wk, wv, *packs)
+    )(at, x, dres, gain.reshape(1, d), tok_a, tok_b, wq, wk, wv, *packs)
 
 
 def layer_kernel(at_ref, res_ref, aa_ref, ab_ref, w_ref, p0, p1, p2, p3, out_ref, wb_ref, sem):
@@ -1034,7 +1062,7 @@
         in_specs=[SMEM_SPEC, cols(d // 2), cols(d // 2), cols(d)],
         out_specs=[cols(d), pl.BlockSpec((8, d), lambda c: (c, 0))],
         out_shape=[sds((d, half), F32), sds((8 * (half // chunk), d), F32)],
-        compiler_params=params(),
+        compiler_params=params(20),
         cost_estimate=cost(5),
         name="inner_done",
     )(at, own, near, w)
@@ -1069,7 +1097,7 @@
         ),
         out_shape=[grad, grad, grad, sds((width, d), F32), sds((8, rows), F32)],
         input_output_aliases={5 + i: i for i in range(len(into))},
-        compiler_params=params(),
+        compiler_params=params(20),
         cost_estimate=cost(3),
         name="attn_done",
     )(half, sums, wq, wk, wv, *into)
@@ -1201,26 +1229,25 @@
     inner_half, gp_a = after(gi_keep + pc.core_swap(gi_send), gp_a)
     inner_parts = pc.exchange(inner_half)
     arrays = [w_inner, gp_a, gp_b, res, q_b, qt_b, k_b, v_b, ctxt_b, nb_b, ant]
-    d_res, d_attn, dq_b, dk_b, dv_b, send_b, keep_b, table_b = mid_bwd(
+    d_res, d_attn, tok_b, send_b, keep_b, table_b = mid_bwd(
         lens, at, g8, row8, gain_ffn, hot_back, lse_b, tf_b, arrays, p_attn, p_inner
     )
+    inner_part, d_attn = after(pc.add(inner_parts), d_attn)
+    inner_all = pc.gather(inner_part)
     half_b, d_attn = after(keep_b + pc.core_swap(send_b), d_attn)
     far_part = pc.across(half_b)
-    inner_part, d_attn = after(pc.add(inner_parts), d_attn)
-    dq_a, dk_a, dv_a, send_a, keep_a, table_a = attn_bwd(
-        lens, at, d_attn, w_out, hot_back, lse_a, tf_a, q_a, qt_a, k_a, v_a, ctxt_a, nb_a, ant
+    tok_a, send_a, keep_a, table_a = attn_bwd(
+        lens, at, d_attn.reshape(n, seq, d), w_out, hot_back, lse_a, tf_a, q_a, qt_a, k_a, v_a, ctxt_a, nb_a, ant
     )
     proj_grad = mm(pooled, d_emb, TN)
     outer_grad = mm(got[:, d:], d_rows, TN)
     inner_all, far_part, far_table, send_a, proj_grad, outer_grad = after(
-        pc.gather(inner_part), far_part, pc.across(table_b), send_a, proj_grad, outer_grad
+        inner_all, far_part, pc.across(table_b), send_a, proj_grad, outer_grad
     )
     table = table_a + far_table
     near_a, near_table = after(pc.core_swap(send_a), pc.core_swap(table))
     parts = pc.exchange(keep_a + far_part + near_a)
-    toks = (dq_a, dk_a, dv_a, dq_b, dk_b, dv_b)
-    input_grad = input_part(at, hidden_in, d_res, gain_attn, toks, w_query, w_key, w_value, p_attn)
-
+    input_grad = input_part(at, hidden_in, d_res, gain_attn, tok_a, tok_b, w_query, w_key, w_value, p_attn)
     inner_sum, gain_ffn_part = inner_done(at, inner_all, pc.core_swap(inner_all), w_inner)
     layer = layer_part(at, res, act_a, act_b, w_outer, p_outer)
     parts, input_grad, layer = after(parts, input_grad, layer)

time: 303 us -> 292 us (0.964)
  Pallas kernels: 158 us -> 147 us
  transfers between devices with their start and end apart: 34 -> 34, of which waited for: 18 -> 17; matrix products, arithmetic and copies ran while one was open for 6% -> 6% of each run, Pallas kernels for 45% -> 44%
where the time goes in v2:
time: 292 us; the launch traced here: 287 us
  Pallas kernels  147 us (50%)
  starting transfers between devices  58.4 us (20%)
  waiting for transfers between devices  49.7 us (17%)
  local copies, waits for them, and re-layouts  14.5 us (5%)
  other arithmetic  10.8 us (4%)
  matrix products  4.9 us (2%)
    pallas_call x1, Pallas kernels, mid_bwd(): pl.pallas_call(mid_bwd_kernel, grid=(n,), in_specs=[SMEM_SPEC, SMEM_SPEC]...  30.7 us
    ppermute x28, starting transfers between devices, swap(): return lax.ppermute(x, axis, [(i, i ^ bit) for i in range(size)])  28.3 us
    ppermute x28, waiting for transfers between devices, swap(): return lax.ppermute(x, axis, [(i, i ^ bit) for i in range(size)])  25.7 us
    pallas_call x1, Pallas kernels, attn_bwd(): pl.pallas_call(attn_bwd_kernel, grid=(n,), in_specs=[SMEM_SPEC, SMEM_SPEC...  18.5 us
    pallas_call x1, Pallas kernels, attn_other(): pl.pallas_call(attn_other_kernel, grid=(n,), in_specs=[SMEM_SPEC, SMEM_SP...  18.5 us
    all_to_all x2, waiting for transfers between devices, share(): return lax.all_to_all(x, ('chip', 'core', 'tensor'), 0, 0, tiled=True)  18.3 us
    pallas_call x1, Pallas kernels, loss_all(): pl.pallas_call(loss_kernel, in_specs=[SMEM_SPEC] * 3 + [vm] * 3 + [ANY] *...  16.6 us
    pallas_call x1, Pallas kernels, ffn_fwd(): pl.pallas_call(ffn_fwd_kernel, grid=(n,), in_specs=[SMEM_SPEC, SMEM_SPEC,...  13.5 us
  transfers between devices with their start and end apart: 34, of which 17 were waited for; matrix products, arithmetic and copies ran while one was open for 6% of the time, Pallas kernels for 44%

profile of v2, /device:TPU:0, one launch (start us, length us, event | category | flops | bytes accessed | tf_op | source)
XLA Modules:
  0.0 287.0 jit_solution(440703159205874271)
XLA Ops:
  0.7 3.5 %pack_weights.1 = (bf16[272,1152]{1,0:T(8,128)(2,1)}, bf16[192,1536]{1,0:T(8,128)(2,1)}, bf16[384,768]{1,0:T(8,128)(2,1)}) custom-call(s32[1]{0:T(128)} %bitcast.at_ref, f32[6,32]{1,0:T(8,128)} %bitcast.34, bf16[768,384]{1,0:T(8,128)(2,1)} %wq.9, bf16[768,384]{1,0:T(8,128)(2,1)} %wk.9, bf16[768,384]{1,0:T(8,128)(2,1)} %wv.9, bf16[384,768]{1,0:T(8,128)(2,1)} %wo_ref.1, ...), custom_call_target="tpu_custom_call" | custom-call | bytes 10800000 | tf_op jit(solution)/shard_map/pack_weights/pallas_call | solution.py:132
  4.2 3.0 %collective-permute-start = (bf16[272,1152]{1,0:T(8,128)(2,1)}, bf16[272,1152]{1,0:T(8,128)(2,1)S(1)}, u32[]{:S(2)}, u32[]{:S(2)}) collective-permute-start(bf16[272,1152]{1,0:T(8,128)(2,1)} %get-tuple-element.125), channel_id=1, source_target_pairs={{0,1},{1,0},{2,3},{3,2},{4,5},{5,4},{6,7},{7,6},{8,9},{9,8},{10,11... | collective-permute-start | bytes 1880072 | tf_op jit(solution)/shard_map/ppermute | solution.py:1111
  8.0 12.3 %attn_own.1 = (bf16[2,512,768]{2,1,0:T(8,128)(2,1)}, bf16[768,1024]{1,0:T(8,128)(2,1)}, bf16[2,512,384]{2,1,0:T(8,128)(2,1)}, bf16[2,384,512]{2,1,0:T(8,128)(2,1...) custom-call(s32[2]{0:T(128)} %copy-done.9, ...), custom_call_target="tpu_custom_call" | custom-call | bytes 43200000 | tf_op jit(solution)/shard_map/attn_own/pallas_call | solution.py:383
  25.5 4.5 %all-to-all-start = ((bf16[32,2,896]{2,1,0:T(2,128)(2,1)}), bf16[32,2,896]{2,1,0:T(2,128)(2,1)S(1)}, u32[]{:S(2)}, u32[]{:S(2)}) async-start(bf16[32,2,896]{2,1,0:T(2,128)(2,1)} %broadcast_in_dim.10), calls=%async_computation | async-start | bytes 229376 | tf_op jit(solution)/shard_map/all_to_all | solution.py:1128
  30.4 8.4 %all-to-all-done = bf16[32,2,896]{2,1,0:T(2,128)(2,1)S(1)} async-done(((bf16[32,2,896]{2,1,0:T(2,128)(2,1)}), bf16[32,2,896]{2,1,0:T(2,128)(2,1)S(1)}, u32[]{:S(2)}, u32[]{:S(2)}) %all-to-all-start) | async-done | bytes 114720 | tf_op jit(solution)/shard_map/all_to_all | solution.py:1128
  42.6 18.5 %attn_other.1 = (bf16[2,512,384]{2,1,0:T(8,128)(2,1)}, bf16[2,384,512]{2,1,0:T(8,128)(2,1)}, bf16[2,512,384]{2,1,0:T(8,128)(2,1)}, bf16[2,512,384]{2,1,0:T(8,128...) custom-call(s32[2]{0:T(128)} %copy-done.9, ...), custom_call_target="tpu_custom_call" | custom-call | bytes 54000000 | tf_op jit(solution)/shard_map/attn_other/pallas_call | solution.py:408
  66.6 13.5 %ffn_fwd.1 = (bf16[2,512,1536]{2,1,0:T(8,128)(2,1)}, bf16[2,512,1536]{2,1,0:T(8,128)(2,1)}, bf16[2,512,1536]{2,1,0:T(8,128)(2,1)}, bf16[2,512,1536]{2,1,0:T(8,12...) custom-call(s32[2]{0:T(128)} %copy-done.9, s32[1]{0:T(128)} %bitcast.at_ref, ...), custom_call_target="tpu_custom_call" | custom-call | bytes 57600000 | tf_op jit(solution)/shard_map/ffn_fwd/pallas_call | solution.py:699
  89.5 5.1 %all-to-all-start.1 = ((bf16[32,2,2304]{2,1,0:T(2,128)(2,1)}), bf16[32,2,2304]{2,1,0:T(2,128)(2,1)S(1)}, u32[]{:S(2)}, u32[]{:S(2)}) async-start(bf16[32,2,2304]{2,1,0:T(2,128)(2,1)} %bitcast.10), calls=%async_computation.1 | async-start | bytes 589824 | tf_op jit(solution)/shard_map/all_to_all | solution.py:1128
  95.9 9.8 %all-to-all-done.1 = bf16[32,2,2304]{2,1,0:T(2,128)(2,1)S(1)} async-done(((bf16[32,2,2304]{2,1,0:T(2,128)(2,1)}), bf16[32,2,2304]{2,1,0:T(2,128)(2,1)S(1)}, u32[]{:S(2)}, u32[]{:S(2)}) %all-to-all-start.1) | async-done | bytes 294944 | tf_op jit(solution)/shard_map/all_to_all | solution.py:1128
  106.5 16.6 %loss_inner.1 = (f32[8,128]{1,0:T(8,128)}, f32[8,768]{1,0:T(8,128)}, f32[8,3072]{1,0:T(8,128)}, bf16[64,768]{1,0:T(8,128)(2,1)}, bf16[64,768]{1,0:T(8,128)(2,1)}...) custom-call(s32[4]{0:T(128)} %get-tuple-element.245.me_ref, s32[1]{0:T(128)} %bitcast.at_ref, ...), custom_call_target="tpu_custom_call" | custom-call | bytes 61200000 | tf_op jit(solution)/shard_map/loss_inner/pallas_call | solution.py:845
  123.4 2.8 collective-permute-done.14
  126.2 2.6 add.92
  128.8 3.8 %all-to-all-start.2 = ((bf16[8,48,1536]{2,1,0:T(8,128)(2,1)}), bf16[8,48,1536]{2,1,0:T(8,128)(2,1)S(1)}, u32[]{:S(2)}, u32[]{:S(2)}) async-start(bf16[8,48,1536]{2,1,0:T(8,128)(2,1)} %bitcast.11), calls=%async_computation.2 | async-start | bytes 2359296 | tf_op jit(solution)/shard_map/all_to_all | solution.py:1138
  132.6 30.7 %mid_bwd.1 = (f32[1024,768]{1,0:T(8,128)}, bf16[1024,768]{1,0:T(8,128)(2,1)}, bf16[1024,1152]{1,0:T(8,128)(2,1)}, bf16[384,1536]{1,0:T(8,128)(2,1)}, bf16[384,1536]{1,0:T(8,128)(2,1)}, /*index=5*/f32[8,128]{1,0:T(8,128)}) custom-call(s32[2]{0:T(128)} %copy-done.9, s32[1]{0:T(128)} %bitcast.at_ref, f32[8,3072]{1,0:T(8,128)} %get-tuple-element.157.g_ref, ...), custom_call_target="tpu_custom_call" | custom-call | bytes 115200000 | tf_op jit(solution)/shard_map/mid_bwd/pallas_call | solution.py:952
  164.9 6.4 %all-to-all-start.3 = ((bf16[8,48,1536]{2,1,0:T(8,128)(2,1)}), bf16[8,48,1536]{2,1,0:T(8,128)(2,1)}, u32[]{:S(2)}, u32[]{:S(2)}) async-start(bf16[8,48,1536]{2,1,0:T(8,128)(2,1)} %broadcast_in_dim.13), calls=%async_computation.3 | async-start | bytes 2359296 | tf_op jit(solution)/shard_map/all_to_all | solution.py:1144
  173.9 3.0 %fusion = f32[1536,768]{1,0:T(8,128)} fusion(bf16[64,768]{1,0:T(8,128)(2,1)S(1)} %copy-done.22, bf16[64,2304]{1,0:T(8,128)(2,1)S(1)} %reshape.101), kind=kOutput, calls=%fused_computation.1 | convolution fusion | flops 150994944 | bytes 5013504 | tf_op jit(solution)/shard_map/dot_general | solution.py:31
  178.0 1.9 fusion.10
  179.9 18.5 %attn_bwd.1 = (bf16[1024,1152]{1,0:T(8,128)(2,1)}, bf16[384,1536]{1,0:T(8,128)(2,1)}, bf16[384,1536]{1,0:T(8,128)(2,1)}, f32[8,128]{1,0:T(8,128)}) custom-call(s32[2]{0:T(128)} %copy-done.9, s32[1]{0:T(128)} %bitcast.at_ref, bf16[2,512,768]{2,1,0:T(8,128)(2,1)} %bitcast.31, bf16[384,768]{1,0:T(8,128)(2,1)} %wo_ref.1, ...), custom_call_target="tpu_custom_call" | custom-call | bytes 57600000 | tf_op jit(solution)/shard_map/attn_bwd/pallas_call | solution.py:629
  198.4 2.7 collective-permute-done.17
  204.2 2.6 add_add_fusion
  206.8 5.9 %all-to-all-start.4 = ((bf16[8,48,1536]{2,1,0:T(8,128)(2,1)}), bf16[8,48,1536]{2,1,0:T(8,128)(2,1)S(1)}, u32[]{:S(2)}, u32[]{:S(2)}) async-start(bf16[8,48,1536]{2,1,0:T(8,128)(2,1)} %bitcast.14), calls=%async_computation.4 | async-start | bytes 2359296 | tf_op jit(solution)/shard_map/all_to_all | solution.py:1138
  212.7 11.6 %layer_part.1 = bf16[2,512,768]{2,1,0:T(8,128)(2,1)} custom-call(s32[1]{0:T(128)} %bitcast.at_ref, f32[2,512,768]{2,1,0:T(8,128)} %get-tuple-element.165.refs_3_.res_ref, bf16[2,512,1536]{2,1,0:T(8,128)(2,1)} %get-tuple-element.202.aa_ref, bf16[2,512,1536]{2,1,0:T(8,128)(2,1)} %get-tuple-element.203.ab_ref, bf16[1536,768]{1,0:T(8,128)(2,1)} %w_ref.2, ...), custom_call_target="tpu_custom_call" | custom-call | bytes 43200000 | tf_op jit(solution)/shard_map/layer_part/pallas_call | solution.py:1025
  224.3 11.5 %input_part.1 = f32[2,512,768]{2,1,0:T(8,128)} custom-call(s32[1]{0:T(128)} %bitcast.at_ref, bf16[2,512,768]{2,1,0:T(8,128)(2,1)} %x_ref.3, f32[1024,768]{1,0:T(8,128)} %get-tuple-element.199.dres_ref, f32[1,768]{1,0:T(1,128)} %reshape.98.gain_ref, bf16[1024,1152]{1,0:T(8,128)(2,1)} %get-tuple-element.200.ta_ref, ...), custom_call_target="tpu_custom_call" | custom-call | bytes 43200000 | tf_op jit(solution)/shard_map/input_part/pallas_call | solution.py:1000
  235.8 5.7 %all-to-all-done.4 = bf16[8,48,1536]{2,1,0:T(8,128)(2,1)S(1)} async-done(((bf16[8,48,1536]{2,1,0:T(8,128)(2,1)}), bf16[8,48,1536]{2,1,0:T(8,128)(2,1)S(1)}, u32[]{:S(2)}, u32[]{:S(2)}) %all-to-all-start.4) | async-done | bytes 1179680 | tf_op jit(solution)/shard_map/all_to_all | solution.py:1138
  242.8 4.4 %all-to-all-start.5 = ((bf16[8,48,1536]{2,1,0:T(8,128)(2,1)}), bf16[8,48,1536]{2,1,0:T(8,128)(2,1)}, u32[]{:S(2)}, u32[]{:S(2)}) async-start(bf16[8,48,1536]{2,1,0:T(8,128)(2,1)} %broadcast_in_dim.14), calls=%async_computation.5 | async-start | bytes 2359296 | tf_op jit(solution)/shard_map/all_to_all | solution.py:1144
  247.3 1.9 collective-permute-start.22
  249.2 5.8 %collective-permute-done.22 = f32[8,128]{1,0:T(8,128)S(1)} collective-permute-done((f32[8,128]{1,0:T(8,128)S(1)}, f32[8,128]{1,0:T(8,128)S(1)}, u32[]{:S(2)}, u32[]{:S(2)}) %collective-permute-start.22) | collective-permute-done | bytes 4128 | tf_op jit(solution)/shard_map/ppermute | solution.py:1111
  255.0 3.3 %collective-permute-start.23 = (f32[8,128]{1,0:T(8,128)S(1)}, f32[8,128]{1,0:T(8,128)S(1)}, u32[]{:S(2)}, u32[]{:S(2)}) collective-permute-start(f32[8,128]{1,0:T(8,128)S(1)} %add.99), channel_id=1, source_target_pairs={{0,8},{4,12},{8,0},{12,4},{16,24},{20,28},{24,16},{28,20},{1,9},{5... | collective-permute-start | bytes 12296 | tf_op jit(solution)/shard_map/ppermute | solution.py:1111
  258.3 4.8 %inner_done.1 = (f32[768,1536]{1,0:T(8,128)}, f32[24,768]{1,0:T(8,128)S(1)}) custom-call(s32[1]{0:T(128)} %bitcast.at_ref, bf16[384,1536]{1,0:T(8,128)(2,1)} %bitcast.13.own_ref, bf16[384,1536]{1,0:T(8,128)(2,1)S(1)} %collective-permute-done.20.near_ref, bf16[768,1536]{1,0:T(8,128)(2,1)S(1)} %copy-done), custom_call_target="tpu_custom_call" | custom-call | bytes 18000000 | tf_op jit(solution)/shard_map/inner_done/pallas_call | solution.py:1059
  266.1 4.6 %collective-permute-start.24 = (f32[8,128]{1,0:T(8,128)S(1)}, f32[8,128]{1,0:T(8,128)S(1)}, u32[]{:S(2)}, u32[]{:S(2)}) collective-permute-start(f32[8,128]{1,0:T(8,128)S(1)} %add.100), channel_id=1, source_target_pairs={{0,16},{4,20},{8,24},{12,28},{16,0},{20,4},{24,8},{28,12},{1,17},{... | collective-permute-start | bytes 12296 | tf_op jit(solution)/shard_map/ppermute | solution.py:1111
  271.2 4.5 %collective-permute-done.24 = f32[8,128]{1,0:T(8,128)S(1)} collective-permute-done((f32[8,128]{1,0:T(8,128)S(1)}, f32[8,128]{1,0:T(8,128)S(1)}, u32[]{:S(2)}, u32[]{:S(2)}) %collective-permute-start.24) | collective-permute-done | bytes 4128 | tf_op jit(solution)/shard_map/ppermute | solution.py:1111
  276.8 2.9 %attn_done.2 = (f32[768,384]{1,0:T(8,128)}, f32[768,384]{1,0:T(8,128)}, f32[768,384]{1,0:T(8,128)}, f32[384,768]{1,0:T(8,128)}, f32[8,384]{1,0:T(8,128)S(1)}) custom-call(s32[1]{0:T(128)} %bitcast.15.half_ref, bf16[384,1536]{1,0:T(8,128)(2,1)} %bitcast.16.sum_ref, bf16[768,384]{1,0:T(8,128)(2,1)S(1)} %copy-done.1, bf16[768,384]{1,0:T(8,128)(2,1)S(1)} %copy-done.2, ...), custom_call_target="tpu_custom_call" | custom-call | bytes 10800000 | tf_op jit(solution)/shard_map/attn_done/pallas_call | solution.py:1090
  (155 shorter events, 48.8 us)
Async XLA Ops:
  4.2 17.4 %collective-permute-start = (bf16[272,1152]{1,0:T(8,128)(2,1)}, bf16[272,1152]{1,0:T(8,128)(2,1)S(1)}, u32[]{:S(2)}, u32[]{:S(2)}) collective-permute-start(bf16[272,1152]{1,0:T(8,128)(2,1)} %get-tuple-element.125), channel_id=1, source_target_pairs={{0,1},{1,0},{2,3},{3,2},{4,5},{5,4},{6,7},{7,6},{8,9},{9,8},{10,11... | collective-permute-start | bytes 1880072 | tf_op jit(solution)/shard_map/ppermute | solution.py:1111
  21.5 17.3 %collective-permute-start.4 = (bf16[272,1152]{1,0:T(8,128)(2,1)S(1)}, bf16[272,1152]{1,0:T(8,128)(2,1)S(1)}, u32[]{:S(2)}, u32[]{:S(2)}) collective-permute-start(bf16[272,1152]{1,0:T(8,128)(2,1)S(1)} %collective-permute-done.p0.refs_11_), channel_id=1, source_target_pairs={{0,4},{4,0},{8,12},{12,8},{16,20},{20,16},{24,28},{28,24},{1,5},{5... | collective-permute-start | bytes 1880072 | tf_op jit(solution)/shard_map/ppermute | solution.py:1111
  23.2 17.1 %collective-permute-start.1 = (bf16[192,1536]{1,0:T(8,128)(2,1)}, bf16[192,1536]{1,0:T(8,128)(2,1)}, u32[]{:S(2)}, u32[]{:S(2)}) collective-permute-start(bf16[192,1536]{1,0:T(8,128)(2,1)} %get-tuple-element.129), channel_id=1, source_target_pairs={{0,1},{1,0},{2,3},{3,2},{4,5},{5,4},{6,7},{7,6},{8,9},{9,8},{10,11... | collective-permute-start | bytes 1769480 | tf_op jit(solution)/shard_map/ppermute | solution.py:1111
  25.5 13.4 %all-to-all-start = ((bf16[32,2,896]{2,1,0:T(2,128)(2,1)}), bf16[32,2,896]{2,1,0:T(2,128)(2,1)S(1)}, u32[]{:S(2)}, u32[]{:S(2)}) async-start(bf16[32,2,896]{2,1,0:T(2,128)(2,1)} %broadcast_in_dim.10), calls=%async_computation | async-start | bytes 229376 | tf_op jit(solution)/shard_map/all_to_all | solution.py:1128
  30.0 11.6 %collective-permute-start.5 = (bf16[272,1152]{1,0:T(8,128)(2,1)S(1)}, bf16[272,1152]{1,0:T(8,128)(2,1)S(1)}, u32[]{:S(2)}, u32[]{:S(2)}) collective-permute-start(bf16[272,1152]{1,0:T(8,128)(2,1)S(1)} %collective-permute-done.p0.refs_11_), channel_id=1, source_target_pairs={{0,2},{2,0},{1,3},{3,1},{4,6},{6,4},{5,7},{7,5},{8,10},{10,8},{9,1... | collective-permute-start | bytes 1880072 | tf_op jit(solution)/shard_map/ppermute | solution.py:1111
  38.8 2.8 collective-permute-start.6
  38.9 22.3 %collective-permute-start.3 = (bf16[384,768]{1,0:T(8,128)(2,1)S(1)}, bf16[384,768]{1,0:T(8,128)(2,1)S(1)}, u32[]{:S(2)}, u32[]{:S(2)}) collective-permute-start(bf16[384,768]{1,0:T(8,128)(2,1)S(1)} %copy-done.28), channel_id=1, source_target_pairs={{0,1},{1,0},{2,3},{3,2},{4,5},{5,4},{6,7},{7,6},{8,9},{9,8},{10,11... | collective-permute-start | bytes 1769480 | tf_op jit(solution)/shard_map/ppermute | solution.py:1111
  40.3 20.9 %collective-permute-start.2 = (bf16[192,1536]{1,0:T(8,128)(2,1)}, bf16[192,1536]{1,0:T(8,128)(2,1)}, u32[]{:S(2)}, u32[]{:S(2)}) collective-permute-start(bf16[192,1536]{1,0:T(8,128)(2,1)} %collective-permute-done.1.p0.refs_15_), channel_id=1, source_target_pairs={{0,4},{4,0},{8,12},{12,8},{16,20},{20,16},{24,28},{28,24},{1,5},{5... | collective-permute-start | bytes 1769480 | tf_op jit(solution)/shard_map/ppermute | solution.py:1111
  61.2 20.7 %collective-permute-start.10 = (bf16[1,512,768]{2,1,0:T(8,128)(2,1)}, bf16[1,512,768]{2,1,0:T(8,128)(2,1)S(1)}, u32[]{:S(2)}, u32[]{:S(2)}) collective-permute-start(bf16[1,512,768]{2,1,0:T(8,128)(2,1)} %get-tuple-element.147), channel_id=1, source_target_pairs={{0,1},{1,0},{2,3},{3,2},{4,5},{5,4},{6,7},{7,6},{8,9},{9,8},{10,11... | collective-permute-start | bytes 2359304 | tf_op jit(solution)/shard_map/ppermute | solution.py:1111
  62.7 2.3 collective-permute-start.8
  62.8 3.1 %collective-permute-start.9 = (bf16[192,1536]{1,0:T(8,128)(2,1)}, bf16[192,1536]{1,0:T(8,128)(2,1)S(1)}, u32[]{:S(2)}, u32[]{:S(2)}) collective-permute-start(bf16[192,1536]{1,0:T(8,128)(2,1)} %collective-permute-done.2.p1.refs_16_), channel_id=1, source_target_pairs={{0,2},{2,0},{1,3},{3,1},{4,6},{6,4},{5,7},{7,5},{8,10},{10,8},{9,1... | collective-permute-start | bytes 1769480 | tf_op jit(solution)/shard_map/ppermute | solution.py:1111
  63.3 16.8 %collective-permute-start.7 = (bf16[384,768]{1,0:T(8,128)(2,1)S(1)}, bf16[384,768]{1,0:T(8,128)(2,1)S(1)}, u32[]{:S(2)}, u32[]{:S(2)}) collective-permute-start(bf16[384,768]{1,0:T(8,128)(2,1)S(1)} %collective-permute-done.3.p0), channel_id=1, source_target_pairs={{0,4},{4,0},{8,12},{12,8},{16,20},{20,16},{24,28},{28,24},{1,5},{5... | collective-permute-start | bytes 1769480 | tf_op jit(solution)/shard_map/ppermute | solution.py:1111
  63.7 42.8 %collective-permute-start.13 = (bf16[1,512,768]{2,1,0:T(8,128)(2,1)}, bf16[1,512,768]{2,1,0:T(8,128)(2,1)}, u32[]{:S(2)}, u32[]{:S(2)}) collective-permute-start(bf16[1,512,768]{2,1,0:T(8,128)(2,1)} %get-tuple-element.156), channel_id=1, source_target_pairs={{0,1},{1,0},{2,3},{3,2},{4,5},{5,4},{6,7},{7,6},{8,9},{9,8},{10,11... | collective-permute-start | bytes 2359304 | tf_op jit(solution)/shard_map/ppermute | solution.py:1111
  82.7 2.8 collective-permute-start.12
  89.5 16.3 %all-to-all-start.1 = ((bf16[32,2,2304]{2,1,0:T(2,128)(2,1)}), bf16[32,2,2304]{2,1,0:T(2,128)(2,1)S(1)}, u32[]{:S(2)}, u32[]{:S(2)}) async-start(bf16[32,2,2304]{2,1,0:T(2,128)(2,1)} %bitcast.10), calls=%async_computation.1 | async-start | bytes 589824 | tf_op jit(solution)/shard_map/all_to_all | solution.py:1128
  123.1 3.1 %collective-permute-start.14 = (bf16[384,1536]{1,0:T(8,128)(2,1)}, bf16[384,1536]{1,0:T(8,128)(2,1)S(1)}, u32[]{:S(2)}, u32[]{:S(2)}) collective-permute-start(bf16[384,1536]{1,0:T(8,128)(2,1)} %get-tuple-element.162), channel_id=1, source_target_pairs={{0,2},{2,0},{1,3},{3,1},{4,6},{6,4},{5,7},{7,5},{8,10},{10,8},{9,1... | collective-permute-start | bytes 3538952 | tf_op jit(solution)/shard_map/ppermute | solution.py:1111
  128.8 34.7 %all-to-all-start.2 = ((bf16[8,48,1536]{2,1,0:T(8,128)(2,1)}), bf16[8,48,1536]{2,1,0:T(8,128)(2,1)S(1)}, u32[]{:S(2)}, u32[]{:S(2)}) async-start(bf16[8,48,1536]{2,1,0:T(8,128)(2,1)} %bitcast.11), calls=%async_computation.2 | async-start | bytes 2359296 | tf_op jit(solution)/shard_map/all_to_all | solution.py:1138
  163.3 8.0 %collective-permute-start.15 = (bf16[384,1536]{1,0:T(8,128)(2,1)}, bf16[384,1536]{1,0:T(8,128)(2,1)}, u32[]{:S(2)}, u32[]{:S(2)}) collective-permute-start(bf16[384,1536]{1,0:T(8,128)(2,1)} %get-tuple-element.174), channel_id=1, source_target_pairs={{0,2},{2,0},{1,3},{3,1},{4,6},{6,4},{5,7},{7,5},{8,10},{10,8},{9,1... | collective-permute-start | bytes 3538952 | tf_op jit(solution)/shard_map/ppermute | solution.py:1111
  164.9 36.3 %all-to-all-start.3 = ((bf16[8,48,1536]{2,1,0:T(8,128)(2,1)}), bf16[8,48,1536]{2,1,0:T(8,128)(2,1)}, u32[]{:S(2)}, u32[]{:S(2)}) async-start(bf16[8,48,1536]{2,1,0:T(8,128)(2,1)} %broadcast_in_dim.13), calls=%async_computation.3 | async-start | bytes 2359296 | tf_op jit(solution)/shard_map/all_to_all | solution.py:1144
  172.9 28.2 %collective-permute-start.16 = (bf16[384,1536]{1,0:T(8,128)(2,1)S(1)}, bf16[384,1536]{1,0:T(8,128)(2,1)S(1)}, u32[]{:S(2)}, u32[]{:S(2)}) collective-permute-start(bf16[384,1536]{1,0:T(8,128)(2,1)S(1)} %add.93), channel_id=1, source_target_pairs={{0,1},{1,0},{2,3},{3,2},{4,5},{5,4},{6,7},{7,6},{8,9},{9,8},{10,11... | collective-permute-start | bytes 3538952 | tf_op jit(solution)/shard_map/ppermute | solution.py:1111
  176.9 24.2 %collective-permute-start.17 = (f32[8,128]{1,0:T(8,128)S(1)}, f32[8,128]{1,0:T(8,128)S(1)}, u32[]{:S(2)}, u32[]{:S(2)}) collective-permute-start(f32[8,128]{1,0:T(8,128)S(1)} %copy-done.29), channel_id=1, source_target_pairs={{0,1},{1,0},{2,3},{3,2},{4,5},{5,4},{6,7},{7,6},{8,9},{9,8},{10,11... | collective-permute-start | bytes 12296 | tf_op jit(solution)/shard_map/ppermute | solution.py:1111
  201.1 3.1 %collective-permute-start.18 = (bf16[384,1536]{1,0:T(8,128)(2,1)}, bf16[384,1536]{1,0:T(8,128)(2,1)S(1)}, u32[]{:S(2)}, u32[]{:S(2)}) collective-permute-start(bf16[384,1536]{1,0:T(8,128)(2,1)} %get-tuple-element.195), channel_id=1, source_target_pairs={{0,2},{2,0},{1,3},{3,1},{4,6},{6,4},{5,7},{7,5},{8,10},{10,8},{9,1... | collective-permute-start | bytes 3538952 | tf_op jit(solution)/shard_map/ppermute | solution.py:1111
  201.8 2.2 collective-permute-start.19
  206.8 34.7 %all-to-all-start.4 = ((bf16[8,48,1536]{2,1,0:T(8,128)(2,1)}), bf16[8,48,1536]{2,1,0:T(8,128)(2,1)S(1)}, u32[]{:S(2)}, u32[]{:S(2)}) async-start(bf16[8,48,1536]{2,1,0:T(8,128)(2,1)} %bitcast.14), calls=%async_computation.4 | async-start | bytes 2359296 | tf_op jit(solution)/shard_map/all_to_all | solution.py:1138
  242.8 32.9 %all-to-all-start.5 = ((bf16[8,48,1536]{2,1,0:T(8,128)(2,1)}), bf16[8,48,1536]{2,1,0:T(8,128)(2,1)}, u32[]{:S(2)}, u32[]{:S(2)}) async-start(bf16[8,48,1536]{2,1,0:T(8,128)(2,1)} %broadcast_in_dim.14), calls=%async_computation.5 | async-start | bytes 2359296 | tf_op jit(solution)/shard_map/all_to_all | solution.py:1144
  247.2 11.1 %collective-permute-start.20 = (bf16[384,1536]{1,0:T(8,128)(2,1)}, bf16[384,1536]{1,0:T(8,128)(2,1)S(1)}, u32[]{:S(2)}, u32[]{:S(2)}) collective-permute-start(bf16[384,1536]{1,0:T(8,128)(2,1)} %bitcast.13.own_ref), channel_id=1, source_target_pairs={{0,2},{2,0},{1,3},{3,1},{4,6},{6,4},{5,7},{7,5},{8,10},{10,8},{9,1... | collective-permute-start | bytes 3538952 | tf_op jit(solution)/shard_map/ppermute | solution.py:1111
  247.3 7.7 %collective-permute-start.22 = (f32[8,128]{1,0:T(8,128)S(1)}, f32[8,128]{1,0:T(8,128)S(1)}, u32[]{:S(2)}, u32[]{:S(2)}) collective-permute-start(f32[8,128]{1,0:T(8,128)S(1)} %add.98), channel_id=1, source_target_pairs={{0,4},{4,0},{8,12},{12,8},{16,20},{20,16},{24,28},{28,24},{1,5},{5... | collective-permute-start | bytes 12296 | tf_op jit(solution)/shard_map/ppermute | solution.py:1111
  255.0 11.0 %collective-permute-start.23 = (f32[8,128]{1,0:T(8,128)S(1)}, f32[8,128]{1,0:T(8,128)S(1)}, u32[]{:S(2)}, u32[]{:S(2)}) collective-permute-start(f32[8,128]{1,0:T(8,128)S(1)} %add.99), channel_id=1, source_target_pairs={{0,8},{4,12},{8,0},{12,4},{16,24},{20,28},{24,16},{28,20},{1,9},{5... | collective-permute-start | bytes 12296 | tf_op jit(solution)/shard_map/ppermute | solution.py:1111
  264.6 6.0 %collective-permute-start.21 = (f32[768]{0:T(1024)S(1)}, f32[768]{0:T(1024)S(1)}, u32[]{:S(2)}, u32[]{:S(2)}) collective-permute-start(f32[768]{0:T(1024)S(1)} %reduce_sum.45), channel_id=1, source_target_pairs={{0,1},{1,0},{2,3},{3,2},{4,5},{5,4},{6,7},{7,6},{8,9},{9,8},{10,11... | collective-permute-start | bytes 9224 | tf_op jit(solution)/shard_map/ppermute | solution.py:1111
  266.1 9.6 %collective-permute-start.24 = (f32[8,128]{1,0:T(8,128)S(1)}, f32[8,128]{1,0:T(8,128)S(1)}, u32[]{:S(2)}, u32[]{:S(2)}) collective-permute-start(f32[8,128]{1,0:T(8,128)S(1)} %add.100), channel_id=1, source_target_pairs={{0,16},{4,20},{8,24},{12,28},{16,0},{20,4},{24,8},{28,12},{1,17},{... | collective-permute-start | bytes 12296 | tf_op jit(solution)/shard_map/ppermute | solution.py:1111
  275.7 7.7 %collective-permute-start.26 = (bf16[384,1536]{1,0:T(8,128)(2,1)}, bf16[384,1536]{1,0:T(8,128)(2,1)S(1)}, u32[]{:S(2)}, u32[]{:S(2)}) collective-permute-start(bf16[384,1536]{1,0:T(8,128)(2,1)} %bitcast.16.sum_ref), channel_id=1, source_target_pairs={{0,2},{2,0},{1,3},{3,1},{4,6},{6,4},{5,7},{7,5},{8,10},{10,8},{9,1... | collective-permute-start | bytes 3538952 | tf_op jit(solution)/shard_map/ppermute | solution.py:1111
  279.8 3.6 %collective-permute-start.25 = (f32[384]{0:T(512)S(1)}, f32[384]{0:T(512)S(1)}, u32[]{:S(2)}, u32[]{:S(2)}) collective-permute-start(f32[384]{0:T(512)S(1)} %slice_reduce_fusion), channel_id=1, source_target_pairs={{0,1},{1,0},{2,3},{3,2},{4,5},{5,4},{6,7},{7,6},{8,9},{9,8},{10,11... | collective-permute-start | bytes 4616 | tf_op jit(solution)/shard_map/ppermute | solution.py:1111
  (32 other events, 269.5 us)

commit v3 on v2

--- a/solution.py
+++ b/solution.py
@@ -428,7 +428,7 @@
         compiler_params=params(),
         cost_estimate=cost(15),
         name="attn_other",
-    )(lens, at, an, hot, gain.reshape(1, d), x, ctx_a, wo, *packs)
+    )(lens, at, an, hot, gain, x, ctx_a, wo, *packs)
 
 
 def attn_back(b, n, length, core, w, d_attn, ins, outs, scratch, late):
@@ -745,16 +745,49 @@
     )(lens, at, asum, rsum, *packs)
 
 
-def loss_kernel(me_ref, at_ref, lens, pool_ref, q_ref, wp_ref, fint_hbm, gp_hbm, fn0, fn1, wi_hbm, wu_hbm, p0, p1, p2, p3, *refs):
+def pre_kernel(lens, fint_ref, gp_ref, fn_ref, w_ref, out_ref, ft_ref, v_ref, s_ref):
+    n, seq, _ = gp_ref.shape
+
+    @pl.when(pl.program_id(0) == 0)
+    def _():
+        valid = lax.broadcasted_iota(jnp.int32, (seq, TILE), 0) < lens[n]
+        ft_ref[...] = jnp.transpose((fn_ref[0].astype(F32) * valid.astype(F32)[:, :1]).astype(BF))
+
+    v_ref[...] = mm(fn_ref[0], w_ref[...])
+    for i in range(n):
+        out_ref[i] = mm(fint_ref[:, seq * i : seq * (i + 1)], gp_ref[i]).astype(BF)
+        for r in range(seq // TILE // n):
+            at = slice(seq // n * i + TILE * r, seq // n * i + TILE * (r + 1))
+            s_ref[at, :] = gelu_parts(v_ref[at, :])[1].astype(BF)
+    out_ref[n] = mm(ft_ref[...], s_ref[...]).astype(BF)
+
+
+def pre_inner(lens4, fint, gp, fn, wi):
+    n, seq, half = gp.shape
+    d = fint.shape[0]
+    chunk = 512
+    return pl.pallas_call(
+        pre_kernel,
+        grid=(half // chunk,),
+        in_specs=[SMEM_SPEC, const_spec(fint.shape), pl.BlockSpec((n, seq, chunk), lambda c: (0, 0, c))]
+        + [const_spec(fn.shape), pl.BlockSpec((d, chunk), lambda c: (0, c))],
+        out_specs=pl.BlockSpec((n + 1, d, chunk), lambda c: (0, 0, c)),
+        out_shape=sds((n + 1, d, half), BF),
+        scratch_shapes=[pltpu.VMEM((d, seq), BF), pltpu.VMEM((seq, chunk), F32), pltpu.VMEM((seq, chunk), BF)],
+        compiler_params=params(),
+        cost_estimate=cost(9),
+        name="pre_inner",
+    )(lens4, fint, gp, fn, wi)
+
+
+def loss_kernel(me_ref, at_ref, lens, pool_ref, q_ref, wp_hbm, pre_hbm, fn_hbm, wi_hbm, wu_hbm, *refs):
     (loss_ref, row_ref, g_ref, drow_ref, demb_ref, send_ref, keep_ref) = refs[:7]
-    (wu_ref, wb_ref, gp_ref, fnb_ref, wi_ref, ft_ref, gn_ref, v_ref, d_ref, sum_ref, sem, sem2) = refs[7:]
-    copies = join_copies(at_ref[0], (p0, p1, p2, p3), wb_ref, sem)
-    moves = [(wu_hbm, wu_ref), (wi_hbm, wi_ref), (gp_hbm, gp_ref)]
-    moves.append((fint_hbm, ft_ref.at[:, pl.ds(0, fint_hbm.shape[1])]))
-    moves += [(f, fnb_ref.at[pl.ds(i, 1)]) for i, f in enumerate((fn0, fn1))]
-    loads = [pltpu.make_async_copy(a, b, sem2.at[i]) for i, (a, b) in enumerate(moves)]
-    for c in [loads[0]] + copies + loads[1:]:
+    (wp_ref, wu_ref, pre_ref, fn_ref, wi_ref, ft_ref, gn_ref, v_ref, d_ref, sum_ref, sem) = refs[7:]
+    moves = ((wp_hbm, wp_ref), (wu_hbm, wu_ref), (fn_hbm, fn_ref), (wi_hbm, wi_ref), (pre_hbm, pre_ref))
+    loads = [pltpu.make_async_copy(a, b, sem.at[i]) for i, (a, b) in enumerate(moves)]
+    for c in loads:
         c.start()
+    loads[0].wait()
     d = wp_ref.shape[0]
     count = pool_ref.shape[0]
     pooled = pool_ref[...]
@@ -780,7 +813,9 @@
     drow_ref[...] = rows.astype(BF)
     index = lax.broadcasted_iota(jnp.int32, (count, 1), 0)
     pick = lambda t, i: jnp.sum(jnp.where(index == i, t, 0.0), axis=0, keepdims=True)
-    n, seq, half = gp_ref.shape
+    seq = fn_ref.shape[1]
+    half = wi_ref.shape[1]
+    n = pre_ref.shape[0] - 1
     own = [pick(rows, me_ref[i]) for i in range(n)]
     near = [pick(rows, me_ref[n + i]) for i in range(n)]
     lost = jnp.broadcast_to(loss, (count, TILE))
@@ -788,97 +823,89 @@
     row_ref[...] = jnp.concatenate(own + [pad], axis=0)
     loss_ref[...] = jnp.concatenate([pick(lost, me_ref[i]) for i in range(n)] + [pad[:, :TILE]], axis=0)
     four = jnp.concatenate(own + near + [jnp.zeros((16 - 2 * n, d), F32)], axis=0).astype(BF)
-    loads[0].wait()
-    ga = mm(four, wu_ref[...], NT)
-    gn_ref[...] = ga[:8]
-    for c in copies:
+    loads[1].wait()
+    gn_ref[...] = mm(four, wu_ref[...], NT)[:8]
+    g_ref[...] = gn_ref[...]
+    for c in loads[2:]:
         c.wait()
-    g_ref[:, :half] = ga[:8]
-    g_ref[:, half:] = mm(four, wb_ref[...], NT)[:8]
-    for c in loads[1:]:
-        c.wait()
-
-    tokens = n * seq
-    for i in range(n):
-        valid = lax.broadcasted_iota(jnp.int32, (seq, TILE), 0) < lens[n + i]
-        fin = (fnb_ref[i].astype(F32) * valid.astype(F32)[:, :1]).astype(BF)
-        ft_ref[:, tokens + seq * i : tokens + seq * (i + 1)] = jnp.transpose(fin)
-    chunk = v_ref.shape[3]
+
+    last = 2 * n - 1
+    valid = lax.broadcasted_iota(jnp.int32, (seq, TILE), 0) < lens[last]
+    ft_ref[...] = jnp.transpose((fn_ref[0].astype(F32) * valid.astype(F32)[:, :1]).astype(BF))
+    chunk = v_ref.shape[2]
     steps = half // chunk
     spot = lambda c: slice(c * chunk, (c + 1) * chunk)
-
-    def project(c):
-        for i in range(n):
-            v_ref[c % 2, i] = mm(fnb_ref[i], wi_ref[:, spot(c)])
-
-    def scale(c):
-        for i in range(n):
-            at = slice(seq * i, seq * (i + 1))
-            d_ref[c % 2, at, :] = (gp_ref[i, :, spot(c)].astype(F32) * gn_ref[i : i + 1, spot(c)]).astype(BF)
-            for r in range(seq // TILE):
-                part = slice(TILE * r, TILE * (r + 1))
-                slope = gelu_parts(v_ref[c % 2, i, part, :])[1]
-                one = slope * gn_ref[n + i : n + i + 1, spot(c)]
-                base = tokens + seq * i + TILE * r
-                d_ref[c % 2, base : base + TILE, :] = one.astype(BF)
-
     rows2 = d // 2
     core = at_ref[0] // 2
+
+    def project(c):
+        v_ref[c % 2] = mm(fn_ref[0], wi_ref[:, spot(c)])
+
+    def scale(c):
+        for r in range(seq // TILE):
+            at = slice(TILE * r, TILE * (r + 1))
+            slope = gelu_parts(v_ref[c % 2, at, :])[1]
+            d_ref[c % 2, at, :] = (slope * gn_ref[last : last + 1, spot(c)]).astype(BF)
+
     project(0)
     scale(0)
     for c in range(steps):
         if c + 1 < steps:
             project(c + 1)
-        sum_ref[...] = mm(ft_ref[...], d_ref[c % 2]).astype(BF)
+        for r in range(d // TILE):
+            at = slice(TILE * r, TILE * (r + 1))
+            total = mm(ft_ref[at, :], d_ref[c % 2])
+            for i in range(n + 1):
+                total = total + pre_ref[i, at, spot(c)].astype(F32) * gn_ref[i : i + 1, spot(c)]
+            sum_ref[at, :] = total.astype(BF)
         for ref, side in ((send_ref, 1 - core), (keep_ref, core)):
             ref[:, spot(c)] = sum_ref[pl.ds(pl.multiple_of(side * rows2, rows2), rows2), :]
         if c + 1 < steps:
             scale(c + 1)
 
 
-def loss_all(me, at, lens4, pooled, queries, wp, fint, gp, fin_nb, wi, wu, packs):
+def loss_all(me, at, lens4, pooled, queries, wp, pre, fn, wi, wu):
     half, d = wu.shape
-    n, seq, _ = gp.shape
+    seq = fn.shape[1]
     count = pooled.shape[0]
     chunk = 512
     vm = pl.BlockSpec(memory_space=pltpu.VMEM)
     return pl.pallas_call(
         loss_kernel,
-        in_specs=[SMEM_SPEC] * 3 + [vm] * 3 + [ANY] * 10,
+        in_specs=[SMEM_SPEC] * 3 + [vm] * 2 + [ANY] * 5,
         out_specs=[vm] * 7,
         out_shape=[
             sds((8, TILE), F32),
             sds((8, d), F32),
-            sds((8, 2 * half), F32),
+            sds((8, half), F32),
             sds((count, d), BF),
             sds((count, d), BF),
             sds((d // 2, half), BF),
             sds((d // 2, half), BF),
         ],
         scratch_shapes=[
+            pltpu.VMEM(wp.shape, BF),
             pltpu.VMEM(wu.shape, BF),
-            pltpu.VMEM(wu.shape, BF),
-            pltpu.VMEM(gp.shape, BF),
-            pltpu.VMEM((n, seq, d), BF),
+            pltpu.VMEM(pre.shape, BF),
+            pltpu.VMEM(fn.shape, BF),
             pltpu.VMEM(wi.shape, BF),
-            pltpu.VMEM((d, 2 * n * seq), BF),
+            pltpu.VMEM((d, seq), BF),
             pltpu.VMEM((8, half), F32),
-            pltpu.VMEM((2, n, seq, chunk), F32),
-            pltpu.VMEM((2, 2 * n * seq, chunk), BF),
+            pltpu.VMEM((2, seq, chunk), F32),
+            pltpu.VMEM((2, seq, chunk), BF),
             pltpu.VMEM((d, chunk), BF),
-            pltpu.SemaphoreType.DMA((4,)),
-            pltpu.SemaphoreType.DMA((6,)),
+            pltpu.SemaphoreType.DMA((5,)),
         ],
         compiler_params=params(),
-        cost_estimate=cost(17),
+        cost_estimate=cost(12),
         name="loss_inner",
-    )(me, at, lens4, pooled, queries, wp, fint, gp, *fin_nb, wi, wu, *packs)
+    )(me, at, lens4, pooled, queries, wp, pre, fn, wi, wu)
 
 
 def mid_bwd_kernel(lens, at_ref, g_ref, row_ref, gain_ref, hot_ref, lse_ref, tf_ref, *refs):
-    hbm, packs0, packs1 = refs[:11], refs[11:15], refs[15:19]
-    (dres_hbm, dattn_hbm), outs, scratch = refs[19:21], refs[21:25], refs[25:35]
-    bufs, (wib_ref, wob_ref, d_ref, dres_ref, sem, sem0, sem1, sem2) = refs[35:46], refs[46:]
+    hbm, packs0, packs1, packs2 = refs[:11], refs[11:15], refs[15:19], refs[19:23]
+    (dres_hbm, dattn_hbm), outs, scratch = refs[23:25], refs[25:29], refs[29:39]
+    bufs, (wib_ref, wob_ref, wub_ref, gb_ref, d_ref, dres_ref, sem, sem0, sem1, sem2, sem3) = refs[39:50], refs[50:]
     da_ref = scratch[7]
     wi_ref, gpa_ref, gpb_ref, res_all, q, qt, k, v, ct, nb, ant = bufs
     b = pl.program_id(0)
@@ -886,6 +913,7 @@
     copies = [pltpu.make_async_copy(x, y, sem.at[i]) for i, (x, y) in enumerate(zip(hbm, bufs))]
     copies0 = out_copies(at_ref[0], packs0, wob_ref, sem0)
     copies1 = join_copies(at_ref[0], packs1, wib_ref, sem1)
+    copies1 += join_copies(at_ref[0], packs2, wub_ref, sem3)
 
     def first(group):
         @pl.when(b == 0)
@@ -907,7 +935,7 @@
 
     def scale(t):
         gp, _, c = parts[t]
-        g = g_ref[pl.ds(b, 1), t * chunk : (t + 1) * chunk]
+        g = (g_ref if t < steps else gb_ref)[pl.ds(b, 1), c * chunk : (c + 1) * chunk]
         d_ref[t % 2] = (gp[b, :, c * chunk : (c + 1) * chunk].astype(F32) * g).astype(BF)
 
     d_two = None
@@ -915,6 +943,12 @@
     for t, (_, w, c) in enumerate(parts):
         if t + 1 == steps:
             first(copies[2:4] + copies1)
+
+            @pl.when(b == 0)
+            def _():
+                rows = jnp.concatenate([row_ref[...], jnp.zeros_like(row_ref)], axis=0).astype(BF)
+                gb_ref[...] = mm(rows, wub_ref[...], NT)[:8]
+
         if t + 1 < len(parts):
             scale(t + 1)
         one = mm(d_ref[t % 2], w[:, c * chunk : (c + 1) * chunk], NT)
@@ -942,7 +976,7 @@
             c.wait()
 
 
-def mid_bwd(lens, at, g, row, gain, hot, lse, tf, arrays, packs0, packs1):
+def mid_bwd(lens, at, g, row, gain, hot, lse, tf, arrays, packs0, packs1, packs2):
     wi, _, _, res = arrays[:4]
     n, seq, d = res.shape
     half = wi.shape[1]
@@ -956,7 +990,7 @@
         + [const_spec(x.shape) for x in (g, row)]
         + [const_spec((1, d))]
         + [const_spec(x.shape) for x in (hot, lse, tf)]
-        + [ANY] * 19,
+        + [ANY] * 23,
         out_specs=[ANY] * 2 + specs,
         out_shape=more + outs,
         scratch_shapes=back_scratch(n, seq, width, d)
@@ -964,17 +998,20 @@
         + [
             pltpu.VMEM((d, half), BF),
             pltpu.VMEM((width, d), BF),
+            pltpu.VMEM((half, d), BF),
+            pltpu.VMEM((8, half), F32),
             pltpu.VMEM((2, seq, 512), BF),
             pltpu.VMEM((n * seq, d), F32),
             pltpu.SemaphoreType.DMA((11,)),
             pltpu.SemaphoreType.DMA((12,)),
             pltpu.SemaphoreType.DMA((4,)),
             pltpu.SemaphoreType.DMA((2, n)),
+            pltpu.SemaphoreType.DMA((4,)),
         ],
         compiler_params=params(),
         cost_estimate=cost(32),
         name="mid_bwd",
-    )(lens, at, g, row, gain.reshape(1, d), hot, lse, tf, *arrays, *packs0, *packs1)
+    )(lens, at, g, row, gain.reshape(1, d), hot, lse, tf, *arrays, *packs0, *packs1, *packs2)
 
 
 def input_kernel(at_ref, x_ref, dres_ref, gain_ref, ta_ref, tb_ref, wq, wk, wv, p0, p1, p2, p3, out_ref, w_ref, sem):
@@ -1184,6 +1221,9 @@
     packs = pack_weights(at, turned, w_query, w_key, w_value, w_out, w_inner, w_outer)
     y_attn = pc.across(packs[0])
 
+    base = (2 * pc.chip + pc.core) * pc.tensor * n
+    me = jnp.stack([base + pc.ti * n, base + pc.ti * n + 1, base + (1 - pc.ti) * n, base + (1 - pc.ti) * n + 1])
+
     qf = queries.astype(F32)
     q_unit = (qf * lax.rsqrt(jnp.sum(qf * qf, axis=-1, keepdims=True) + EPS)).astype(BF)
     ints = jnp.stack([positives // 256, positives % 256, lens // 256, lens % 256], axis=1)
@@ -1197,12 +1237,12 @@
     y_inner, y_outer = [pc.across(p) for p in packs]
     x_attn = pc.side(y_attn)
     q_all = pc.share(jnp.broadcast_to(q_all[None], (devices,) + q_all.shape))
-    x_attn, q_all = after(x_attn, q_all)
+    x_attn, q_all, lens4, me, gain_two = after(x_attn, q_all, lens4, me, gain_ffn.reshape(1, d))
     p_attn = pc.spread(y_attn, x_attn)
     y_inner, an = after(y_inner, an)
     x_inner = pc.side(y_inner)
     q_b, qt_b, k_b, v_b, ctxt_b, lse_b, nb_b, tf_b, res, fin, fint, rsum, *fins = attn_other(
-        lens, at, an, hot_t, hidden_in, ctx_a, w_out, gain_ffn, p_attn
+        lens, at, an, hot_t, hidden_in, ctx_a, w_out, gain_two, p_attn
     )
     y_inner, x_inner, y_outer, fin, *fins = after(y_inner, x_inner, y_outer, fin, *fins)
     x_outer = pc.side(y_outer)
@@ -1217,12 +1257,11 @@
     sums = jnp.where(pc.ti > 0, jnp.stack([sums_b, sums_a]), jnp.stack([sums_a, sums_b]))
     msg = jnp.concatenate([jnp.broadcast_to(pooled[None], (2,) + pooled.shape), sums], axis=2)
     msg = jnp.broadcast_to(msg[None], (2 * pc.chips,) + msg.shape).reshape((devices,) + msg.shape[1:])
-    got = pc.share(msg).reshape(devices * n, -1)
+    got, pre = after(pc.share(msg), pre_inner(lens4, fint, gp_a, fin_nb[0], w_inner))
+    got = got.reshape(devices * n, -1)
     pooled = got[:, :d]
-    base = (2 * pc.chip + pc.core) * pc.tensor * n
-    me = jnp.stack([base + pc.ti * n, base + pc.ti * n + 1, base + (1 - pc.ti) * n, base + (1 - pc.ti) * n + 1])
     loss8, row8, g8, d_rows, d_emb, gi_send, gi_keep = loss_all(
-        me, at, lens4, pooled, q_all.reshape(devices * n, -1), w_proj, fint, gp_a, fin_nb, w_inner, w_outer, p_outer
+        me, at, lens4, pooled, q_all.reshape(devices * n, -1), w_proj, pre, fin_nb[1], w_inner, w_outer
     )
     query_loss = loss8[:n, 0]
 
@@ -1230,7 +1269,7 @@
     inner_parts = pc.exchange(inner_half)
     arrays = [w_inner, gp_a, gp_b, res, q_b, qt_b, k_b, v_b, ctxt_b, nb_b, ant]
     d_res, d_attn, tok_b, send_b, keep_b, table_b = mid_bwd(
-        lens, at, g8, row8, gain_ffn, hot_back, lse_b, tf_b, arrays, p_attn, p_inner
+        lens, at, g8, row8, gain_ffn, hot_back, lse_b, tf_b, arrays, p_attn, p_inner, p_outer
     )
     inner_part, d_attn = after(pc.add(inner_parts), d_attn)
     inner_all = pc.gather(inner_part)
@@ -1255,7 +1294,9 @@
     table_sum = pc.total(table + near_table)
     gain_ffn_part = jnp.sum(gain_ffn_part[::8], axis=0)
     gain_ffn_grad = (gain_ffn_part + pc.across(gain_ffn_part)) / gain_ffn
-    attn_all, gain_ffn_grad, table_sum, inner_sum = after(attn_all, gain_ffn_grad, table_sum, inner_sum)
+    attn_all, gain_ffn_grad, table_sum, inner_sum, query_loss = after(
+        attn_all, gain_ffn_grad, table_sum, inner_sum, query_loss
+    )
     half = pc.core.reshape(1)
     near = pc.core_swap(attn_all)
     *grads, gain_own = attn_done(half, attn_all, w_query, w_key, w_value)

time: 292 us -> 289 us (0.990)
  waiting for transfers between devices: 49.7 us -> 39 us
  Pallas kernels: 147 us -> 153 us
    all_to_all x2, waiting for transfers between devices: 18.3 us -> 7.14 us  [share(): return lax.all_to_all(x, ('chip', 'core', 'tensor'), 0, 0, tiled=True)]
    pallas_call x1 -> x2, Pallas kernels: 16.6 us -> 21.8 us  [the longest x1 11.5 us: loss_all(): pl.pallas_call(loss_kernel, in_specs=[SMEM_SPEC] * 3 + [vm] * 2 + [ANY] *...]
  transfers between devices with their start and end apart: 34 -> 34, of which waited for: 17 -> 17; matrix products, arithmetic and copies ran while one was open for 6% -> 7% of each run, Pallas kernels for 44% -> 48%
where the time goes in v3:
time: 289 us; the launch traced here: 284 us
  Pallas kernels  153 us (53%)
  starting transfers between devices  60 us (21%)
  waiting for transfers between devices  39 us (13%)
  local copies, waits for them, and re-layouts  14.5 us (5%)
  other arithmetic  11.3 us (4%)
  matrix products  4.9 us (2%)
    pallas_call x1, Pallas kernels, mid_bwd(): pl.pallas_call(mid_bwd_kernel, grid=(n,), in_specs=[SMEM_SPEC, SMEM_SPEC]...  31.1 us
    ppermute x28, starting transfers between devices, swap(): return lax.ppermute(x, axis, [(i, i ^ bit) for i in range(size)])  27.7 us
    ppermute x28, waiting for transfers between devices, swap(): return lax.ppermute(x, axis, [(i, i ^ bit) for i in range(size)])  26.1 us
    pallas_call x1, Pallas kernels, attn_other(): pl.pallas_call(attn_other_kernel, grid=(n,), in_specs=[SMEM_SPEC, SMEM_SP...  18.5 us
    pallas_call x1, Pallas kernels, attn_bwd(): pl.pallas_call(attn_bwd_kernel, grid=(n,), in_specs=[SMEM_SPEC, SMEM_SPEC...  18.4 us
    pallas_call x1, Pallas kernels, ffn_fwd(): pl.pallas_call(ffn_fwd_kernel, grid=(n,), in_specs=[SMEM_SPEC, SMEM_SPEC,...  13.5 us
    pallas_call x1, Pallas kernels, attn_own(): pl.pallas_call(attn_own_kernel, grid=(n,), in_specs=[SMEM_SPEC, row_spec(...  12.3 us
    all_to_all x2, starting transfers between devices, exchange(): lax.all_to_all(x.reshape(self.chips, rows // self.chips, width), 'chip',...  12.2 us
  transfers between devices with their start and end apart: 34, of which 17 were waited for; matrix products, arithmetic and copies ran while one was open for 7% of the time, Pallas kernels for 48%

profile of v3, /device:TPU:0, one launch (start us, length us, event | category | flops | bytes accessed | tf_op | source)
XLA Modules:
  0.0 284.1 jit_solution(7120680358281171560)
XLA Ops:
  0.7 3.5 %pack_weights.1 = (bf16[272,1152]{1,0:T(8,128)(2,1)}, bf16[192,1536]{1,0:T(8,128)(2,1)}, bf16[384,768]{1,0:T(8,128)(2,1)}) custom-call(s32[1]{0:T(128)} %bitcast.at_ref, f32[6,32]{1,0:T(8,128)} %bitcast.34, bf16[768,384]{1,0:T(8,128)(2,1)} %wq.9, bf16[768,384]{1,0:T(8,128)(2,1)} %wk.9, bf16[768,384]{1,0:T(8,128)(2,1)} %wv.9, bf16[384,768]{1,0:T(8,128)(2,1)} %wo_ref.1, ...), custom_call_target="tpu_custom_call" | custom-call | bytes 10800000 | tf_op jit(solution)/shard_map/pack_weights/pallas_call | solution.py:132
  4.2 3.0 %collective-permute-start = (bf16[272,1152]{1,0:T(8,128)(2,1)}, bf16[272,1152]{1,0:T(8,128)(2,1)S(1)}, u32[]{:S(2)}, u32[]{:S(2)}) collective-permute-start(bf16[272,1152]{1,0:T(8,128)(2,1)} %get-tuple-element.131), channel_id=1, source_target_pairs={{0,1},{1,0},{2,3},{3,2},{4,5},{5,4},{6,7},{7,6},{8,9},{9,8},{10,11... | collective-permute-start | bytes 1880072 | tf_op jit(solution)/shard_map/ppermute | solution.py:1148
  8.0 12.3 %attn_own.1 = (bf16[2,512,768]{2,1,0:T(8,128)(2,1)}, bf16[768,1024]{1,0:T(8,128)(2,1)}, bf16[2,512,384]{2,1,0:T(8,128)(2,1)}, bf16[2,384,512]{2,1,0:T(8,128)(2,1...) custom-call(s32[2]{0:T(128)} %copy-done.10, ...), custom_call_target="tpu_custom_call" | custom-call | bytes 43200000 | tf_op jit(solution)/shard_map/attn_own/pallas_call | solution.py:383
  25.5 4.2 %all-to-all-start = ((bf16[32,2,896]{2,1,0:T(2,128)(2,1)}), bf16[32,2,896]{2,1,0:T(2,128)(2,1)S(1)}, u32[]{:S(2)}, u32[]{:S(2)}) async-start(bf16[32,2,896]{2,1,0:T(2,128)(2,1)} %broadcast_in_dim.10), calls=%async_computation | async-start | bytes 229376 | tf_op jit(solution)/shard_map/all_to_all | solution.py:1165
  31.9 6.9 %all-to-all-done = bf16[32,2,896]{2,1,0:T(2,128)(2,1)S(1)} async-done(((bf16[32,2,896]{2,1,0:T(2,128)(2,1)}), bf16[32,2,896]{2,1,0:T(2,128)(2,1)S(1)}, u32[]{:S(2)}, u32[]{:S(2)}) %all-to-all-start) | async-done | bytes 114720 | tf_op jit(solution)/shard_map/all_to_all | solution.py:1165
  42.1 18.5 %attn_other.1 = (bf16[2,512,384]{2,1,0:T(8,128)(2,1)}, bf16[2,384,512]{2,1,0:T(8,128)(2,1)}, bf16[2,512,384]{2,1,0:T(8,128)(2,1)}, bf16[2,512,384]{2,1,0:T(8,128...) custom-call(s32[2]{0:T(128)} %copy-done.10, ...), custom_call_target="tpu_custom_call" | custom-call | bytes 54000000 | tf_op jit(solution)/shard_map/attn_other/pallas_call | solution.py:408
  66.1 13.5 %ffn_fwd.1 = (bf16[2,512,1536]{2,1,0:T(8,128)(2,1)}, bf16[2,512,1536]{2,1,0:T(8,128)(2,1)}, bf16[2,512,1536]{2,1,0:T(8,128)(2,1)}, bf16[2,512,1536]{2,1,0:T(8,12...) custom-call(s32[2]{0:T(128)} %copy-done.10, s32[1]{0:T(128)} %bitcast.at_ref, ...), custom_call_target="tpu_custom_call" | custom-call | bytes 57600000 | tf_op jit(solution)/shard_map/ffn_fwd/pallas_call | solution.py:699
  88.9 5.2 %all-to-all-start.1 = ((bf16[32,2,2304]{2,1,0:T(2,128)(2,1)}), bf16[32,2,2304]{2,1,0:T(2,128)(2,1)S(1)}, u32[]{:S(2)}, u32[]{:S(2)}) async-start(bf16[32,2,2304]{2,1,0:T(2,128)(2,1)} %bitcast.10), calls=%async_computation.1 | async-start | bytes 589824 | tf_op jit(solution)/shard_map/all_to_all | solution.py:1165
  94.8 10.3 %pre_inner.1.pre_hbm = bf16[3,768,1536]{2,1,0:T(8,128)(2,1)} custom-call(s32[4]{0:T(128)} %get-tuple-element.138.lens, bf16[768,1024]{1,0:T(8,128)(2,1)} %get-tuple-element.161.fint_ref, bf16[2,512,1536]{2,1,0:T(8,128)(2,1)} %get-tuple-element.174.gp_ref.refs_1_, bf16[1,512,768]{2,1,0:T(8,128)(2,1)} %copy-done.21, bf16[768,1536]{1,0:T(8,128)(2,1)} %w_ref.5), custom_call_target="tpu_custom_call" | custom-call | bytes 32400000 | tf_op jit(solution)/shard_map/pre_inner/pallas_call | solution.py:769
  106.1 11.5 %loss_inner.1 = (f32[8,128]{1,0:T(8,128)}, f32[8,768]{1,0:T(8,128)}, f32[8,1536]{1,0:T(8,128)}, bf16[64,768]{1,0:T(8,128)(2,1)}, bf16[64,768]{1,0:T(8,128)(2,1)}...) custom-call(s32[4]{0:T(128)} %get-tuple-element.137.me_ref, s32[1]{0:T(128)} %bitcast.at_ref, ...), custom_call_target="tpu_custom_call" | custom-call | bytes 43200000 | tf_op jit(solution)/shard_map/loss_inner/pallas_call | solution.py:873
  117.9 2.8 collective-permute-done.14
  120.8 2.6 add.92
  123.3 6.2 %all-to-all-start.2 = ((bf16[8,48,1536]{2,1,0:T(8,128)(2,1)}), bf16[8,48,1536]{2,1,0:T(8,128)(2,1)S(1)}, u32[]{:S(2)}, u32[]{:S(2)}) async-start(bf16[8,48,1536]{2,1,0:T(8,128)(2,1)} %bitcast.11), calls=%async_computation.2 | async-start | bytes 2359296 | tf_op jit(solution)/shard_map/all_to_all | solution.py:1175
  129.5 31.1 %mid_bwd.1 = (f32[1024,768]{1,0:T(8,128)}, bf16[1024,768]{1,0:T(8,128)(2,1)}, bf16[1024,1152]{1,0:T(8,128)(2,1)}, bf16[384,1536]{1,0:T(8,128)(2,1)}, bf16[384,1536]{1,0:T(8,128)(2,1)}, /*index=5*/f32[8,128]{1,0:T(8,128)}) custom-call(s32[2]{0:T(128)} %copy-done.10, s32[1]{0:T(128)} %bitcast.at_ref, f32[8,1536]{1,0:T(8,128)} %get-tuple-element.168.g_ref, ...), custom_call_target="tpu_custom_call" | custom-call | bytes 115200000 | tf_op jit(solution)/shard_map/mid_bwd/pallas_call | solution.py:986
  162.0 6.4 %all-to-all-start.3 = ((bf16[8,48,1536]{2,1,0:T(8,128)(2,1)}), bf16[8,48,1536]{2,1,0:T(8,128)(2,1)}, u32[]{:S(2)}, u32[]{:S(2)}) async-start(bf16[8,48,1536]{2,1,0:T(8,128)(2,1)} %broadcast_in_dim.13), calls=%async_computation.3 | async-start | bytes 2359296 | tf_op jit(solution)/shard_map/all_to_all | solution.py:1181
  171.5 3.0 %fusion = f32[1536,768]{1,0:T(8,128)} fusion(bf16[64,768]{1,0:T(8,128)(2,1)S(1)} %copy-done.23, bf16[64,2304]{1,0:T(8,128)(2,1)S(1)} %reshape.101), kind=kOutput, calls=%fused_computation.1 | convolution fusion | flops 150994944 | bytes 5013504 | tf_op jit(solution)/shard_map/dot_general | solution.py:31
  175.1 1.9 fusion.10
  177.0 18.4 %attn_bwd.1 = (bf16[1024,1152]{1,0:T(8,128)(2,1)}, bf16[384,1536]{1,0:T(8,128)(2,1)}, bf16[384,1536]{1,0:T(8,128)(2,1)}, f32[8,128]{1,0:T(8,128)}) custom-call(s32[2]{0:T(128)} %copy-done.10, s32[1]{0:T(128)} %bitcast.at_ref, bf16[2,512,768]{2,1,0:T(8,128)(2,1)} %bitcast.31, bf16[384,768]{1,0:T(8,128)(2,1)} %wo_ref.1, ...), custom_call_target="tpu_custom_call" | custom-call | bytes 57600000 | tf_op jit(solution)/shard_map/attn_bwd/pallas_call | solution.py:629
  195.4 2.8 %collective-permute-done.17 = f32[8,128]{1,0:T(8,128)S(1)} collective-permute-done((f32[8,128]{1,0:T(8,128)S(1)}, f32[8,128]{1,0:T(8,128)S(1)}, u32[]{:S(2)}, u32[]{:S(2)}) %collective-permute-start.17) | collective-permute-done | bytes 4128 | tf_op jit(solution)/shard_map/ppermute | solution.py:1148
  201.3 2.5 add_add_fusion
  203.8 6.0 %all-to-all-start.4 = ((bf16[8,48,1536]{2,1,0:T(8,128)(2,1)}), bf16[8,48,1536]{2,1,0:T(8,128)(2,1)S(1)}, u32[]{:S(2)}, u32[]{:S(2)}) async-start(bf16[8,48,1536]{2,1,0:T(8,128)(2,1)} %bitcast.14), calls=%async_computation.4 | async-start | bytes 2359296 | tf_op jit(solution)/shard_map/all_to_all | solution.py:1175
  209.7 11.6 %layer_part.1 = bf16[2,512,768]{2,1,0:T(8,128)(2,1)} custom-call(s32[1]{0:T(128)} %bitcast.at_ref, f32[2,512,768]{2,1,0:T(8,128)} %get-tuple-element.176.refs_3_.res_ref, bf16[2,512,1536]{2,1,0:T(8,128)(2,1)} %get-tuple-element.213.aa_ref, bf16[2,512,1536]{2,1,0:T(8,128)(2,1)} %get-tuple-element.214.ab_ref, bf16[1536,768]{1,0:T(8,128)(2,1)} %w_ref.4, ...), custom_call_target="tpu_custom_call" | custom-call | bytes 43200000 | tf_op jit(solution)/shard_map/layer_part/pallas_call | solution.py:1062
  221.3 11.5 %input_part.1 = f32[2,512,768]{2,1,0:T(8,128)} custom-call(s32[1]{0:T(128)} %bitcast.at_ref, bf16[2,512,768]{2,1,0:T(8,128)(2,1)} %x_ref.3, f32[1024,768]{1,0:T(8,128)} %get-tuple-element.210.dres_ref, f32[1,768]{1,0:T(1,128)} %reshape.98.gain_ref, bf16[1024,1152]{1,0:T(8,128)(2,1)} %get-tuple-element.211.ta_ref, ...), custom_call_target="tpu_custom_call" | custom-call | bytes 43200000 | tf_op jit(solution)/shard_map/input_part/pallas_call | solution.py:1037
  232.8 5.7 %all-to-all-done.4 = bf16[8,48,1536]{2,1,0:T(8,128)(2,1)S(1)} async-done(((bf16[8,48,1536]{2,1,0:T(8,128)(2,1)}), bf16[8,48,1536]{2,1,0:T(8,128)(2,1)S(1)}, u32[]{:S(2)}, u32[]{:S(2)}) %all-to-all-start.4) | async-done | bytes 1179680 | tf_op jit(solution)/shard_map/all_to_all | solution.py:1175
  239.9 4.4 %all-to-all-start.5 = ((bf16[8,48,1536]{2,1,0:T(8,128)(2,1)}), bf16[8,48,1536]{2,1,0:T(8,128)(2,1)}, u32[]{:S(2)}, u32[]{:S(2)}) async-start(bf16[8,48,1536]{2,1,0:T(8,128)(2,1)} %broadcast_in_dim.14), calls=%async_computation.5 | async-start | bytes 2359296 | tf_op jit(solution)/shard_map/all_to_all | solution.py:1181
  244.4 1.9 collective-permute-start.22
  247.4 4.8 %inner_done.1 = (f32[768,1536]{1,0:T(8,128)}, f32[24,768]{1,0:T(8,128)S(1)}) custom-call(s32[1]{0:T(128)} %bitcast.at_ref, bf16[384,1536]{1,0:T(8,128)(2,1)} %bitcast.13.own_ref, bf16[384,1536]{1,0:T(8,128)(2,1)S(1)} %collective-permute-done.20.near_ref, bf16[768,1536]{1,0:T(8,128)(2,1)S(1)} %copy-done), custom_call_target="tpu_custom_call" | custom-call | bytes 18000000 | tf_op jit(solution)/shard_map/inner_done/pallas_call | solution.py:1096
  258.4 4.7 %collective-permute-done.23 = f32[8,128]{1,0:T(8,128)S(1)} collective-permute-done((f32[8,128]{1,0:T(8,128)S(1)}, f32[8,128]{1,0:T(8,128)S(1)}, u32[]{:S(2)}, u32[]{:S(2)}) %collective-permute-start.23) | collective-permute-done | bytes 4128 | tf_op jit(solution)/shard_map/ppermute | solution.py:1148
  263.1 4.6 %collective-permute-start.24 = (f32[8,128]{1,0:T(8,128)S(1)}, f32[8,128]{1,0:T(8,128)S(1)}, u32[]{:S(2)}, u32[]{:S(2)}) collective-permute-start(f32[8,128]{1,0:T(8,128)S(1)} %add.100), channel_id=1, source_target_pairs={{0,16},{4,20},{8,24},{12,28},{16,0},{20,4},{24,8},{28,12},{1,17},{... | collective-permute-start | bytes 12296 | tf_op jit(solution)/shard_map/ppermute | solution.py:1148
  268.3 4.5 %collective-permute-done.24 = f32[8,128]{1,0:T(8,128)S(1)} collective-permute-done((f32[8,128]{1,0:T(8,128)S(1)}, f32[8,128]{1,0:T(8,128)S(1)}, u32[]{:S(2)}, u32[]{:S(2)}) %collective-permute-start.24) | collective-permute-done | bytes 4128 | tf_op jit(solution)/shard_map/ppermute | solution.py:1148
  273.8 3.0 %attn_done.2 = (f32[768,384]{1,0:T(8,128)}, f32[768,384]{1,0:T(8,128)}, f32[768,384]{1,0:T(8,128)}, f32[384,768]{1,0:T(8,128)}, f32[8,384]{1,0:T(8,128)S(1)}) custom-call(s32[1]{0:T(128)} %bitcast.16.half_ref, bf16[384,1536]{1,0:T(8,128)(2,1)} %bitcast.15.sum_ref, bf16[768,384]{1,0:T(8,128)(2,1)S(1)} %copy-done.1, bf16[768,384]{1,0:T(8,128)(2,1)S(1)} %copy-done.2, ...), custom_call_target="tpu_custom_call" | custom-call | bytes 10800000 | tf_op jit(solution)/shard_map/attn_done/pallas_call | solution.py:1127
  278.4 2.1 collective-permute-done.25
  (162 shorter events, 51.6 us)
Async XLA Ops:
  4.2 17.4 %collective-permute-start = (bf16[272,1152]{1,0:T(8,128)(2,1)}, bf16[272,1152]{1,0:T(8,128)(2,1)S(1)}, u32[]{:S(2)}, u32[]{:S(2)}) collective-permute-start(bf16[272,1152]{1,0:T(8,128)(2,1)} %get-tuple-element.131), channel_id=1, source_target_pairs={{0,1},{1,0},{2,3},{3,2},{4,5},{5,4},{6,7},{7,6},{8,9},{9,8},{10,11... | collective-permute-start | bytes 1880072 | tf_op jit(solution)/shard_map/ppermute | solution.py:1148
  21.5 17.3 %collective-permute-start.1 = (bf16[272,1152]{1,0:T(8,128)(2,1)S(1)}, bf16[272,1152]{1,0:T(8,128)(2,1)S(1)}, u32[]{:S(2)}, u32[]{:S(2)}) collective-permute-start(bf16[272,1152]{1,0:T(8,128)(2,1)S(1)} %collective-permute-done.p0.refs_11_), channel_id=1, source_target_pairs={{0,4},{4,0},{8,12},{12,8},{16,20},{20,16},{24,28},{28,24},{1,5},{5... | collective-permute-start | bytes 1880072 | tf_op jit(solution)/shard_map/ppermute | solution.py:1148
  23.2 17.1 %collective-permute-start.2 = (bf16[192,1536]{1,0:T(8,128)(2,1)}, bf16[192,1536]{1,0:T(8,128)(2,1)}, u32[]{:S(2)}, u32[]{:S(2)}) collective-permute-start(bf16[192,1536]{1,0:T(8,128)(2,1)} %get-tuple-element.139), channel_id=1, source_target_pairs={{0,1},{1,0},{2,3},{3,2},{4,5},{5,4},{6,7},{7,6},{8,9},{9,8},{10,11... | collective-permute-start | bytes 1769480 | tf_op jit(solution)/shard_map/ppermute | solution.py:1148
  25.5 13.4 %all-to-all-start = ((bf16[32,2,896]{2,1,0:T(2,128)(2,1)}), bf16[32,2,896]{2,1,0:T(2,128)(2,1)S(1)}, u32[]{:S(2)}, u32[]{:S(2)}) async-start(bf16[32,2,896]{2,1,0:T(2,128)(2,1)} %broadcast_in_dim.10), calls=%async_computation | async-start | bytes 229376 | tf_op jit(solution)/shard_map/all_to_all | solution.py:1165
  31.5 9.5 %collective-permute-start.5 = (bf16[272,1152]{1,0:T(8,128)(2,1)S(1)}, bf16[272,1152]{1,0:T(8,128)(2,1)S(1)}, u32[]{:S(2)}, u32[]{:S(2)}) collective-permute-start(bf16[272,1152]{1,0:T(8,128)(2,1)S(1)} %collective-permute-done.p0.refs_11_), channel_id=1, source_target_pairs={{0,2},{2,0},{1,3},{3,1},{4,6},{6,4},{5,7},{7,5},{8,10},{10,8},{9,1... | collective-permute-start | bytes 1880072 | tf_op jit(solution)/shard_map/ppermute | solution.py:1148
  38.8 2.2 collective-permute-start.6
  38.9 21.7 %collective-permute-start.4 = (bf16[384,768]{1,0:T(8,128)(2,1)S(1)}, bf16[384,768]{1,0:T(8,128)(2,1)S(1)}, u32[]{:S(2)}, u32[]{:S(2)}) collective-permute-start(bf16[384,768]{1,0:T(8,128)(2,1)S(1)} %copy-done.31), channel_id=1, source_target_pairs={{0,1},{1,0},{2,3},{3,2},{4,5},{5,4},{6,7},{7,6},{8,9},{9,8},{10,11... | collective-permute-start | bytes 1769480 | tf_op jit(solution)/shard_map/ppermute | solution.py:1148
  40.3 20.3 %collective-permute-start.3 = (bf16[192,1536]{1,0:T(8,128)(2,1)}, bf16[192,1536]{1,0:T(8,128)(2,1)}, u32[]{:S(2)}, u32[]{:S(2)}) collective-permute-start(bf16[192,1536]{1,0:T(8,128)(2,1)} %collective-permute-done.2.p0.refs_15_), channel_id=1, source_target_pairs={{0,4},{4,0},{8,12},{12,8},{16,20},{20,16},{24,28},{28,24},{1,5},{5... | collective-permute-start | bytes 1769480 | tf_op jit(solution)/shard_map/ppermute | solution.py:1148
  60.6 20.7 %collective-permute-start.10 = (bf16[1,512,768]{2,1,0:T(8,128)(2,1)}, bf16[1,512,768]{2,1,0:T(8,128)(2,1)S(1)}, u32[]{:S(2)}, u32[]{:S(2)}) collective-permute-start(bf16[1,512,768]{2,1,0:T(8,128)(2,1)} %get-tuple-element.156), channel_id=1, source_target_pairs={{0,1},{1,0},{2,3},{3,2},{4,5},{5,4},{6,7},{7,6},{8,9},{9,8},{10,11... | collective-permute-start | bytes 2359304 | tf_op jit(solution)/shard_map/ppermute | solution.py:1148
  62.2 2.4 collective-permute-start.8
  62.2 3.1 %collective-permute-start.9 = (bf16[192,1536]{1,0:T(8,128)(2,1)}, bf16[192,1536]{1,0:T(8,128)(2,1)S(1)}, u32[]{:S(2)}, u32[]{:S(2)}) collective-permute-start(bf16[192,1536]{1,0:T(8,128)(2,1)} %collective-permute-done.3.p1.refs_16_), channel_id=1, source_target_pairs={{0,2},{2,0},{1,3},{3,1},{4,6},{6,4},{5,7},{7,5},{8,10},{10,8},{9,1... | collective-permute-start | bytes 1769480 | tf_op jit(solution)/shard_map/ppermute | solution.py:1148
  62.7 16.8 %collective-permute-start.7 = (bf16[384,768]{1,0:T(8,128)(2,1)S(1)}, bf16[384,768]{1,0:T(8,128)(2,1)S(1)}, u32[]{:S(2)}, u32[]{:S(2)}) collective-permute-start(bf16[384,768]{1,0:T(8,128)(2,1)S(1)} %collective-permute-done.4.p0.refs_19_), channel_id=1, source_target_pairs={{0,4},{4,0},{8,12},{12,8},{16,20},{20,16},{24,28},{28,24},{1,5},{5... | collective-permute-start | bytes 1769480 | tf_op jit(solution)/shard_map/ppermute | solution.py:1148
  63.2 42.9 %collective-permute-start.13 = (bf16[1,512,768]{2,1,0:T(8,128)(2,1)}, bf16[1,512,768]{2,1,0:T(8,128)(2,1)}, u32[]{:S(2)}, u32[]{:S(2)}) collective-permute-start(bf16[1,512,768]{2,1,0:T(8,128)(2,1)} %get-tuple-element.167), channel_id=1, source_target_pairs={{0,1},{1,0},{2,3},{3,2},{4,5},{5,4},{6,7},{7,6},{8,9},{9,8},{10,11... | collective-permute-start | bytes 2359304 | tf_op jit(solution)/shard_map/ppermute | solution.py:1148
  82.2 2.8 collective-permute-start.12
  88.9 16.4 %all-to-all-start.1 = ((bf16[32,2,2304]{2,1,0:T(2,128)(2,1)}), bf16[32,2,2304]{2,1,0:T(2,128)(2,1)S(1)}, u32[]{:S(2)}, u32[]{:S(2)}) async-start(bf16[32,2,2304]{2,1,0:T(2,128)(2,1)} %bitcast.10), calls=%async_computation.1 | async-start | bytes 589824 | tf_op jit(solution)/shard_map/all_to_all | solution.py:1165
  117.6 3.1 %collective-permute-start.14 = (bf16[384,1536]{1,0:T(8,128)(2,1)}, bf16[384,1536]{1,0:T(8,128)(2,1)S(1)}, u32[]{:S(2)}, u32[]{:S(2)}) collective-permute-start(bf16[384,1536]{1,0:T(8,128)(2,1)} %get-tuple-element.173), channel_id=1, source_target_pairs={{0,2},{2,0},{1,3},{3,1},{4,6},{6,4},{5,7},{7,5},{8,10},{10,8},{9,1... | collective-permute-start | bytes 3538952 | tf_op jit(solution)/shard_map/ppermute | solution.py:1148
  123.3 37.4 %all-to-all-start.2 = ((bf16[8,48,1536]{2,1,0:T(8,128)(2,1)}), bf16[8,48,1536]{2,1,0:T(8,128)(2,1)S(1)}, u32[]{:S(2)}, u32[]{:S(2)}) async-start(bf16[8,48,1536]{2,1,0:T(8,128)(2,1)} %bitcast.11), calls=%async_computation.2 | async-start | bytes 2359296 | tf_op jit(solution)/shard_map/all_to_all | solution.py:1175
  160.6 7.8 %collective-permute-start.15 = (bf16[384,1536]{1,0:T(8,128)(2,1)}, bf16[384,1536]{1,0:T(8,128)(2,1)}, u32[]{:S(2)}, u32[]{:S(2)}) collective-permute-start(bf16[384,1536]{1,0:T(8,128)(2,1)} %get-tuple-element.185), channel_id=1, source_target_pairs={{0,2},{2,0},{1,3},{3,1},{4,6},{6,4},{5,7},{7,5},{8,10},{10,8},{9,1... | collective-permute-start | bytes 3538952 | tf_op jit(solution)/shard_map/ppermute | solution.py:1148
  162.0 36.2 %all-to-all-start.3 = ((bf16[8,48,1536]{2,1,0:T(8,128)(2,1)}), bf16[8,48,1536]{2,1,0:T(8,128)(2,1)}, u32[]{:S(2)}, u32[]{:S(2)}) async-start(bf16[8,48,1536]{2,1,0:T(8,128)(2,1)} %broadcast_in_dim.13), calls=%async_computation.3 | async-start | bytes 2359296 | tf_op jit(solution)/shard_map/all_to_all | solution.py:1181
  170.0 28.2 %collective-permute-start.16 = (bf16[384,1536]{1,0:T(8,128)(2,1)S(1)}, bf16[384,1536]{1,0:T(8,128)(2,1)S(1)}, u32[]{:S(2)}, u32[]{:S(2)}) collective-permute-start(bf16[384,1536]{1,0:T(8,128)(2,1)S(1)} %add.93), channel_id=1, source_target_pairs={{0,1},{1,0},{2,3},{3,2},{4,5},{5,4},{6,7},{7,6},{8,9},{9,8},{10,11... | collective-permute-start | bytes 3538952 | tf_op jit(solution)/shard_map/ppermute | solution.py:1148
  174.5 23.7 %collective-permute-start.17 = (f32[8,128]{1,0:T(8,128)S(1)}, f32[8,128]{1,0:T(8,128)S(1)}, u32[]{:S(2)}, u32[]{:S(2)}) collective-permute-start(f32[8,128]{1,0:T(8,128)S(1)} %copy-done.32), channel_id=1, source_target_pairs={{0,1},{1,0},{2,3},{3,2},{4,5},{5,4},{6,7},{7,6},{8,9},{9,8},{10,11... | collective-permute-start | bytes 12296 | tf_op jit(solution)/shard_map/ppermute | solution.py:1148
  198.2 3.1 %collective-permute-start.18 = (bf16[384,1536]{1,0:T(8,128)(2,1)}, bf16[384,1536]{1,0:T(8,128)(2,1)S(1)}, u32[]{:S(2)}, u32[]{:S(2)}) collective-permute-start(bf16[384,1536]{1,0:T(8,128)(2,1)} %get-tuple-element.206), channel_id=1, source_target_pairs={{0,2},{2,0},{1,3},{3,1},{4,6},{6,4},{5,7},{7,5},{8,10},{10,8},{9,1... | collective-permute-start | bytes 3538952 | tf_op jit(solution)/shard_map/ppermute | solution.py:1148
  198.9 2.2 collective-permute-start.19
  203.8 34.8 %all-to-all-start.4 = ((bf16[8,48,1536]{2,1,0:T(8,128)(2,1)}), bf16[8,48,1536]{2,1,0:T(8,128)(2,1)S(1)}, u32[]{:S(2)}, u32[]{:S(2)}) async-start(bf16[8,48,1536]{2,1,0:T(8,128)(2,1)} %bitcast.14), calls=%async_computation.4 | async-start | bytes 2359296 | tf_op jit(solution)/shard_map/all_to_all | solution.py:1175
  239.9 32.9 %all-to-all-start.5 = ((bf16[8,48,1536]{2,1,0:T(8,128)(2,1)}), bf16[8,48,1536]{2,1,0:T(8,128)(2,1)}, u32[]{:S(2)}, u32[]{:S(2)}) async-start(bf16[8,48,1536]{2,1,0:T(8,128)(2,1)} %broadcast_in_dim.14), calls=%async_computation.5 | async-start | bytes 2359296 | tf_op jit(solution)/shard_map/all_to_all | solution.py:1181
  244.3 3.1 %collective-permute-start.20 = (bf16[384,1536]{1,0:T(8,128)(2,1)}, bf16[384,1536]{1,0:T(8,128)(2,1)S(1)}, u32[]{:S(2)}, u32[]{:S(2)}) collective-permute-start(bf16[384,1536]{1,0:T(8,128)(2,1)} %bitcast.13.own_ref), channel_id=1, source_target_pairs={{0,2},{2,0},{1,3},{3,1},{4,6},{6,4},{5,7},{7,5},{8,10},{10,8},{9,1... | collective-permute-start | bytes 3538952 | tf_op jit(solution)/shard_map/ppermute | solution.py:1148
  244.4 10.9 %collective-permute-start.22 = (f32[8,128]{1,0:T(8,128)S(1)}, f32[8,128]{1,0:T(8,128)S(1)}, u32[]{:S(2)}, u32[]{:S(2)}) collective-permute-start(f32[8,128]{1,0:T(8,128)S(1)} %add.98), channel_id=1, source_target_pairs={{0,4},{4,0},{8,12},{12,8},{16,20},{20,16},{24,28},{28,24},{1,5},{5... | collective-permute-start | bytes 12296 | tf_op jit(solution)/shard_map/ppermute | solution.py:1148
  253.7 14.0 %collective-permute-start.21 = (f32[768]{0:T(1024)S(1)}, f32[768]{0:T(1024)S(1)}, u32[]{:S(2)}, u32[]{:S(2)}) collective-permute-start(f32[768]{0:T(1024)S(1)} %reduce_sum.45), channel_id=1, source_target_pairs={{0,1},{1,0},{2,3},{3,2},{4,5},{5,4},{6,7},{7,6},{8,9},{9,8},{10,11... | collective-permute-start | bytes 9224 | tf_op jit(solution)/shard_map/ppermute | solution.py:1148
  255.3 7.8 %collective-permute-start.23 = (f32[8,128]{1,0:T(8,128)S(1)}, f32[8,128]{1,0:T(8,128)S(1)}, u32[]{:S(2)}, u32[]{:S(2)}) collective-permute-start(f32[8,128]{1,0:T(8,128)S(1)} %add.99), channel_id=1, source_target_pairs={{0,8},{4,12},{8,0},{12,4},{16,24},{20,28},{24,16},{28,20},{1,9},{5... | collective-permute-start | bytes 12296 | tf_op jit(solution)/shard_map/ppermute | solution.py:1148
  263.1 9.6 %collective-permute-start.24 = (f32[8,128]{1,0:T(8,128)S(1)}, f32[8,128]{1,0:T(8,128)S(1)}, u32[]{:S(2)}, u32[]{:S(2)}) collective-permute-start(f32[8,128]{1,0:T(8,128)S(1)} %add.100), channel_id=1, source_target_pairs={{0,16},{4,20},{8,24},{12,28},{16,0},{20,4},{24,8},{28,12},{1,17},{... | collective-permute-start | bytes 12296 | tf_op jit(solution)/shard_map/ppermute | solution.py:1148
  272.7 7.8 %collective-permute-start.26 = (bf16[384,1536]{1,0:T(8,128)(2,1)}, bf16[384,1536]{1,0:T(8,128)(2,1)S(1)}, u32[]{:S(2)}, u32[]{:S(2)}) collective-permute-start(bf16[384,1536]{1,0:T(8,128)(2,1)} %bitcast.15.sum_ref), channel_id=1, source_target_pairs={{0,2},{2,0},{1,3},{3,1},{4,6},{6,4},{5,7},{7,5},{8,10},{10,8},{9,1... | collective-permute-start | bytes 3538952 | tf_op jit(solution)/shard_map/ppermute | solution.py:1148
  276.8 3.6 %collective-permute-start.25 = (f32[384]{0:T(512)S(1)}, f32[384]{0:T(512)S(1)}, u32[]{:S(2)}, u32[]{:S(2)}) collective-permute-start(f32[384]{0:T(512)S(1)} %slice_reduce_fusion), channel_id=1, source_target_pairs={{0,1},{1,0},{2,3},{3,2},{4,5},{5,4},{6,7},{7,6},{8,9},{9,8},{10,11... | collective-permute-start | bytes 4616 | tf_op jit(solution)/shard_map/ppermute | solution.py:1148
  (35 other events, 279.4 us)

commit v4 on v3

--- a/solution.py
+++ b/solution.py
@@ -1249,7 +1249,7 @@
     p_inner = pc.spread(y_inner, x_inner)
     fin_nb = [pc.across(f) for f in fins]
     act_a, gp_a, act_b, gp_b, asum, rsum = ffn_fwd(lens, at, fin, rsum, w_inner, w_outer, p_inner)
-    y_outer, x_outer, asum, fin_nb[0] = after(y_outer, x_outer, asum, fin_nb[0])
+    y_outer, x_outer, asum = after(y_outer, x_outer, asum)
     p_outer = pc.spread(y_outer, x_outer)
     pooled = pool(lens, at, asum, rsum, p_outer)[:n].astype(BF)
 
@@ -1257,6 +1257,7 @@
     sums = jnp.where(pc.ti > 0, jnp.stack([sums_b, sums_a]), jnp.stack([sums_a, sums_b]))
     msg = jnp.concatenate([jnp.broadcast_to(pooled[None], (2,) + pooled.shape), sums], axis=2)
     msg = jnp.broadcast_to(msg[None], (2 * pc.chips,) + msg.shape).reshape((devices,) + msg.shape[1:])
+    msg, fin_nb[0] = after(msg, fin_nb[0])
     got, pre = after(pc.share(msg), pre_inner(lens4, fint, gp_a, fin_nb[0], w_inner))
     got = got.reshape(devices * n, -1)
     pooled = got[:, :d]
@@ -1301,9 +1302,10 @@
     near = pc.core_swap(attn_all)
     *grads, gain_own = attn_done(half, attn_all, w_query, w_key, w_value)
     near, *grads = after(near, *grads)
-    gain_own = gain_own[0] + pc.across(gain_own[0])
+    gain_far = pc.across(gain_own[0])
     *grads, _ = attn_done(1 - half, near, w_query, w_key, w_value, grads)
-    gain_own, *grads = after(gain_own, *grads)
+    gain_far, *grads = after(gain_far, *grads)
+    gain_own = gain_own[0] + gain_far
     q_grad, k_grad, v_grad, out_grad = grads
     gain_near = pc.core_swap(gain_own)
     gain_attn_grad = jnp.where(

time: 289 us -> 286 us (0.990)
  waiting for transfers between devices: 39 us -> 34.9 us
    ppermute x28, waiting for transfers between devices: 26.1 us -> 22 us  [swap(): return lax.ppermute(x, axis, [(i, i ^ bit) for i in range(size)])]
  transfers between devices with their start and end apart: 34 -> 34, of which waited for: 17 -> 15; matrix products, arithmetic and copies ran while one was open for 7% -> 7% of each run, Pallas kernels for 48% -> 49%
where the time goes in v4:
time: 286 us; the launch traced here: 281 us
  Pallas kernels  153 us (53%)
  starting transfers between devices  60.1 us (21%)
  waiting for transfers between devices  34.9 us (12%)
  local copies, waits for them, and re-layouts  14.8 us (5%)
  other arithmetic  11.3 us (4%)
  matrix products  4.9 us (2%)
    pallas_call x1, Pallas kernels, mid_bwd(): pl.pallas_call(mid_bwd_kernel, grid=(n,), in_specs=[SMEM_SPEC, SMEM_SPEC]...  31.1 us
    ppermute x28, starting transfers between devices, swap(): return lax.ppermute(x, axis, [(i, i ^ bit) for i in range(size)])  27.7 us
    ppermute x28, waiting for transfers between devices, swap(): return lax.ppermute(x, axis, [(i, i ^ bit) for i in range(size)])  22 us
    pallas_call x1, Pallas kernels, attn_other(): pl.pallas_call(attn_other_kernel, grid=(n,), in_specs=[SMEM_SPEC, SMEM_SP...  18.5 us
    pallas_call x1, Pallas kernels, attn_bwd(): pl.pallas_call(attn_bwd_kernel, grid=(n,), in_specs=[SMEM_SPEC, SMEM_SPEC...  18.4 us
    pallas_call x1, Pallas kernels, ffn_fwd(): pl.pallas_call(ffn_fwd_kernel, grid=(n,), in_specs=[SMEM_SPEC, SMEM_SPEC,...  13.5 us
    pallas_call x1, Pallas kernels, attn_own(): pl.pallas_call(attn_own_kernel, grid=(n,), in_specs=[SMEM_SPEC, row_spec(...  12.3 us
    all_to_all x2, starting transfers between devices, exchange(): lax.all_to_all(x.reshape(self.chips, rows // self.chips, width), 'chip',...  12.2 us
  transfers between devices with their start and end apart: 34, of which 15 were waited for; matrix products, arithmetic and copies ran while one was open for 7% of the time, Pallas kernels for 49%

profile of v4, /device:TPU:0, one launch (start us, length us, event | category | flops | bytes accessed | tf_op | source)
XLA Modules:
  0.0 280.5 jit_solution(7891849637634814649)
XLA Ops:
  0.7 3.5 %pack_weights.1 = (bf16[272,1152]{1,0:T(8,128)(2,1)}, bf16[192,1536]{1,0:T(8,128)(2,1)}, bf16[384,768]{1,0:T(8,128)(2,1)}) custom-call(s32[1]{0:T(128)} %bitcast.at_ref, f32[6,32]{1,0:T(8,128)} %bitcast.34, bf16[768,384]{1,0:T(8,128)(2,1)} %wq.9, bf16[768,384]{1,0:T(8,128)(2,1)} %wk.9, bf16[768,384]{1,0:T(8,128)(2,1)} %wv.9, bf16[384,768]{1,0:T(8,128)(2,1)} %wo_ref.1, ...), custom_call_target="tpu_custom_call" | custom-call | bytes 10800000 | tf_op jit(solution)/shard_map/pack_weights/pallas_call | solution.py:132
  4.2 3.0 %collective-permute-start = (bf16[272,1152]{1,0:T(8,128)(2,1)}, bf16[272,1152]{1,0:T(8,128)(2,1)S(1)}, u32[]{:S(2)}, u32[]{:S(2)}) collective-permute-start(bf16[272,1152]{1,0:T(8,128)(2,1)} %get-tuple-element.132), channel_id=1, source_target_pairs={{0,1},{1,0},{2,3},{3,2},{4,5},{5,4},{6,7},{7,6},{8,9},{9,8},{10,11... | collective-permute-start | bytes 1880072 | tf_op jit(solution)/shard_map/ppermute | solution.py:1148
  8.0 12.3 %attn_own.1 = (bf16[2,512,768]{2,1,0:T(8,128)(2,1)}, bf16[768,1024]{1,0:T(8,128)(2,1)}, bf16[2,512,384]{2,1,0:T(8,128)(2,1)}, bf16[2,384,512]{2,1,0:T(8,128)(2,1...) custom-call(s32[2]{0:T(128)} %copy-done.10, ...), custom_call_target="tpu_custom_call" | custom-call | bytes 43200000 | tf_op jit(solution)/shard_map/attn_own/pallas_call | solution.py:383
  25.5 4.2 %all-to-all-start = ((bf16[32,2,896]{2,1,0:T(2,128)(2,1)}), bf16[32,2,896]{2,1,0:T(2,128)(2,1)S(1)}, u32[]{:S(2)}, u32[]{:S(2)}) async-start(bf16[32,2,896]{2,1,0:T(2,128)(2,1)} %broadcast_in_dim.10), calls=%async_computation | async-start | bytes 229376 | tf_op jit(solution)/shard_map/all_to_all | solution.py:1165
  31.9 6.9 %all-to-all-done = bf16[32,2,896]{2,1,0:T(2,128)(2,1)S(1)} async-done(((bf16[32,2,896]{2,1,0:T(2,128)(2,1)}), bf16[32,2,896]{2,1,0:T(2,128)(2,1)S(1)}, u32[]{:S(2)}, u32[]{:S(2)}) %all-to-all-start) | async-done | bytes 114720 | tf_op jit(solution)/shard_map/all_to_all | solution.py:1165
  42.1 18.5 %attn_other.1 = (bf16[2,512,384]{2,1,0:T(8,128)(2,1)}, bf16[2,384,512]{2,1,0:T(8,128)(2,1)}, bf16[2,512,384]{2,1,0:T(8,128)(2,1)}, bf16[2,512,384]{2,1,0:T(8,128...) custom-call(s32[2]{0:T(128)} %copy-done.10, ...), custom_call_target="tpu_custom_call" | custom-call | bytes 54000000 | tf_op jit(solution)/shard_map/attn_other/pallas_call | solution.py:408
  65.6 13.5 %ffn_fwd.1 = (bf16[2,512,1536]{2,1,0:T(8,128)(2,1)}, bf16[2,512,1536]{2,1,0:T(8,128)(2,1)}, bf16[2,512,1536]{2,1,0:T(8,128)(2,1)}, bf16[2,512,1536]{2,1,0:T(8,12...) custom-call(s32[2]{0:T(128)} %copy-done.10, s32[1]{0:T(128)} %bitcast.at_ref, ...), custom_call_target="tpu_custom_call" | custom-call | bytes 57600000 | tf_op jit(solution)/shard_map/ffn_fwd/pallas_call | solution.py:699
  86.9 5.3 %all-to-all-start.1 = ((bf16[32,2,2304]{2,1,0:T(2,128)(2,1)}), bf16[32,2,2304]{2,1,0:T(2,128)(2,1)S(1)}, u32[]{:S(2)}, u32[]{:S(2)}) async-start(bf16[32,2,2304]{2,1,0:T(2,128)(2,1)} %bitcast.10), calls=%async_computation.1 | async-start | bytes 589824 | tf_op jit(solution)/shard_map/all_to_all | solution.py:1165
  92.9 10.3 %pre_inner.1.pre_hbm = bf16[3,768,1536]{2,1,0:T(8,128)(2,1)} custom-call(s32[4]{0:T(128)} %get-tuple-element.139.lens, bf16[768,1024]{1,0:T(8,128)(2,1)} %get-tuple-element.163.fint_ref, bf16[2,512,1536]{2,1,0:T(8,128)(2,1)} %get-tuple-element.176.gp_ref.refs_1_, bf16[1,512,768]{2,1,0:T(8,128)(2,1)} %copy-done.21, bf16[768,1536]{1,0:T(8,128)(2,1)} %w_ref.5), custom_call_target="tpu_custom_call" | custom-call | bytes 32400000 | tf_op jit(solution)/shard_map/pre_inner/pallas_call | solution.py:769
  104.1 11.5 %loss_inner.1 = (f32[8,128]{1,0:T(8,128)}, f32[8,768]{1,0:T(8,128)}, f32[8,1536]{1,0:T(8,128)}, bf16[64,768]{1,0:T(8,128)(2,1)}, bf16[64,768]{1,0:T(8,128)(2,1)}...) custom-call(s32[4]{0:T(128)} %get-tuple-element.138.me_ref, s32[1]{0:T(128)} %bitcast.at_ref, ...), custom_call_target="tpu_custom_call" | custom-call | bytes 43200000 | tf_op jit(solution)/shard_map/loss_inner/pallas_call | solution.py:873
  116.0 2.8 %collective-permute-done.14 = bf16[384,1536]{1,0:T(8,128)(2,1)S(1)} collective-permute-done((bf16[384,1536]{1,0:T(8,128)(2,1)}, bf16[384,1536]{1,0:T(8,128)(2,1)S(1)}, u32[]{:S(2)}, u32[]{:S(2)}) %collective-permute-start.14) | collective-permute-done | bytes 1179680 | tf_op jit(solution)/shard_map/ppermute | solution.py:1148
  118.8 2.6 add.92
  121.4 6.2 %all-to-all-start.2 = ((bf16[8,48,1536]{2,1,0:T(8,128)(2,1)}), bf16[8,48,1536]{2,1,0:T(8,128)(2,1)S(1)}, u32[]{:S(2)}, u32[]{:S(2)}) async-start(bf16[8,48,1536]{2,1,0:T(8,128)(2,1)} %bitcast.11), calls=%async_computation.2 | async-start | bytes 2359296 | tf_op jit(solution)/shard_map/all_to_all | solution.py:1175
  127.6 31.1 %mid_bwd.1 = (f32[1024,768]{1,0:T(8,128)}, bf16[1024,768]{1,0:T(8,128)(2,1)}, bf16[1024,1152]{1,0:T(8,128)(2,1)}, bf16[384,1536]{1,0:T(8,128)(2,1)}, bf16[384,1536]{1,0:T(8,128)(2,1)}, /*index=5*/f32[8,128]{1,0:T(8,128)}) custom-call(s32[2]{0:T(128)} %copy-done.10, s32[1]{0:T(128)} %bitcast.at_ref, f32[8,1536]{1,0:T(8,128)} %get-tuple-element.170.g_ref, ...), custom_call_target="tpu_custom_call" | custom-call | bytes 115200000 | tf_op jit(solution)/shard_map/mid_bwd/pallas_call | solution.py:986
  160.0 6.4 %all-to-all-start.3 = ((bf16[8,48,1536]{2,1,0:T(8,128)(2,1)}), bf16[8,48,1536]{2,1,0:T(8,128)(2,1)}, u32[]{:S(2)}, u32[]{:S(2)}) async-start(bf16[8,48,1536]{2,1,0:T(8,128)(2,1)} %broadcast_in_dim.13), calls=%async_computation.3 | async-start | bytes 2359296 | tf_op jit(solution)/shard_map/all_to_all | solution.py:1181
  169.6 3.0 %fusion = f32[1536,768]{1,0:T(8,128)} fusion(bf16[64,768]{1,0:T(8,128)(2,1)S(1)} %copy-done.23, bf16[64,2304]{1,0:T(8,128)(2,1)S(1)} %reshape.101), kind=kOutput, calls=%fused_computation.1 | convolution fusion | flops 150994944 | bytes 5013504 | tf_op jit(solution)/shard_map/dot_general | solution.py:31
  173.1 1.9 fusion.10
  175.0 18.4 %attn_bwd.1 = (bf16[1024,1152]{1,0:T(8,128)(2,1)}, bf16[384,1536]{1,0:T(8,128)(2,1)}, bf16[384,1536]{1,0:T(8,128)(2,1)}, f32[8,128]{1,0:T(8,128)}) custom-call(s32[2]{0:T(128)} %copy-done.10, s32[1]{0:T(128)} %bitcast.at_ref, bf16[2,512,768]{2,1,0:T(8,128)(2,1)} %bitcast.31, bf16[384,768]{1,0:T(8,128)(2,1)} %wo_ref.1, ...), custom_call_target="tpu_custom_call" | custom-call | bytes 57600000 | tf_op jit(solution)/shard_map/attn_bwd/pallas_call | solution.py:629
  193.4 2.8 %collective-permute-done.17 = f32[8,128]{1,0:T(8,128)S(1)} collective-permute-done((f32[8,128]{1,0:T(8,128)S(1)}, f32[8,128]{1,0:T(8,128)S(1)}, u32[]{:S(2)}, u32[]{:S(2)}) %collective-permute-start.17) | collective-permute-done | bytes 4128 | tf_op jit(solution)/shard_map/ppermute | solution.py:1148
  199.3 2.5 add_add_fusion
  201.8 6.0 %all-to-all-start.4 = ((bf16[8,48,1536]{2,1,0:T(8,128)(2,1)}), bf16[8,48,1536]{2,1,0:T(8,128)(2,1)S(1)}, u32[]{:S(2)}, u32[]{:S(2)}) async-start(bf16[8,48,1536]{2,1,0:T(8,128)(2,1)} %bitcast.14), calls=%async_computation.4 | async-start | bytes 2359296 | tf_op jit(solution)/shard_map/all_to_all | solution.py:1175
  207.8 11.6 %layer_part.1 = bf16[2,512,768]{2,1,0:T(8,128)(2,1)} custom-call(s32[1]{0:T(128)} %bitcast.at_ref, f32[2,512,768]{2,1,0:T(8,128)} %get-tuple-element.178.refs_3_.res_ref, bf16[2,512,1536]{2,1,0:T(8,128)(2,1)} %get-tuple-element.215.aa_ref, bf16[2,512,1536]{2,1,0:T(8,128)(2,1)} %get-tuple-element.216.ab_ref, bf16[1536,768]{1,0:T(8,128)(2,1)} %w_ref.4, ...), custom_call_target="tpu_custom_call" | custom-call | bytes 43200000 | tf_op jit(solution)/shard_map/layer_part/pallas_call | solution.py:1062
  219.3 11.5 %input_part.1 = f32[2,512,768]{2,1,0:T(8,128)} custom-call(s32[1]{0:T(128)} %bitcast.at_ref, bf16[2,512,768]{2,1,0:T(8,128)(2,1)} %x_ref.3, f32[1024,768]{1,0:T(8,128)} %get-tuple-element.212.dres_ref, f32[1,768]{1,0:T(1,128)} %reshape.98.gain_ref, bf16[1024,1152]{1,0:T(8,128)(2,1)} %get-tuple-element.213.ta_ref, ...), custom_call_target="tpu_custom_call" | custom-call | bytes 43200000 | tf_op jit(solution)/shard_map/input_part/pallas_call | solution.py:1037
  230.9 5.7 %all-to-all-done.4 = bf16[8,48,1536]{2,1,0:T(8,128)(2,1)S(1)} async-done(((bf16[8,48,1536]{2,1,0:T(8,128)(2,1)}), bf16[8,48,1536]{2,1,0:T(8,128)(2,1)S(1)}, u32[]{:S(2)}, u32[]{:S(2)}) %all-to-all-start.4) | async-done | bytes 1179680 | tf_op jit(solution)/shard_map/all_to_all | solution.py:1175
  237.9 4.4 %all-to-all-start.5 = ((bf16[8,48,1536]{2,1,0:T(8,128)(2,1)}), bf16[8,48,1536]{2,1,0:T(8,128)(2,1)}, u32[]{:S(2)}, u32[]{:S(2)}) async-start(bf16[8,48,1536]{2,1,0:T(8,128)(2,1)} %broadcast_in_dim.14), calls=%async_computation.5 | async-start | bytes 2359296 | tf_op jit(solution)/shard_map/all_to_all | solution.py:1181
  242.4 1.9 collective-permute-start.22
  245.4 4.8 %inner_done.1 = (f32[768,1536]{1,0:T(8,128)}, f32[24,768]{1,0:T(8,128)S(1)}) custom-call(s32[1]{0:T(128)} %bitcast.at_ref, bf16[384,1536]{1,0:T(8,128)(2,1)} %bitcast.13.own_ref, bf16[384,1536]{1,0:T(8,128)(2,1)S(1)} %collective-permute-done.20.near_ref, bf16[768,1536]{1,0:T(8,128)(2,1)S(1)} %copy-done), custom_call_target="tpu_custom_call" | custom-call | bytes 18000000 | tf_op jit(solution)/shard_map/inner_done/pallas_call | solution.py:1096
  253.3 1.8 collective-permute-start.23
  256.4 4.7 %collective-permute-done.23 = f32[8,128]{1,0:T(8,128)S(1)} collective-permute-done((f32[8,128]{1,0:T(8,128)S(1)}, f32[8,128]{1,0:T(8,128)S(1)}, u32[]{:S(2)}, u32[]{:S(2)}) %collective-permute-start.23) | collective-permute-done | bytes 4128 | tf_op jit(solution)/shard_map/ppermute | solution.py:1148
  261.1 4.6 %collective-permute-start.24 = (f32[8,128]{1,0:T(8,128)S(1)}, f32[8,128]{1,0:T(8,128)S(1)}, u32[]{:S(2)}, u32[]{:S(2)}) collective-permute-start(f32[8,128]{1,0:T(8,128)S(1)} %add.100), channel_id=1, source_target_pairs={{0,16},{4,20},{8,24},{12,28},{16,0},{20,4},{24,8},{28,12},{1,17},{... | collective-permute-start | bytes 12296 | tf_op jit(solution)/shard_map/ppermute | solution.py:1148
  266.3 4.5 %collective-permute-done.24 = f32[8,128]{1,0:T(8,128)S(1)} collective-permute-done((f32[8,128]{1,0:T(8,128)S(1)}, f32[8,128]{1,0:T(8,128)S(1)}, u32[]{:S(2)}, u32[]{:S(2)}) %collective-permute-start.24) | collective-permute-done | bytes 4128 | tf_op jit(solution)/shard_map/ppermute | solution.py:1148
  271.9 3.0 %attn_done.2 = (f32[768,384]{1,0:T(8,128)}, f32[768,384]{1,0:T(8,128)}, f32[768,384]{1,0:T(8,128)}, f32[384,768]{1,0:T(8,128)}, f32[8,384]{1,0:T(8,128)S(1)}) custom-call(s32[1]{0:T(128)} %bitcast.16.half_ref, bf16[384,1536]{1,0:T(8,128)(2,1)} %bitcast.15.sum_ref, bf16[768,384]{1,0:T(8,128)(2,1)S(1)} %copy-done.1, bf16[768,384]{1,0:T(8,128)(2,1)S(1)} %copy-done.2, ...), custom_call_target="tpu_custom_call" | custom-call | bytes 10800000 | tf_op jit(solution)/shard_map/attn_done/pallas_call | solution.py:1127
  (162 shorter events, 48.1 us)
Async XLA Ops:
  4.2 17.4 %collective-permute-start = (bf16[272,1152]{1,0:T(8,128)(2,1)}, bf16[272,1152]{1,0:T(8,128)(2,1)S(1)}, u32[]{:S(2)}, u32[]{:S(2)}) collective-permute-start(bf16[272,1152]{1,0:T(8,128)(2,1)} %get-tuple-element.132), channel_id=1, source_target_pairs={{0,1},{1,0},{2,3},{3,2},{4,5},{5,4},{6,7},{7,6},{8,9},{9,8},{10,11... | collective-permute-start | bytes 1880072 | tf_op jit(solution)/shard_map/ppermute | solution.py:1148
  21.5 17.3 %collective-permute-start.1 = (bf16[272,1152]{1,0:T(8,128)(2,1)S(1)}, bf16[272,1152]{1,0:T(8,128)(2,1)S(1)}, u32[]{:S(2)}, u32[]{:S(2)}) collective-permute-start(bf16[272,1152]{1,0:T(8,128)(2,1)S(1)} %collective-permute-done.p0.refs_11_), channel_id=1, source_target_pairs={{0,4},{4,0},{8,12},{12,8},{16,20},{20,16},{24,28},{28,24},{1,5},{5... | collective-permute-start | bytes 1880072 | tf_op jit(solution)/shard_map/ppermute | solution.py:1148
  23.2 17.1 %collective-permute-start.2 = (bf16[192,1536]{1,0:T(8,128)(2,1)}, bf16[192,1536]{1,0:T(8,128)(2,1)}, u32[]{:S(2)}, u32[]{:S(2)}) collective-permute-start(bf16[192,1536]{1,0:T(8,128)(2,1)} %get-tuple-element.140), channel_id=1, source_target_pairs={{0,1},{1,0},{2,3},{3,2},{4,5},{5,4},{6,7},{7,6},{8,9},{9,8},{10,11... | collective-permute-start | bytes 1769480 | tf_op jit(solution)/shard_map/ppermute | solution.py:1148
  25.5 13.4 %all-to-all-start = ((bf16[32,2,896]{2,1,0:T(2,128)(2,1)}), bf16[32,2,896]{2,1,0:T(2,128)(2,1)S(1)}, u32[]{:S(2)}, u32[]{:S(2)}) async-start(bf16[32,2,896]{2,1,0:T(2,128)(2,1)} %broadcast_in_dim.10), calls=%async_computation | async-start | bytes 229376 | tf_op jit(solution)/shard_map/all_to_all | solution.py:1165
  31.5 9.5 %collective-permute-start.5 = (bf16[272,1152]{1,0:T(8,128)(2,1)S(1)}, bf16[272,1152]{1,0:T(8,128)(2,1)S(1)}, u32[]{:S(2)}, u32[]{:S(2)}) collective-permute-start(bf16[272,1152]{1,0:T(8,128)(2,1)S(1)} %collective-permute-done.p0.refs_11_), channel_id=1, source_target_pairs={{0,2},{2,0},{1,3},{3,1},{4,6},{6,4},{5,7},{7,5},{8,10},{10,8},{9,1... | collective-permute-start | bytes 1880072 | tf_op jit(solution)/shard_map/ppermute | solution.py:1148
  38.8 2.2 collective-permute-start.6
  38.9 21.7 %collective-permute-start.4 = (bf16[384,768]{1,0:T(8,128)(2,1)S(1)}, bf16[384,768]{1,0:T(8,128)(2,1)S(1)}, u32[]{:S(2)}, u32[]{:S(2)}) collective-permute-start(bf16[384,768]{1,0:T(8,128)(2,1)S(1)} %copy-done.31), channel_id=1, source_target_pairs={{0,1},{1,0},{2,3},{3,2},{4,5},{5,4},{6,7},{7,6},{8,9},{9,8},{10,11... | collective-permute-start | bytes 1769480 | tf_op jit(solution)/shard_map/ppermute | solution.py:1148
  40.3 20.3 %collective-permute-start.3 = (bf16[192,1536]{1,0:T(8,128)(2,1)}, bf16[192,1536]{1,0:T(8,128)(2,1)}, u32[]{:S(2)}, u32[]{:S(2)}) collective-permute-start(bf16[192,1536]{1,0:T(8,128)(2,1)} %collective-permute-done.2.p0.refs_15_), channel_id=1, source_target_pairs={{0,4},{4,0},{8,12},{12,8},{16,20},{20,16},{24,28},{28,24},{1,5},{5... | collective-permute-start | bytes 1769480 | tf_op jit(solution)/shard_map/ppermute | solution.py:1148
  60.6 4.0 %collective-permute-start.8 = (bf16[192,1536]{1,0:T(8,128)(2,1)}, bf16[192,1536]{1,0:T(8,128)(2,1)S(1)}, u32[]{:S(2)}, u32[]{:S(2)}) collective-permute-start(bf16[192,1536]{1,0:T(8,128)(2,1)} %collective-permute-done.2.p0.refs_15_), channel_id=1, source_target_pairs={{0,2},{2,0},{1,3},{3,1},{4,6},{6,4},{5,7},{7,5},{8,10},{10,8},{9,1... | collective-permute-start | bytes 1769480 | tf_op jit(solution)/shard_map/ppermute | solution.py:1148
  60.7 3.9 %collective-permute-start.9 = (bf16[192,1536]{1,0:T(8,128)(2,1)}, bf16[192,1536]{1,0:T(8,128)(2,1)S(1)}, u32[]{:S(2)}, u32[]{:S(2)}) collective-permute-start(bf16[192,1536]{1,0:T(8,128)(2,1)} %collective-permute-done.3.p1.refs_16_), channel_id=1, source_target_pairs={{0,2},{2,0},{1,3},{3,1},{4,6},{6,4},{5,7},{7,5},{8,10},{10,8},{9,1... | collective-permute-start | bytes 1769480 | tf_op jit(solution)/shard_map/ppermute | solution.py:1148
  61.2 17.9 %collective-permute-start.7 = (bf16[384,768]{1,0:T(8,128)(2,1)S(1)}, bf16[384,768]{1,0:T(8,128)(2,1)S(1)}, u32[]{:S(2)}, u32[]{:S(2)}) collective-permute-start(bf16[384,768]{1,0:T(8,128)(2,1)S(1)} %collective-permute-done.4.p0.refs_19_), channel_id=1, source_target_pairs={{0,4},{4,0},{8,12},{12,8},{16,20},{20,16},{24,28},{28,24},{1,5},{5... | collective-permute-start | bytes 1769480 | tf_op jit(solution)/shard_map/ppermute | solution.py:1148
  62.6 23.3 %collective-permute-start.12 = (bf16[1,512,768]{2,1,0:T(8,128)(2,1)}, bf16[1,512,768]{2,1,0:T(8,128)(2,1)S(1)}, u32[]{:S(2)}, u32[]{:S(2)}) collective-permute-start(bf16[1,512,768]{2,1,0:T(8,128)(2,1)} %get-tuple-element.161), channel_id=1, source_target_pairs={{0,1},{1,0},{2,3},{3,2},{4,5},{5,4},{6,7},{7,6},{8,9},{9,8},{10,11... | collective-permute-start | bytes 2359304 | tf_op jit(solution)/shard_map/ppermute | solution.py:1148
  63.2 40.9 %collective-permute-start.13 = (bf16[1,512,768]{2,1,0:T(8,128)(2,1)}, bf16[1,512,768]{2,1,0:T(8,128)(2,1)}, u32[]{:S(2)}, u32[]{:S(2)}) collective-permute-start(bf16[1,512,768]{2,1,0:T(8,128)(2,1)} %get-tuple-element.169), channel_id=1, source_target_pairs={{0,1},{1,0},{2,3},{3,2},{4,5},{5,4},{6,7},{7,6},{8,9},{9,8},{10,11... | collective-permute-start | bytes 2359304 | tf_op jit(solution)/shard_map/ppermute | solution.py:1148
  80.0 2.8 %collective-permute-start.11 = (bf16[384,768]{1,0:T(8,128)(2,1)S(1)}, bf16[384,768]{1,0:T(8,128)(2,1)S(1)}, u32[]{:S(2)}, u32[]{:S(2)}) collective-permute-start(bf16[384,768]{1,0:T(8,128)(2,1)S(1)} %collective-permute-done.7.p1.refs_20_), channel_id=1, source_target_pairs={{0,2},{2,0},{1,3},{3,1},{4,6},{6,4},{5,7},{7,5},{8,10},{10,8},{9,1... | collective-permute-start | bytes 1769480 | tf_op jit(solution)/shard_map/ppermute | solution.py:1148
  86.9 16.5 %all-to-all-start.1 = ((bf16[32,2,2304]{2,1,0:T(2,128)(2,1)}), bf16[32,2,2304]{2,1,0:T(2,128)(2,1)S(1)}, u32[]{:S(2)}, u32[]{:S(2)}) async-start(bf16[32,2,2304]{2,1,0:T(2,128)(2,1)} %bitcast.10), calls=%async_computation.1 | async-start | bytes 589824 | tf_op jit(solution)/shard_map/all_to_all | solution.py:1165
  115.7 3.1 %collective-permute-start.14 = (bf16[384,1536]{1,0:T(8,128)(2,1)}, bf16[384,1536]{1,0:T(8,128)(2,1)S(1)}, u32[]{:S(2)}, u32[]{:S(2)}) collective-permute-start(bf16[384,1536]{1,0:T(8,128)(2,1)} %get-tuple-element.175), channel_id=1, source_target_pairs={{0,2},{2,0},{1,3},{3,1},{4,6},{6,4},{5,7},{7,5},{8,10},{10,8},{9,1... | collective-permute-start | bytes 3538952 | tf_op jit(solution)/shard_map/ppermute | solution.py:1148
  121.4 37.4 %all-to-all-start.2 = ((bf16[8,48,1536]{2,1,0:T(8,128)(2,1)}), bf16[8,48,1536]{2,1,0:T(8,128)(2,1)S(1)}, u32[]{:S(2)}, u32[]{:S(2)}) async-start(bf16[8,48,1536]{2,1,0:T(8,128)(2,1)} %bitcast.11), calls=%async_computation.2 | async-start | bytes 2359296 | tf_op jit(solution)/shard_map/all_to_all | solution.py:1175
  158.7 7.8 %collective-permute-start.15 = (bf16[384,1536]{1,0:T(8,128)(2,1)}, bf16[384,1536]{1,0:T(8,128)(2,1)}, u32[]{:S(2)}, u32[]{:S(2)}) collective-permute-start(bf16[384,1536]{1,0:T(8,128)(2,1)} %get-tuple-element.187), channel_id=1, source_target_pairs={{0,2},{2,0},{1,3},{3,1},{4,6},{6,4},{5,7},{7,5},{8,10},{10,8},{9,1... | collective-permute-start | bytes 3538952 | tf_op jit(solution)/shard_map/ppermute | solution.py:1148
  160.0 36.2 %all-to-all-start.3 = ((bf16[8,48,1536]{2,1,0:T(8,128)(2,1)}), bf16[8,48,1536]{2,1,0:T(8,128)(2,1)}, u32[]{:S(2)}, u32[]{:S(2)}) async-start(bf16[8,48,1536]{2,1,0:T(8,128)(2,1)} %broadcast_in_dim.13), calls=%async_computation.3 | async-start | bytes 2359296 | tf_op jit(solution)/shard_map/all_to_all | solution.py:1181
  168.0 28.2 %collective-permute-start.16 = (bf16[384,1536]{1,0:T(8,128)(2,1)S(1)}, bf16[384,1536]{1,0:T(8,128)(2,1)S(1)}, u32[]{:S(2)}, u32[]{:S(2)}) collective-permute-start(bf16[384,1536]{1,0:T(8,128)(2,1)S(1)} %add.93), channel_id=1, source_target_pairs={{0,1},{1,0},{2,3},{3,2},{4,5},{5,4},{6,7},{7,6},{8,9},{9,8},{10,11... | collective-permute-start | bytes 3538952 | tf_op jit(solution)/shard_map/ppermute | solution.py:1148
  172.6 23.7 %collective-permute-start.17 = (f32[8,128]{1,0:T(8,128)S(1)}, f32[8,128]{1,0:T(8,128)S(1)}, u32[]{:S(2)}, u32[]{:S(2)}) collective-permute-start(f32[8,128]{1,0:T(8,128)S(1)} %copy-done.32), channel_id=1, source_target_pairs={{0,1},{1,0},{2,3},{3,2},{4,5},{5,4},{6,7},{7,6},{8,9},{9,8},{10,11... | collective-permute-start | bytes 12296 | tf_op jit(solution)/shard_map/ppermute | solution.py:1148
  196.3 3.1 %collective-permute-start.18 = (bf16[384,1536]{1,0:T(8,128)(2,1)}, bf16[384,1536]{1,0:T(8,128)(2,1)S(1)}, u32[]{:S(2)}, u32[]{:S(2)}) collective-permute-start(bf16[384,1536]{1,0:T(8,128)(2,1)} %get-tuple-element.208), channel_id=1, source_target_pairs={{0,2},{2,0},{1,3},{3,1},{4,6},{6,4},{5,7},{7,5},{8,10},{10,8},{9,1... | collective-permute-start | bytes 3538952 | tf_op jit(solution)/shard_map/ppermute | solution.py:1148
  197.0 2.2 collective-permute-start.19
  201.8 34.8 %all-to-all-start.4 = ((bf16[8,48,1536]{2,1,0:T(8,128)(2,1)}), bf16[8,48,1536]{2,1,0:T(8,128)(2,1)S(1)}, u32[]{:S(2)}, u32[]{:S(2)}) async-start(bf16[8,48,1536]{2,1,0:T(8,128)(2,1)} %bitcast.14), calls=%async_computation.4 | async-start | bytes 2359296 | tf_op jit(solution)/shard_map/all_to_all | solution.py:1175
  237.9 32.9 %all-to-all-start.5 = ((bf16[8,48,1536]{2,1,0:T(8,128)(2,1)}), bf16[8,48,1536]{2,1,0:T(8,128)(2,1)}, u32[]{:S(2)}, u32[]{:S(2)}) async-start(bf16[8,48,1536]{2,1,0:T(8,128)(2,1)} %broadcast_in_dim.14), calls=%async_computation.5 | async-start | bytes 2359296 | tf_op jit(solution)/shard_map/all_to_all | solution.py:1181
  242.3 3.1 %collective-permute-start.20 = (bf16[384,1536]{1,0:T(8,128)(2,1)}, bf16[384,1536]{1,0:T(8,128)(2,1)S(1)}, u32[]{:S(2)}, u32[]{:S(2)}) collective-permute-start(bf16[384,1536]{1,0:T(8,128)(2,1)} %bitcast.13.own_ref), channel_id=1, source_target_pairs={{0,2},{2,0},{1,3},{3,1},{4,6},{6,4},{5,7},{7,5},{8,10},{10,8},{9,1... | collective-permute-start | bytes 3538952 | tf_op jit(solution)/shard_map/ppermute | solution.py:1148
  242.4 10.9 %collective-permute-start.22 = (f32[8,128]{1,0:T(8,128)S(1)}, f32[8,128]{1,0:T(8,128)S(1)}, u32[]{:S(2)}, u32[]{:S(2)}) collective-permute-start(f32[8,128]{1,0:T(8,128)S(1)} %add.98), channel_id=1, source_target_pairs={{0,4},{4,0},{8,12},{12,8},{16,20},{20,16},{24,28},{28,24},{1,5},{5... | collective-permute-start | bytes 12296 | tf_op jit(solution)/shard_map/ppermute | solution.py:1148
  251.7 14.0 %collective-permute-start.21 = (f32[768]{0:T(1024)S(1)}, f32[768]{0:T(1024)S(1)}, u32[]{:S(2)}, u32[]{:S(2)}) collective-permute-start(f32[768]{0:T(1024)S(1)} %reduce_sum.45), channel_id=1, source_target_pairs={{0,1},{1,0},{2,3},{3,2},{4,5},{5,4},{6,7},{7,6},{8,9},{9,8},{10,11... | collective-permute-start | bytes 9224 | tf_op jit(solution)/shard_map/ppermute | solution.py:1148
  253.3 7.8 %collective-permute-start.23 = (f32[8,128]{1,0:T(8,128)S(1)}, f32[8,128]{1,0:T(8,128)S(1)}, u32[]{:S(2)}, u32[]{:S(2)}) collective-permute-start(f32[8,128]{1,0:T(8,128)S(1)} %add.99), channel_id=1, source_target_pairs={{0,8},{4,12},{8,0},{12,4},{16,24},{20,28},{24,16},{28,20},{1,9},{5... | collective-permute-start | bytes 12296 | tf_op jit(solution)/shard_map/ppermute | solution.py:1148
  261.1 9.6 %collective-permute-start.24 = (f32[8,128]{1,0:T(8,128)S(1)}, f32[8,128]{1,0:T(8,128)S(1)}, u32[]{:S(2)}, u32[]{:S(2)}) collective-permute-start(f32[8,128]{1,0:T(8,128)S(1)} %add.100), channel_id=1, source_target_pairs={{0,16},{4,20},{8,24},{12,28},{16,0},{20,4},{24,8},{28,12},{1,17},{... | collective-permute-start | bytes 12296 | tf_op jit(solution)/shard_map/ppermute | solution.py:1148
  270.8 5.7 %collective-permute-start.26 = (bf16[384,1536]{1,0:T(8,128)(2,1)}, bf16[384,1536]{1,0:T(8,128)(2,1)S(1)}, u32[]{:S(2)}, u32[]{:S(2)}) collective-permute-start(bf16[384,1536]{1,0:T(8,128)(2,1)} %bitcast.15.sum_ref), channel_id=1, source_target_pairs={{0,2},{2,0},{1,3},{3,1},{4,6},{6,4},{5,7},{7,5},{8,10},{10,8},{9,1... | collective-permute-start | bytes 3538952 | tf_op jit(solution)/shard_map/ppermute | solution.py:1148
  274.9 3.6 %collective-permute-start.25 = (f32[384]{0:T(512)S(1)}, f32[384]{0:T(512)S(1)}, u32[]{:S(2)}, u32[]{:S(2)}) collective-permute-start(f32[384]{0:T(512)S(1)} %slice_reduce_fusion), channel_id=1, source_target_pairs={{0,1},{1,0},{2,3},{3,2},{4,5},{5,4},{6,7},{7,6},{8,9},{9,8},{10,11... | collective-permute-start | bytes 4616 | tf_op jit(solution)/shard_map/ppermute | solution.py:1148
  (35 other events, 272.2 us)

commit v5 on v4

--- a/solution.py
+++ b/solution.py
@@ -896,7 +896,7 @@
             pltpu.VMEM((d, chunk), BF),
             pltpu.SemaphoreType.DMA((5,)),
         ],
-        compiler_params=params(),
+        compiler_params=params(44),
         cost_estimate=cost(12),
         name="loss_inner",
     )(me, at, lens4, pooled, queries, wp, pre, fn, wi, wu)
@@ -1181,10 +1181,11 @@
         got = lax.all_to_all(jnp.broadcast_to(x[None], (self.chips,) + x.shape), "chip", 0, 0, tiled=True)
         return got.reshape(-1, x.shape[1])
 
-    def total(self, x):
-        for i in range(self.chips.bit_length() - 1):
-            x = x + swap(x, "chip", 1 << i, self.chips)
-        return x
+    def steps(self):
+        return [1 << i for i in range(self.chips.bit_length() - 1)]
+
+    def plus(self, x, bit):
+        return x + swap(x, "chip", bit, self.chips)
 
 
 def body(
@@ -1292,12 +1293,16 @@
     layer = layer_part(at, res, act_a, act_b, w_outer, p_outer)
     parts, input_grad, layer = after(parts, input_grad, layer)
     attn_all = pc.gather(pc.add(parts))
-    table_sum = pc.total(table + near_table)
+    *early, late = pc.steps()
+    table_sum = table + near_table
+    for bit in early:
+        table_sum = pc.plus(table_sum, bit)
     gain_ffn_part = jnp.sum(gain_ffn_part[::8], axis=0)
     gain_ffn_grad = (gain_ffn_part + pc.across(gain_ffn_part)) / gain_ffn
     attn_all, gain_ffn_grad, table_sum, inner_sum, query_loss = after(
         attn_all, gain_ffn_grad, table_sum, inner_sum, query_loss
     )
+    table_sum = pc.plus(table_sum, late)
     half = pc.core.reshape(1)
     near = pc.core_swap(attn_all)
     *grads, gain_own = attn_done(half, attn_all, w_query, w_key, w_value)

time: 286 us -> 285 us (level)
  starting transfers between devices: 60.1 us -> 55.3 us
  waiting for transfers between devices: 34.9 us -> 39.5 us
  local copies, waits for them, and re-layouts: 14.8 us -> 18.6 us
  Pallas kernels: 153 us -> 150 us
    all_to_all x2, waiting for transfers between devices: 0.01 us -> 10.2 us  [gather(): lax.all_to_all(jnp.broadcast_to(x[None], (self.chips,) + x.shape), 'chip'...]
    ppermute x28, waiting for transfers between devices: 22 us -> 16.6 us  [swap(): return lax.ppermute(x, axis, [(i, i ^ bit) for i in range(size)])]
    ppermute x28, starting transfers between devices: 27.7 us -> 23.3 us  [swap(): return lax.ppermute(x, axis, [(i, i ^ bit) for i in range(size)])]
    pallas_call x1, Pallas kernels: 11.5 us -> 8.48 us  [loss_all(): pl.pallas_call(loss_kernel, in_specs=[SMEM_SPEC] * 3 + [vm] * 2 + [ANY] *...]
    unnamed x69 -> x89, local copies, waits for them, and re-layouts: 5.44 us -> 8.01 us
  transfers between devices with their start and end apart: 34 -> 34, of which waited for: 15 -> 16; matrix products, arithmetic and copies ran while one was open for 7% -> 7% of each run, Pallas kernels for 49% -> 49%
where the time goes in v5:
time: 285 us; the launch traced here: 279 us
  Pallas kernels  150 us (53%)
  starting transfers between devices  55.3 us (19%)
  waiting for transfers between devices  39.5 us (14%)
  local copies, waits for them, and re-layouts  18.6 us (7%)
  other arithmetic  9.45 us (3%)
  matrix products  4.9 us (2%)
    pallas_call x1, Pallas kernels, mid_bwd(): pl.pallas_call(mid_bwd_kernel, grid=(n,), in_specs=[SMEM_SPEC, SMEM_SPEC]...  31 us
    ppermute x28, starting transfers between devices, swap(): return lax.ppermute(x, axis, [(i, i ^ bit) for i in range(size)])  23.3 us
    pallas_call x1, Pallas kernels, attn_other(): pl.pallas_call(attn_other_kernel, grid=(n,), in_specs=[SMEM_SPEC, SMEM_SP...  18.5 us
    pallas_call x1, Pallas kernels, attn_bwd(): pl.pallas_call(attn_bwd_kernel, grid=(n,), in_specs=[SMEM_SPEC, SMEM_SPEC...  18.4 us
    ppermute x28, waiting for transfers between devices, swap(): return lax.ppermute(x, axis, [(i, i ^ bit) for i in range(size)])  16.6 us
    pallas_call x1, Pallas kernels, ffn_fwd(): pl.pallas_call(ffn_fwd_kernel, grid=(n,), in_specs=[SMEM_SPEC, SMEM_SPEC,...  13.5 us
    pallas_call x1, Pallas kernels, attn_own(): pl.pallas_call(attn_own_kernel, grid=(n,), in_specs=[SMEM_SPEC, row_spec(...  12.2 us
    all_to_all x2, starting transfers between devices, exchange(): lax.all_to_all(x.reshape(self.chips, rows // self.chips, width), 'chip',...  11.6 us
  transfers between devices with their start and end apart: 34, of which 16 were waited for; matrix products, arithmetic and copies ran while one was open for 7% of the time, Pallas kernels for 49%

profile of v5, /device:TPU:0, one launch (start us, length us, event | category | flops | bytes accessed | tf_op | source)
XLA Modules:
  0.0 279.3 jit_solution(17484880661219152089)
XLA Ops:
  0.7 3.5 %pack_weights.1 = (bf16[272,1152]{1,0:T(8,128)(2,1)}, bf16[192,1536]{1,0:T(8,128)(2,1)}, bf16[384,768]{1,0:T(8,128)(2,1)}) custom-call(s32[1]{0:T(128)} %bitcast.at_ref, f32[6,32]{1,0:T(8,128)} %bitcast.34, bf16[768,384]{1,0:T(8,128)(2,1)} %wq.9, bf16[768,384]{1,0:T(8,128)(2,1)} %wk.9, bf16[768,384]{1,0:T(8,128)(2,1)} %wv.9, bf16[384,768]{1,0:T(8,128)(2,1)} %wo_ref.1, ...), custom_call_target="tpu_custom_call" | custom-call | bytes 10800000 | tf_op jit(solution)/shard_map/pack_weights/pallas_call | solution.py:132
  4.2 3.0 %collective-permute-start = (bf16[272,1152]{1,0:T(8,128)(2,1)}, bf16[272,1152]{1,0:T(8,128)(2,1)S(1)}, u32[]{:S(2)}, u32[]{:S(2)}) collective-permute-start(bf16[272,1152]{1,0:T(8,128)(2,1)} %get-tuple-element.132), channel_id=1, source_target_pairs={{0,1},{1,0},{2,3},{3,2},{4,5},{5,4},{6,7},{7,6},{8,9},{9,8},{10,11... | collective-permute-start | bytes 1880072 | tf_op jit(solution)/shard_map/ppermute | solution.py:1148
  8.0 12.2 %attn_own.1 = (bf16[2,512,768]{2,1,0:T(8,128)(2,1)}, bf16[768,1024]{1,0:T(8,128)(2,1)}, bf16[2,512,384]{2,1,0:T(8,128)(2,1)}, bf16[2,384,512]{2,1,0:T(8,128)(2,1...) custom-call(s32[2]{0:T(128)} %copy-done.19, ...), custom_call_target="tpu_custom_call" | custom-call | bytes 43200000 | tf_op jit(solution)/shard_map/attn_own/pallas_call | solution.py:383
  21.5 1.7 collective-permute-start.1
  25.5 4.2 %all-to-all-start = ((bf16[32,2,896]{2,1,0:T(2,128)(2,1)}), bf16[32,2,896]{2,1,0:T(2,128)(2,1)S(1)}, u32[]{:S(2)}, u32[]{:S(2)}) async-start(bf16[32,2,896]{2,1,0:T(2,128)(2,1)} %broadcast_in_dim.10), calls=%async_computation | async-start | bytes 229376 | tf_op jit(solution)/shard_map/all_to_all | solution.py:1165
  31.9 6.9 %all-to-all-done = bf16[32,2,896]{2,1,0:T(2,128)(2,1)S(1)} async-done(((bf16[32,2,896]{2,1,0:T(2,128)(2,1)}), bf16[32,2,896]{2,1,0:T(2,128)(2,1)S(1)}, u32[]{:S(2)}, u32[]{:S(2)}) %all-to-all-start) | async-done | bytes 114720 | tf_op jit(solution)/shard_map/all_to_all | solution.py:1165
  42.1 18.5 %attn_other.1 = (bf16[2,512,384]{2,1,0:T(8,128)(2,1)}, bf16[2,384,512]{2,1,0:T(8,128)(2,1)}, bf16[2,512,384]{2,1,0:T(8,128)(2,1)}, bf16[2,512,384]{2,1,0:T(8,128...) custom-call(s32[2]{0:T(128)} %copy-done.19, ...), custom_call_target="tpu_custom_call" | custom-call | bytes 54000000 | tf_op jit(solution)/shard_map/attn_other/pallas_call | solution.py:408
  65.6 13.5 %ffn_fwd.1 = (bf16[2,512,1536]{2,1,0:T(8,128)(2,1)}, bf16[2,512,1536]{2,1,0:T(8,128)(2,1)}, bf16[2,512,1536]{2,1,0:T(8,128)(2,1)}, bf16[2,512,1536]{2,1,0:T(8,12...) custom-call(s32[2]{0:T(128)} %copy-done.19, s32[1]{0:T(128)} %bitcast.at_ref, ...), custom_call_target="tpu_custom_call" | custom-call | bytes 57600000 | tf_op jit(solution)/shard_map/ffn_fwd/pallas_call | solution.py:699
  86.9 5.4 %all-to-all-start.1 = ((bf16[32,2,2304]{2,1,0:T(2,128)(2,1)}), bf16[32,2,2304]{2,1,0:T(2,128)(2,1)}, u32[]{:S(2)}, u32[]{:S(2)}) async-start(bf16[32,2,2304]{2,1,0:T(2,128)(2,1)} %bitcast.10), calls=%async_computation.1 | async-start | bytes 589824 | tf_op jit(solution)/shard_map/all_to_all | solution.py:1165
  93.0 10.4 %pre_inner.1.pre_hbm = bf16[3,768,1536]{2,1,0:T(8,128)(2,1)} custom-call(s32[4]{0:T(128)} %get-tuple-element.139.lens, bf16[768,1024]{1,0:T(8,128)(2,1)} %get-tuple-element.163.fint_ref, bf16[2,512,1536]{2,1,0:T(8,128)(2,1)} %get-tuple-element.176.gp_ref.refs_1_, bf16[1,512,768]{2,1,0:T(8,128)(2,1)} %copy-done.33, bf16[768,1536]{1,0:T(8,128)(2,1)} %w_ref.5), custom_call_target="tpu_custom_call" | custom-call | bytes 32400000 | tf_op jit(solution)/shard_map/pre_inner/pallas_call | solution.py:769
  103.5 1.8 reshape.101
  108.8 8.5 %loss_inner.1 = (f32[8,128]{1,0:T(8,128)S(1)}, f32[8,768]{1,0:T(8,128)S(1)}, f32[8,1536]{1,0:T(8,128)S(1)}, bf16[64,768]{1,0:T(8,128)(2,1)S(1)}, bf16[64,768]{1,...) custom-call(s32[4]{0:T(128)S(1)} %get-tuple-element.138.me_ref, s32[1]{0:T(128)} %bitcast.at_ref, ...), custom_call_target="tpu_custom_call" | custom-call | bytes 43200000 | tf_op jit(solution)/shard_map/loss_inner/pallas_call | solution.py:873
  117.6 2.6 collective-permute-done.14
  121.5 6.3 %all-to-all-start.2 = ((bf16[8,48,1536]{2,1,0:T(8,128)(2,1)}), bf16[8,48,1536]{2,1,0:T(8,128)(2,1)S(1)}, u32[]{:S(2)}, u32[]{:S(2)}) async-start(bf16[8,48,1536]{2,1,0:T(8,128)(2,1)} %bitcast.11), calls=%async_computation.2 | async-start | bytes 2359296 | tf_op jit(solution)/shard_map/all_to_all | solution.py:1175
  127.9 31.0 %mid_bwd.1 = (f32[1024,768]{1,0:T(8,128)}, bf16[1024,768]{1,0:T(8,128)(2,1)}, bf16[1024,1152]{1,0:T(8,128)(2,1)}, bf16[384,1536]{1,0:T(8,128)(2,1)}, bf16[384,1536]{1,0:T(8,128)(2,1)}, /*index=5*/f32[8,128]{1,0:T(8,128)}) custom-call(s32[2]{0:T(128)} %copy-done.19, s32[1]{0:T(128)} %bitcast.at_ref, f32[8,1536]{1,0:T(8,128)} %copy-done.18, ...), custom_call_target="tpu_custom_call" | custom-call | bytes 115200000 | tf_op jit(solution)/shard_map/mid_bwd/pallas_call | solution.py:986
  160.2 6.4 %all-to-all-start.3 = ((bf16[8,48,1536]{2,1,0:T(8,128)(2,1)}), bf16[8,48,1536]{2,1,0:T(8,128)(2,1)}, u32[]{:S(2)}, u32[]{:S(2)}) async-start(bf16[8,48,1536]{2,1,0:T(8,128)(2,1)} %broadcast_in_dim.13), calls=%async_computation.3 | async-start | bytes 2359296 | tf_op jit(solution)/shard_map/all_to_all | solution.py:1181
  168.5 3.0 %fusion = f32[1536,768]{1,0:T(8,128)} fusion(bf16[64,768]{1,0:T(8,128)(2,1)S(1)} %copy-done.17, bf16[64,2304]{1,0:T(8,128)(2,1)S(1)} %copy-done.31), kind=kOutput, calls=%fused_computation.1 | convolution fusion | flops 150994944 | bytes 5013504 | tf_op jit(solution)/shard_map/dot_general | solution.py:31
  172.2 1.9 fusion.10
  174.1 18.4 %attn_bwd.1 = (bf16[1024,1152]{1,0:T(8,128)(2,1)}, bf16[384,1536]{1,0:T(8,128)(2,1)}, bf16[384,1536]{1,0:T(8,128)(2,1)}, f32[8,128]{1,0:T(8,128)}) custom-call(s32[2]{0:T(128)} %copy-done.19, s32[1]{0:T(128)} %bitcast.at_ref, bf16[2,512,768]{2,1,0:T(8,128)(2,1)} %bitcast.31, bf16[384,768]{1,0:T(8,128)(2,1)} %wo_ref.1, ...), custom_call_target="tpu_custom_call" | custom-call | bytes 57600000 | tf_op jit(solution)/shard_map/attn_bwd/pallas_call | solution.py:629
  192.5 2.7 collective-permute-done.17
  198.9 2.5 add_add_fusion
  201.4 5.3 %all-to-all-start.4 = ((bf16[8,48,1536]{2,1,0:T(8,128)(2,1)}), bf16[8,48,1536]{2,1,0:T(8,128)(2,1)S(1)}, u32[]{:S(2)}, u32[]{:S(2)}) async-start(bf16[8,48,1536]{2,1,0:T(8,128)(2,1)} %bitcast.14), calls=%async_computation.4 | async-start | bytes 2359296 | tf_op jit(solution)/shard_map/all_to_all | solution.py:1175
  206.7 11.6 %layer_part.1 = bf16[2,512,768]{2,1,0:T(8,128)(2,1)} custom-call(s32[1]{0:T(128)} %bitcast.at_ref, f32[2,512,768]{2,1,0:T(8,128)} %get-tuple-element.178.refs_3_.res_ref, bf16[2,512,1536]{2,1,0:T(8,128)(2,1)} %get-tuple-element.215.aa_ref, bf16[2,512,1536]{2,1,0:T(8,128)(2,1)} %get-tuple-element.216.ab_ref, bf16[1536,768]{1,0:T(8,128)(2,1)} %w_ref.4, ...), custom_call_target="tpu_custom_call" | custom-call | bytes 43200000 | tf_op jit(solution)/shard_map/layer_part/pallas_call | solution.py:1062
  218.2 11.5 %input_part.1 = f32[2,512,768]{2,1,0:T(8,128)} custom-call(s32[1]{0:T(128)} %bitcast.at_ref, bf16[2,512,768]{2,1,0:T(8,128)(2,1)} %x_ref.3, f32[1024,768]{1,0:T(8,128)} %get-tuple-element.212.dres_ref, f32[1,768]{1,0:T(1,128)} %reshape.98.gain_ref, bf16[1024,1152]{1,0:T(8,128)(2,1)} %get-tuple-element.213.ta_ref, ...), custom_call_target="tpu_custom_call" | custom-call | bytes 43200000 | tf_op jit(solution)/shard_map/input_part/pallas_call | solution.py:1037
  229.8 5.7 %all-to-all-done.4 = bf16[8,48,1536]{2,1,0:T(8,128)(2,1)S(1)} async-done(((bf16[8,48,1536]{2,1,0:T(8,128)(2,1)}), bf16[8,48,1536]{2,1,0:T(8,128)(2,1)S(1)}, u32[]{:S(2)}, u32[]{:S(2)}) %all-to-all-start.4) | async-done | bytes 1179680 | tf_op jit(solution)/shard_map/all_to_all | solution.py:1175
  236.8 4.4 %all-to-all-start.5 = ((bf16[8,48,1536]{2,1,0:T(8,128)(2,1)}), bf16[8,48,1536]{2,1,0:T(8,128)(2,1)}, u32[]{:S(2)}, u32[]{:S(2)}) async-start(bf16[8,48,1536]{2,1,0:T(8,128)(2,1)} %broadcast_in_dim.14), calls=%async_computation.5 | async-start | bytes 2359296 | tf_op jit(solution)/shard_map/all_to_all | solution.py:1181
  241.3 1.9 collective-permute-start.22
  244.3 4.8 %inner_done.1 = (f32[768,1536]{1,0:T(8,128)}, f32[24,768]{1,0:T(8,128)S(1)}) custom-call(s32[1]{0:T(128)} %bitcast.at_ref, bf16[384,1536]{1,0:T(8,128)(2,1)} %bitcast.13.own_ref, bf16[384,1536]{1,0:T(8,128)(2,1)S(1)} %collective-permute-done.20.near_ref, bf16[768,1536]{1,0:T(8,128)(2,1)S(1)} %copy-done.1), custom_call_target="tpu_custom_call" | custom-call | bytes 18000000 | tf_op jit(solution)/shard_map/inner_done/pallas_call | solution.py:1096
  253.5 1.8 collective-permute-start.23
  255.9 4.1 %collective-permute-done.23 = f32[8,128]{1,0:T(8,128)S(1)} collective-permute-done((f32[8,128]{1,0:T(8,128)S(1)}, f32[8,128]{1,0:T(8,128)S(1)}, u32[]{:S(2)}, u32[]{:S(2)}) %collective-permute-start.23) | collective-permute-done | bytes 4128 | tf_op jit(solution)/shard_map/ppermute | solution.py:1148
  260.0 9.5 %all-to-all-done.5 = bf16[8,48,1536]{2,1,0:T(8,128)(2,1)} async-done(((bf16[8,48,1536]{2,1,0:T(8,128)(2,1)}), bf16[8,48,1536]{2,1,0:T(8,128)(2,1)}, u32[]{:S(2)}, u32[]{:S(2)}) %all-to-all-start.5) | async-done | bytes 1179680 | tf_op jit(solution)/shard_map/all_to_all | solution.py:1181
  270.6 3.0 %attn_done.2 = (f32[768,384]{1,0:T(8,128)}, f32[768,384]{1,0:T(8,128)}, f32[768,384]{1,0:T(8,128)}, f32[384,768]{1,0:T(8,128)}, f32[8,384]{1,0:T(8,128)S(1)}) custom-call(s32[1]{0:T(128)} %bitcast.16.half_ref, bf16[384,1536]{1,0:T(8,128)(2,1)} %bitcast.15.sum_ref, bf16[768,384]{1,0:T(8,128)(2,1)S(1)} %copy-done.3, bf16[768,384]{1,0:T(8,128)(2,1)S(1)} %copy-done.4, ...), custom_call_target="tpu_custom_call" | custom-call | bytes 10800000 | tf_op jit(solution)/shard_map/attn_done/pallas_call | solution.py:1127
  (182 shorter events, 49.9 us)
Async XLA Ops:
  4.2 17.4 %collective-permute-start = (bf16[272,1152]{1,0:T(8,128)(2,1)}, bf16[272,1152]{1,0:T(8,128)(2,1)S(1)}, u32[]{:S(2)}, u32[]{:S(2)}) collective-permute-start(bf16[272,1152]{1,0:T(8,128)(2,1)} %get-tuple-element.132), channel_id=1, source_target_pairs={{0,1},{1,0},{2,3},{3,2},{4,5},{5,4},{6,7},{7,6},{8,9},{9,8},{10,11... | collective-permute-start | bytes 1880072 | tf_op jit(solution)/shard_map/ppermute | solution.py:1148
  21.5 17.3 %collective-permute-start.1 = (bf16[272,1152]{1,0:T(8,128)(2,1)S(1)}, bf16[272,1152]{1,0:T(8,128)(2,1)S(1)}, u32[]{:S(2)}, u32[]{:S(2)}) collective-permute-start(bf16[272,1152]{1,0:T(8,128)(2,1)S(1)} %collective-permute-done.p0.refs_11_), channel_id=1, source_target_pairs={{0,4},{4,0},{8,12},{12,8},{16,20},{20,16},{24,28},{28,24},{1,5},{5... | collective-permute-start | bytes 1880072 | tf_op jit(solution)/shard_map/ppermute | solution.py:1148
  23.2 17.1 %collective-permute-start.2 = (bf16[192,1536]{1,0:T(8,128)(2,1)}, bf16[192,1536]{1,0:T(8,128)(2,1)}, u32[]{:S(2)}, u32[]{:S(2)}) collective-permute-start(bf16[192,1536]{1,0:T(8,128)(2,1)} %get-tuple-element.140), channel_id=1, source_target_pairs={{0,1},{1,0},{2,3},{3,2},{4,5},{5,4},{6,7},{7,6},{8,9},{9,8},{10,11... | collective-permute-start | bytes 1769480 | tf_op jit(solution)/shard_map/ppermute | solution.py:1148
  25.5 13.4 %all-to-all-start = ((bf16[32,2,896]{2,1,0:T(2,128)(2,1)}), bf16[32,2,896]{2,1,0:T(2,128)(2,1)S(1)}, u32[]{:S(2)}, u32[]{:S(2)}) async-start(bf16[32,2,896]{2,1,0:T(2,128)(2,1)} %broadcast_in_dim.10), calls=%async_computation | async-start | bytes 229376 | tf_op jit(solution)/shard_map/all_to_all | solution.py:1165
  31.6 9.4 %collective-permute-start.5 = (bf16[272,1152]{1,0:T(8,128)(2,1)S(1)}, bf16[272,1152]{1,0:T(8,128)(2,1)S(1)}, u32[]{:S(2)}, u32[]{:S(2)}) collective-permute-start(bf16[272,1152]{1,0:T(8,128)(2,1)S(1)} %collective-permute-done.p0.refs_11_), channel_id=1, source_target_pairs={{0,2},{2,0},{1,3},{3,1},{4,6},{6,4},{5,7},{7,5},{8,10},{10,8},{9,1... | collective-permute-start | bytes 1880072 | tf_op jit(solution)/shard_map/ppermute | solution.py:1148
  38.8 2.2 collective-permute-start.6
  38.8 21.8 %collective-permute-start.4 = (bf16[384,768]{1,0:T(8,128)(2,1)}, bf16[384,768]{1,0:T(8,128)(2,1)S(1)}, u32[]{:S(2)}, u32[]{:S(2)}) collective-permute-start(bf16[384,768]{1,0:T(8,128)(2,1)} %get-tuple-element.143), channel_id=1, source_target_pairs={{0,1},{1,0},{2,3},{3,2},{4,5},{5,4},{6,7},{7,6},{8,9},{9,8},{10,11... | collective-permute-start | bytes 1769480 | tf_op jit(solution)/shard_map/ppermute | solution.py:1148
  40.3 20.4 %collective-permute-start.3 = (bf16[192,1536]{1,0:T(8,128)(2,1)}, bf16[192,1536]{1,0:T(8,128)(2,1)}, u32[]{:S(2)}, u32[]{:S(2)}) collective-permute-start(bf16[192,1536]{1,0:T(8,128)(2,1)} %collective-permute-done.2.p0.refs_15_), channel_id=1, source_target_pairs={{0,4},{4,0},{8,12},{12,8},{16,20},{20,16},{24,28},{28,24},{1,5},{5... | collective-permute-start | bytes 1769480 | tf_op jit(solution)/shard_map/ppermute | solution.py:1148
  60.7 3.9 %collective-permute-start.8 = (bf16[192,1536]{1,0:T(8,128)(2,1)}, bf16[192,1536]{1,0:T(8,128)(2,1)S(1)}, u32[]{:S(2)}, u32[]{:S(2)}) collective-permute-start(bf16[192,1536]{1,0:T(8,128)(2,1)} %collective-permute-done.2.p0.refs_15_), channel_id=1, source_target_pairs={{0,2},{2,0},{1,3},{3,1},{4,6},{6,4},{5,7},{7,5},{8,10},{10,8},{9,1... | collective-permute-start | bytes 1769480 | tf_op jit(solution)/shard_map/ppermute | solution.py:1148
  60.7 3.9 %collective-permute-start.9 = (bf16[192,1536]{1,0:T(8,128)(2,1)}, bf16[192,1536]{1,0:T(8,128)(2,1)S(1)}, u32[]{:S(2)}, u32[]{:S(2)}) collective-permute-start(bf16[192,1536]{1,0:T(8,128)(2,1)} %collective-permute-done.3.p1.refs_16_), channel_id=1, source_target_pairs={{0,2},{2,0},{1,3},{3,1},{4,6},{6,4},{5,7},{7,5},{8,10},{10,8},{9,1... | collective-permute-start | bytes 1769480 | tf_op jit(solution)/shard_map/ppermute | solution.py:1148
  61.2 17.9 %collective-permute-start.7 = (bf16[384,768]{1,0:T(8,128)(2,1)S(1)}, bf16[384,768]{1,0:T(8,128)(2,1)S(1)}, u32[]{:S(2)}, u32[]{:S(2)}) collective-permute-start(bf16[384,768]{1,0:T(8,128)(2,1)S(1)} %collective-permute-done.4.p0.refs_19_), channel_id=1, source_target_pairs={{0,4},{4,0},{8,12},{12,8},{16,20},{20,16},{24,28},{28,24},{1,5},{5... | collective-permute-start | bytes 1769480 | tf_op jit(solution)/shard_map/ppermute | solution.py:1148
  62.6 23.3 %collective-permute-start.12 = (bf16[1,512,768]{2,1,0:T(8,128)(2,1)}, bf16[1,512,768]{2,1,0:T(8,128)(2,1)S(1)}, u32[]{:S(2)}, u32[]{:S(2)}) collective-permute-start(bf16[1,512,768]{2,1,0:T(8,128)(2,1)} %get-tuple-element.161), channel_id=1, source_target_pairs={{0,1},{1,0},{2,3},{3,2},{4,5},{5,4},{6,7},{7,6},{8,9},{9,8},{10,11... | collective-permute-start | bytes 2359304 | tf_op jit(solution)/shard_map/ppermute | solution.py:1148
  63.2 43.0 %collective-permute-start.13 = (bf16[1,512,768]{2,1,0:T(8,128)(2,1)}, bf16[1,512,768]{2,1,0:T(8,128)(2,1)}, u32[]{:S(2)}, u32[]{:S(2)}) collective-permute-start(bf16[1,512,768]{2,1,0:T(8,128)(2,1)} %get-tuple-element.169), channel_id=1, source_target_pairs={{0,1},{1,0},{2,3},{3,2},{4,5},{5,4},{6,7},{7,6},{8,9},{9,8},{10,11... | collective-permute-start | bytes 2359304 | tf_op jit(solution)/shard_map/ppermute | solution.py:1148
  80.0 2.8 %collective-permute-start.11 = (bf16[384,768]{1,0:T(8,128)(2,1)S(1)}, bf16[384,768]{1,0:T(8,128)(2,1)S(1)}, u32[]{:S(2)}, u32[]{:S(2)}) collective-permute-start(bf16[384,768]{1,0:T(8,128)(2,1)S(1)} %collective-permute-done.7.p1.refs_20_), channel_id=1, source_target_pairs={{0,2},{2,0},{1,3},{3,1},{4,6},{6,4},{5,7},{7,5},{8,10},{10,8},{9,1... | collective-permute-start | bytes 1769480 | tf_op jit(solution)/shard_map/ppermute | solution.py:1148
  86.9 16.6 %all-to-all-start.1 = ((bf16[32,2,2304]{2,1,0:T(2,128)(2,1)}), bf16[32,2,2304]{2,1,0:T(2,128)(2,1)}, u32[]{:S(2)}, u32[]{:S(2)}) async-start(bf16[32,2,2304]{2,1,0:T(2,128)(2,1)} %bitcast.10), calls=%async_computation.1 | async-start | bytes 589824 | tf_op jit(solution)/shard_map/all_to_all | solution.py:1165
  117.3 2.9 %collective-permute-start.14 = (bf16[384,1536]{1,0:T(8,128)(2,1)S(1)}, bf16[384,1536]{1,0:T(8,128)(2,1)S(1)}, u32[]{:S(2)}, u32[]{:S(2)}) collective-permute-start(bf16[384,1536]{1,0:T(8,128)(2,1)S(1)} %get-tuple-element.175), channel_id=1, source_target_pairs={{0,2},{2,0},{1,3},{3,1},{4,6},{6,4},{5,7},{7,5},{8,10},{10,8},{9,1... | collective-permute-start | bytes 3538952 | tf_op jit(solution)/shard_map/ppermute | solution.py:1148
  121.5 37.4 %all-to-all-start.2 = ((bf16[8,48,1536]{2,1,0:T(8,128)(2,1)}), bf16[8,48,1536]{2,1,0:T(8,128)(2,1)S(1)}, u32[]{:S(2)}, u32[]{:S(2)}) async-start(bf16[8,48,1536]{2,1,0:T(8,128)(2,1)} %bitcast.11), calls=%async_computation.2 | async-start | bytes 2359296 | tf_op jit(solution)/shard_map/all_to_all | solution.py:1175
  158.9 7.8 %collective-permute-start.15 = (bf16[384,1536]{1,0:T(8,128)(2,1)}, bf16[384,1536]{1,0:T(8,128)(2,1)S(1)}, u32[]{:S(2)}, u32[]{:S(2)}) collective-permute-start(bf16[384,1536]{1,0:T(8,128)(2,1)} %get-tuple-element.187), channel_id=1, source_target_pairs={{0,2},{2,0},{1,3},{3,1},{4,6},{6,4},{5,7},{7,5},{8,10},{10,8},{9,1... | collective-permute-start | bytes 3538952 | tf_op jit(solution)/shard_map/ppermute | solution.py:1148
  160.2 35.6 %all-to-all-start.3 = ((bf16[8,48,1536]{2,1,0:T(8,128)(2,1)}), bf16[8,48,1536]{2,1,0:T(8,128)(2,1)}, u32[]{:S(2)}, u32[]{:S(2)}) async-start(bf16[8,48,1536]{2,1,0:T(8,128)(2,1)} %broadcast_in_dim.13), calls=%async_computation.3 | async-start | bytes 2359296 | tf_op jit(solution)/shard_map/all_to_all | solution.py:1181
  166.9 28.2 %collective-permute-start.16 = (bf16[384,1536]{1,0:T(8,128)(2,1)S(1)}, bf16[384,1536]{1,0:T(8,128)(2,1)S(1)}, u32[]{:S(2)}, u32[]{:S(2)}) collective-permute-start(bf16[384,1536]{1,0:T(8,128)(2,1)S(1)} %add.93), channel_id=1, source_target_pairs={{0,1},{1,0},{2,3},{3,2},{4,5},{5,4},{6,7},{7,6},{8,9},{9,8},{10,11... | collective-permute-start | bytes 3538952 | tf_op jit(solution)/shard_map/ppermute | solution.py:1148
  171.5 23.7 %collective-permute-start.17 = (f32[8,128]{1,0:T(8,128)S(1)}, f32[8,128]{1,0:T(8,128)S(1)}, u32[]{:S(2)}, u32[]{:S(2)}) collective-permute-start(f32[8,128]{1,0:T(8,128)S(1)} %copy-done.42), channel_id=1, source_target_pairs={{0,1},{1,0},{2,3},{3,2},{4,5},{5,4},{6,7},{7,6},{8,9},{9,8},{10,11... | collective-permute-start | bytes 12296 | tf_op jit(solution)/shard_map/ppermute | solution.py:1148
  195.9 3.1 %collective-permute-start.18 = (bf16[384,1536]{1,0:T(8,128)(2,1)}, bf16[384,1536]{1,0:T(8,128)(2,1)S(1)}, u32[]{:S(2)}, u32[]{:S(2)}) collective-permute-start(bf16[384,1536]{1,0:T(8,128)(2,1)} %get-tuple-element.208), channel_id=1, source_target_pairs={{0,2},{2,0},{1,3},{3,1},{4,6},{6,4},{5,7},{7,5},{8,10},{10,8},{9,1... | collective-permute-start | bytes 3538952 | tf_op jit(solution)/shard_map/ppermute | solution.py:1148
  196.6 2.2 collective-permute-start.19
  201.4 34.1 %all-to-all-start.4 = ((bf16[8,48,1536]{2,1,0:T(8,128)(2,1)}), bf16[8,48,1536]{2,1,0:T(8,128)(2,1)S(1)}, u32[]{:S(2)}, u32[]{:S(2)}) async-start(bf16[8,48,1536]{2,1,0:T(8,128)(2,1)} %bitcast.14), calls=%async_computation.4 | async-start | bytes 2359296 | tf_op jit(solution)/shard_map/all_to_all | solution.py:1175
  236.8 32.7 %all-to-all-start.5 = ((bf16[8,48,1536]{2,1,0:T(8,128)(2,1)}), bf16[8,48,1536]{2,1,0:T(8,128)(2,1)}, u32[]{:S(2)}, u32[]{:S(2)}) async-start(bf16[8,48,1536]{2,1,0:T(8,128)(2,1)} %broadcast_in_dim.14), calls=%async_computation.5 | async-start | bytes 2359296 | tf_op jit(solution)/shard_map/all_to_all | solution.py:1181
  241.2 3.1 %collective-permute-start.20 = (bf16[384,1536]{1,0:T(8,128)(2,1)}, bf16[384,1536]{1,0:T(8,128)(2,1)S(1)}, u32[]{:S(2)}, u32[]{:S(2)}) collective-permute-start(bf16[384,1536]{1,0:T(8,128)(2,1)} %bitcast.13.own_ref), channel_id=1, source_target_pairs={{0,2},{2,0},{1,3},{3,1},{4,6},{6,4},{5,7},{7,5},{8,10},{10,8},{9,1... | collective-permute-start | bytes 3538952 | tf_op jit(solution)/shard_map/ppermute | solution.py:1148
  241.3 11.5 %collective-permute-start.22 = (f32[8,128]{1,0:T(8,128)S(1)}, f32[8,128]{1,0:T(8,128)}, u32[]{:S(2)}, u32[]{:S(2)}) collective-permute-start(f32[8,128]{1,0:T(8,128)S(1)} %add.98), channel_id=1, source_target_pairs={{0,4},{4,0},{8,12},{12,8},{16,20},{20,16},{24,28},{28,24},{1,5},{5... | collective-permute-start | bytes 12296 | tf_op jit(solution)/shard_map/ppermute | solution.py:1148
  250.6 4.7 %collective-permute-start.21 = (f32[768]{0:T(1024)S(1)}, f32[768]{0:T(1024)S(1)}, u32[]{:S(2)}, u32[]{:S(2)}) collective-permute-start(f32[768]{0:T(1024)S(1)} %reduce_sum.45), channel_id=1, source_target_pairs={{0,1},{1,0},{2,3},{3,2},{4,5},{5,4},{6,7},{7,6},{8,9},{9,8},{10,11... | collective-permute-start | bytes 9224 | tf_op jit(solution)/shard_map/ppermute | solution.py:1148
  253.5 6.5 %collective-permute-start.23 = (f32[8,128]{1,0:T(8,128)S(1)}, f32[8,128]{1,0:T(8,128)S(1)}, u32[]{:S(2)}, u32[]{:S(2)}) collective-permute-start(f32[8,128]{1,0:T(8,128)S(1)} %add.99), channel_id=1, source_target_pairs={{0,8},{4,12},{8,0},{12,4},{16,24},{20,28},{24,16},{28,20},{1,9},{5... | collective-permute-start | bytes 12296 | tf_op jit(solution)/shard_map/ppermute | solution.py:1148
  269.5 5.7 %collective-permute-start.25 = (bf16[384,1536]{1,0:T(8,128)(2,1)}, bf16[384,1536]{1,0:T(8,128)(2,1)S(1)}, u32[]{:S(2)}, u32[]{:S(2)}) collective-permute-start(bf16[384,1536]{1,0:T(8,128)(2,1)} %bitcast.15.sum_ref), channel_id=1, source_target_pairs={{0,2},{2,0},{1,3},{3,1},{4,6},{6,4},{5,7},{7,5},{8,10},{10,8},{9,1... | collective-permute-start | bytes 3538952 | tf_op jit(solution)/shard_map/ppermute | solution.py:1148
  269.5 5.6 %collective-permute-start.27 = (f32[8,128]{1,0:T(8,128)S(1)}, f32[8,128]{1,0:T(8,128)S(1)}, u32[]{:S(2)}, u32[]{:S(2)}) collective-permute-start(f32[8,128]{1,0:T(8,128)S(1)} %add.100), channel_id=1, source_target_pairs={{0,16},{4,20},{8,24},{12,28},{16,0},{20,4},{24,8},{28,12},{1,17},{... | collective-permute-start | bytes 12296 | tf_op jit(solution)/shard_map/ppermute | solution.py:1148
  273.6 3.6 %collective-permute-start.24 = (f32[384]{0:T(512)S(1)}, f32[384]{0:T(512)S(1)}, u32[]{:S(2)}, u32[]{:S(2)}) collective-permute-start(f32[384]{0:T(512)S(1)} %slice_reduce_fusion), channel_id=1, source_target_pairs={{0,1},{1,0},{2,3},{3,2},{4,5},{5,4},{6,7},{7,6},{8,9},{9,8},{10,11... | collective-permute-start | bytes 4616 | tf_op jit(solution)/shard_map/ppermute | solution.py:1148
  (45 other events, 313.1 us)

commit v6 on v5

--- a/solution.py
+++ b/solution.py
@@ -1282,8 +1282,8 @@
     )
     proj_grad = mm(pooled, d_emb, TN)
     outer_grad = mm(got[:, d:], d_rows, TN)
-    inner_all, far_part, far_table, send_a, proj_grad, outer_grad = after(
-        inner_all, far_part, pc.across(table_b), send_a, proj_grad, outer_grad
+    inner_all, far_part, far_table, proj_grad, outer_grad = after(
+        inner_all, far_part, pc.across(table_b), proj_grad, outer_grad
     )
     table = table_a + far_table
     near_a, near_table = after(pc.core_swap(send_a), pc.core_swap(table))

time: 285 us -> 284 us (level)
    all_to_all x2, waiting for transfers between devices: 10.2 us -> 7.21 us  [gather(): lax.all_to_all(jnp.broadcast_to(x[None], (self.chips,) + x.shape), 'chip'...]
    unnamed x89 -> x93, local copies, waits for them, and re-layouts: 8.01 us -> 7.98 us
  transfers between devices with their start and end apart: 34 -> 34, of which waited for: 16 -> 14; matrix products, arithmetic and copies ran while one was open for 7% -> 7% of each run, Pallas kernels for 49% -> 50%
where the time goes in v6:
time: 284 us; the launch traced here: 278 us
  Pallas kernels  150 us (53%)
  starting transfers between devices  56.4 us (20%)
  waiting for transfers between devices  37.3 us (13%)
  local copies, waits for them, and re-layouts  18.6 us (7%)
  other arithmetic  9.31 us (3%)
  matrix products  4.9 us (2%)
    pallas_call x1, Pallas kernels, mid_bwd(): pl.pallas_call(mid_bwd_kernel, grid=(n,), in_specs=[SMEM_SPEC, SMEM_SPEC]...  30.9 us
    ppermute x28, starting transfers between devices, swap(): return lax.ppermute(x, axis, [(i, i ^ bit) for i in range(size)])  24.3 us
    pallas_call x1, Pallas kernels, attn_other(): pl.pallas_call(attn_other_kernel, grid=(n,), in_specs=[SMEM_SPEC, SMEM_SP...  18.6 us
    pallas_call x1, Pallas kernels, attn_bwd(): pl.pallas_call(attn_bwd_kernel, grid=(n,), in_specs=[SMEM_SPEC, SMEM_SPEC...  18.5 us
    ppermute x28, waiting for transfers between devices, swap(): return lax.ppermute(x, axis, [(i, i ^ bit) for i in range(size)])  17.3 us
    pallas_call x1, Pallas kernels, ffn_fwd(): pl.pallas_call(ffn_fwd_kernel, grid=(n,), in_specs=[SMEM_SPEC, SMEM_SPEC,...  13.5 us
    pallas_call x1, Pallas kernels, attn_own(): pl.pallas_call(attn_own_kernel, grid=(n,), in_specs=[SMEM_SPEC, row_spec(...  12.2 us
    all_to_all x2, starting transfers between devices, exchange(): lax.all_to_all(x.reshape(self.chips, rows // self.chips, width), 'chip',...  11.7 us
  transfers between devices with their start and end apart: 34, of which 14 were waited for; matrix products, arithmetic and copies ran while one was open for 7% of the time, Pallas kernels for 50%

profile of v6, /device:TPU:0, one launch (start us, length us, event | category | flops | bytes accessed | tf_op | source)
XLA Modules:
  0.0 278.2 jit_solution(1200311733401976257)
XLA Ops:
  0.7 3.5 %pack_weights.1 = (bf16[272,1152]{1,0:T(8,128)(2,1)}, bf16[192,1536]{1,0:T(8,128)(2,1)}, bf16[384,768]{1,0:T(8,128)(2,1)}) custom-call(s32[1]{0:T(128)} %bitcast.at_ref, f32[6,32]{1,0:T(8,128)} %bitcast.34, bf16[768,384]{1,0:T(8,128)(2,1)} %wq.9, bf16[768,384]{1,0:T(8,128)(2,1)} %wk.9, bf16[768,384]{1,0:T(8,128)(2,1)} %wv.9, bf16[384,768]{1,0:T(8,128)(2,1)} %wo_ref.1, ...), custom_call_target="tpu_custom_call" | custom-call | bytes 10800000 | tf_op jit(solution)/shard_map/pack_weights/pallas_call | solution.py:132
  4.2 3.0 %collective-permute-start = (bf16[272,1152]{1,0:T(8,128)(2,1)}, bf16[272,1152]{1,0:T(8,128)(2,1)S(1)}, u32[]{:S(2)}, u32[]{:S(2)}) collective-permute-start(bf16[272,1152]{1,0:T(8,128)(2,1)} %get-tuple-element.131), channel_id=1, source_target_pairs={{0,1},{1,0},{2,3},{3,2},{4,5},{5,4},{6,7},{7,6},{8,9},{9,8},{10,11... | collective-permute-start | bytes 1880072 | tf_op jit(solution)/shard_map/ppermute | solution.py:1148
  8.0 12.2 %attn_own.1 = (bf16[2,512,768]{2,1,0:T(8,128)(2,1)}, bf16[768,1024]{1,0:T(8,128)(2,1)}, bf16[2,512,384]{2,1,0:T(8,128)(2,1)}, bf16[2,384,512]{2,1,0:T(8,128)(2,1...) custom-call(s32[2]{0:T(128)} %copy-done.19, ...), custom_call_target="tpu_custom_call" | custom-call | bytes 43200000 | tf_op jit(solution)/shard_map/attn_own/pallas_call | solution.py:383
  21.5 1.7 collective-permute-start.1
  25.5 4.2 %all-to-all-start = ((bf16[32,2,896]{2,1,0:T(2,128)(2,1)}), bf16[32,2,896]{2,1,0:T(2,128)(2,1)S(1)}, u32[]{:S(2)}, u32[]{:S(2)}) async-start(bf16[32,2,896]{2,1,0:T(2,128)(2,1)} %broadcast_in_dim.10), calls=%async_computation | async-start | bytes 229376 | tf_op jit(solution)/shard_map/all_to_all | solution.py:1165
  31.8 7.0 %all-to-all-done = bf16[32,2,896]{2,1,0:T(2,128)(2,1)S(1)} async-done(((bf16[32,2,896]{2,1,0:T(2,128)(2,1)}), bf16[32,2,896]{2,1,0:T(2,128)(2,1)S(1)}, u32[]{:S(2)}, u32[]{:S(2)}) %all-to-all-start) | async-done | bytes 114720 | tf_op jit(solution)/shard_map/all_to_all | solution.py:1165
  42.0 18.6 %attn_other.1 = (bf16[2,512,384]{2,1,0:T(8,128)(2,1)}, bf16[2,384,512]{2,1,0:T(8,128)(2,1)}, bf16[2,512,384]{2,1,0:T(8,128)(2,1)}, bf16[2,512,384]{2,1,0:T(8,128...) custom-call(s32[2]{0:T(128)} %copy-done.19, ...), custom_call_target="tpu_custom_call" | custom-call | bytes 54000000 | tf_op jit(solution)/shard_map/attn_other/pallas_call | solution.py:408
  65.6 13.5 %ffn_fwd.1 = (bf16[2,512,1536]{2,1,0:T(8,128)(2,1)}, bf16[2,512,1536]{2,1,0:T(8,128)(2,1)}, bf16[2,512,1536]{2,1,0:T(8,128)(2,1)}, bf16[2,512,1536]{2,1,0:T(8,12...) custom-call(s32[2]{0:T(128)} %copy-done.19, s32[1]{0:T(128)} %bitcast.at_ref, ...), custom_call_target="tpu_custom_call" | custom-call | bytes 57600000 | tf_op jit(solution)/shard_map/ffn_fwd/pallas_call | solution.py:699
  86.9 5.4 %all-to-all-start.1 = ((bf16[32,2,2304]{2,1,0:T(2,128)(2,1)}), bf16[32,2,2304]{2,1,0:T(2,128)(2,1)}, u32[]{:S(2)}, u32[]{:S(2)}) async-start(bf16[32,2,2304]{2,1,0:T(2,128)(2,1)} %bitcast.10), calls=%async_computation.1 | async-start | bytes 589824 | tf_op jit(solution)/shard_map/all_to_all | solution.py:1165
  93.0 10.5 %pre_inner.1.pre_hbm = bf16[3,768,1536]{2,1,0:T(8,128)(2,1)} custom-call(s32[4]{0:T(128)} %get-tuple-element.138.lens, bf16[768,1024]{1,0:T(8,128)(2,1)} %get-tuple-element.162.fint_ref, bf16[2,512,1536]{2,1,0:T(8,128)(2,1)} %get-tuple-element.175.gp_ref.refs_1_, bf16[1,512,768]{2,1,0:T(8,128)(2,1)} %copy-done.34, bf16[768,1536]{1,0:T(8,128)(2,1)} %w_ref.5), custom_call_target="tpu_custom_call" | custom-call | bytes 32400000 | tf_op jit(solution)/shard_map/pre_inner/pallas_call | solution.py:769
  103.5 1.8 reshape.101
  108.8 8.5 %loss_inner.1 = (f32[8,128]{1,0:T(8,128)S(1)}, f32[8,768]{1,0:T(8,128)S(1)}, f32[8,1536]{1,0:T(8,128)S(1)}, bf16[64,768]{1,0:T(8,128)(2,1)S(1)}, bf16[64,768]{1,...) custom-call(s32[4]{0:T(128)S(1)} %get-tuple-element.137.me_ref, s32[1]{0:T(128)} %bitcast.at_ref, ...), custom_call_target="tpu_custom_call" | custom-call | bytes 43200000 | tf_op jit(solution)/shard_map/loss_inner/pallas_call | solution.py:873
  117.7 2.5 collective-permute-done.14
  121.5 6.4 %all-to-all-start.2 = ((bf16[8,48,1536]{2,1,0:T(8,128)(2,1)}), bf16[8,48,1536]{2,1,0:T(8,128)(2,1)S(1)}, u32[]{:S(2)}, u32[]{:S(2)}) async-start(bf16[8,48,1536]{2,1,0:T(8,128)(2,1)} %bitcast.11), calls=%async_computation.2 | async-start | bytes 2359296 | tf_op jit(solution)/shard_map/all_to_all | solution.py:1175
  127.9 30.9 %mid_bwd.1 = (f32[1024,768]{1,0:T(8,128)}, bf16[1024,768]{1,0:T(8,128)(2,1)}, bf16[1024,1152]{1,0:T(8,128)(2,1)}, bf16[384,1536]{1,0:T(8,128)(2,1)}, bf16[384,1536]{1,0:T(8,128)(2,1)}, /*index=5*/f32[8,128]{1,0:T(8,128)}) custom-call(s32[2]{0:T(128)} %copy-done.19, s32[1]{0:T(128)} %bitcast.at_ref, f32[8,1536]{1,0:T(8,128)} %copy-done.18, ...), custom_call_target="tpu_custom_call" | custom-call | bytes 115200000 | tf_op jit(solution)/shard_map/mid_bwd/pallas_call | solution.py:986
  160.2 6.4 %all-to-all-start.3 = ((bf16[8,48,1536]{2,1,0:T(8,128)(2,1)}), bf16[8,48,1536]{2,1,0:T(8,128)(2,1)}, u32[]{:S(2)}, u32[]{:S(2)}) async-start(bf16[8,48,1536]{2,1,0:T(8,128)(2,1)} %broadcast_in_dim.13), calls=%async_computation.3 | async-start | bytes 2359296 | tf_op jit(solution)/shard_map/all_to_all | solution.py:1181
  168.5 18.5 %attn_bwd.1 = (bf16[1024,1152]{1,0:T(8,128)(2,1)}, bf16[384,1536]{1,0:T(8,128)(2,1)}, bf16[384,1536]{1,0:T(8,128)(2,1)}, f32[8,128]{1,0:T(8,128)}) custom-call(s32[2]{0:T(128)} %copy-done.19, s32[1]{0:T(128)} %bitcast.at_ref, bf16[2,512,768]{2,1,0:T(8,128)(2,1)} %bitcast.31, bf16[384,768]{1,0:T(8,128)(2,1)} %wo_ref.1, ...), custom_call_target="tpu_custom_call" | custom-call | bytes 57600000 | tf_op jit(solution)/shard_map/attn_bwd/pallas_call | solution.py:629
  187.1 3.0 %fusion = f32[1536,768]{1,0:T(8,128)} fusion(bf16[64,768]{1,0:T(8,128)(2,1)S(1)} %copy-done.17, bf16[64,2304]{1,0:T(8,128)(2,1)S(1)} %copy-done.31), kind=kOutput, calls=%fused_computation.1 | convolution fusion | flops 150994944 | bytes 5013504 | tf_op jit(solution)/shard_map/dot_general | solution.py:31
  190.6 1.9 fusion.10
  192.5 2.8 collective-permute-done.17
  197.7 2.5 add_add_fusion
  200.2 5.3 %all-to-all-start.4 = ((bf16[8,48,1536]{2,1,0:T(8,128)(2,1)}), bf16[8,48,1536]{2,1,0:T(8,128)(2,1)S(1)}, u32[]{:S(2)}, u32[]{:S(2)}) async-start(bf16[8,48,1536]{2,1,0:T(8,128)(2,1)} %bitcast.14), calls=%async_computation.4 | async-start | bytes 2359296 | tf_op jit(solution)/shard_map/all_to_all | solution.py:1175
  205.5 11.6 %layer_part.1 = bf16[2,512,768]{2,1,0:T(8,128)(2,1)} custom-call(s32[1]{0:T(128)} %bitcast.at_ref, f32[2,512,768]{2,1,0:T(8,128)} %get-tuple-element.177.refs_3_.res_ref, bf16[2,512,1536]{2,1,0:T(8,128)(2,1)} %get-tuple-element.213.aa_ref, bf16[2,512,1536]{2,1,0:T(8,128)(2,1)} %get-tuple-element.214.ab_ref, bf16[1536,768]{1,0:T(8,128)(2,1)} %w_ref.4, ...), custom_call_target="tpu_custom_call" | custom-call | bytes 43200000 | tf_op jit(solution)/shard_map/layer_part/pallas_call | solution.py:1062
  217.1 11.6 %input_part.1 = f32[2,512,768]{2,1,0:T(8,128)} custom-call(s32[1]{0:T(128)} %bitcast.at_ref, bf16[2,512,768]{2,1,0:T(8,128)(2,1)} %x_ref.3, f32[1024,768]{1,0:T(8,128)} %get-tuple-element.210.dres_ref, f32[1,768]{1,0:T(1,128)} %reshape.98.gain_ref, bf16[1024,1152]{1,0:T(8,128)(2,1)} %get-tuple-element.211.ta_ref, ...), custom_call_target="tpu_custom_call" | custom-call | bytes 43200000 | tf_op jit(solution)/shard_map/input_part/pallas_call | solution.py:1037
  228.7 5.7 %all-to-all-done.4 = bf16[8,48,1536]{2,1,0:T(8,128)(2,1)S(1)} async-done(((bf16[8,48,1536]{2,1,0:T(8,128)(2,1)}), bf16[8,48,1536]{2,1,0:T(8,128)(2,1)S(1)}, u32[]{:S(2)}, u32[]{:S(2)}) %all-to-all-start.4) | async-done | bytes 1179680 | tf_op jit(solution)/shard_map/all_to_all | solution.py:1175
  235.7 4.4 %all-to-all-start.5 = ((bf16[8,48,1536]{2,1,0:T(8,128)(2,1)}), bf16[8,48,1536]{2,1,0:T(8,128)(2,1)}, u32[]{:S(2)}, u32[]{:S(2)}) async-start(bf16[8,48,1536]{2,1,0:T(8,128)(2,1)} %broadcast_in_dim.14), calls=%async_computation.5 | async-start | bytes 2359296 | tf_op jit(solution)/shard_map/all_to_all | solution.py:1181
  240.2 1.9 collective-permute-start.22
  242.1 5.8 %collective-permute-done.22 = f32[8,128]{1,0:T(8,128)S(1)} collective-permute-done((f32[8,128]{1,0:T(8,128)S(1)}, f32[8,128]{1,0:T(8,128)S(1)}, u32[]{:S(2)}, u32[]{:S(2)}) %collective-permute-start.22) | collective-permute-done | bytes 4128 | tf_op jit(solution)/shard_map/ppermute | solution.py:1148
  247.9 3.4 %collective-permute-start.23 = (f32[8,128]{1,0:T(8,128)S(1)}, f32[8,128]{1,0:T(8,128)}, u32[]{:S(2)}, u32[]{:S(2)}) collective-permute-start(f32[8,128]{1,0:T(8,128)S(1)} %add.99), channel_id=1, source_target_pairs={{0,8},{4,12},{8,0},{12,4},{16,24},{20,28},{24,16},{28,20},{1,9},{5... | collective-permute-start | bytes 12296 | tf_op jit(solution)/shard_map/ppermute | solution.py:1148
  251.3 4.8 %inner_done.1 = (f32[768,1536]{1,0:T(8,128)}, f32[24,768]{1,0:T(8,128)S(1)}) custom-call(s32[1]{0:T(128)} %bitcast.at_ref, bf16[384,1536]{1,0:T(8,128)(2,1)} %bitcast.13.own_ref, bf16[384,1536]{1,0:T(8,128)(2,1)S(1)} %collective-permute-done.20.near_ref, bf16[768,1536]{1,0:T(8,128)(2,1)S(1)} %copy-done.1), custom_call_target="tpu_custom_call" | custom-call | bytes 18000000 | tf_op jit(solution)/shard_map/inner_done/pallas_call | solution.py:1096
  261.9 6.6 %all-to-all-done.5 = bf16[8,48,1536]{2,1,0:T(8,128)(2,1)} async-done(((bf16[8,48,1536]{2,1,0:T(8,128)(2,1)}), bf16[8,48,1536]{2,1,0:T(8,128)(2,1)}, u32[]{:S(2)}, u32[]{:S(2)}) %all-to-all-start.5) | async-done | bytes 1179680 | tf_op jit(solution)/shard_map/all_to_all | solution.py:1181
  269.5 3.0 %attn_done.2 = (f32[768,384]{1,0:T(8,128)}, f32[768,384]{1,0:T(8,128)}, f32[768,384]{1,0:T(8,128)}, f32[384,768]{1,0:T(8,128)}, f32[8,384]{1,0:T(8,128)S(1)}) custom-call(s32[1]{0:T(128)} %bitcast.16.half_ref, bf16[384,1536]{1,0:T(8,128)(2,1)} %bitcast.15.sum_ref, bf16[768,384]{1,0:T(8,128)(2,1)S(1)} %copy-done.3, bf16[768,384]{1,0:T(8,128)(2,1)S(1)} %copy-done.4, ...), custom_call_target="tpu_custom_call" | custom-call | bytes 10800000 | tf_op jit(solution)/shard_map/attn_done/pallas_call | solution.py:1127
  (186 shorter events, 48.1 us)
Async XLA Ops:
  4.2 17.4 %collective-permute-start = (bf16[272,1152]{1,0:T(8,128)(2,1)}, bf16[272,1152]{1,0:T(8,128)(2,1)S(1)}, u32[]{:S(2)}, u32[]{:S(2)}) collective-permute-start(bf16[272,1152]{1,0:T(8,128)(2,1)} %get-tuple-element.131), channel_id=1, source_target_pairs={{0,1},{1,0},{2,3},{3,2},{4,5},{5,4},{6,7},{7,6},{8,9},{9,8},{10,11... | collective-permute-start | bytes 1880072 | tf_op jit(solution)/shard_map/ppermute | solution.py:1148
  21.5 17.3 %collective-permute-start.1 = (bf16[272,1152]{1,0:T(8,128)(2,1)S(1)}, bf16[272,1152]{1,0:T(8,128)(2,1)S(1)}, u32[]{:S(2)}, u32[]{:S(2)}) collective-permute-start(bf16[272,1152]{1,0:T(8,128)(2,1)S(1)} %collective-permute-done.p0.refs_11_), channel_id=1, source_target_pairs={{0,4},{4,0},{8,12},{12,8},{16,20},{20,16},{24,28},{28,24},{1,5},{5... | collective-permute-start | bytes 1880072 | tf_op jit(solution)/shard_map/ppermute | solution.py:1148
  23.2 17.1 %collective-permute-start.2 = (bf16[192,1536]{1,0:T(8,128)(2,1)}, bf16[192,1536]{1,0:T(8,128)(2,1)}, u32[]{:S(2)}, u32[]{:S(2)}) collective-permute-start(bf16[192,1536]{1,0:T(8,128)(2,1)} %get-tuple-element.139), channel_id=1, source_target_pairs={{0,1},{1,0},{2,3},{3,2},{4,5},{5,4},{6,7},{7,6},{8,9},{9,8},{10,11... | collective-permute-start | bytes 1769480 | tf_op jit(solution)/shard_map/ppermute | solution.py:1148
  25.5 13.4 %all-to-all-start = ((bf16[32,2,896]{2,1,0:T(2,128)(2,1)}), bf16[32,2,896]{2,1,0:T(2,128)(2,1)S(1)}, u32[]{:S(2)}, u32[]{:S(2)}) async-start(bf16[32,2,896]{2,1,0:T(2,128)(2,1)} %broadcast_in_dim.10), calls=%async_computation | async-start | bytes 229376 | tf_op jit(solution)/shard_map/all_to_all | solution.py:1165
  31.5 9.5 %collective-permute-start.5 = (bf16[272,1152]{1,0:T(8,128)(2,1)S(1)}, bf16[272,1152]{1,0:T(8,128)(2,1)S(1)}, u32[]{:S(2)}, u32[]{:S(2)}) collective-permute-start(bf16[272,1152]{1,0:T(8,128)(2,1)S(1)} %collective-permute-done.p0.refs_11_), channel_id=1, source_target_pairs={{0,2},{2,0},{1,3},{3,1},{4,6},{6,4},{5,7},{7,5},{8,10},{10,8},{9,1... | collective-permute-start | bytes 1880072 | tf_op jit(solution)/shard_map/ppermute | solution.py:1148
  38.8 2.2 collective-permute-start.6
  38.8 21.8 %collective-permute-start.4 = (bf16[384,768]{1,0:T(8,128)(2,1)}, bf16[384,768]{1,0:T(8,128)(2,1)S(1)}, u32[]{:S(2)}, u32[]{:S(2)}) collective-permute-start(bf16[384,768]{1,0:T(8,128)(2,1)} %get-tuple-element.142), channel_id=1, source_target_pairs={{0,1},{1,0},{2,3},{3,2},{4,5},{5,4},{6,7},{7,6},{8,9},{9,8},{10,11... | collective-permute-start | bytes 1769480 | tf_op jit(solution)/shard_map/ppermute | solution.py:1148
  40.3 20.3 %collective-permute-start.3 = (bf16[192,1536]{1,0:T(8,128)(2,1)}, bf16[192,1536]{1,0:T(8,128)(2,1)}, u32[]{:S(2)}, u32[]{:S(2)}) collective-permute-start(bf16[192,1536]{1,0:T(8,128)(2,1)} %collective-permute-done.2.p0.refs_15_), channel_id=1, source_target_pairs={{0,4},{4,0},{8,12},{12,8},{16,20},{20,16},{24,28},{28,24},{1,5},{5... | collective-permute-start | bytes 1769480 | tf_op jit(solution)/shard_map/ppermute | solution.py:1148
  60.6 3.9 %collective-permute-start.8 = (bf16[192,1536]{1,0:T(8,128)(2,1)}, bf16[192,1536]{1,0:T(8,128)(2,1)S(1)}, u32[]{:S(2)}, u32[]{:S(2)}) collective-permute-start(bf16[192,1536]{1,0:T(8,128)(2,1)} %collective-permute-done.2.p0.refs_15_), channel_id=1, source_target_pairs={{0,2},{2,0},{1,3},{3,1},{4,6},{6,4},{5,7},{7,5},{8,10},{10,8},{9,1... | collective-permute-start | bytes 1769480 | tf_op jit(solution)/shard_map/ppermute | solution.py:1148
  60.7 3.9 %collective-permute-start.9 = (bf16[192,1536]{1,0:T(8,128)(2,1)}, bf16[192,1536]{1,0:T(8,128)(2,1)S(1)}, u32[]{:S(2)}, u32[]{:S(2)}) collective-permute-start(bf16[192,1536]{1,0:T(8,128)(2,1)} %collective-permute-done.3.p1.refs_16_), channel_id=1, source_target_pairs={{0,2},{2,0},{1,3},{3,1},{4,6},{6,4},{5,7},{7,5},{8,10},{10,8},{9,1... | collective-permute-start | bytes 1769480 | tf_op jit(solution)/shard_map/ppermute | solution.py:1148
  61.2 17.9 %collective-permute-start.7 = (bf16[384,768]{1,0:T(8,128)(2,1)S(1)}, bf16[384,768]{1,0:T(8,128)(2,1)S(1)}, u32[]{:S(2)}, u32[]{:S(2)}) collective-permute-start(bf16[384,768]{1,0:T(8,128)(2,1)S(1)} %collective-permute-done.4.p0.refs_19_), channel_id=1, source_target_pairs={{0,4},{4,0},{8,12},{12,8},{16,20},{20,16},{24,28},{28,24},{1,5},{5... | collective-permute-start | bytes 1769480 | tf_op jit(solution)/shard_map/ppermute | solution.py:1148
  62.5 23.3 %collective-permute-start.12 = (bf16[1,512,768]{2,1,0:T(8,128)(2,1)}, bf16[1,512,768]{2,1,0:T(8,128)(2,1)S(1)}, u32[]{:S(2)}, u32[]{:S(2)}) collective-permute-start(bf16[1,512,768]{2,1,0:T(8,128)(2,1)} %get-tuple-element.160), channel_id=1, source_target_pairs={{0,1},{1,0},{2,3},{3,2},{4,5},{5,4},{6,7},{7,6},{8,9},{9,8},{10,11... | collective-permute-start | bytes 2359304 | tf_op jit(solution)/shard_map/ppermute | solution.py:1148
  63.2 43.0 %collective-permute-start.13 = (bf16[1,512,768]{2,1,0:T(8,128)(2,1)}, bf16[1,512,768]{2,1,0:T(8,128)(2,1)}, u32[]{:S(2)}, u32[]{:S(2)}) collective-permute-start(bf16[1,512,768]{2,1,0:T(8,128)(2,1)} %get-tuple-element.168), channel_id=1, source_target_pairs={{0,1},{1,0},{2,3},{3,2},{4,5},{5,4},{6,7},{7,6},{8,9},{9,8},{10,11... | collective-permute-start | bytes 2359304 | tf_op jit(solution)/shard_map/ppermute | solution.py:1148
  79.9 2.1 collective-permute-start.10
  80.0 2.8 %collective-permute-start.11 = (bf16[384,768]{1,0:T(8,128)(2,1)S(1)}, bf16[384,768]{1,0:T(8,128)(2,1)S(1)}, u32[]{:S(2)}, u32[]{:S(2)}) collective-permute-start(bf16[384,768]{1,0:T(8,128)(2,1)S(1)} %collective-permute-done.7.p1.refs_20_), channel_id=1, source_target_pairs={{0,2},{2,0},{1,3},{3,1},{4,6},{6,4},{5,7},{7,5},{8,10},{10,8},{9,1... | collective-permute-start | bytes 1769480 | tf_op jit(solution)/shard_map/ppermute | solution.py:1148
  86.9 16.6 %all-to-all-start.1 = ((bf16[32,2,2304]{2,1,0:T(2,128)(2,1)}), bf16[32,2,2304]{2,1,0:T(2,128)(2,1)}, u32[]{:S(2)}, u32[]{:S(2)}) async-start(bf16[32,2,2304]{2,1,0:T(2,128)(2,1)} %bitcast.10), calls=%async_computation.1 | async-start | bytes 589824 | tf_op jit(solution)/shard_map/all_to_all | solution.py:1165
  117.3 2.9 %collective-permute-start.14 = (bf16[384,1536]{1,0:T(8,128)(2,1)S(1)}, bf16[384,1536]{1,0:T(8,128)(2,1)S(1)}, u32[]{:S(2)}, u32[]{:S(2)}) collective-permute-start(bf16[384,1536]{1,0:T(8,128)(2,1)S(1)} %get-tuple-element.174), channel_id=1, source_target_pairs={{0,2},{2,0},{1,3},{3,1},{4,6},{6,4},{5,7},{7,5},{8,10},{10,8},{9,1... | collective-permute-start | bytes 3538952 | tf_op jit(solution)/shard_map/ppermute | solution.py:1148
  121.5 37.4 %all-to-all-start.2 = ((bf16[8,48,1536]{2,1,0:T(8,128)(2,1)}), bf16[8,48,1536]{2,1,0:T(8,128)(2,1)S(1)}, u32[]{:S(2)}, u32[]{:S(2)}) async-start(bf16[8,48,1536]{2,1,0:T(8,128)(2,1)} %bitcast.11), calls=%async_computation.2 | async-start | bytes 2359296 | tf_op jit(solution)/shard_map/all_to_all | solution.py:1175
  158.9 7.8 %collective-permute-start.15 = (bf16[384,1536]{1,0:T(8,128)(2,1)}, bf16[384,1536]{1,0:T(8,128)(2,1)S(1)}, u32[]{:S(2)}, u32[]{:S(2)}) collective-permute-start(bf16[384,1536]{1,0:T(8,128)(2,1)} %get-tuple-element.186), channel_id=1, source_target_pairs={{0,2},{2,0},{1,3},{3,1},{4,6},{6,4},{5,7},{7,5},{8,10},{10,8},{9,1... | collective-permute-start | bytes 3538952 | tf_op jit(solution)/shard_map/ppermute | solution.py:1148
  160.2 35.6 %all-to-all-start.3 = ((bf16[8,48,1536]{2,1,0:T(8,128)(2,1)}), bf16[8,48,1536]{2,1,0:T(8,128)(2,1)}, u32[]{:S(2)}, u32[]{:S(2)}) async-start(bf16[8,48,1536]{2,1,0:T(8,128)(2,1)} %broadcast_in_dim.13), calls=%async_computation.3 | async-start | bytes 2359296 | tf_op jit(solution)/shard_map/all_to_all | solution.py:1181
  166.9 28.3 %collective-permute-start.16 = (bf16[384,1536]{1,0:T(8,128)(2,1)S(1)}, bf16[384,1536]{1,0:T(8,128)(2,1)S(1)}, u32[]{:S(2)}, u32[]{:S(2)}) collective-permute-start(bf16[384,1536]{1,0:T(8,128)(2,1)S(1)} %add.93), channel_id=1, source_target_pairs={{0,1},{1,0},{2,3},{3,2},{4,5},{5,4},{6,7},{7,6},{8,9},{9,8},{10,11... | collective-permute-start | bytes 3538952 | tf_op jit(solution)/shard_map/ppermute | solution.py:1148
  187.0 9.6 %collective-permute-start.18 = (bf16[384,1536]{1,0:T(8,128)(2,1)}, bf16[384,1536]{1,0:T(8,128)(2,1)}, u32[]{:S(2)}, u32[]{:S(2)}) collective-permute-start(bf16[384,1536]{1,0:T(8,128)(2,1)} %get-tuple-element.206), channel_id=1, source_target_pairs={{0,2},{2,0},{1,3},{3,1},{4,6},{6,4},{5,7},{7,5},{8,10},{10,8},{9,1... | collective-permute-start | bytes 3538952 | tf_op jit(solution)/shard_map/ppermute | solution.py:1148
  190.1 5.2 %collective-permute-start.17 = (f32[8,128]{1,0:T(8,128)S(1)}, f32[8,128]{1,0:T(8,128)}, u32[]{:S(2)}, u32[]{:S(2)}) collective-permute-start(f32[8,128]{1,0:T(8,128)S(1)} %copy-done.44), channel_id=1, source_target_pairs={{0,1},{1,0},{2,3},{3,2},{4,5},{5,4},{6,7},{7,6},{8,9},{9,8},{10,11... | collective-permute-start | bytes 12296 | tf_op jit(solution)/shard_map/ppermute | solution.py:1148
  200.2 34.2 %all-to-all-start.4 = ((bf16[8,48,1536]{2,1,0:T(8,128)(2,1)}), bf16[8,48,1536]{2,1,0:T(8,128)(2,1)S(1)}, u32[]{:S(2)}, u32[]{:S(2)}) async-start(bf16[8,48,1536]{2,1,0:T(8,128)(2,1)} %bitcast.14), calls=%async_computation.4 | async-start | bytes 2359296 | tf_op jit(solution)/shard_map/all_to_all | solution.py:1175
  235.7 32.7 %all-to-all-start.5 = ((bf16[8,48,1536]{2,1,0:T(8,128)(2,1)}), bf16[8,48,1536]{2,1,0:T(8,128)(2,1)}, u32[]{:S(2)}, u32[]{:S(2)}) async-start(bf16[8,48,1536]{2,1,0:T(8,128)(2,1)} %broadcast_in_dim.14), calls=%async_computation.5 | async-start | bytes 2359296 | tf_op jit(solution)/shard_map/all_to_all | solution.py:1181
  240.1 11.2 %collective-permute-start.20 = (bf16[384,1536]{1,0:T(8,128)(2,1)}, bf16[384,1536]{1,0:T(8,128)(2,1)S(1)}, u32[]{:S(2)}, u32[]{:S(2)}) collective-permute-start(bf16[384,1536]{1,0:T(8,128)(2,1)} %bitcast.13.own_ref), channel_id=1, source_target_pairs={{0,2},{2,0},{1,3},{3,1},{4,6},{6,4},{5,7},{7,5},{8,10},{10,8},{9,1... | collective-permute-start | bytes 3538952 | tf_op jit(solution)/shard_map/ppermute | solution.py:1148
  240.2 7.7 %collective-permute-start.22 = (f32[8,128]{1,0:T(8,128)S(1)}, f32[8,128]{1,0:T(8,128)S(1)}, u32[]{:S(2)}, u32[]{:S(2)}) collective-permute-start(f32[8,128]{1,0:T(8,128)S(1)} %add.98), channel_id=1, source_target_pairs={{0,4},{4,0},{8,12},{12,8},{16,20},{20,16},{24,28},{28,24},{1,5},{5... | collective-permute-start | bytes 12296 | tf_op jit(solution)/shard_map/ppermute | solution.py:1148
  247.9 11.9 %collective-permute-start.23 = (f32[8,128]{1,0:T(8,128)S(1)}, f32[8,128]{1,0:T(8,128)}, u32[]{:S(2)}, u32[]{:S(2)}) collective-permute-start(f32[8,128]{1,0:T(8,128)S(1)} %add.99), channel_id=1, source_target_pairs={{0,8},{4,12},{8,0},{12,4},{16,24},{20,28},{24,16},{28,20},{1,9},{5... | collective-permute-start | bytes 12296 | tf_op jit(solution)/shard_map/ppermute | solution.py:1148
  257.6 3.7 %collective-permute-start.21 = (f32[768]{0:T(1024)S(1)}, f32[768]{0:T(1024)S(1)}, u32[]{:S(2)}, u32[]{:S(2)}) collective-permute-start(f32[768]{0:T(1024)S(1)} %reduce_sum.45), channel_id=1, source_target_pairs={{0,1},{1,0},{2,3},{3,2},{4,5},{5,4},{6,7},{7,6},{8,9},{9,8},{10,11... | collective-permute-start | bytes 9224 | tf_op jit(solution)/shard_map/ppermute | solution.py:1148
  268.4 5.7 %collective-permute-start.25 = (bf16[384,1536]{1,0:T(8,128)(2,1)}, bf16[384,1536]{1,0:T(8,128)(2,1)S(1)}, u32[]{:S(2)}, u32[]{:S(2)}) collective-permute-start(bf16[384,1536]{1,0:T(8,128)(2,1)} %bitcast.15.sum_ref), channel_id=1, source_target_pairs={{0,2},{2,0},{1,3},{3,1},{4,6},{6,4},{5,7},{7,5},{8,10},{10,8},{9,1... | collective-permute-start | bytes 3538952 | tf_op jit(solution)/shard_map/ppermute | solution.py:1148
  268.5 5.7 %collective-permute-start.27 = (f32[8,128]{1,0:T(8,128)S(1)}, f32[8,128]{1,0:T(8,128)S(1)}, u32[]{:S(2)}, u32[]{:S(2)}) collective-permute-start(f32[8,128]{1,0:T(8,128)S(1)} %add.100), channel_id=1, source_target_pairs={{0,16},{4,20},{8,24},{12,28},{16,0},{20,4},{24,8},{28,12},{1,17},{... | collective-permute-start | bytes 12296 | tf_op jit(solution)/shard_map/ppermute | solution.py:1148
  272.5 3.6 %collective-permute-start.24 = (f32[384]{0:T(512)S(1)}, f32[384]{0:T(512)S(1)}, u32[]{:S(2)}, u32[]{:S(2)}) collective-permute-start(f32[384]{0:T(512)S(1)} %slice_reduce_fusion), channel_id=1, source_target_pairs={{0,1},{1,0},{2,3},{3,2},{4,5},{5,4},{6,7},{7,6},{8,9},{9,8},{10,11... | collective-permute-start | bytes 4616 | tf_op jit(solution)/shard_map/ppermute | solution.py:1148
  (47 other events, 349.7 us)
